TPU v7x, 32 devices: a whole 2x2x4 slice. The times are simulated.
32 devices in a mesh: chol: 16 (over z, y, x), walker: 1, orb: 2 (over core).
Axes of the slice: x: 2, y: 2, z: 4, core: 2. Of those that a mesh axis runs over, the one named last changes fastest.
Arguments:
- chol_vals: bfloat16 [4096, 4, 64, 128], P('chol', 'orb'), may hold values from -0.05 to 0.05, as said below
- chol_cols: int32 [4096, 4, 2], P('chol', 'orb'), may hold values from 0 to 4, as said below
- greens: bfloat16 [32, 256, 256], P('walker', 'orb'), may hold values from -0.75 to 0.75
- walkers: bfloat16 [32, 256, 128], P('walker', 'orb'), may hold values from -6 to 6
- fields: float32 [4096, 32], P('chol', 'walker'), may hold values from -6 to 6
Outputs:
- new_walkers: bfloat16 [32, 256, 128], P('walker', 'orb')
- energy: float32 [32], P('walker')
Inputs may be any that keep to these rules, and one draw needn't show every extreme that they name: `chol_cols`: for every vector g and block row r, slot 0 holds r; the other slots hold distinct block columns different from r, or 4 for an empty slot. `chol_vals`: values of the stored blocks; entries in empty slots are not used.
All inputs are finite; a program needn't handle non-finite values.
Results may differ from a plain program's by a relative error of at most 0.0055.
Values may be sent and summed in bfloat16 or wider, within the bound.
No kernel may reach another device: no remote copies, remote signals or barrier semaphores. Data moves between devices by JAX's collectives and lax.ppermute only.
A program may use at most 128 MiB of HBM per device.

v0:
```python
import jax
import jax.numpy as jnp
from jax import lax
from jax.sharding import PartitionSpec as P

NORB = 256
BLOCK = 64
SLOTS = 2
TAYLOR = 4
ROWBLK = 4


def dense_rows(values, columns):
    vectors = values.shape[0]
    row_blocks = values.shape[1]
    pieces = values.reshape(vectors, row_blocks, BLOCK, SLOTS, BLOCK)
    onehot = (columns[..., None] == jnp.arange(ROWBLK, dtype=jnp.int32)).astype(jnp.bfloat16)
    placed = jnp.einsum("grsc,grisj->gricj", onehot, pieces, preferred_element_type=jnp.float32)
    return placed.astype(jnp.bfloat16).reshape(vectors, row_blocks * BLOCK * NORB)


def per_device(chol_vals, chol_cols, greens, walkers, fields):
    vectors = chol_vals.shape[0]
    walk_count = greens.shape[0]
    half_rows = greens.shape[1]
    step_factor = 72.0 / float(vectors * lax.axis_size("chol") * BLOCK) ** 0.5
    matrix = dense_rows(chol_vals, chol_cols)
    green_flat = greens.reshape(walk_count, half_rows * NORB)
    partial_bias = lax.dot_general(
        matrix, green_flat, (((1,), (1,)), ((), ())), preferred_element_type=jnp.float32
    )
    force_bias = lax.psum(partial_bias.astype(jnp.bfloat16), "orb").astype(jnp.float32)
    energy = lax.psum(0.5 * jnp.sum(force_bias * force_bias, axis=0), "chol")
    shifted = (fields - force_bias).astype(jnp.bfloat16)
    own_count = walk_count // lax.axis_size("chol")
    summed = lax.dot_general(
        shifted, matrix, (((0,), (0,)), ((), ())), preferred_element_type=jnp.float32
    )
    summed_field = lax.psum_scatter(
        summed.reshape(own_count * lax.axis_size("chol"), half_rows, NORB),
        "chol",
        scatter_dimension=0,
        tiled=True,
    )
    potential = (step_factor * summed_field).astype(jnp.bfloat16)
    first_walker = lax.axis_index("chol") * own_count
    start_rows = lax.dynamic_slice_in_dim(walkers, first_walker, own_count, 0)
    series_term = start_rows
    series_sum = jnp.zeros(start_rows.shape, jnp.float32)
    for degree in range(1, TAYLOR + 1):
        full_rows = lax.all_gather(series_term, "orb", axis=1, tiled=True)
        product = jnp.einsum(
            "wij,wja->wia", potential, full_rows, preferred_element_type=jnp.float32
        )
        series_term = (product / degree).astype(jnp.bfloat16)
        series_sum = series_sum + series_term.astype(jnp.float32)
    moved = (start_rows.astype(jnp.float32) + series_sum).astype(jnp.bfloat16)
    new_walkers = lax.all_gather(moved, "chol", axis=0, tiled=True)
    return (new_walkers, energy)


def solution(mesh):
    in_specs = (
        P("chol", "orb", None, None),
        P("chol", "orb", None),
        P("walker", "orb", None),
        P("walker", "orb", None),
        P("chol", "walker"),
    )
    out_specs = (P("walker", "orb", None), P("walker"))
    return jax.shard_map(
        per_device, mesh=mesh, in_specs=in_specs, out_specs=out_specs, check_vma=False
    )
```

profile of v0, /device:TPU:0, one launch (start us, length us, event | category | flops | bytes accessed | tf_op | source)
XLA Modules:
  0.0 338.0 jit_solution(4633083214097971021)
XLA Ops:
  7.2 0.0 copy-start
  7.2 0.0 reduce-scatter.2.cloned.1.call-start
  7.2 12.5 %copy.22 = bf16[256,2,64,128]{0,3,2,1:T(8,128)(2,1)} copy(bf16[256,2,64,128]{3,2,1,0:T(8,128)(2,1)} %param.5) | data formatting | bytes 16777216 | tf_op args[0]
  19.7 0.0 copy-start.3
  19.8 34.2 %copy.23 = bf16[256,2,64,2,64]{4,3,2,1,0:T(2,128)(2,1)} copy(bf16[256,2,64,2,64]{0,4,3,2,1:T(8,128)(2,1)} %bitcast.36) | data formatting | bytes 16777216 | tf_op jit(solution)/shard_map/reshape | solution.py:16
  53.9 0.0 copy-done.3
  53.9 0.2 copy.21
  54.1 31.5 %convert_bitcast_fusion = bf16[256,2,64,4,64]{4,3,2,1,0:T(4,128)(2,1)} fusion(bf16[256,2,64,2,64]{4,3,2,1,0:T(2,128)(2,1)} %copy.23, s32[256,2,2]{2,1,0:T(2,128)S(1)} %copy.21), kind=kOutput, calls=%fused_computation | convolution fusion | flops 41947136 | bytes 25169920 | tf_op jit(solution)/shard_map/grsc,grisj->gricj/dot_general | solution.py:18
  85.6 0.0 copy-start.1
  85.6 49.5 %copy.24 = bf16[256,2,64,4,64]{0,4,3,2,1:T(8,128)(2,1)} copy(bf16[256,2,64,4,64]{4,3,2,1,0:T(4,128)(2,1)} %convert_bitcast_fusion) | data formatting | bytes 33554432 | tf_op jit(solution)/shard_map/convert_element_type | solution.py:19
  135.1 0.0 copy-start.2
  135.1 0.0 copy-done.1
  135.1 1.2 copy.27
  136.3 8.8 %convolution_convert_fusion.1 = bf16[256,32]{0,1:T(8,128)(2,1)S(1)} fusion(bf16[32,32768]{1,0:T(8,128)(2,1)S(1)} %bitcast.37, bf16[256,32768]{0,1:T(8,128)(2,1)} %bitcast.34), kind=kOutput, calls=%fused_computation.12 | convolution fusion | flops 536879104 | bytes 18890752 | tf_op jit(solution)/shard_map/dot_general | solution.py:29
  145.1 3.6 %psum.14 = bf16[256,32]{0,1:T(8,128)(2,1)S(1)} all-reduce(bf16[256,32]{0,1:T(8,128)(2,1)S(1)} %convolution_convert_fusion.1), channel_id=1, replica_groups=mesh['chol'=16,'walker'=1,'orb'=2] {'orb'}, use_global_device_ids=true, to_apply=%region_0.0 | all-reduce | flops 8192 | bytes 32768 | tf_op jit(solution)/shard_map/psum | solution.py:32
  148.7 0.0 copy-done.2
  148.7 12.7 %fusion.14 = f32[32,128,256]{2,0,1:T(8,128)} fusion(bf16[128,256,256]{2,1,0:T(8,128)(2,1)} %bitcast.35, f32[256,32]{0,1:T(8,128)S(1)} %copy-done.2, bf16[256,32]{0,1:T(8,128)(2,1)S(1)} %psum.14), kind=kOutput, calls=%fused_computation.23 | convolution fusion | flops 536895488 | bytes 21020672 | tf_op jit(solution)/shard_map/dot_general | solution.py:36
  161.4 6.6 %copy.25 = f32[32,128,256]{2,1,0:T(8,128)} copy(f32[32,128,256]{2,0,1:T(8,128)} %fusion.14) | data formatting | bytes 8388608 | tf_op jit(solution)/shard_map/dot_general | solution.py:36
  168.0 0.0 reduce-scatter.2.cloned.1.call-update
  168.0 0.0 all-gather.2.cloned.1.call-start
  168.0 0.0 copy-done
  168.1 1.9 all_gather.15
  170.0 95.7 %reduce-scatter.2.cloned.1.call-done = f32[2,128,256]{2,1,0:T(8,128)} async-done(((f32[32,128,256]{2,1,0:T(8,128)}), f32[2,128,256]{2,1,0:T(8,128)}) %reduce-scatter.2.cloned.1.call-update) | async-done | bytes 262160 | tf_op jit(solution)/shard_map/reduce_scatter | solution.py:39
  265.7 1.0 multiply_convert_fusion
  266.7 0.2 convolution_convert_fusion
  266.9 1.9 all_gather.16
  268.8 0.2 fusion
  269.0 1.9 all_gather.17
  270.9 0.2 fusion.1
  271.0 1.9 all_gather.18
  272.9 0.8 fusion.6
  273.7 0.0 all-gather.2.cloned.1.call-update
  273.8 0.1 fusion.12
  273.9 40.5 %psum.15 = f32[32]{0:T(128)} all-reduce(f32[32]{0:T(128)S(1)} %broadcast_multiply_fusion), channel_id=1, replica_groups=mesh['chol'=16,'walker'=1,'orb'=2] {'chol'}, use_global_device_ids=true, to_apply=%region_3.0 | all-reduce | flops 32 | bytes 256 | tf_op jit(solution)/shard_map/psum | solution.py:33
  314.4 14.4 %all-gather.2.cloned.1.call-done = bf16[32,128,128]{2,1,0:T(8,128)(2,1)} async-done(((bf16[2,128,128]{2,1,0:T(8,128)(2,1)}), bf16[32,128,128]{2,1,0:T(8,128)(2,1)}) %all-gather.2.cloned.1.call-update) | async-done | bytes 1048592 | tf_op jit(solution)/shard_map/all_gather | solution.py:58
  328.9 2.3 copy.29
  (2 shorter events, 0.0 us)
Async XLA Ops:
  7.2 160.9 %copy-start = (bf16[32,128,128]{2,1,0:T(8,128)(2,1)S(1)}, bf16[32,128,128]{2,1,0:T(8,128)(2,1)}, u32[]{:S(2)}) copy-start(bf16[32,128,128]{2,1,0:T(8,128)(2,1)} %param.8) | copy-start | bytes 3145732
  7.2 258.5 %reduce-scatter.2.cloned.1.call-start = ((), (), s32[]{:S(2)}) async-start(), calls=%async_computation.1 | async-start | bytes 4456448 | tf_op jit(solution)/shard_map/reduce_scatter | solution.py:39
  19.7 34.2 %copy-start.3 = (s32[256,2,2]{0,2,1:T(2,128)S(1)}, s32[256,2,2]{0,2,1:T(2,128)}, u32[]{:S(2)}) copy-start(s32[256,2,2]{0,2,1:T(2,128)} %param.6) | copy-start | bytes 12292
  85.6 49.5 %copy-start.1 = (bf16[32,128,256]{2,1,0:T(8,128)(2,1)S(1)}, bf16[32,128,256]{2,1,0:T(8,128)(2,1)}, u32[]{:S(2)}) copy-start(bf16[32,128,256]{2,1,0:T(8,128)(2,1)} %param.7) | copy-start | bytes 6291460
  135.1 13.6 %copy-start.2 = (f32[256,32]{0,1:T(8,128)S(1)}, f32[256,32]{0,1:T(8,128)}, u32[]{:S(2)}) copy-start(f32[256,32]{0,1:T(8,128)} %param.9) | copy-start | bytes 98308
  168.0 160.9 %all-gather.2.cloned.1.call-start = ((), (), s32[]{:S(2)}) async-start(), calls=%async_computation.2 | async-start | bytes 1114112 | tf_op jit(solution)/shard_map/all_gather | solution.py:58
Sparse Core Ops, SparseCore 0:
  168.1 97.5 reduce-scatter.1
  273.9 54.9 all-gather.1
where the time goes:
time: 341 us; the launch traced here: 338 us
  waiting for transfers between devices  110 us (32%)
  local copies, waits for them, and re-layouts  106 us (31%)
  matrix products  54.3 us (16%)
  blocking collectives  51.8 us (15%)
  between operations  14.1 us (4%)
    reduce_scatter x1, waiting for transfers between devices, per_device(): lax.psum_scatter(summed.reshape(own_count * lax.axis_size('chol'), half_r...  95.7 us
    convert_element_type x1, local copies, waits for them, and re-layouts, dense_rows(): placed.astype(jnp.bfloat16).reshape(vectors, row_blocks * BLOCK * NORB)  49.5 us
    psum x1, blocking collectives, per_device(): energy = lax.psum(0.5 * jnp.sum(force_bias * force_bias, axis=0), 'chol')  40.5 us
    reshape x1, local copies, waits for them, and re-layouts, dense_rows(): pieces = values.reshape(vectors, row_blocks, BLOCK, SLOTS, BLOCK)  34.2 us
    dot_general x1, matrix products, dense_rows(): jnp.einsum('grsc,grisj->gricj', onehot, pieces, preferred_element_type=jn...  31.5 us
    unnamed x12, local copies, waits for them, and re-layouts  16.2 us
    all_gather x1, waiting for transfers between devices, per_device(): new_walkers = lax.all_gather(moved, 'chol', axis=0, tiled=True)  14.4 us
    dot_general x1, matrix products, per_device(): lax.dot_general(shifted, matrix, (((0,), (0,)), ((), ())), preferred_elem...  12.7 us
  transfers between devices with their start and end apart: 2, of which 2 were waited for; matrix products, arithmetic and copies ran while one was open for 0% of the time, Pallas kernels for 0%

commit v1 on v0

v1 whole, which is shorter than its diff:
```python
import functools

import jax
import jax.numpy as jnp
from jax import lax
from jax.experimental import pallas as pl
from jax.experimental.pallas import tpu as pltpu
from jax.sharding import PartitionSpec as P

BLOCK = 64
TAYLOR = 4
ROWBLK = 4
LANES = 2 * BLOCK
CHUNK = 16
VMEM_LIMIT = 56 * 1024 * 1024


def params():
    return pltpu.CompilerParams(vmem_limit_bytes=VMEM_LIMIT)


def column_order(row):
    other = 2 - 2 * (row // 2)
    return row, row + 1 - 2 * (row % 2), other, other + 1


def slot_masks(cols, row):
    return [cols == column for column in column_order(row)[1:]]


def bias_kernel(steps, vals_ref, greens_ref, cols_ref, turned_ref, bias_ref, v32, gx, gy, gyr, gs, acc):
    t = pl.program_id(0)
    local = t // steps
    row = lax.axis_index("orb") * cols_ref.shape[0] + local
    vectors = vals_ref.shape[0]
    walk = greens_ref.shape[0]

    v32[...] = vals_ref[:, 0].astype(jnp.float32).reshape(vectors * CHUNK, LANES)
    for i in range(CHUNK):
        turned_ref[:, i * LANES:(i + 1) * LANES] = v32[pl.ds(i, vectors, stride=CHUNK), :].astype(jnp.bfloat16)

    green = greens_ref[...].astype(jnp.float32)
    left = green[:, :, :LANES].reshape(walk * CHUNK, LANES)
    right = green[:, :, LANES:].reshape(walk * CHUNK, LANES)
    upper = row // 2 == 1
    pair = jnp.where(upper, right, left)
    rest = jnp.where(upper, left, right)
    gx[...] = jnp.where(row % 2 == 1, pltpu.roll(pair, BLOCK, 1), pair)
    gy[...] = rest
    gyr[...] = pltpu.roll(rest, BLOCK, 1)
    first = lax.broadcasted_iota(jnp.int32, (walk, LANES), 1) < BLOCK
    for i in range(CHUNK):
        cut = slice(i * LANES, (i + 1) * LANES)
        rows = pl.ds(i, walk, stride=CHUNK)
        x = gx[rows, :]
        gs[0:walk, cut] = jnp.where(first, x, 0.0).astype(jnp.bfloat16)
        gs[walk:2 * walk, cut] = jnp.where(first, 0.0, x).astype(jnp.bfloat16)
        gs[2 * walk:3 * walk, cut] = jnp.where(first, 0.0, gyr[rows, :]).astype(jnp.bfloat16)
        gs[3 * walk:4 * walk, cut] = jnp.where(first, 0.0, gy[rows, :]).astype(jnp.bfloat16)

    part = lax.dot_general(
        gs[...], turned_ref[...], (((1,), (1,)), ((), ())), preferred_element_type=jnp.float32
    )

    @pl.when(t % steps == 0)
    def _():
        acc[...] = part

    @pl.when(t % steps != 0)
    def _():
        acc[...] += part

    @pl.when(t == 0)
    def _():
        bias_ref[...] = jnp.zeros_like(bias_ref)

    @pl.when(t % steps == steps - 1)
    def _():
        total = acc[0:walk]
        cols = cols_ref[pl.ds(local, 1), 1, :]
        for k, mask in enumerate(slot_masks(cols, row)):
            total = total + jnp.where(mask, acc[(k + 1) * walk:(k + 2) * walk], 0.0)
        bias_ref[...] += total


def bias_call(vals, greens, cols):
    vectors, rowblocks = vals.shape[:2]
    walk, half_rows, norb = greens.shape
    steps = BLOCK // CHUNK
    wide = CHUNK * LANES
    grid = (rowblocks * steps,)
    return pl.pallas_call(
        functools.partial(bias_kernel, steps),
        grid=grid,
        in_specs=[
            pl.BlockSpec((vectors, 1, CHUNK, LANES), lambda t: (0, t // steps, t % steps, 0)),
            pl.BlockSpec((walk, CHUNK, norb), lambda t: (0, t, 0)),
            pl.BlockSpec(cols.shape, lambda t: (0, 0, 0)),
        ],
        out_specs=[
            pl.BlockSpec((vectors, wide), lambda t: (0, t)),
            pl.BlockSpec((walk, vectors), lambda t: (0, 0)),
        ],
        out_shape=[
            jax.ShapeDtypeStruct((vectors, rowblocks * BLOCK * LANES), jnp.bfloat16),
            jax.ShapeDtypeStruct((walk, vectors), jnp.float32),
        ],
        scratch_shapes=[
            pltpu.VMEM((vectors * CHUNK, LANES), jnp.float32),
            pltpu.VMEM((walk * CHUNK, LANES), jnp.float32),
            pltpu.VMEM((walk * CHUNK, LANES), jnp.float32),
            pltpu.VMEM((walk * CHUNK, LANES), jnp.float32),
            pltpu.VMEM((4 * walk, wide), jnp.bfloat16),
            pltpu.VMEM((4 * walk, vectors), jnp.float32),
        ],
        compiler_params=params(),
        name="force_bias",
    )(vals, greens, cols)


def potential_kernel(start, steps, layout, by_plane, fields_ref, own_ref, *refs):
    nz, plane, own = layout
    others = refs[:lax.axis_size("orb") - 1]
    cols_ref, turned_ref = refs[len(others):len(others) + 2]
    groups = plane if by_plane else nz
    outs = refs[len(others) + 2:len(others) + 2 + groups]
    energy_ref, s_ref, scratch = refs[len(others) + 2 + groups:]
    t = pl.program_id(0)
    walk, vectors = fields_ref.shape
    rowblocks = cols_ref.shape[0]

    @pl.when(t == 0)
    def _():
        me = lax.axis_index("chol")
        bias = own_ref[...]
        for other in others:
            bias = bias + other[...]
        energy = 0.5 * jnp.sum(bias * bias, axis=1, keepdims=True)
        energy_ref[...] = jnp.broadcast_to(energy, energy_ref.shape)
        shifted = (fields_ref[...] - bias).astype(jnp.bfloat16)
        at = lax.broadcasted_iota(jnp.int32, (walk, walk), 0)
        source = lax.broadcasted_iota(jnp.int32, (walk, walk), 1)
        chip = at // own
        z = (me // plane + chip // plane) % nz
        p = (me % plane) ^ (chip % plane)
        wanted = (z * plane + p) * own + at % own
        pick = (wanted == source).astype(jnp.float32).astype(jnp.bfloat16)
        ordered = jnp.dot(pick, shifted, preferred_element_type=jnp.float32)
        for local in range(rowblocks):
            row = lax.axis_index("orb") * rowblocks + local
            s_ref[local, 0:walk] = ordered.astype(jnp.bfloat16)
            for k, mask in enumerate(slot_masks(cols_ref[local, 1:2, :], row)):
                s_ref[local, (k + 1) * walk:(k + 2) * walk] = jnp.where(mask, ordered, 0.0).astype(jnp.bfloat16)

    left = s_ref[(start + t) // (BLOCK // CHUNK)]
    first = lax.broadcasted_iota(jnp.int32, (walk, LANES), 1) < BLOCK
    for i in range(0, CHUNK, 2):
        both = jnp.dot(left, turned_ref[:, i * LANES:(i + 2) * LANES], preferred_element_type=jnp.float32)
        for side in range(2):
            out = both[:, side * LANES:(side + 1) * LANES]
            near = jnp.where(first, out[0:walk], out[walk:2 * walk])
            far = jnp.where(first, pltpu.roll(out[2 * walk:3 * walk], BLOCK, 1), out[3 * walk:])
            scratch[(i + side) * walk:(i + side + 1) * walk, :] = near
            scratch[(CHUNK + i + side) * walk:(CHUNK + i + side + 1) * walk, :] = far
    for w in range(walk):
        chip, j = w // own, w % own
        group, inner = (chip % plane, chip // plane) if by_plane else (chip // plane, chip % plane)
        for half in range(2):
            tile = scratch[pl.ds(half * CHUNK * walk + w, CHUNK, stride=walk), :]
            outs[group][inner, j, half * CHUNK:(half + 1) * CHUNK, :] = tile.astype(jnp.bfloat16)


def potential_call(start, steps, layout, by_plane, fields, bias, others, cols, turned):
    nz, plane, own = layout
    walk, vectors = fields.shape
    groups, inner = (plane, nz) if by_plane else (nz, plane)
    whole = lambda a: pl.BlockSpec(a.shape, lambda t: (0,) * a.ndim)
    small = [fields, bias, *others, cols]
    rows = 2 * CHUNK
    energy = jax.ShapeDtypeStruct((walk, LANES), jnp.float32)
    *parts, energy = pl.pallas_call(
        functools.partial(potential_kernel, start, steps, layout, by_plane),
        grid=(steps,),
        in_specs=[
            *map(whole, small),
            pl.BlockSpec((vectors, CHUNK * LANES), lambda t: (0, start + t)),
        ],
        out_specs=[
            *[pl.BlockSpec((inner, own, rows, LANES), lambda t: (0, 0, t, 0))] * groups,
            whole(energy),
        ],
        out_shape=[
            *[jax.ShapeDtypeStruct((inner, own, steps * rows, LANES), jnp.bfloat16)] * groups,
            energy,
        ],
        scratch_shapes=[
            pltpu.VMEM((cols.shape[0], 4 * walk, vectors), jnp.bfloat16),
            pltpu.VMEM((2 * CHUNK * walk, LANES), jnp.float32),
        ],
        compiler_params=params(),
        name="potential",
    )(*small, turned)
    return parts, energy


def sum_kernel(count, *refs):
    ins, outs = refs[:count], refs[count:]
    for k, out in enumerate(outs):
        total = ins[0][k].astype(jnp.float32)
        for ref in ins[1:]:
            total = total + ref[k].astype(jnp.float32)
        out[...] = total.astype(out.dtype)


def sum_call(arrays):
    pieces = arrays[0].shape[0]
    shape = jax.ShapeDtypeStruct(arrays[0].shape[1:], jnp.bfloat16)
    return pl.pallas_call(
        functools.partial(sum_kernel, len(arrays)),
        out_shape=[shape] * pieces,
        compiler_params=params(),
        name="sum_parts",
    )(*arrays)


def series_kernel(sizes, *refs):
    n_orb, late_steps, early_steps = sizes
    late, early, start = refs[:n_orb], refs[n_orb:2 * n_orb], refs[2 * n_orb:3 * n_orb]
    plane_ref, z_ref, pot, term, total = refs[3 * n_orb:]
    me = lax.axis_index("orb")
    own, half_rows = start[0].shape[:2]
    rowblocks = half_rows // BLOCK
    per = BLOCK // CHUNK
    for d in range(n_orb):
        at = lax.rem(me + d, n_orb)
        term[pl.ds(at, 1)] = start[d][...][None]
        for t in range(rowblocks * per):
            ref, k = (early[d], t) if t < early_steps else (late[d], t - early_steps)
            for half in range(2):
                rows = slice((2 * k + half) * CHUNK, (2 * k + half + 1) * CHUNK)
                pot[pl.ds(at * rowblocks + t // per, 1), :, (t % per) * CHUNK:(t % per + 1) * CHUNK,
                    half * LANES:(half + 1) * LANES] = ref[:, rows, :][None]
    for j in range(own):
        blocks = [term[r // rowblocks, j, (r % rowblocks) * BLOCK:(r % rowblocks + 1) * BLOCK] for r in range(ROWBLK)]
        sums = [jnp.zeros(blocks[0].shape, jnp.float32)] * ROWBLK
        begin = blocks
        for degree in range(1, TAYLOR + 1):
            after = []
            for r in range(ROWBLK):
                right = jnp.concatenate([blocks[c] for c in column_order(r)], axis=0)
                product = jnp.dot(pot[r, j], right, preferred_element_type=jnp.float32)
                after.append((product / degree).astype(jnp.bfloat16))
            blocks = after
            sums = [s + b.astype(jnp.float32) for s, b in zip(sums, blocks)]
        for r in range(ROWBLK):
            moved = begin[r].astype(jnp.float32) + sums[r]
            total[r // rowblocks, j, (r % rowblocks) * BLOCK:(r % rowblocks + 1) * BLOCK] = moved.astype(jnp.bfloat16)
    mine = total[pl.ds(me, 1)][0]
    cut = z_ref.shape[1]
    z_ref[...] = mine[:, :cut]
    plane_ref[...] = mine[:, cut:]


def series_call(sizes, cut, late, early, start):
    n_orb = sizes[0]
    own, half_rows, nocc = start[0].shape
    return pl.pallas_call(
        functools.partial(series_kernel, sizes),
        out_shape=[
            jax.ShapeDtypeStruct((own, half_rows - cut, nocc), jnp.bfloat16),
            jax.ShapeDtypeStruct((own, cut, nocc), jnp.bfloat16),
        ],
        scratch_shapes=[
            pltpu.VMEM((ROWBLK, own, BLOCK, 2 * LANES), jnp.bfloat16),
            pltpu.VMEM((n_orb, own, half_rows, nocc), jnp.bfloat16),
            pltpu.VMEM((n_orb, own, half_rows, nocc), jnp.bfloat16),
        ],
        compiler_params=params(),
        name="series",
    )(*late, *early, *start)


def place_kernel(layout, *refs):
    nz, plane, own = layout
    z_first, plane_first = refs[:plane], refs[plane:plane + nz]
    out, sems = refs[plane + nz:]
    me = lax.axis_index("chol")
    cut = z_first[0].shape[2]
    copies = []
    for dp in range(plane):
        for dz in range(nz):
            chip = lax.rem(me // plane + nz - dz, nz) * plane + (lax.rem(me, plane) ^ dp)
            to = pl.ds(chip * own, own)
            n = 2 * (dp * nz + dz)
            copies.append(pltpu.make_async_copy(z_first[dp].at[dz], out.at[to, :cut], sems.at[n]))
            copies.append(pltpu.make_async_copy(plane_first[dz].at[dp], out.at[to, cut:], sems.at[n + 1]))
    for copy in copies:
        copy.start()
    for copy in copies:
        copy.wait()


def place_call(layout, z_first, plane_first):
    nz, plane, own = layout
    cut, rest, nocc = z_first[0].shape[2], plane_first[0].shape[2], z_first[0].shape[3]
    return pl.pallas_call(
        functools.partial(place_kernel, layout),
        in_specs=[pl.BlockSpec(memory_space=pl.ANY)] * (nz + plane),
        out_specs=pl.BlockSpec(memory_space=pl.ANY),
        out_shape=jax.ShapeDtypeStruct((nz * plane * own, cut + rest, nocc), jnp.bfloat16),
        scratch_shapes=[pltpu.SemaphoreType.DMA((2 * nz * plane,))],
        compiler_params=params(),
        name="place_walkers",
    )(*z_first, *plane_first)


def per_device(chol_vals, chol_cols, greens, walkers, fields):
    vectors, rowblocks = chol_vals.shape[:2]
    walk, half_rows = greens.shape[:2]
    chips = lax.axis_size("chol")
    n_orb = lax.axis_size("orb")
    plane = 4 if chips % 4 == 0 else 1
    nz = chips // plane
    own = walk // chips
    layout = (nz, plane, own)
    step_factor = 72.0 / float(vectors * chips * BLOCK) ** 0.5
    me = lax.axis_index("chol")

    def to_plane(a, dp):
        return lax.ppermute(a, "chol", [(c, (c // plane) * plane + ((c % plane) ^ dp)) for c in range(chips)])

    def to_z(a, dz):
        return lax.ppermute(a, "chol", [(c, ((c // plane + dz) % nz) * plane + c % plane) for c in range(chips)])

    def around_orb(a):
        return [a] + [lax.ppermute(a, "orb", [((c + d) % n_orb, c) for c in range(n_orb)]) for d in range(1, n_orb)]

    cols = jnp.transpose(chol_cols, (1, 2, 0))
    mine = lax.dynamic_slice_in_dim(walkers, me * own, own, 0)
    start = around_orb(mine)

    turned, partial_bias = bias_call(chol_vals, greens, cols)
    bias, *others = around_orb(partial_bias)

    total_steps = rowblocks * BLOCK // CHUNK
    early_steps = total_steps * 3 // 8
    late_steps = total_steps - early_steps
    fields_t = fields.T
    early, energy = potential_call(0, early_steps, layout, False, fields_t, bias, others, cols, turned)
    early_in = [early[0]] + [to_z(early[dz], dz) for dz in range(1, nz)]
    late, _ = potential_call(early_steps, late_steps, layout, True, fields_t, bias, others, cols, turned)
    late_in = [late[0]] + [to_plane(late[dp], dp) for dp in range(1, plane)]
    early_sums = sum_call(early_in)
    early_in = [early_sums[0]] + [to_plane(early_sums[dp], dp) for dp in range(1, plane)]
    late_sums = sum_call(late_in)
    late_in = [late_sums[0]] + [to_z(late_sums[dz], dz) for dz in range(1, nz)]

    energy = energy[:, 0]
    energy = energy + sum(to_plane(energy, dp) for dp in range(1, plane))
    energy = energy + sum(to_z(energy, dz) for dz in range(1, nz))

    def finish(arrays):
        total = arrays[0].astype(jnp.float32)
        for a in arrays[1:]:
            total = total + a.astype(jnp.float32)
        return around_orb((step_factor * total).astype(jnp.bfloat16))

    cut = half_rows // CHUNK * 5 // 8 * CHUNK
    b_part, a_part = series_call((n_orb, late_steps, early_steps), cut, finish(late_in), finish(early_in), start)

    a_all = jnp.stack([a_part] + [to_z(a_part, dz) for dz in range(1, nz)])
    b_all = jnp.stack([b_part] + [to_plane(b_part, dp) for dp in range(1, plane)])
    z_first = [a_all] + [to_plane(a_all, dp) for dp in range(1, plane)]
    plane_first = [b_all] + [to_z(b_all, dz) for dz in range(1, nz)]
    return place_call(layout, z_first, plane_first), energy


def solution(mesh):
    in_specs = (
        P("chol", "orb", None, None),
        P("chol", "orb", None),
        P("walker", "orb", None),
        P("walker", "orb", None),
        P("chol", "walker"),
    )
    out_specs = (P("walker", "orb", None), P("walker"))
    return jax.shard_map(
        per_device, mesh=mesh, in_specs=in_specs, out_specs=out_specs, check_vma=False
    )
```

time: 341 us -> 143 us (0.42)
  local copies, waits for them, and re-layouts: 106 us -> 4.12 us
  waiting for transfers between devices: 110 us -> 26 us
  Pallas kernels: 0 us -> 66.3 us
  matrix products: 54.3 us -> 0 us
  blocking collectives: 51.8 us -> 0 us
  starting transfers between devices: 0.08 us -> 41.2 us
  between operations: 14.1 us -> 0.94 us
    reduce_scatter x1 -> x0, waiting for transfers between devices: 95.7 us -> none  [per_device(): lax.psum_scatter(summed.reshape(own_count * lax.axis_size('chol'), half_r...]
    pallas_call x0 -> x7, Pallas kernels: none -> 66.3 us  [the longest x1 33.2 us: place_call(): pl.pallas_call(functools.partial(place_kernel, layout), in_specs=[pl.Bloc...]
    dot_general x7 -> x0, matrix products: 54.3 us -> none  [the longest x1 31.5 us: dense_rows(): jnp.einsum('grsc,grisj->gricj', onehot, pieces, preferred_element_type=jn...]
    convert_element_type x1 -> x0, local copies, waits for them, and re-layouts: 49.5 us -> none  [dense_rows(): placed.astype(jnp.bfloat16).reshape(vectors, row_blocks * BLOCK * NORB)]
    psum x2 -> x0, blocking collectives: 44.2 us -> none  [the longest x1 40.5 us: per_device(): energy = lax.psum(0.5 * jnp.sum(force_bias * force_bias, axis=0), 'chol')]
    ppermute x0 -> x34, starting transfers between devices: none -> 41.2 us  [the longest x15 22.7 us: to_z(): lax.ppermute(a, 'chol', [(c, (c // plane + dz) % nz * plane + c % plane)...]
    reshape x1 -> x0, local copies, waits for them, and re-layouts: 34.2 us -> none  [dense_rows(): pieces = values.reshape(vectors, row_blocks, BLOCK, SLOTS, BLOCK)]
    ppermute x0 -> x34, waiting for transfers between devices: none -> 26 us  [the longest x15 20.2 us: to_z(): lax.ppermute(a, 'chol', [(c, (c // plane + dz) % nz * plane + c % plane)...]
  transfers between devices with their start and end apart: 2 -> 34, of which waited for: 2 -> 10; matrix products, arithmetic and copies ran while one was open for 0% -> 3% of each run, Pallas kernels for 0% -> 9%
where the time goes in v1:
time: 143 us; the launch traced here: 142 us
  Pallas kernels  66.3 us (46%)
  starting transfers between devices  41.2 us (29%)
  waiting for transfers between devices  26 us (18%)
  local copies, waits for them, and re-layouts  4.12 us (3%)
  other arithmetic  3.84 us (3%)
    pallas_call x1, Pallas kernels, place_call(): pl.pallas_call(functools.partial(place_kernel, layout), in_specs=[pl.Bloc...  33.2 us
    ppermute x15, starting transfers between devices, to_z(): lax.ppermute(a, 'chol', [(c, (c // plane + dz) % nz * plane + c % plane)...  22.7 us
    ppermute x15, waiting for transfers between devices, to_z(): lax.ppermute(a, 'chol', [(c, (c // plane + dz) % nz * plane + c % plane)...  20.2 us
    ppermute x15, starting transfers between devices, to_plane(): lax.ppermute(a, 'chol', [(c, c // plane * plane + (c % plane ^ dp)) for c...  17.7 us
    pallas_call x1, Pallas kernels, bias_call(): pl.pallas_call(functools.partial(bias_kernel, steps), grid=grid, in_specs...  15.1 us
    pallas_call x2, Pallas kernels, potential_call(): pl.pallas_call(functools.partial(potential_kernel, start, steps, layout,...  11.2 us
    ppermute x15, waiting for transfers between devices, to_plane(): lax.ppermute(a, 'chol', [(c, c // plane * plane + (c % plane ^ dp)) for c...  4.76 us
    pallas_call x2, Pallas kernels, sum_call(): pl.pallas_call(functools.partial(sum_kernel, len(arrays)), out_shape=[sha...  4.01 us
  transfers between devices with their start and end apart: 34, of which 10 were waited for; matrix products, arithmetic and copies ran while one was open for 3% of the time, Pallas kernels for 9%

profile of v1, /device:TPU:0, one launch (start us, length us, event | category | flops | bytes accessed | tf_op | source)
XLA Modules:
  0.0 142.4 jit_solution(12676787910298123311)
XLA Ops:
  0.6 15.1 %force_bias.1 = (bf16[256,16384]{1,0:T(8,128)(2,1)}, f32[32,256]{1,0:T(8,128)}) custom-call(bf16[256,2,64,128]{3,2,1,0:T(8,128)(2,1)} %vals_ref.1, bf16[32,128,256]{2,1,0:T(8,128)(2,1)} %greens_ref.1, s32[2,2,256]{2,1,0:T(2,128)} %bitcast.16), custom_call_target="tpu_custom_call" | custom-call | tf_op jit(solution)/shard_map/force_bias/pallas_call | solution.py:92
  15.7 0.5 collective-permute-start
  16.2 1.1 collective-permute-done.refs_0_
  17.2 0.6 copy-done.15
  17.8 4.6 %potential.3 = (bf16[4,2,96,128]{3,2,1,0:T(8,128)(2,1)}, bf16[4,2,96,128]{3,2,1,0:T(8,128)(2,1)}, bf16[4,2,96,128]{3,2,1,0:T(8,128)(2,1)}, bf16[4,2,96,128]{3,2,1,0:T(8,128)(2,1)}, f32[32,128]{1,0:T(8,128)}) custom-call(f32[32,256]{1,0:T(8,128)} %bitcast.10, f32[32,256]{1,0:T(8,128)} %get-tuple-element.23.own_ref, f32[32,256]{1,0:T(8,128)} %copy-done.15, ...), custom_call_target="tpu_custom_call" | custom-call | tf_op jit(solution)/shard_map/potential/pallas_call | solution.py:181
  22.5 5.0 %collective-permute-start.10 = (bf16[4,2,96,128]{3,2,1,0:T(8,128)(2,1)}, bf16[4,2,96,128]{3,2,1,0:T(8,128)(2,1)S(1)}, u32[]{:S(2)}, u32[]{:S(2)}) collective-permute-start(bf16[4,2,96,128]{3,2,1,0:T(8,128)(2,1)} %get-tuple-element.36), channel_id=1, source_target_pairs={{0,24},{2,26},{4,28},{6,30},{8,0},{10,2},{12,4},{14,6},{16,8},{18,... | collective-permute-start | bytes 589832 | tf_op jit(solution)/shard_map/ppermute | solution.py:333
  27.5 6.6 %potential.2 = (bf16[4,2,160,128]{3,2,1,0:T(8,128)(2,1)}, bf16[4,2,160,128]{3,2,1,0:T(8,128)(2,1)}, bf16[4,2,160,128]{3,2,1,0:T(8,128)(2,1)}, bf16[4,2,160,128]{3,2,1,0:T(8,128)(2,1)}, f32[32,128]{1,0:T(8,128)}) custom-call(f32[32,256]{1,0:T(8,128)} %bitcast.11, f32[32,256]{1,0:T(8,128)} %get-tuple-element.23.own_ref, f32[32,256]{1,0:T(8,128)} %copy-done.15, ...), custom_call_target="tpu_custom_call" | custom-call | tf_op jit(solution)/shard_map/potential/pallas_call | solution.py:181
  34.1 1.5 %collective-permute-start.1 = (bf16[4,2,160,128]{3,2,1,0:T(8,128)(2,1)}, bf16[4,2,160,128]{3,2,1,0:T(8,128)(2,1)S(1)}, u32[]{:S(2)}, u32[]{:S(2)}) collective-permute-start(bf16[4,2,160,128]{3,2,1,0:T(8,128)(2,1)} %get-tuple-element.26), channel_id=1, source_target_pairs={{0,2},{2,0},{4,6},{6,4},{8,10},{10,8},{12,14},{14,12},{16,18},{18,... | collective-permute-start | bytes 983048 | tf_op jit(solution)/shard_map/ppermute | solution.py:330
  35.6 1.5 %collective-permute-start.2 = (bf16[4,2,160,128]{3,2,1,0:T(8,128)(2,1)}, bf16[4,2,160,128]{3,2,1,0:T(8,128)(2,1)S(1)}, u32[]{:S(2)}, u32[]{:S(2)}) collective-permute-start(bf16[4,2,160,128]{3,2,1,0:T(8,128)(2,1)} %get-tuple-element.27), channel_id=1, source_target_pairs={{0,4},{2,6},{4,0},{6,2},{8,12},{10,14},{12,8},{14,10},{16,20},{18,... | collective-permute-start | bytes 983048 | tf_op jit(solution)/shard_map/ppermute | solution.py:330
  37.1 0.5 collective-permute-start.3
  37.6 1.0 collective-permute-start.9
  38.7 8.6 %collective-permute-done.8.refs_1_ = bf16[4,2,96,128]{3,2,1,0:T(8,128)(2,1)S(1)} collective-permute-done((bf16[4,2,96,128]{3,2,1,0:T(8,128)(2,1)S(1)}, bf16[4,2,96,128]{3,2,1,0:T(8,128)(2,1)S(1)}, u32[]{:S(2)}, u32[]{:S(2)}) %collective-permute-start.8) | collective-permute-done | bytes 196640 | tf_op jit(solution)/shard_map/ppermute | solution.py:333
  47.3 5.6 %collective-permute-done.9.refs_2_ = bf16[4,2,96,128]{3,2,1,0:T(8,128)(2,1)S(1)} collective-permute-done((bf16[4,2,96,128]{3,2,1,0:T(8,128)(2,1)S(1)}, bf16[4,2,96,128]{3,2,1,0:T(8,128)(2,1)S(1)}, u32[]{:S(2)}, u32[]{:S(2)}) %collective-permute-start.9) | collective-permute-done | bytes 196640 | tf_op jit(solution)/shard_map/ppermute | solution.py:333
  52.9 0.7 copy-done.10
  53.6 1.9 %sum_parts.3 = (bf16[2,96,128]{2,1,0:T(8,128)(2,1)}, bf16[2,96,128]{2,1,0:T(8,128)(2,1)}, bf16[2,96,128]{2,1,0:T(8,128)(2,1)}, bf16[2,96,128]{2,1,0:T(8,128)(2,1)}) custom-call(bf16[4,2,96,128]{3,2,1,0:T(8,128)(2,1)} %get-tuple-element.33.refs_0_, bf16[4,2,96,128]{3,2,1,0:T(8,128)(2,1)} %copy-done.9, bf16[4,2,96,128]{3,2,1,0:T(8,128)(2,1)} %copy-done.10, ...), custom_call_target="tpu_custom_call" | custom-call | tf_op jit(solution)/shard_map/sum_parts/pallas_call | solution.py:218
  55.5 1.5 %collective-permute-start.11 = (bf16[2,96,128]{2,1,0:T(8,128)(2,1)}, bf16[2,96,128]{2,1,0:T(8,128)(2,1)S(1)}, u32[]{:S(2)}, u32[]{:S(2)}) collective-permute-start(bf16[2,96,128]{2,1,0:T(8,128)(2,1)} %get-tuple-element.38), channel_id=1, source_target_pairs={{0,2},{2,0},{4,6},{6,4},{8,10},{10,8},{12,14},{14,12},{16,18},{18,... | collective-permute-start | bytes 147464 | tf_op jit(solution)/shard_map/ppermute | solution.py:330
  57.0 1.5 %collective-permute-start.12 = (bf16[2,96,128]{2,1,0:T(8,128)(2,1)}, bf16[2,96,128]{2,1,0:T(8,128)(2,1)S(1)}, u32[]{:S(2)}, u32[]{:S(2)}) collective-permute-start(bf16[2,96,128]{2,1,0:T(8,128)(2,1)} %get-tuple-element.39), channel_id=1, source_target_pairs={{0,4},{2,6},{4,0},{6,2},{8,12},{10,14},{12,8},{14,10},{16,20},{18,... | collective-permute-start | bytes 147464 | tf_op jit(solution)/shard_map/ppermute | solution.py:330
  58.5 0.5 collective-permute-start.13
  59.0 0.1 collective-permute-start.15
  59.1 0.1 copy-done.3
  59.3 0.5 copy-done.4
  59.8 0.1 copy-done.5
  59.9 2.1 %sum_parts.2 = (bf16[2,160,128]{2,1,0:T(8,128)(2,1)}, bf16[2,160,128]{2,1,0:T(8,128)(2,1)}, bf16[2,160,128]{2,1,0:T(8,128)(2,1)}, bf16[2,160,128]{2,1,0:T(8,128)(2,1)}) custom-call(bf16[4,2,160,128]{3,2,1,0:T(8,128)(2,1)} %get-tuple-element.25.refs_0_, bf16[4,2,160,128]{3,2,1,0:T(8,128)(2,1)} %copy-done.3, bf16[4,2,160,128]{3,2,1,0:T(8,128)(2,1)} %copy-done.4, ...), custom_call_target="tpu_custom_call" | custom-call | tf_op jit(solution)/shard_map/sum_parts/pallas_call | solution.py:218
  62.0 0.1 collective-permute-start.5
  62.1 3.8 %collective-permute-start.6 = (bf16[2,160,128]{2,1,0:T(8,128)(2,1)}, bf16[2,160,128]{2,1,0:T(8,128)(2,1)S(1)}, u32[]{:S(2)}, u32[]{:S(2)}) collective-permute-start(bf16[2,160,128]{2,1,0:T(8,128)(2,1)} %get-tuple-element.32), channel_id=1, source_target_pairs={{0,24},{2,26},{4,28},{6,30},{8,0},{10,2},{12,4},{14,6},{16,8},{18,... | collective-permute-start | bytes 245768 | tf_op jit(solution)/shard_map/ppermute | solution.py:333
  65.9 0.8 multiply_convert_fusion.1.refs_2_
  66.7 0.1 collective-permute-start.14
  66.8 2.5 %collective-permute-done.4 = bf16[2,160,128]{2,1,0:T(8,128)(2,1)S(1)} collective-permute-done((bf16[2,160,128]{2,1,0:T(8,128)(2,1)}, bf16[2,160,128]{2,1,0:T(8,128)(2,1)S(1)}, u32[]{:S(2)}, u32[]{:S(2)}) %collective-permute-start.4) | collective-permute-done | bytes 81952 | tf_op jit(solution)/shard_map/ppermute | solution.py:333
  69.4 2.6 %collective-permute-done.5 = bf16[2,160,128]{2,1,0:T(8,128)(2,1)S(1)} collective-permute-done((bf16[2,160,128]{2,1,0:T(8,128)(2,1)}, bf16[2,160,128]{2,1,0:T(8,128)(2,1)S(1)}, u32[]{:S(2)}, u32[]{:S(2)}) %collective-permute-start.5) | collective-permute-done | bytes 81952 | tf_op jit(solution)/shard_map/ppermute | solution.py:333
  71.9 0.9 multiply_convert_fusion.refs_0_
  72.9 0.1 collective-permute-start.7
  73.0 0.1 slice_reduce_fusion
  73.1 1.6 %collective-permute-start.28 = (f32[32]{0:T(128)S(1)}, f32[32]{0:T(128)S(1)}, u32[]{:S(2)}, u32[]{:S(2)}) collective-permute-start(f32[32]{0:T(128)S(1)} %slice_reduce_fusion), channel_id=1, source_target_pairs={{0,2},{2,0},{4,6},{6,4},{8,10},{10,8},{12,14},{14,12},{16,18},{18,... | collective-permute-start | bytes 392 | tf_op jit(solution)/shard_map/ppermute | solution.py:330
  74.6 1.5 %collective-permute-start.29 = (f32[32]{0:T(128)S(1)}, f32[32]{0:T(128)S(1)}, u32[]{:S(2)}, u32[]{:S(2)}) collective-permute-start(f32[32]{0:T(128)S(1)} %slice_reduce_fusion), channel_id=1, source_target_pairs={{0,4},{2,6},{4,0},{6,2},{8,12},{10,14},{12,8},{14,10},{16,20},{18,... | collective-permute-start | bytes 392 | tf_op jit(solution)/shard_map/ppermute | solution.py:330
  76.2 0.5 collective-permute-start.30
  76.7 0.1 copy-done.20
  76.8 0.5 copy-done.21
  77.3 0.6 copy-done.19
  77.9 2.9 %series.1 = (bf16[2,48,128]{2,1,0:T(8,128)(2,1)}, bf16[2,80,128]{2,1,0:T(8,128)(2,1)}) custom-call(bf16[2,160,128]{2,1,0:T(8,128)(2,1)} %copy-done.6, bf16[2,160,128]{2,1,0:T(8,128)(2,1)} %copy-done.19, bf16[2,96,128]{2,1,0:T(8,128)(2,1)} %copy-done.11, bf16[2,96,128]{2,1,0:T(8,128)(2,1)} %copy-done.21, bf16[2,128,128]{2,1,0:T(8,128)(2,1)} %copy-done.7, ...), custom_call_target="tpu_custom_call" | custom-call | tf_op jit(solution)/shard_map/series/pallas_call | solution.py:267
  80.8 1.5 %collective-permute-start.22 = (bf16[2,48,128]{2,1,0:T(8,128)(2,1)}, bf16[2,48,128]{2,1,0:T(8,128)(2,1)S(1)}, u32[]{:S(2)}, u32[]{:S(2)}) collective-permute-start(bf16[2,48,128]{2,1,0:T(8,128)(2,1)} %get-tuple-element.42), channel_id=1, source_target_pairs={{0,2},{2,0},{4,6},{6,4},{8,10},{10,8},{12,14},{14,12},{16,18},{18,... | collective-permute-start | bytes 73736 | tf_op jit(solution)/shard_map/ppermute | solution.py:330
  82.3 1.5 %collective-permute-start.23 = (bf16[2,48,128]{2,1,0:T(8,128)(2,1)}, bf16[2,48,128]{2,1,0:T(8,128)(2,1)S(1)}, u32[]{:S(2)}, u32[]{:S(2)}) collective-permute-start(bf16[2,48,128]{2,1,0:T(8,128)(2,1)} %get-tuple-element.42), channel_id=1, source_target_pairs={{0,4},{2,6},{4,0},{6,2},{8,12},{10,14},{12,8},{14,10},{16,20},{18,... | collective-permute-start | bytes 73736 | tf_op jit(solution)/shard_map/ppermute | solution.py:330
  83.8 0.5 collective-permute-start.24
  84.3 1.9 %collective-permute-start.31 = (f32[32]{0:T(128)S(1)}, f32[32]{0:T(128)S(1)}, u32[]{:S(2)}, u32[]{:S(2)}) collective-permute-start(f32[32]{0:T(128)S(1)} %add_add_fusion.1), channel_id=1, source_target_pairs={{0,8},{2,10},{4,12},{6,14},{8,16},{10,18},{12,20},{14,22},{16,24},... | collective-permute-start | bytes 392 | tf_op jit(solution)/shard_map/ppermute | solution.py:333
  86.2 1.1 collective-permute-start.32
  87.3 1.4 %collective-permute-start.16 = (bf16[2,80,128]{2,1,0:T(8,128)(2,1)}, bf16[2,80,128]{2,1,0:T(8,128)(2,1)S(1)}, u32[]{:S(2)}, u32[]{:S(2)}) collective-permute-start(bf16[2,80,128]{2,1,0:T(8,128)(2,1)} %get-tuple-element.41), channel_id=1, source_target_pairs={{0,8},{2,10},{4,12},{6,14},{8,16},{10,18},{12,20},{14,22},{16,24},... | collective-permute-start | bytes 122888 | tf_op jit(solution)/shard_map/ppermute | solution.py:333
  88.8 0.5 collective-permute-start.17
  89.2 2.8 %collective-permute-start.18 = (bf16[2,80,128]{2,1,0:T(8,128)(2,1)}, bf16[2,80,128]{2,1,0:T(8,128)(2,1)S(1)}, u32[]{:S(2)}, u32[]{:S(2)}) collective-permute-start(bf16[2,80,128]{2,1,0:T(8,128)(2,1)} %get-tuple-element.41), channel_id=1, source_target_pairs={{0,24},{2,26},{4,28},{6,30},{8,0},{10,2},{12,4},{14,6},{16,8},{18,... | collective-permute-start | bytes 122888 | tf_op jit(solution)/shard_map/ppermute | solution.py:333
  92.1 0.8 pad_maximum_fusion.1.refs_4_
  92.8 0.5 collective-permute-done.16
  93.3 0.6 collective-permute-start.33
  94.0 1.4 collective-permute-start.25
  95.4 1.9 %collective-permute-start.26 = (bf16[4,2,48,128]{3,2,1,0:T(8,128)(2,1)S(1)}, bf16[4,2,48,128]{3,2,1,0:T(8,128)(2,1)S(1)}, u32[]{:S(2)}, u32[]{:S(2)}) collective-permute-start(bf16[4,2,48,128]{3,2,1,0:T(8,128)(2,1)S(1)} %pad_maximum_fusion.1.refs_4_), channel_id=1, source_target_pairs={{0,16},{2,18},{4,20},{6,22},{8,24},{10,26},{12,28},{14,30},{16,0},... | collective-permute-start | bytes 294920 | tf_op jit(solution)/shard_map/ppermute | solution.py:333
  97.3 0.8 pad_maximum_fusion.refs_0_
  98.1 1.2 collective-permute-start.27
  99.3 1.5 %collective-permute-start.19 = (bf16[4,2,80,128]{3,2,1,0:T(8,128)(2,1)S(1)}, bf16[4,2,80,128]{3,2,1,0:T(8,128)(2,1)S(1)}, u32[]{:S(2)}, u32[]{:S(2)}) collective-permute-start(bf16[4,2,80,128]{3,2,1,0:T(8,128)(2,1)S(1)} %pad_maximum_fusion.refs_0_), channel_id=1, source_target_pairs={{0,2},{2,0},{4,6},{6,4},{8,10},{10,8},{12,14},{14,12},{16,18},{18,... | collective-permute-start | bytes 491528 | tf_op jit(solution)/shard_map/ppermute | solution.py:330
  100.8 1.5 %collective-permute-start.20 = (bf16[4,2,80,128]{3,2,1,0:T(8,128)(2,1)S(1)}, bf16[4,2,80,128]{3,2,1,0:T(8,128)(2,1)S(1)}, u32[]{:S(2)}, u32[]{:S(2)}) collective-permute-start(bf16[4,2,80,128]{3,2,1,0:T(8,128)(2,1)S(1)} %pad_maximum_fusion.refs_0_), channel_id=1, source_target_pairs={{0,4},{2,6},{4,0},{6,2},{8,12},{10,14},{12,8},{14,10},{16,20},{18,... | collective-permute-start | bytes 491528 | tf_op jit(solution)/shard_map/ppermute | solution.py:330
  102.3 0.7 collective-permute-start.21
  102.9 0.5 add_add_fusion
  103.5 0.3 collective-permute-done.27.refs_7_
  103.8 0.8 collective-permute-done.19.refs_1_
  104.6 2.3 %collective-permute-done.20.refs_2_ = bf16[4,2,80,128]{3,2,1,0:T(8,128)(2,1)S(1)} collective-permute-done((bf16[4,2,80,128]{3,2,1,0:T(8,128)(2,1)S(1)}, bf16[4,2,80,128]{3,2,1,0:T(8,128)(2,1)S(1)}, u32[]{:S(2)}, u32[]{:S(2)}) %collective-permute-start.20) | collective-permute-done | bytes 163872 | tf_op jit(solution)/shard_map/ppermute | solution.py:330
  106.9 1.6 %collective-permute-done.21.refs_3_ = bf16[4,2,80,128]{3,2,1,0:T(8,128)(2,1)S(1)} collective-permute-done((bf16[4,2,80,128]{3,2,1,0:T(8,128)(2,1)S(1)}, bf16[4,2,80,128]{3,2,1,0:T(8,128)(2,1)S(1)}, u32[]{:S(2)}, u32[]{:S(2)}) %collective-permute-start.21) | collective-permute-done | bytes 163872 | tf_op jit(solution)/shard_map/ppermute | solution.py:330
  108.6 0.6 copy-done.14
  109.2 33.2 %place_walkers.1 = bf16[32,128,128]{2,1,0:T(8,128)(2,1)} custom-call(bf16[4,2,80,128]{3,2,1,0:T(8,128)(2,1)} %copy-done.1, bf16[4,2,80,128]{3,2,1,0:T(8,128)(2,1)} %copy-done.12, bf16[4,2,80,128]{3,2,1,0:T(8,128)(2,1)} %copy-done.13, bf16[4,2,80,128]{3,2,1,0:T(8,128)(2,1)} %copy-done.14, bf16[4,2,48,128]{3,2,1,0:T(8,128)(2,1)} %copy-done.2, ...), custom_call_target="tpu_custom_call" | custom-call | tf_op jit(solution)/shard_map/place_walkers/pallas_call | solution.py:306
  (69 shorter events, 0.2 us)
Async XLA Ops:
  0.6 58.4 %copy-start = (bf16[32,128,128]{2,1,0:T(8,128)(2,1)S(1)}, bf16[32,128,128]{2,1,0:T(8,128)(2,1)}, u32[]{:S(2)}) copy-start(bf16[32,128,128]{2,1,0:T(8,128)(2,1)} %param.8) | copy-start | bytes 3145732
  15.7 1.5 %collective-permute-start = (f32[32,256]{1,0:T(8,128)}, f32[32,256]{1,0:T(8,128)S(1)}, u32[]{:S(2)}, u32[]{:S(2)}) collective-permute-start(f32[32,256]{1,0:T(8,128)} %get-tuple-element.23.own_ref), channel_id=1, source_target_pairs={{1,0},{0,1},{3,2},{2,3},{5,4},{4,5},{7,6},{6,7},{9,8},{8,9},{11,10... | collective-permute-start | bytes 98312 | tf_op jit(solution)/shard_map/ppermute | solution.py:336
  17.2 0.6 copy-start.15
  22.5 15.1 %copy-start.24 = (bf16[4,2,96,128]{3,2,1,0:T(8,128)(2,1)S(1)}, bf16[4,2,96,128]{3,2,1,0:T(8,128)(2,1)}, u32[]{:S(2)}) copy-start(bf16[4,2,96,128]{3,2,1,0:T(8,128)(2,1)} %get-tuple-element.34) | copy-start | bytes 589828
  22.5 15.2 %copy-start.23 = (bf16[4,2,96,128]{3,2,1,0:T(8,128)(2,1)S(1)}, bf16[4,2,96,128]{3,2,1,0:T(8,128)(2,1)}, u32[]{:S(2)}) copy-start(bf16[4,2,96,128]{3,2,1,0:T(8,128)(2,1)} %get-tuple-element.35) | copy-start | bytes 589828
  22.5 50.5 %copy-start.22 = (f32[32,128]{1,0:T(8,128)S(1)}, f32[32,128]{1,0:T(8,128)}, u32[]{:S(2)}) copy-start(f32[32,128]{1,0:T(8,128)} %get-tuple-element.43) | copy-start | bytes 49156
  22.5 15.1 %collective-permute-start.10 = (bf16[4,2,96,128]{3,2,1,0:T(8,128)(2,1)}, bf16[4,2,96,128]{3,2,1,0:T(8,128)(2,1)S(1)}, u32[]{:S(2)}, u32[]{:S(2)}) collective-permute-start(bf16[4,2,96,128]{3,2,1,0:T(8,128)(2,1)} %get-tuple-element.36), channel_id=1, source_target_pairs={{0,24},{2,26},{4,28},{6,30},{8,0},{10,2},{12,4},{14,6},{16,8},{18,... | collective-permute-start | bytes 589832 | tf_op jit(solution)/shard_map/ppermute | solution.py:333
  34.1 24.4 %collective-permute-start.1 = (bf16[4,2,160,128]{3,2,1,0:T(8,128)(2,1)}, bf16[4,2,160,128]{3,2,1,0:T(8,128)(2,1)S(1)}, u32[]{:S(2)}, u32[]{:S(2)}) collective-permute-start(bf16[4,2,160,128]{3,2,1,0:T(8,128)(2,1)} %get-tuple-element.26), channel_id=1, source_target_pairs={{0,2},{2,0},{4,6},{6,4},{8,10},{10,8},{12,14},{14,12},{16,18},{18,... | collective-permute-start | bytes 983048 | tf_op jit(solution)/shard_map/ppermute | solution.py:330
  35.6 23.4 %collective-permute-start.2 = (bf16[4,2,160,128]{3,2,1,0:T(8,128)(2,1)}, bf16[4,2,160,128]{3,2,1,0:T(8,128)(2,1)S(1)}, u32[]{:S(2)}, u32[]{:S(2)}) collective-permute-start(bf16[4,2,160,128]{3,2,1,0:T(8,128)(2,1)} %get-tuple-element.27), channel_id=1, source_target_pairs={{0,4},{2,6},{4,0},{6,2},{8,12},{10,14},{12,8},{14,10},{16,20},{18,... | collective-permute-start | bytes 983048 | tf_op jit(solution)/shard_map/ppermute | solution.py:330
  37.1 22.0 %collective-permute-start.3 = (bf16[4,2,160,128]{3,2,1,0:T(8,128)(2,1)}, bf16[4,2,160,128]{3,2,1,0:T(8,128)(2,1)S(1)}, u32[]{:S(2)}, u32[]{:S(2)}) collective-permute-start(bf16[4,2,160,128]{3,2,1,0:T(8,128)(2,1)} %get-tuple-element.28), channel_id=1, source_target_pairs={{0,6},{2,4},{4,2},{6,0},{8,14},{10,12},{12,10},{14,8},{16,22},{18,... | collective-permute-start | bytes 983048 | tf_op jit(solution)/shard_map/ppermute | solution.py:330
  37.6 9.7 %collective-permute-start.8 = (bf16[4,2,96,128]{3,2,1,0:T(8,128)(2,1)S(1)}, bf16[4,2,96,128]{3,2,1,0:T(8,128)(2,1)S(1)}, u32[]{:S(2)}, u32[]{:S(2)}) collective-permute-start(bf16[4,2,96,128]{3,2,1,0:T(8,128)(2,1)S(1)} %copy-done.24), channel_id=1, source_target_pairs={{0,8},{2,10},{4,12},{6,14},{8,16},{10,18},{12,20},{14,22},{16,24},... | collective-permute-start | bytes 589832 | tf_op jit(solution)/shard_map/ppermute | solution.py:333
  37.6 15.3 %copy-start.8 = (bf16[4,2,96,128]{3,2,1,0:T(8,128)(2,1)}, bf16[4,2,96,128]{3,2,1,0:T(8,128)(2,1)S(1)}, u32[]{:S(2)}) copy-start(bf16[4,2,96,128]{3,2,1,0:T(8,128)(2,1)S(1)} %collective-permute-done.10.refs_3_) | copy-start | bytes 589828
  37.6 15.2 %collective-permute-start.9 = (bf16[4,2,96,128]{3,2,1,0:T(8,128)(2,1)S(1)}, bf16[4,2,96,128]{3,2,1,0:T(8,128)(2,1)S(1)}, u32[]{:S(2)}, u32[]{:S(2)}) collective-permute-start(bf16[4,2,96,128]{3,2,1,0:T(8,128)(2,1)S(1)} %copy-done.23), channel_id=1, source_target_pairs={{0,16},{2,18},{4,20},{6,22},{8,24},{10,26},{12,28},{14,30},{16,0},... | collective-permute-start | bytes 589832 | tf_op jit(solution)/shard_map/ppermute | solution.py:333
  47.3 5.6 %copy-start.9 = (bf16[4,2,96,128]{3,2,1,0:T(8,128)(2,1)}, bf16[4,2,96,128]{3,2,1,0:T(8,128)(2,1)S(1)}, u32[]{:S(2)}) copy-start(bf16[4,2,96,128]{3,2,1,0:T(8,128)(2,1)S(1)} %collective-permute-done.8.refs_1_) | copy-start | bytes 589828
  52.9 0.7 copy-start.10
  55.5 6.5 %collective-permute-start.11 = (bf16[2,96,128]{2,1,0:T(8,128)(2,1)}, bf16[2,96,128]{2,1,0:T(8,128)(2,1)S(1)}, u32[]{:S(2)}, u32[]{:S(2)}) collective-permute-start(bf16[2,96,128]{2,1,0:T(8,128)(2,1)} %get-tuple-element.38), channel_id=1, source_target_pairs={{0,2},{2,0},{4,6},{6,4},{8,10},{10,8},{12,14},{14,12},{16,18},{18,... | collective-permute-start | bytes 147464 | tf_op jit(solution)/shard_map/ppermute | solution.py:330
  57.0 5.1 %collective-permute-start.12 = (bf16[2,96,128]{2,1,0:T(8,128)(2,1)}, bf16[2,96,128]{2,1,0:T(8,128)(2,1)S(1)}, u32[]{:S(2)}, u32[]{:S(2)}) collective-permute-start(bf16[2,96,128]{2,1,0:T(8,128)(2,1)} %get-tuple-element.39), channel_id=1, source_target_pairs={{0,4},{2,6},{4,0},{6,2},{8,12},{10,14},{12,8},{14,10},{16,20},{18,... | collective-permute-start | bytes 147464 | tf_op jit(solution)/shard_map/ppermute | solution.py:330
  58.5 0.7 copy-start.3
  58.5 7.4 %collective-permute-start.13 = (bf16[2,96,128]{2,1,0:T(8,128)(2,1)}, bf16[2,96,128]{2,1,0:T(8,128)(2,1)S(1)}, u32[]{:S(2)}, u32[]{:S(2)}) collective-permute-start(bf16[2,96,128]{2,1,0:T(8,128)(2,1)} %get-tuple-element.40), channel_id=1, source_target_pairs={{0,6},{2,4},{4,2},{6,0},{8,14},{10,12},{12,10},{14,8},{16,22},{18,... | collective-permute-start | bytes 147464 | tf_op jit(solution)/shard_map/ppermute | solution.py:330
  59.0 17.7 %copy-start.7 = (bf16[2,128,128]{2,1,0:T(8,128)(2,1)}, bf16[2,128,128]{2,1,0:T(8,128)(2,1)S(1)}, u32[]{:S(2)}) copy-start(bf16[2,128,128]{2,1,0:T(8,128)(2,1)S(1)} %constant_dynamic-slice_fusion.refs_4_) | copy-start | bytes 196612
  59.0 0.8 copy-start.4
  59.0 17.1 %collective-permute-start.15 = (bf16[2,128,128]{2,1,0:T(8,128)(2,1)S(1)}, bf16[2,128,128]{2,1,0:T(8,128)(2,1)S(1)}, u32[]{:S(2)}, u32[]{:S(2)}) collective-permute-start(bf16[2,128,128]{2,1,0:T(8,128)(2,1)S(1)} %constant_dynamic-slice_fusion.refs_4_), channel_id=1, source_target_pairs={{1,0},{0,1},{3,2},{2,3},{5,4},{4,5},{7,6},{6,7},{9,8},{8,9},{11,10... | collective-permute-start | bytes 196616 | tf_op jit(solution)/shard_map/ppermute | solution.py:336
  59.1 0.8 copy-start.5
  62.0 7.4 %collective-permute-start.4 = (bf16[2,160,128]{2,1,0:T(8,128)(2,1)}, bf16[2,160,128]{2,1,0:T(8,128)(2,1)S(1)}, u32[]{:S(2)}, u32[]{:S(2)}) collective-permute-start(bf16[2,160,128]{2,1,0:T(8,128)(2,1)} %get-tuple-element.30), channel_id=1, source_target_pairs={{0,8},{2,10},{4,12},{6,14},{8,16},{10,18},{12,20},{14,22},{16,24},... | collective-permute-start | bytes 245768 | tf_op jit(solution)/shard_map/ppermute | solution.py:333
  62.0 9.9 %collective-permute-start.5 = (bf16[2,160,128]{2,1,0:T(8,128)(2,1)}, bf16[2,160,128]{2,1,0:T(8,128)(2,1)S(1)}, u32[]{:S(2)}, u32[]{:S(2)}) collective-permute-start(bf16[2,160,128]{2,1,0:T(8,128)(2,1)} %get-tuple-element.31), channel_id=1, source_target_pairs={{0,16},{2,18},{4,20},{6,22},{8,24},{10,26},{12,28},{14,30},{16,0},... | collective-permute-start | bytes 245768 | tf_op jit(solution)/shard_map/ppermute | solution.py:333
  62.1 9.9 %collective-permute-start.6 = (bf16[2,160,128]{2,1,0:T(8,128)(2,1)}, bf16[2,160,128]{2,1,0:T(8,128)(2,1)S(1)}, u32[]{:S(2)}, u32[]{:S(2)}) collective-permute-start(bf16[2,160,128]{2,1,0:T(8,128)(2,1)} %get-tuple-element.32), channel_id=1, source_target_pairs={{0,24},{2,26},{4,28},{6,30},{8,0},{10,2},{12,4},{14,6},{16,8},{18,... | collective-permute-start | bytes 245768 | tf_op jit(solution)/shard_map/ppermute | solution.py:333
  66.7 10.0 %copy-start.11 = (bf16[2,96,128]{2,1,0:T(8,128)(2,1)}, bf16[2,96,128]{2,1,0:T(8,128)(2,1)S(1)}, u32[]{:S(2)}) copy-start(bf16[2,96,128]{2,1,0:T(8,128)(2,1)S(1)} %multiply_convert_fusion.1.refs_2_) | copy-start | bytes 147460
  66.7 9.9 %collective-permute-start.14 = (bf16[2,96,128]{2,1,0:T(8,128)(2,1)S(1)}, bf16[2,96,128]{2,1,0:T(8,128)(2,1)S(1)}, u32[]{:S(2)}, u32[]{:S(2)}) collective-permute-start(bf16[2,96,128]{2,1,0:T(8,128)(2,1)S(1)} %multiply_convert_fusion.1.refs_2_), channel_id=1, source_target_pairs={{1,0},{0,1},{3,2},{2,3},{5,4},{4,5},{7,6},{6,7},{9,8},{8,9},{11,10... | collective-permute-start | bytes 147464 | tf_op jit(solution)/shard_map/ppermute | solution.py:336
  72.9 3.8 %copy-start.6 = (bf16[2,160,128]{2,1,0:T(8,128)(2,1)}, bf16[2,160,128]{2,1,0:T(8,128)(2,1)S(1)}, u32[]{:S(2)}) copy-start(bf16[2,160,128]{2,1,0:T(8,128)(2,1)S(1)} %multiply_convert_fusion.refs_0_) | copy-start | bytes 245764
  72.9 3.8 %collective-permute-start.7 = (bf16[2,160,128]{2,1,0:T(8,128)(2,1)S(1)}, bf16[2,160,128]{2,1,0:T(8,128)(2,1)S(1)}, u32[]{:S(2)}, u32[]{:S(2)}) collective-permute-start(bf16[2,160,128]{2,1,0:T(8,128)(2,1)S(1)} %multiply_convert_fusion.refs_0_), channel_id=1, source_target_pairs={{1,0},{0,1},{3,2},{2,3},{5,4},{4,5},{7,6},{6,7},{9,8},{8,9},{11,10... | collective-permute-start | bytes 245768 | tf_op jit(solution)/shard_map/ppermute | solution.py:336
  73.1 10.7 %collective-permute-start.28 = (f32[32]{0:T(128)S(1)}, f32[32]{0:T(128)S(1)}, u32[]{:S(2)}, u32[]{:S(2)}) collective-permute-start(f32[32]{0:T(128)S(1)} %slice_reduce_fusion), channel_id=1, source_target_pairs={{0,2},{2,0},{4,6},{6,4},{8,10},{10,8},{12,14},{14,12},{16,18},{18,... | collective-permute-start | bytes 392 | tf_op jit(solution)/shard_map/ppermute | solution.py:330
  74.6 9.6 %collective-permute-start.29 = (f32[32]{0:T(128)S(1)}, f32[32]{0:T(128)S(1)}, u32[]{:S(2)}, u32[]{:S(2)}) collective-permute-start(f32[32]{0:T(128)S(1)} %slice_reduce_fusion), channel_id=1, source_target_pairs={{0,4},{2,6},{4,0},{6,2},{8,12},{10,14},{12,8},{14,10},{16,20},{18,... | collective-permute-start | bytes 392 | tf_op jit(solution)/shard_map/ppermute | solution.py:330
  76.2 0.6 copy-start.20
  76.2 8.1 %collective-permute-start.30 = (f32[32]{0:T(128)S(1)}, f32[32]{0:T(128)S(1)}, u32[]{:S(2)}, u32[]{:S(2)}) collective-permute-start(f32[32]{0:T(128)S(1)} %slice_reduce_fusion), channel_id=1, source_target_pairs={{0,6},{2,4},{4,2},{6,0},{8,14},{10,12},{12,10},{14,8},{16,22},{18,... | collective-permute-start | bytes 392 | tf_op jit(solution)/shard_map/ppermute | solution.py:330
  76.7 0.6 copy-start.21
  77.3 0.6 copy-start.19
  80.8 6.5 %collective-permute-start.22 = (bf16[2,48,128]{2,1,0:T(8,128)(2,1)}, bf16[2,48,128]{2,1,0:T(8,128)(2,1)S(1)}, u32[]{:S(2)}, u32[]{:S(2)}) collective-permute-start(bf16[2,48,128]{2,1,0:T(8,128)(2,1)} %get-tuple-element.42), channel_id=1, source_target_pairs={{0,2},{2,0},{4,6},{6,4},{8,10},{10,8},{12,14},{14,12},{16,18},{18,... | collective-permute-start | bytes 73736 | tf_op jit(solution)/shard_map/ppermute | solution.py:330
  82.3 6.5 %collective-permute-start.23 = (bf16[2,48,128]{2,1,0:T(8,128)(2,1)}, bf16[2,48,128]{2,1,0:T(8,128)(2,1)S(1)}, u32[]{:S(2)}, u32[]{:S(2)}) collective-permute-start(bf16[2,48,128]{2,1,0:T(8,128)(2,1)} %get-tuple-element.42), channel_id=1, source_target_pairs={{0,4},{2,6},{4,0},{6,2},{8,12},{10,14},{12,8},{14,10},{16,20},{18,... | collective-permute-start | bytes 73736 | tf_op jit(solution)/shard_map/ppermute | solution.py:330
  83.8 5.4 %collective-permute-start.24 = (bf16[2,48,128]{2,1,0:T(8,128)(2,1)}, bf16[2,48,128]{2,1,0:T(8,128)(2,1)S(1)}, u32[]{:S(2)}, u32[]{:S(2)}) collective-permute-start(bf16[2,48,128]{2,1,0:T(8,128)(2,1)} %get-tuple-element.42), channel_id=1, source_target_pairs={{0,6},{2,4},{4,2},{6,0},{8,14},{10,12},{12,10},{14,8},{16,22},{18,... | collective-permute-start | bytes 73736 | tf_op jit(solution)/shard_map/ppermute | solution.py:330
  84.3 13.8 %collective-permute-start.31 = (f32[32]{0:T(128)S(1)}, f32[32]{0:T(128)S(1)}, u32[]{:S(2)}, u32[]{:S(2)}) collective-permute-start(f32[32]{0:T(128)S(1)} %add_add_fusion.1), channel_id=1, source_target_pairs={{0,8},{2,10},{4,12},{6,14},{8,16},{10,18},{12,20},{14,22},{16,24},... | collective-permute-start | bytes 392 | tf_op jit(solution)/shard_map/ppermute | solution.py:333
  86.2 13.1 %collective-permute-start.32 = (f32[32]{0:T(128)S(1)}, f32[32]{0:T(128)S(1)}, u32[]{:S(2)}, u32[]{:S(2)}) collective-permute-start(f32[32]{0:T(128)S(1)} %add_add_fusion.1), channel_id=1, source_target_pairs={{0,16},{2,18},{4,20},{6,22},{8,24},{10,26},{12,28},{14,30},{16,0},... | collective-permute-start | bytes 392 | tf_op jit(solution)/shard_map/ppermute | solution.py:333
  87.3 6.0 %collective-permute-start.16 = (bf16[2,80,128]{2,1,0:T(8,128)(2,1)}, bf16[2,80,128]{2,1,0:T(8,128)(2,1)S(1)}, u32[]{:S(2)}, u32[]{:S(2)}) collective-permute-start(bf16[2,80,128]{2,1,0:T(8,128)(2,1)} %get-tuple-element.41), channel_id=1, source_target_pairs={{0,8},{2,10},{4,12},{6,14},{8,16},{10,18},{12,20},{14,22},{16,24},... | collective-permute-start | bytes 122888 | tf_op jit(solution)/shard_map/ppermute | solution.py:333
  88.8 5.2 %collective-permute-start.17 = (bf16[2,80,128]{2,1,0:T(8,128)(2,1)}, bf16[2,80,128]{2,1,0:T(8,128)(2,1)S(1)}, u32[]{:S(2)}, u32[]{:S(2)}) collective-permute-start(bf16[2,80,128]{2,1,0:T(8,128)(2,1)} %get-tuple-element.41), channel_id=1, source_target_pairs={{0,16},{2,18},{4,20},{6,22},{8,24},{10,26},{12,28},{14,30},{16,0},... | collective-permute-start | bytes 122888 | tf_op jit(solution)/shard_map/ppermute | solution.py:333
  89.2 6.2 %collective-permute-start.18 = (bf16[2,80,128]{2,1,0:T(8,128)(2,1)}, bf16[2,80,128]{2,1,0:T(8,128)(2,1)S(1)}, u32[]{:S(2)}, u32[]{:S(2)}) collective-permute-start(bf16[2,80,128]{2,1,0:T(8,128)(2,1)} %get-tuple-element.41), channel_id=1, source_target_pairs={{0,24},{2,26},{4,28},{6,30},{8,0},{10,2},{12,4},{14,6},{16,8},{18,... | collective-permute-start | bytes 122888 | tf_op jit(solution)/shard_map/ppermute | solution.py:333
  92.8 15.7 %copy-start.2 = (bf16[4,2,48,128]{3,2,1,0:T(8,128)(2,1)}, bf16[4,2,48,128]{3,2,1,0:T(8,128)(2,1)S(1)}, u32[]{:S(2)}) copy-start(bf16[4,2,48,128]{3,2,1,0:T(8,128)(2,1)S(1)} %pad_maximum_fusion.1.refs_4_) | copy-start | bytes 294916
  93.3 7.4 %collective-permute-start.33 = (f32[32]{0:T(128)S(1)}, f32[32]{0:T(128)S(1)}, u32[]{:S(2)}, u32[]{:S(2)}) collective-permute-start(f32[32]{0:T(128)S(1)} %add_add_fusion.1), channel_id=1, source_target_pairs={{0,24},{2,26},{4,28},{6,30},{8,0},{10,2},{12,4},{14,6},{16,8},{18,... | collective-permute-start | bytes 392 | tf_op jit(solution)/shard_map/ppermute | solution.py:333
  94.0 8.3 %collective-permute-start.25 = (bf16[4,2,48,128]{3,2,1,0:T(8,128)(2,1)S(1)}, bf16[4,2,48,128]{3,2,1,0:T(8,128)(2,1)S(1)}, u32[]{:S(2)}, u32[]{:S(2)}) collective-permute-start(bf16[4,2,48,128]{3,2,1,0:T(8,128)(2,1)S(1)} %pad_maximum_fusion.1.refs_4_), channel_id=1, source_target_pairs={{0,8},{2,10},{4,12},{6,14},{8,16},{10,18},{12,20},{14,22},{16,24},... | collective-permute-start | bytes 294920 | tf_op jit(solution)/shard_map/ppermute | solution.py:333
  95.4 8.1 %collective-permute-start.26 = (bf16[4,2,48,128]{3,2,1,0:T(8,128)(2,1)S(1)}, bf16[4,2,48,128]{3,2,1,0:T(8,128)(2,1)S(1)}, u32[]{:S(2)}, u32[]{:S(2)}) collective-permute-start(bf16[4,2,48,128]{3,2,1,0:T(8,128)(2,1)S(1)} %pad_maximum_fusion.1.refs_4_), channel_id=1, source_target_pairs={{0,16},{2,18},{4,20},{6,22},{8,24},{10,26},{12,28},{14,30},{16,0},... | collective-permute-start | bytes 294920 | tf_op jit(solution)/shard_map/ppermute | solution.py:333
  98.1 10.4 %copy-start.1 = (bf16[4,2,80,128]{3,2,1,0:T(8,128)(2,1)}, bf16[4,2,80,128]{3,2,1,0:T(8,128)(2,1)S(1)}, u32[]{:S(2)}) copy-start(bf16[4,2,80,128]{3,2,1,0:T(8,128)(2,1)S(1)} %pad_maximum_fusion.refs_0_) | copy-start | bytes 491524
  98.1 5.7 %collective-permute-start.27 = (bf16[4,2,48,128]{3,2,1,0:T(8,128)(2,1)S(1)}, bf16[4,2,48,128]{3,2,1,0:T(8,128)(2,1)S(1)}, u32[]{:S(2)}, u32[]{:S(2)}) collective-permute-start(bf16[4,2,48,128]{3,2,1,0:T(8,128)(2,1)S(1)} %pad_maximum_fusion.1.refs_4_), channel_id=1, source_target_pairs={{0,24},{2,26},{4,28},{6,30},{8,0},{10,2},{12,4},{14,6},{16,8},{18,... | collective-permute-start | bytes 294920 | tf_op jit(solution)/shard_map/ppermute | solution.py:333
  99.3 5.3 %collective-permute-start.19 = (bf16[4,2,80,128]{3,2,1,0:T(8,128)(2,1)S(1)}, bf16[4,2,80,128]{3,2,1,0:T(8,128)(2,1)S(1)}, u32[]{:S(2)}, u32[]{:S(2)}) collective-permute-start(bf16[4,2,80,128]{3,2,1,0:T(8,128)(2,1)S(1)} %pad_maximum_fusion.refs_0_), channel_id=1, source_target_pairs={{0,2},{2,0},{4,6},{6,4},{8,10},{10,8},{12,14},{14,12},{16,18},{18,... | collective-permute-start | bytes 491528 | tf_op jit(solution)/shard_map/ppermute | solution.py:330
  100.8 6.1 %collective-permute-start.20 = (bf16[4,2,80,128]{3,2,1,0:T(8,128)(2,1)S(1)}, bf16[4,2,80,128]{3,2,1,0:T(8,128)(2,1)S(1)}, u32[]{:S(2)}, u32[]{:S(2)}) collective-permute-start(bf16[4,2,80,128]{3,2,1,0:T(8,128)(2,1)S(1)} %pad_maximum_fusion.refs_0_), channel_id=1, source_target_pairs={{0,4},{2,6},{4,0},{6,2},{8,12},{10,14},{12,8},{14,10},{16,20},{18,... | collective-permute-start | bytes 491528 | tf_op jit(solution)/shard_map/ppermute | solution.py:330
  102.3 6.2 %copy-start.16 = (bf16[4,2,48,128]{3,2,1,0:T(8,128)(2,1)}, bf16[4,2,48,128]{3,2,1,0:T(8,128)(2,1)S(1)}, u32[]{:S(2)}) copy-start(bf16[4,2,48,128]{3,2,1,0:T(8,128)(2,1)S(1)} %collective-permute-done.25.refs_5_) | copy-start | bytes 294916
  102.3 6.2 %collective-permute-start.21 = (bf16[4,2,80,128]{3,2,1,0:T(8,128)(2,1)S(1)}, bf16[4,2,80,128]{3,2,1,0:T(8,128)(2,1)S(1)}, u32[]{:S(2)}, u32[]{:S(2)}) collective-permute-start(bf16[4,2,80,128]{3,2,1,0:T(8,128)(2,1)S(1)} %pad_maximum_fusion.refs_0_), channel_id=1, source_target_pairs={{0,6},{2,4},{4,2},{6,0},{8,14},{10,12},{12,10},{14,8},{16,22},{18,... | collective-permute-start | bytes 491528 | tf_op jit(solution)/shard_map/ppermute | solution.py:330
  103.5 5.1 %copy-start.17 = (bf16[4,2,48,128]{3,2,1,0:T(8,128)(2,1)}, bf16[4,2,48,128]{3,2,1,0:T(8,128)(2,1)S(1)}, u32[]{:S(2)}) copy-start(bf16[4,2,48,128]{3,2,1,0:T(8,128)(2,1)S(1)} %collective-permute-done.26.refs_6_) | copy-start | bytes 294916
  103.8 4.8 %copy-start.18 = (bf16[4,2,48,128]{3,2,1,0:T(8,128)(2,1)}, bf16[4,2,48,128]{3,2,1,0:T(8,128)(2,1)S(1)}, u32[]{:S(2)}) copy-start(bf16[4,2,48,128]{3,2,1,0:T(8,128)(2,1)S(1)} %collective-permute-done.27.refs_7_) | copy-start | bytes 294916
  104.6 4.0 %copy-start.12 = (bf16[4,2,80,128]{3,2,1,0:T(8,128)(2,1)}, bf16[4,2,80,128]{3,2,1,0:T(8,128)(2,1)S(1)}, u32[]{:S(2)}) copy-start(bf16[4,2,80,128]{3,2,1,0:T(8,128)(2,1)S(1)} %collective-permute-done.19.refs_1_) | copy-start | bytes 491524
  106.9 1.6 %copy-start.13 = (bf16[4,2,80,128]{3,2,1,0:T(8,128)(2,1)}, bf16[4,2,80,128]{3,2,1,0:T(8,128)(2,1)S(1)}, u32[]{:S(2)}) copy-start(bf16[4,2,80,128]{3,2,1,0:T(8,128)(2,1)S(1)} %collective-permute-done.20.refs_2_) | copy-start | bytes 491524
  108.6 0.7 copy-start.14

commit v2 on v1

v2 whole, which is shorter than its diff:
```python
import functools

import jax
import jax.numpy as jnp
from jax import lax
from jax.experimental import pallas as pl
from jax.experimental.pallas import tpu as pltpu
from jax.sharding import PartitionSpec as P

BLOCK = 64
TAYLOR = 4
ROWBLK = 4
LANES = 2 * BLOCK
CHUNK = 16
MIB = 1024 * 1024


def params(mib):
    return pltpu.CompilerParams(vmem_limit_bytes=mib * MIB)


def in_vmem(*arrays):
    return [pltpu.with_memory_space_constraint(a, pltpu.VMEM) for a in arrays]


def swap_matrix():
    to = lax.broadcasted_iota(jnp.int32, (CHUNK * CHUNK, CHUNK * CHUNK), 0)
    at = lax.broadcasted_iota(jnp.int32, (CHUNK * CHUNK, CHUNK * CHUNK), 1)
    same = (to // CHUNK == at % CHUNK) & (to % CHUNK == at // CHUNK)
    return same.astype(jnp.float32).astype(jnp.bfloat16)


def column_order(row):
    other = 2 - 2 * (row // 2)
    return row, row + 1 - 2 * (row % 2), other, other + 1


def slot_masks(cols, row):
    return [cols == column for column in column_order(row)[1:]]


def bias_kernel(vals_hbm, greens_hbm, cols_ref, turned_ref, bias_ref, vals, greens, swap, gs, acc, vsem, gsem):
    total_steps, vectors = turned_ref.shape[:2]
    walk = bias_ref.shape[0]
    steps = BLOCK // CHUNK

    def copies(t):
        rows = pl.ds(lax.rem(t, steps) * CHUNK, CHUNK)
        return (
            pltpu.make_async_copy(vals_hbm.at[:, lax.div(t, steps), rows, :], vals.at[t], vsem.at[t]),
            pltpu.make_async_copy(greens_hbm.at[:, pl.ds(t * CHUNK, CHUNK), :], greens.at[t], gsem.at[t]),
        )

    def begin(t, carry):
        for copy in copies(t):
            copy.start()
        return carry

    lax.fori_loop(0, total_steps, begin, 0)
    swap[...] = swap_matrix()
    bias_ref[...] = jnp.zeros_like(bias_ref)
    first = lax.broadcasted_iota(jnp.int32, (CHUNK * CHUNK, LANES), 1) < BLOCK

    def step(t, carry):
        for copy in copies(t):
            copy.wait()
        local = lax.div(t, steps)
        row = lax.axis_index("orb") * cols_ref.shape[0] + local
        upper = row // 2 == 1
        odd = row % 2 == 1
        for w in range(0, walk, CHUNK):
            mixed = greens[t, w:w + CHUNK].reshape(CHUNK * CHUNK, 2 * LANES)
            mixed = jnp.dot(swap[...], mixed, preferred_element_type=jnp.float32)
            pair = jnp.where(upper, mixed[:, LANES:], mixed[:, :LANES])
            rest = jnp.where(upper, mixed[:, :LANES], mixed[:, LANES:])
            pair = jnp.where(odd, pltpu.roll(pair, BLOCK, 1), pair)
            pieces = (
                jnp.where(first, pair, 0.0),
                jnp.where(first, 0.0, pair),
                jnp.where(first, 0.0, pltpu.roll(rest, BLOCK, 1)),
                jnp.where(first, 0.0, rest),
            )
            for k, piece in enumerate(pieces):
                piece = piece.astype(jnp.bfloat16)
                for i in range(CHUNK):
                    gs[k * walk + w:k * walk + w + CHUNK, i * LANES:(i + 1) * LANES] = piece[i * CHUNK:(i + 1) * CHUNK]
        for g in range(0, vectors, 2 * CHUNK):
            both = [vals[t, g + side * CHUNK:g + (side + 1) * CHUNK].reshape(CHUNK * CHUNK, LANES) for side in range(2)]
            both = jnp.dot(swap[...], jnp.concatenate(both, axis=1), preferred_element_type=jnp.float32)
            both = both.astype(jnp.bfloat16)
            for i in range(CHUNK):
                for side in range(2):
                    turned_ref[t, g + side * CHUNK:g + (side + 1) * CHUNK, i * LANES:(i + 1) * LANES] = (
                        both[i * CHUNK:(i + 1) * CHUNK, side * LANES:(side + 1) * LANES]
                    )
        part = lax.dot_general(
            turned_ref[t], gs[...], (((1,), (1,)), ((), ())), preferred_element_type=jnp.float32
        )
        begins = lax.rem(t, steps) == 0
        acc[...] = jnp.where(begins, 0.0, acc[...]) + part

        @pl.when(lax.rem(t, steps) == steps - 1)
        def _():
            flat = acc[...].T
            total = flat[0:walk]
            cols = cols_ref[local, 1:2, :]
            for k, mask in enumerate(slot_masks(cols, row)):
                total = total + jnp.where(mask, flat[(k + 1) * walk:(k + 2) * walk], 0.0)
            bias_ref[...] += total

        return carry

    acc[...] = jnp.zeros_like(acc)
    lax.fori_loop(0, total_steps, step, 0)


def bias_call(vals, greens, cols):
    vectors, rowblocks = vals.shape[:2]
    walk, half_rows, norb = greens.shape
    steps = half_rows // CHUNK
    wide = CHUNK * LANES
    return pl.pallas_call(
        bias_kernel,
        in_specs=[
            pl.BlockSpec(memory_space=pl.ANY),
            pl.BlockSpec(memory_space=pl.ANY),
            pl.BlockSpec(memory_space=pltpu.VMEM),
        ],
        out_specs=[pl.BlockSpec(memory_space=pltpu.VMEM)] * 2,
        out_shape=[
            pltpu.VMEM((steps, vectors, wide), jnp.bfloat16),
            pltpu.VMEM((walk, vectors), jnp.float32),
        ],
        scratch_shapes=[
            pltpu.VMEM((steps, vectors, CHUNK, LANES), jnp.bfloat16),
            pltpu.VMEM((steps, walk, CHUNK, norb), jnp.bfloat16),
            pltpu.VMEM((CHUNK * CHUNK, CHUNK * CHUNK), jnp.bfloat16),
            pltpu.VMEM((4 * walk, wide), jnp.bfloat16),
            pltpu.VMEM((vectors, 4 * walk), jnp.float32),
            pltpu.SemaphoreType.DMA((steps,)),
            pltpu.SemaphoreType.DMA((steps,)),
        ],
        compiler_params=params(24),
        name="force_bias",
    )(vals, greens, cols)


def potential_kernel(start, steps, layout, by_plane, fields_ref, own_ref, *refs):
    nz, plane, own = layout
    others = refs[:lax.axis_size("orb") - 1]
    cols_ref, turned_ref = refs[len(others):len(others) + 2]
    groups = plane if by_plane else nz
    outs = refs[len(others) + 2:len(others) + 2 + groups]
    energy_ref, s_ref, swap = refs[len(others) + 2 + groups:]
    walk, vectors = fields_ref.shape
    rowblocks = cols_ref.shape[0]

    me = lax.axis_index("chol")
    bias = own_ref[...]
    for other in others:
        bias = bias + other[...]
    energy = 0.5 * jnp.sum(bias * bias, axis=1, keepdims=True)
    energy_ref[...] = jnp.broadcast_to(energy, energy_ref.shape)
    shifted = (fields_ref[...] - bias).astype(jnp.bfloat16)
    at = lax.broadcasted_iota(jnp.int32, (walk, walk), 0)
    source = lax.broadcasted_iota(jnp.int32, (walk, walk), 1)
    chip = at // own
    z = (me // plane + chip // plane) % nz
    p = (me % plane) ^ (chip % plane)
    wanted = (z * plane + p) * own + at % own
    pick = (wanted == source).astype(jnp.float32).astype(jnp.bfloat16)
    ordered = jnp.dot(pick, shifted, preferred_element_type=jnp.float32)
    for local in range(rowblocks):
        row = lax.axis_index("orb") * rowblocks + local
        s_ref[local, 0:walk] = ordered.astype(jnp.bfloat16)
        for k, mask in enumerate(slot_masks(cols_ref[local, 1:2, :], row)):
            s_ref[local, (k + 1) * walk:(k + 2) * walk] = jnp.where(mask, ordered, 0.0).astype(jnp.bfloat16)
    swap[...] = swap_matrix()
    first = lax.broadcasted_iota(jnp.int32, (walk, LANES), 1) < BLOCK

    def step(t, carry):
        left = s_ref[lax.div(start + t, BLOCK // CHUNK)]
        tiles = []
        for i in range(0, CHUNK, 2):
            both = jnp.dot(
                left, turned_ref[start + t, :, i * LANES:(i + 2) * LANES], preferred_element_type=jnp.float32
            )
            for side in range(2):
                out = both[:, side * LANES:(side + 1) * LANES]
                near = jnp.where(first, out[0:walk], out[walk:2 * walk])
                far = jnp.where(first, pltpu.roll(out[2 * walk:3 * walk], BLOCK, 1), out[3 * walk:])
                tiles.append(jnp.concatenate([near, far], axis=1).astype(jnp.bfloat16))
        for w0 in range(0, walk, CHUNK):
            mixed = jnp.concatenate([tile[w0:w0 + CHUNK] for tile in tiles], axis=0)
            mixed = jnp.dot(swap[...], mixed, preferred_element_type=jnp.float32).astype(jnp.bfloat16)
            for w in range(CHUNK):
                chip, j = (w0 + w) // own, (w0 + w) % own
                group, inner = (chip % plane, chip // plane) if by_plane else (chip // plane, chip % plane)
                for half in range(2):
                    rows = pl.ds(pl.multiple_of((2 * t + half) * CHUNK, CHUNK), CHUNK)
                    outs[group][inner, j, rows, :] = (
                        mixed[w * CHUNK:(w + 1) * CHUNK, half * LANES:(half + 1) * LANES]
                    )
        return carry

    lax.fori_loop(0, steps, step, 0)


def potential_call(start, steps, layout, by_plane, fields, bias, others, cols, turned):
    nz, plane, own = layout
    walk, vectors = fields.shape
    groups, inner = (plane, nz) if by_plane else (nz, plane)
    rows = 2 * CHUNK
    *parts, energy = pl.pallas_call(
        functools.partial(potential_kernel, start, steps, layout, by_plane),
        out_shape=[
            *[pltpu.VMEM((inner, own, steps * rows, LANES), jnp.bfloat16)] * groups,
            pltpu.VMEM((walk, LANES), jnp.float32),
        ],
        scratch_shapes=[
            pltpu.VMEM((cols.shape[0], 4 * walk, vectors), jnp.bfloat16),
            pltpu.VMEM((CHUNK * CHUNK, CHUNK * CHUNK), jnp.bfloat16),
        ],
        compiler_params=params(16),
        name="potential",
    )(fields, *in_vmem(bias, *others), cols, *in_vmem(turned))
    return parts, energy


def sum_kernel(count, *refs):
    ins, outs = refs[:count], refs[count:]
    for k, out in enumerate(outs):
        total = ins[0][k].astype(jnp.float32)
        for ref in ins[1:]:
            total = total + ref[k].astype(jnp.float32)
        out[...] = total.astype(out.dtype)


def sum_call(arrays):
    pieces = arrays[0].shape[0]
    shape = pltpu.VMEM(arrays[0].shape[1:], jnp.bfloat16)
    return pl.pallas_call(
        functools.partial(sum_kernel, len(arrays)),
        out_shape=[shape] * pieces,
        compiler_params=params(16),
        name="sum_parts",
    )(*in_vmem(*arrays))


def series_kernel(sizes, *refs):
    n_orb, late_steps, early_steps = sizes
    late, early, start = refs[:n_orb], refs[n_orb:2 * n_orb], refs[2 * n_orb:3 * n_orb]
    plane_ref, z_ref, pot, term, total = refs[3 * n_orb:]
    me = lax.axis_index("orb")
    own, half_rows = start[0].shape[:2]
    rowblocks = half_rows // BLOCK
    per = BLOCK // CHUNK
    for d in range(n_orb):
        at = lax.rem(me + d, n_orb)
        term[pl.ds(at, 1)] = start[d][...][None]
        for t in range(rowblocks * per):
            ref, k = (early[d], t) if t < early_steps else (late[d], t - early_steps)
            for half in range(2):
                rows = slice((2 * k + half) * CHUNK, (2 * k + half + 1) * CHUNK)
                pot[pl.ds(at * rowblocks + t // per, 1), :, (t % per) * CHUNK:(t % per + 1) * CHUNK,
                    half * LANES:(half + 1) * LANES] = ref[:, rows, :][None]
    for j in range(own):
        blocks = [term[r // rowblocks, j, (r % rowblocks) * BLOCK:(r % rowblocks + 1) * BLOCK] for r in range(ROWBLK)]
        sums = [jnp.zeros(blocks[0].shape, jnp.float32)] * ROWBLK
        begin = blocks
        for degree in range(1, TAYLOR + 1):
            after = []
            for r in range(ROWBLK):
                right = jnp.concatenate([blocks[c] for c in column_order(r)], axis=0)
                product = jnp.dot(pot[r, j], right, preferred_element_type=jnp.float32)
                after.append((product / degree).astype(jnp.bfloat16))
            blocks = after
            sums = [s + b.astype(jnp.float32) for s, b in zip(sums, blocks)]
        for r in range(ROWBLK):
            moved = begin[r].astype(jnp.float32) + sums[r]
            total[r // rowblocks, j, (r % rowblocks) * BLOCK:(r % rowblocks + 1) * BLOCK] = moved.astype(jnp.bfloat16)
    mine = total[pl.ds(me, 1)][0]
    cut = z_ref.shape[1]
    z_ref[...] = mine[:, :cut]
    plane_ref[...] = mine[:, cut:]


def series_call(sizes, cut, late, early, start):
    n_orb = sizes[0]
    own, half_rows, nocc = start[0].shape
    return pl.pallas_call(
        functools.partial(series_kernel, sizes),
        out_shape=[
            pltpu.VMEM((own, half_rows - cut, nocc), jnp.bfloat16),
            pltpu.VMEM((own, cut, nocc), jnp.bfloat16),
        ],
        scratch_shapes=[
            pltpu.VMEM((ROWBLK, own, BLOCK, 2 * LANES), jnp.bfloat16),
            pltpu.VMEM((n_orb, own, half_rows, nocc), jnp.bfloat16),
            pltpu.VMEM((n_orb, own, half_rows, nocc), jnp.bfloat16),
        ],
        compiler_params=params(16),
        name="series",
    )(*in_vmem(*late, *early, *start))


def place_kernel(layout, *refs):
    nz, plane, own = layout
    z_first, plane_first = refs[:plane], refs[plane:plane + nz]
    out = refs[plane + nz]
    me = lax.axis_index("chol")
    cut = z_first[0].shape[2]
    for dp in range(plane):
        for dz in range(nz):
            chip = lax.rem(me // plane + nz - dz, nz) * plane + (lax.rem(me, plane) ^ dp)
            to = pl.ds(chip * own, own)
            out[to, :cut, :] = z_first[dp][dz]
            out[to, cut:, :] = plane_first[dz][dp]


def place_call(layout, z_first, plane_first):
    nz, plane, own = layout
    cut, rest, nocc = z_first[0].shape[2], plane_first[0].shape[2], z_first[0].shape[3]
    return pl.pallas_call(
        functools.partial(place_kernel, layout),
        out_shape=jax.ShapeDtypeStruct((nz * plane * own, cut + rest, nocc), jnp.bfloat16),
        compiler_params=params(16),
        name="place_walkers",
    )(*in_vmem(*z_first, *plane_first))


def per_device(chol_vals, chol_cols, greens, walkers, fields):
    vectors, rowblocks = chol_vals.shape[:2]
    walk, half_rows = greens.shape[:2]
    chips = lax.axis_size("chol")
    n_orb = lax.axis_size("orb")
    plane = 4 if chips % 4 == 0 else 1
    nz = chips // plane
    own = walk // chips
    layout = (nz, plane, own)
    step_factor = 72.0 / float(vectors * chips * BLOCK) ** 0.5
    me = lax.axis_index("chol")

    def to_plane(a, dp):
        return lax.ppermute(a, "chol", [(c, (c // plane) * plane + ((c % plane) ^ dp)) for c in range(chips)])

    def to_z(a, dz):
        return lax.ppermute(a, "chol", [(c, ((c // plane + dz) % nz) * plane + c % plane) for c in range(chips)])

    def around_orb(a):
        return [a] + [lax.ppermute(a, "orb", [((c + d) % n_orb, c) for c in range(n_orb)]) for d in range(1, n_orb)]

    cols = jnp.transpose(chol_cols, (1, 2, 0))
    mine = lax.dynamic_slice_in_dim(walkers, me * own, own, 0)
    start = around_orb(mine)

    turned, partial_bias = bias_call(chol_vals, greens, cols)
    bias, *others = around_orb(partial_bias)

    total_steps = rowblocks * BLOCK // CHUNK
    early_steps = total_steps * 3 // 8
    late_steps = total_steps - early_steps
    fields_t = fields.T
    early, energy = potential_call(0, early_steps, layout, False, fields_t, bias, others, cols, turned)
    early_in = [early[0]] + [to_z(early[dz], dz) for dz in range(1, nz)]
    late, _ = potential_call(early_steps, late_steps, layout, True, fields_t, bias, others, cols, turned)
    late_in = [late[0]] + [to_plane(late[dp], dp) for dp in range(1, plane)]
    energy = energy[:, 0]
    energy_in = [to_plane(energy, dp) for dp in range(1, plane)]
    start, energy_in, early_in = lax.optimization_barrier((start, energy_in, early_in))
    energy = energy + sum(energy_in)
    early_sums = sum_call(early_in)
    early_in = [early_sums[0]] + [to_plane(early_sums[dp], dp) for dp in range(1, plane)]
    late_sums = sum_call(late_in)
    late_in = [late_sums[0]] + [to_z(late_sums[dz], dz) for dz in range(1, nz)]

    energy_in = [to_z(energy, dz) for dz in range(1, nz)]
    energy_in, late_in = lax.optimization_barrier((energy_in, late_in))
    energy = energy + sum(energy_in)

    def finish(arrays):
        total = arrays[0].astype(jnp.float32)
        for a in arrays[1:]:
            total = total + a.astype(jnp.float32)
        return around_orb((step_factor * total).astype(jnp.bfloat16))

    cut = half_rows // CHUNK * 5 // 8 * CHUNK
    b_part, a_part = series_call((n_orb, late_steps, early_steps), cut, finish(late_in), finish(early_in), start)

    a_all = jnp.stack([a_part] + [to_z(a_part, dz) for dz in range(1, nz)])
    b_all = jnp.stack([b_part] + [to_plane(b_part, dp) for dp in range(1, plane)])
    z_first = [a_all] + [to_plane(a_all, dp) for dp in range(1, plane)]
    plane_first = [b_all] + [to_z(b_all, dz) for dz in range(1, nz)]
    return place_call(layout, z_first, plane_first), energy


def solution(mesh):
    in_specs = (
        P("chol", "orb", None, None),
        P("chol", "orb", None),
        P("walker", "orb", None),
        P("walker", "orb", None),
        P("chol", "walker"),
    )
    out_specs = (P("walker", "orb", None), P("walker"))
    return jax.shard_map(
        per_device, mesh=mesh, in_specs=in_specs, out_specs=out_specs, check_vma=False
    )
```

time: 143 us -> 102 us (0.71)
  Pallas kernels: 66.3 us -> 16.9 us
  local copies, waits for them, and re-layouts: 4.12 us -> 12.5 us
  other arithmetic: 3.84 us -> 0.65 us
  starting transfers between devices: 41.2 us -> 44.3 us
    pallas_call x3, Pallas kernels: 51.1 us -> 11 us  [the longest x1 8.66 us: bias_call(): pl.pallas_call(bias_kernel, in_specs=[pl.BlockSpec(memory_space=pl.ANY),...]
    unnamed x50 -> x16, local copies, waits for them, and re-layouts: 4 us -> 12.4 us
    pallas_call x2, Pallas kernels: 11.2 us -> 5.64 us  [potential_call(): pl.pallas_call(functools.partial(potential_kernel, start, steps, layout,...]
    ppermute x15, waiting for transfers between devices: 20.2 us -> 16 us  [to_z(): lax.ppermute(a, 'chol', [(c, (c // plane + dz) % nz * plane + c % plane)...]
    pallas_call x2, Pallas kernels: 4.01 us -> 0.26 us  [sum_call(): pl.pallas_call(functools.partial(sum_kernel, len(arrays)), out_shape=[sha...]
    ppermute x15, waiting for transfers between devices: 4.76 us -> 7.13 us  [to_plane(): lax.ppermute(a, 'chol', [(c, c // plane * plane + (c % plane ^ dp)) for c...]
    ppermute x4, waiting for transfers between devices: 1.08 us -> 3.32 us  [around_orb(): lax.ppermute(a, 'orb', [((c + d) % n_orb, c) for c in range(n_orb)])]
    ppermute x15, starting transfers between devices: 22.7 us -> 24.9 us  [to_z(): lax.ppermute(a, 'chol', [(c, (c // plane + dz) % nz * plane + c % plane)...]
  transfers between devices with their start and end apart: 34 -> 34, of which waited for: 10 -> 13; matrix products, arithmetic and copies ran while one was open for 3% -> 1% of each run, Pallas kernels for 9% -> 4%
where the time goes in v2:
time: 102 us
  starting transfers between devices  44.3 us (43%)
  waiting for transfers between devices  26.5 us (26%)
  Pallas kernels  16.9 us (17%)
  local copies, waits for them, and re-layouts  12.5 us (12%)
    ppermute x15, starting transfers between devices, to_z(): lax.ppermute(a, 'chol', [(c, (c // plane + dz) % nz * plane + c % plane)...  24.9 us
    ppermute x15, starting transfers between devices, to_plane(): lax.ppermute(a, 'chol', [(c, c // plane * plane + (c % plane ^ dp)) for c...  18.7 us
    ppermute x15, waiting for transfers between devices, to_z(): lax.ppermute(a, 'chol', [(c, (c // plane + dz) % nz * plane + c % plane)...  16 us
    unnamed x16, local copies, waits for them, and re-layouts  12.4 us
    pallas_call x1, Pallas kernels, bias_call(): pl.pallas_call(bias_kernel, in_specs=[pl.BlockSpec(memory_space=pl.ANY),...  8.66 us
    ppermute x15, waiting for transfers between devices, to_plane(): lax.ppermute(a, 'chol', [(c, c // plane * plane + (c % plane ^ dp)) for c...  7.13 us
    pallas_call x2, Pallas kernels, potential_call(): pl.pallas_call(functools.partial(potential_kernel, start, steps, layout,...  5.64 us
    ppermute x4, waiting for transfers between devices, around_orb(): lax.ppermute(a, 'orb', [((c + d) % n_orb, c) for c in range(n_orb)])  3.32 us
  transfers between devices with their start and end apart: 34, of which 13 were waited for; matrix products, arithmetic and copies ran while one was open for 1% of the time, Pallas kernels for 4%

profile of v2, /device:TPU:0, one launch (start us, length us, event | category | flops | bytes accessed | tf_op | source)
XLA Modules:
  0.0 101.6 jit_solution(11393394123690886534)
XLA Ops:
  0.6 0.0 copy-start
  0.7 3.5 %copy-done.3 = bf16[256,2,64,128]{3,2,1,0:T(8,128)(2,1)S(1)} copy-done((bf16[256,2,64,128]{3,2,1,0:T(8,128)(2,1)S(1)}, bf16[256,2,64,128]{3,2,1,0:T(8,128)(2,1)}, u32[]{:S(2)}) %copy-start.3) | copy-done | bytes 8388632
  4.1 1.6 %copy-done.4 = bf16[32,128,256]{2,1,0:T(8,128)(2,1)S(1)} copy-done((bf16[32,128,256]{2,1,0:T(8,128)(2,1)S(1)}, bf16[32,128,256]{2,1,0:T(8,128)(2,1)}, u32[]{:S(2)}) %copy-start.4) | copy-done | bytes 2097176
  5.7 0.7 copy-done.6
  6.4 8.7 %force_bias.1 = (bf16[8,256,2048]{2,1,0:T(8,128)(2,1)S(1)}, f32[32,256]{1,0:T(8,128)S(1)}) custom-call(bf16[256,2,64,128]{3,2,1,0:T(8,128)(2,1)S(1)} %copy-done.3, bf16[32,128,256]{2,1,0:T(8,128)(2,1)S(1)} %copy-done.4, s32[2,2,256]{2,1,0:T(2,128)S(1)} %bitcast.13), custom_call_target="tpu_custom_call" | custom-call | tf_op jit(solution)/shard_map/force_bias/pallas_call | solution.py:122
  15.1 3.3 %copy-done.1 = bf16[8,256,2048]{2,1,0:T(8,128)(2,1)} copy-done((bf16[8,256,2048]{2,1,0:T(8,128)(2,1)}, bf16[8,256,2048]{2,1,0:T(8,128)(2,1)S(1)}, u32[]{:S(2)}) %copy-start.1) | copy-done | bytes 8388632
  18.3 0.5 collective-permute-start
  18.8 0.9 collective-permute-done.refs_0_
  19.7 3.4 %copy-done.2 = bf16[8,256,2048]{2,1,0:T(8,128)(2,1)S(1)} copy-done((bf16[8,256,2048]{2,1,0:T(8,128)(2,1)S(1)}, bf16[8,256,2048]{2,1,0:T(8,128)(2,1)}, u32[]{:S(2)}) %copy-start.2) | copy-done | bytes 8388632
  23.0 1.9 %potential.2 = (bf16[4,2,96,128]{3,2,1,0:T(8,128)(2,1)S(1)}, bf16[4,2,96,128]{3,2,1,0:T(8,128)(2,1)S(1)}, bf16[4,2,96,128]{3,2,1,0:T(8,128)(2,1)S(1)}, bf16[4,2,96,128]{3,2,1,0:T(8,128)(2,1)S(1)}, f32[32,128]{1,0:T(8,128)S(1)}) custom-call(f32[32,256]{1,0:T(8,128)S(1)} %bitcast.10, f32[32,256]{1,0:T(8,128)S(1)} %get-tuple-element.39.own_ref, ...), custom_call_target="tpu_custom_call" | custom-call | tf_op jit(solution)/shard_map/potential/pallas_call | solution.py:214
  25.0 3.0 %collective-permute-start.5 = (bf16[4,2,96,128]{3,2,1,0:T(8,128)(2,1)S(1)}, bf16[4,2,96,128]{3,2,1,0:T(8,128)(2,1)S(1)}, u32[]{:S(2)}, u32[]{:S(2)}) collective-permute-start(bf16[4,2,96,128]{3,2,1,0:T(8,128)(2,1)S(1)} %get-tuple-element.43), channel_id=1, source_target_pairs={{0,8},{2,10},{4,12},{6,14},{8,16},{10,18},{12,20},{14,22},{16,24},... | collective-permute-start | bytes 589832 | tf_op jit(solution)/shard_map/ppermute | solution.py:348
  28.0 0.1 slice_reduce_fusion
  28.1 1.5 %collective-permute-start.2 = (f32[32]{0:T(128)S(1)}, f32[32]{0:T(128)S(1)}, u32[]{:S(2)}, u32[]{:S(2)}) collective-permute-start(f32[32]{0:T(128)S(1)} %slice_reduce_fusion), channel_id=1, source_target_pairs={{0,2},{2,0},{4,6},{6,4},{8,10},{10,8},{12,14},{14,12},{16,18},{18,... | collective-permute-start | bytes 392 | tf_op jit(solution)/shard_map/ppermute | solution.py:345
  29.6 1.5 %collective-permute-start.3 = (f32[32]{0:T(128)S(1)}, f32[32]{0:T(128)S(1)}, u32[]{:S(2)}, u32[]{:S(2)}) collective-permute-start(f32[32]{0:T(128)S(1)} %slice_reduce_fusion), channel_id=1, source_target_pairs={{0,4},{2,6},{4,0},{6,2},{8,12},{10,14},{12,8},{14,10},{16,20},{18,... | collective-permute-start | bytes 392 | tf_op jit(solution)/shard_map/ppermute | solution.py:345
  31.2 0.5 collective-permute-start.4
  31.6 3.7 %potential.3 = (bf16[4,2,160,128]{3,2,1,0:T(8,128)(2,1)S(1)}, bf16[4,2,160,128]{3,2,1,0:T(8,128)(2,1)S(1)}, bf16[4,2,160,128]{3,2,1,0:T(8,128)(2,1)S(1)}, bf16[4,2,160,128]{3,2,1,0:T(8,128)(2,1)S(1)}, f32[32,128]{1,0:T(8,128)}) custom-call(f32[32,256]{1,0:T(8,128)S(1)} %bitcast.11, f32[32,256]{1,0:T(8,128)S(1)} %get-tuple-element.39.own_ref, ...), custom_call_target="tpu_custom_call" | custom-call | tf_op jit(solution)/shard_map/potential/pallas_call | solution.py:214
  35.3 1.5 %collective-permute-start.11 = (bf16[4,2,160,128]{3,2,1,0:T(8,128)(2,1)S(1)}, bf16[4,2,160,128]{3,2,1,0:T(8,128)(2,1)S(1)}, u32[]{:S(2)}, u32[]{:S(2)}) collective-permute-start(bf16[4,2,160,128]{3,2,1,0:T(8,128)(2,1)S(1)} %get-tuple-element.50), channel_id=1, source_target_pairs={{0,2},{2,0},{4,6},{6,4},{8,10},{10,8},{12,14},{14,12},{16,18},{18,... | collective-permute-start | bytes 983048 | tf_op jit(solution)/shard_map/ppermute | solution.py:345
  36.8 1.5 %collective-permute-start.12 = (bf16[4,2,160,128]{3,2,1,0:T(8,128)(2,1)S(1)}, bf16[4,2,160,128]{3,2,1,0:T(8,128)(2,1)S(1)}, u32[]{:S(2)}, u32[]{:S(2)}) collective-permute-start(bf16[4,2,160,128]{3,2,1,0:T(8,128)(2,1)S(1)} %get-tuple-element.51), channel_id=1, source_target_pairs={{0,4},{2,6},{4,0},{6,2},{8,12},{10,14},{12,8},{14,10},{16,20},{18,... | collective-permute-start | bytes 983048 | tf_op jit(solution)/shard_map/ppermute | solution.py:345
  38.3 0.0 collective-permute-done.3
  38.3 0.5 collective-permute-start.13
  38.8 0.1 collective-permute-start.1
  38.9 1.2 %collective-permute-done.1.refs_5_ = bf16[2,128,128]{2,1,0:T(8,128)(2,1)S(1)} collective-permute-done((bf16[2,128,128]{2,1,0:T(8,128)(2,1)S(1)}, bf16[2,128,128]{2,1,0:T(8,128)(2,1)S(1)}, u32[]{:S(2)}, u32[]{:S(2)}) %collective-permute-start.1) | collective-permute-done | bytes 65568 | tf_op jit(solution)/shard_map/ppermute | solution.py:351
  40.2 2.6 %collective-permute-start.6 = (bf16[4,2,96,128]{3,2,1,0:T(8,128)(2,1)S(1)}, bf16[4,2,96,128]{3,2,1,0:T(8,128)(2,1)S(1)}, u32[]{:S(2)}, u32[]{:S(2)}) collective-permute-start(bf16[4,2,96,128]{3,2,1,0:T(8,128)(2,1)S(1)} %get-tuple-element.44), channel_id=1, source_target_pairs={{0,16},{2,18},{4,20},{6,22},{8,24},{10,26},{12,28},{14,30},{16,0},... | collective-permute-start | bytes 589832 | tf_op jit(solution)/shard_map/ppermute | solution.py:348
  42.8 1.3 %collective-permute-start.7 = (bf16[4,2,96,128]{3,2,1,0:T(8,128)(2,1)S(1)}, bf16[4,2,96,128]{3,2,1,0:T(8,128)(2,1)S(1)}, u32[]{:S(2)}, u32[]{:S(2)}) collective-permute-start(bf16[4,2,96,128]{3,2,1,0:T(8,128)(2,1)S(1)} %get-tuple-element.45), channel_id=1, source_target_pairs={{0,24},{2,26},{4,28},{6,30},{8,0},{10,2},{12,4},{14,6},{16,8},{18,... | collective-permute-start | bytes 589832 | tf_op jit(solution)/shard_map/ppermute | solution.py:348
  44.1 9.0 %collective-permute-done.6.refs_2_ = bf16[4,2,96,128]{3,2,1,0:T(8,128)(2,1)S(1)} collective-permute-done((bf16[4,2,96,128]{3,2,1,0:T(8,128)(2,1)S(1)}, bf16[4,2,96,128]{3,2,1,0:T(8,128)(2,1)S(1)}, u32[]{:S(2)}, u32[]{:S(2)}) %collective-permute-start.6) | collective-permute-done | bytes 196640 | tf_op jit(solution)/shard_map/ppermute | solution.py:348
  53.1 0.2 sum_parts.2
  53.3 4.0 %collective-permute-start.14 = (bf16[2,160,128]{2,1,0:T(8,128)(2,1)S(1)}, bf16[2,160,128]{2,1,0:T(8,128)(2,1)S(1)}, u32[]{:S(2)}, u32[]{:S(2)}) collective-permute-start(bf16[2,160,128]{2,1,0:T(8,128)(2,1)S(1)} %get-tuple-element.54), channel_id=1, source_target_pairs={{0,8},{2,10},{4,12},{6,14},{8,16},{10,18},{12,20},{14,22},{16,24},... | collective-permute-start | bytes 245768 | tf_op jit(solution)/shard_map/ppermute | solution.py:348
  57.3 2.0 %collective-permute-start.15 = (bf16[2,160,128]{2,1,0:T(8,128)(2,1)S(1)}, bf16[2,160,128]{2,1,0:T(8,128)(2,1)S(1)}, u32[]{:S(2)}, u32[]{:S(2)}) collective-permute-start(bf16[2,160,128]{2,1,0:T(8,128)(2,1)S(1)} %get-tuple-element.55), channel_id=1, source_target_pairs={{0,16},{2,18},{4,20},{6,22},{8,24},{10,26},{12,28},{14,30},{16,0},... | collective-permute-start | bytes 245768 | tf_op jit(solution)/shard_map/ppermute | solution.py:348
  59.3 0.4 collective-permute-start.16
  59.8 1.9 %collective-permute-start.10 = (f32[32]{0:T(128)S(1)}, f32[32]{0:T(128)S(1)}, u32[]{:S(2)}, u32[]{:S(2)}) collective-permute-start(f32[32]{0:T(128)S(1)} %add_add_fusion.1), channel_id=1, source_target_pairs={{0,24},{2,26},{4,28},{6,30},{8,0},{10,2},{12,4},{14,6},{16,8},{18,... | collective-permute-start | bytes 392 | tf_op jit(solution)/shard_map/ppermute | solution.py:348
  61.7 0.1 collective-permute-start.8
  61.8 0.1 sum_parts.3
  61.9 3.0 %collective-permute-done.10 = f32[32]{0:T(128)S(1)} collective-permute-done((f32[32]{0:T(128)S(1)}, f32[32]{0:T(128)S(1)}, u32[]{:S(2)}, u32[]{:S(2)}) %collective-permute-start.10) | collective-permute-done | bytes 160 | tf_op jit(solution)/shard_map/ppermute | solution.py:348
  64.9 0.6 collective-permute-start.9
  65.5 1.5 %collective-permute-done.8 = f32[32]{0:T(128)S(1)} collective-permute-done((f32[32]{0:T(128)S(1)}, f32[32]{0:T(128)S(1)}, u32[]{:S(2)}, u32[]{:S(2)}) %collective-permute-start.8) | collective-permute-done | bytes 160 | tf_op jit(solution)/shard_map/ppermute | solution.py:348
  67.0 1.5 %collective-permute-start.18 = (bf16[2,96,128]{2,1,0:T(8,128)(2,1)S(1)}, bf16[2,96,128]{2,1,0:T(8,128)(2,1)S(1)}, u32[]{:S(2)}, u32[]{:S(2)}) collective-permute-start(bf16[2,96,128]{2,1,0:T(8,128)(2,1)S(1)} %get-tuple-element.66), channel_id=1, source_target_pairs={{0,2},{2,0},{4,6},{6,4},{8,10},{10,8},{12,14},{14,12},{16,18},{18,... | collective-permute-start | bytes 147464 | tf_op jit(solution)/shard_map/ppermute | solution.py:345
  68.5 0.8 collective-permute-done.9
  69.4 1.7 %collective-permute-start.19 = (bf16[2,96,128]{2,1,0:T(8,128)(2,1)S(1)}, bf16[2,96,128]{2,1,0:T(8,128)(2,1)S(1)}, u32[]{:S(2)}, u32[]{:S(2)}) collective-permute-start(bf16[2,96,128]{2,1,0:T(8,128)(2,1)S(1)} %get-tuple-element.67), channel_id=1, source_target_pairs={{0,4},{2,6},{4,0},{6,2},{8,12},{10,14},{12,8},{14,10},{16,20},{18,... | collective-permute-start | bytes 147464 | tf_op jit(solution)/shard_map/ppermute | solution.py:345
  71.1 1.4 %collective-permute-start.20 = (bf16[2,96,128]{2,1,0:T(8,128)(2,1)S(1)}, bf16[2,96,128]{2,1,0:T(8,128)(2,1)S(1)}, u32[]{:S(2)}, u32[]{:S(2)}) collective-permute-start(bf16[2,96,128]{2,1,0:T(8,128)(2,1)S(1)} %get-tuple-element.68), channel_id=1, source_target_pairs={{0,6},{2,4},{4,2},{6,0},{8,14},{10,12},{12,10},{14,8},{16,22},{18,... | collective-permute-start | bytes 147464 | tf_op jit(solution)/shard_map/ppermute | solution.py:345
  72.5 0.1 multiply_convert_fusion.refs_0_
  72.6 0.1 collective-permute-start.17
  72.7 0.8 collective-permute-done.19
  73.4 2.6 %collective-permute-done.20 = bf16[2,96,128]{2,1,0:T(8,128)(2,1)S(1)} collective-permute-done((bf16[2,96,128]{2,1,0:T(8,128)(2,1)S(1)}, bf16[2,96,128]{2,1,0:T(8,128)(2,1)S(1)}, u32[]{:S(2)}, u32[]{:S(2)}) %collective-permute-start.20) | collective-permute-done | bytes 49184 | tf_op jit(solution)/shard_map/ppermute | solution.py:345
  76.1 0.1 collective-permute-start.21
  76.2 1.2 %collective-permute-done.21.refs_3_ = bf16[2,96,128]{2,1,0:T(8,128)(2,1)S(1)} collective-permute-done((bf16[2,96,128]{2,1,0:T(8,128)(2,1)S(1)}, bf16[2,96,128]{2,1,0:T(8,128)(2,1)S(1)}, u32[]{:S(2)}, u32[]{:S(2)}) %collective-permute-start.21) | collective-permute-done | bytes 49184 | tf_op jit(solution)/shard_map/ppermute | solution.py:351
  77.4 1.3 %series.1 = (bf16[2,48,128]{2,1,0:T(8,128)(2,1)S(1)}, bf16[2,80,128]{2,1,0:T(8,128)(2,1)S(1)}) custom-call(bf16[2,160,128]{2,1,0:T(8,128)(2,1)S(1)} %multiply_convert_fusion.refs_0_, bf16[2,160,128]{2,1,0:T(8,128)(2,1)S(1)} %collective-permute-done.17.refs_1_, bf16[2,96,128]{2,1,0:T(8,128)(2,1)S(1)} %multiply_convert_fusion.1.refs_2_, ...), custom_call_target="tpu_custom_call" | custom-call | tf_op jit(solution)/shard_map/series/pallas_call | solution.py:291
  78.7 1.6 %collective-permute-start.28 = (bf16[2,48,128]{2,1,0:T(8,128)(2,1)S(1)}, bf16[2,48,128]{2,1,0:T(8,128)(2,1)S(1)}, u32[]{:S(2)}, u32[]{:S(2)}) collective-permute-start(bf16[2,48,128]{2,1,0:T(8,128)(2,1)S(1)} %get-tuple-element.72), channel_id=1, source_target_pairs={{0,2},{2,0},{4,6},{6,4},{8,10},{10,8},{12,14},{14,12},{16,18},{18,... | collective-permute-start | bytes 73736 | tf_op jit(solution)/shard_map/ppermute | solution.py:345
  80.2 0.5 collective-permute-start.29
  80.7 1.5 %collective-permute-start.30 = (bf16[2,48,128]{2,1,0:T(8,128)(2,1)S(1)}, bf16[2,48,128]{2,1,0:T(8,128)(2,1)S(1)}, u32[]{:S(2)}, u32[]{:S(2)}) collective-permute-start(bf16[2,48,128]{2,1,0:T(8,128)(2,1)S(1)} %get-tuple-element.72), channel_id=1, source_target_pairs={{0,6},{2,4},{4,2},{6,0},{8,14},{10,12},{12,10},{14,8},{16,22},{18,... | collective-permute-start | bytes 73736 | tf_op jit(solution)/shard_map/ppermute | solution.py:345
  82.2 1.7 %collective-permute-start.22 = (bf16[2,80,128]{2,1,0:T(8,128)(2,1)S(1)}, bf16[2,80,128]{2,1,0:T(8,128)(2,1)S(1)}, u32[]{:S(2)}, u32[]{:S(2)}) collective-permute-start(bf16[2,80,128]{2,1,0:T(8,128)(2,1)S(1)} %get-tuple-element.71), channel_id=1, source_target_pairs={{0,8},{2,10},{4,12},{6,14},{8,16},{10,18},{12,20},{14,22},{16,24},... | collective-permute-start | bytes 122888 | tf_op jit(solution)/shard_map/ppermute | solution.py:348
  83.9 1.0 collective-permute-start.23
  84.9 1.4 %collective-permute-start.24 = (bf16[2,80,128]{2,1,0:T(8,128)(2,1)S(1)}, bf16[2,80,128]{2,1,0:T(8,128)(2,1)S(1)}, u32[]{:S(2)}, u32[]{:S(2)}) collective-permute-start(bf16[2,80,128]{2,1,0:T(8,128)(2,1)S(1)} %get-tuple-element.71), channel_id=1, source_target_pairs={{0,24},{2,26},{4,28},{6,30},{8,0},{10,2},{12,4},{14,6},{16,8},{18,... | collective-permute-start | bytes 122888 | tf_op jit(solution)/shard_map/ppermute | solution.py:348
  86.3 0.9 collective-permute-start.31
  87.3 1.7 %collective-permute-start.32 = (bf16[4,2,48,128]{3,2,1,0:T(8,128)(2,1)S(1)}, bf16[4,2,48,128]{3,2,1,0:T(8,128)(2,1)S(1)}, u32[]{:S(2)}, u32[]{:S(2)}) collective-permute-start(bf16[4,2,48,128]{3,2,1,0:T(8,128)(2,1)S(1)} %pad_maximum_fusion.1.refs_4_), channel_id=1, source_target_pairs={{0,16},{2,18},{4,20},{6,22},{8,24},{10,26},{12,28},{14,30},{16,0},... | collective-permute-start | bytes 294920 | tf_op jit(solution)/shard_map/ppermute | solution.py:348
  89.0 2.1 %collective-permute-start.33 = (bf16[4,2,48,128]{3,2,1,0:T(8,128)(2,1)S(1)}, bf16[4,2,48,128]{3,2,1,0:T(8,128)(2,1)S(1)}, u32[]{:S(2)}, u32[]{:S(2)}) collective-permute-start(bf16[4,2,48,128]{3,2,1,0:T(8,128)(2,1)S(1)} %pad_maximum_fusion.1.refs_4_), channel_id=1, source_target_pairs={{0,24},{2,26},{4,28},{6,30},{8,0},{10,2},{12,4},{14,6},{16,8},{18,... | collective-permute-start | bytes 294920 | tf_op jit(solution)/shard_map/ppermute | solution.py:348
  91.1 1.6 %collective-permute-start.25 = (bf16[4,2,80,128]{3,2,1,0:T(8,128)(2,1)S(1)}, bf16[4,2,80,128]{3,2,1,0:T(8,128)(2,1)S(1)}, u32[]{:S(2)}, u32[]{:S(2)}) collective-permute-start(bf16[4,2,80,128]{3,2,1,0:T(8,128)(2,1)S(1)} %pad_maximum_fusion.refs_0_), channel_id=1, source_target_pairs={{0,2},{2,0},{4,6},{6,4},{8,10},{10,8},{12,14},{14,12},{16,18},{18,... | collective-permute-start | bytes 491528 | tf_op jit(solution)/shard_map/ppermute | solution.py:345
  92.7 0.5 collective-permute-start.26
  93.2 0.8 collective-permute-done.31.refs_5_
  94.0 1.4 %collective-permute-start.27 = (bf16[4,2,80,128]{3,2,1,0:T(8,128)(2,1)S(1)}, bf16[4,2,80,128]{3,2,1,0:T(8,128)(2,1)S(1)}, u32[]{:S(2)}, u32[]{:S(2)}) collective-permute-start(bf16[4,2,80,128]{3,2,1,0:T(8,128)(2,1)S(1)} %pad_maximum_fusion.refs_0_), channel_id=1, source_target_pairs={{0,6},{2,4},{4,2},{6,0},{8,14},{10,12},{12,10},{14,8},{16,22},{18,... | collective-permute-start | bytes 491528 | tf_op jit(solution)/shard_map/ppermute | solution.py:345
  95.4 0.5 add_add_fusion
  95.9 0.9 collective-permute-done.32.refs_6_
  96.8 0.5 collective-permute-done.25.refs_1_
  97.3 3.2 %collective-permute-done.26.refs_2_ = bf16[4,2,80,128]{3,2,1,0:T(8,128)(2,1)S(1)} collective-permute-done((bf16[4,2,80,128]{3,2,1,0:T(8,128)(2,1)S(1)}, bf16[4,2,80,128]{3,2,1,0:T(8,128)(2,1)S(1)}, u32[]{:S(2)}, u32[]{:S(2)}) %collective-permute-start.26) | collective-permute-done | bytes 163872 | tf_op jit(solution)/shard_map/ppermute | solution.py:345
  100.5 1.1 %place_walkers.1 = bf16[32,128,128]{2,1,0:T(8,128)(2,1)} custom-call(bf16[4,2,80,128]{3,2,1,0:T(8,128)(2,1)S(1)} %pad_maximum_fusion.refs_0_, bf16[4,2,80,128]{3,2,1,0:T(8,128)(2,1)S(1)} %collective-permute-done.25.refs_1_, bf16[4,2,80,128]{3,2,1,0:T(8,128)(2,1)S(1)} %collective-permute-done.26.refs_2_, ...), custom_call_target="tpu_custom_call" | custom-call | tf_op jit(solution)/shard_map/place_walkers/pallas_call | solution.py:324
  (35 shorter events, 0.2 us)
Async XLA Ops:
  0.6 38.2 %copy-start = (bf16[32,128,128]{2,1,0:T(8,128)(2,1)S(1)}, bf16[32,128,128]{2,1,0:T(8,128)(2,1)}, u32[]{:S(2)}) copy-start(bf16[32,128,128]{2,1,0:T(8,128)(2,1)} %param.8) | copy-start | bytes 3145732
  0.6 3.5 %copy-start.3 = (bf16[256,2,64,128]{3,2,1,0:T(8,128)(2,1)S(1)}, bf16[256,2,64,128]{3,2,1,0:T(8,128)(2,1)}, u32[]{:S(2)}) copy-start(bf16[256,2,64,128]{3,2,1,0:T(8,128)(2,1)} %vals_hbm.1) | copy-start | bytes 25165828
  4.1 1.6 %copy-start.4 = (bf16[32,128,256]{2,1,0:T(8,128)(2,1)S(1)}, bf16[32,128,256]{2,1,0:T(8,128)(2,1)}, u32[]{:S(2)}) copy-start(bf16[32,128,256]{2,1,0:T(8,128)(2,1)} %greens_hbm.1) | copy-start | bytes 6291460
  5.7 0.7 copy-start.6
  6.4 13.3 %copy-start.5 = (f32[256,32]{0,1:T(8,128)S(1)}, f32[256,32]{0,1:T(8,128)}, u32[]{:S(2)}) copy-start(f32[256,32]{0,1:T(8,128)} %param.9) | copy-start | bytes 98308
  6.4 13.3 %copy-start.7 = (s32[256,2,2]{0,2,1:T(2,128)S(1)}, s32[256,2,2]{0,2,1:T(2,128)}, u32[]{:S(2)}) copy-start(s32[256,2,2]{0,2,1:T(2,128)} %param.6) | copy-start | bytes 12292
  15.1 3.3 %copy-start.1 = (bf16[8,256,2048]{2,1,0:T(8,128)(2,1)}, bf16[8,256,2048]{2,1,0:T(8,128)(2,1)S(1)}, u32[]{:S(2)}) copy-start(bf16[8,256,2048]{2,1,0:T(8,128)(2,1)S(1)} %get-tuple-element.40.refs_2_) | copy-start | bytes 25165828
  18.3 1.3 %collective-permute-start = (f32[32,256]{1,0:T(8,128)S(1)}, f32[32,256]{1,0:T(8,128)S(1)}, u32[]{:S(2)}, u32[]{:S(2)}) collective-permute-start(f32[32,256]{1,0:T(8,128)S(1)} %get-tuple-element.39.own_ref), channel_id=1, source_target_pairs={{1,0},{0,1},{3,2},{2,3},{5,4},{4,5},{7,6},{6,7},{9,8},{8,9},{11,10... | collective-permute-start | bytes 98312 | tf_op jit(solution)/shard_map/ppermute | solution.py:351
  19.7 3.4 %copy-start.2 = (bf16[8,256,2048]{2,1,0:T(8,128)(2,1)S(1)}, bf16[8,256,2048]{2,1,0:T(8,128)(2,1)}, u32[]{:S(2)}) copy-start(bf16[8,256,2048]{2,1,0:T(8,128)(2,1)} %copy-done.1) | copy-start | bytes 25165828
  25.0 17.8 %collective-permute-start.5 = (bf16[4,2,96,128]{3,2,1,0:T(8,128)(2,1)S(1)}, bf16[4,2,96,128]{3,2,1,0:T(8,128)(2,1)S(1)}, u32[]{:S(2)}, u32[]{:S(2)}) collective-permute-start(bf16[4,2,96,128]{3,2,1,0:T(8,128)(2,1)S(1)} %get-tuple-element.43), channel_id=1, source_target_pairs={{0,8},{2,10},{4,12},{6,14},{8,16},{10,18},{12,20},{14,22},{16,24},... | collective-permute-start | bytes 589832 | tf_op jit(solution)/shard_map/ppermute | solution.py:348
  28.1 8.7 %collective-permute-start.2 = (f32[32]{0:T(128)S(1)}, f32[32]{0:T(128)S(1)}, u32[]{:S(2)}, u32[]{:S(2)}) collective-permute-start(f32[32]{0:T(128)S(1)} %slice_reduce_fusion), channel_id=1, source_target_pairs={{0,2},{2,0},{4,6},{6,4},{8,10},{10,8},{12,14},{14,12},{16,18},{18,... | collective-permute-start | bytes 392 | tf_op jit(solution)/shard_map/ppermute | solution.py:345
  29.6 8.7 %collective-permute-start.3 = (f32[32]{0:T(128)S(1)}, f32[32]{0:T(128)S(1)}, u32[]{:S(2)}, u32[]{:S(2)}) collective-permute-start(f32[32]{0:T(128)S(1)} %slice_reduce_fusion), channel_id=1, source_target_pairs={{0,4},{2,6},{4,0},{6,2},{8,12},{10,14},{12,8},{14,10},{16,20},{18,... | collective-permute-start | bytes 392 | tf_op jit(solution)/shard_map/ppermute | solution.py:345
  31.2 7.7 %collective-permute-start.4 = (f32[32]{0:T(128)S(1)}, f32[32]{0:T(128)S(1)}, u32[]{:S(2)}, u32[]{:S(2)}) collective-permute-start(f32[32]{0:T(128)S(1)} %slice_reduce_fusion), channel_id=1, source_target_pairs={{0,6},{2,4},{4,2},{6,0},{8,14},{10,12},{12,10},{14,8},{16,22},{18,... | collective-permute-start | bytes 392 | tf_op jit(solution)/shard_map/ppermute | solution.py:345
  35.3 17.8 %collective-permute-start.11 = (bf16[4,2,160,128]{3,2,1,0:T(8,128)(2,1)S(1)}, bf16[4,2,160,128]{3,2,1,0:T(8,128)(2,1)S(1)}, u32[]{:S(2)}, u32[]{:S(2)}) collective-permute-start(bf16[4,2,160,128]{3,2,1,0:T(8,128)(2,1)S(1)} %get-tuple-element.50), channel_id=1, source_target_pairs={{0,2},{2,0},{4,6},{6,4},{8,10},{10,8},{12,14},{14,12},{16,18},{18,... | collective-permute-start | bytes 983048 | tf_op jit(solution)/shard_map/ppermute | solution.py:345
  36.8 16.3 %collective-permute-start.12 = (bf16[4,2,160,128]{3,2,1,0:T(8,128)(2,1)S(1)}, bf16[4,2,160,128]{3,2,1,0:T(8,128)(2,1)S(1)}, u32[]{:S(2)}, u32[]{:S(2)}) collective-permute-start(bf16[4,2,160,128]{3,2,1,0:T(8,128)(2,1)S(1)} %get-tuple-element.51), channel_id=1, source_target_pairs={{0,4},{2,6},{4,0},{6,2},{8,12},{10,14},{12,8},{14,10},{16,20},{18,... | collective-permute-start | bytes 983048 | tf_op jit(solution)/shard_map/ppermute | solution.py:345
  38.3 14.7 %collective-permute-start.13 = (bf16[4,2,160,128]{3,2,1,0:T(8,128)(2,1)S(1)}, bf16[4,2,160,128]{3,2,1,0:T(8,128)(2,1)S(1)}, u32[]{:S(2)}, u32[]{:S(2)}) collective-permute-start(bf16[4,2,160,128]{3,2,1,0:T(8,128)(2,1)S(1)} %get-tuple-element.52), channel_id=1, source_target_pairs={{0,6},{2,4},{4,2},{6,0},{8,14},{10,12},{12,10},{14,8},{16,22},{18,... | collective-permute-start | bytes 983048 | tf_op jit(solution)/shard_map/ppermute | solution.py:345
  38.8 1.3 %collective-permute-start.1 = (bf16[2,128,128]{2,1,0:T(8,128)(2,1)S(1)}, bf16[2,128,128]{2,1,0:T(8,128)(2,1)S(1)}, u32[]{:S(2)}, u32[]{:S(2)}) collective-permute-start(bf16[2,128,128]{2,1,0:T(8,128)(2,1)S(1)} %constant_dynamic-slice_fusion.refs_4_), channel_id=1, source_target_pairs={{1,0},{0,1},{3,2},{2,3},{5,4},{4,5},{7,6},{6,7},{9,8},{8,9},{11,10... | collective-permute-start | bytes 196616 | tf_op jit(solution)/shard_map/ppermute | solution.py:351
  40.2 12.9 %collective-permute-start.6 = (bf16[4,2,96,128]{3,2,1,0:T(8,128)(2,1)S(1)}, bf16[4,2,96,128]{3,2,1,0:T(8,128)(2,1)S(1)}, u32[]{:S(2)}, u32[]{:S(2)}) collective-permute-start(bf16[4,2,96,128]{3,2,1,0:T(8,128)(2,1)S(1)} %get-tuple-element.44), channel_id=1, source_target_pairs={{0,16},{2,18},{4,20},{6,22},{8,24},{10,26},{12,28},{14,30},{16,0},... | collective-permute-start | bytes 589832 | tf_op jit(solution)/shard_map/ppermute | solution.py:348
  42.8 10.3 %collective-permute-start.7 = (bf16[4,2,96,128]{3,2,1,0:T(8,128)(2,1)S(1)}, bf16[4,2,96,128]{3,2,1,0:T(8,128)(2,1)S(1)}, u32[]{:S(2)}, u32[]{:S(2)}) collective-permute-start(bf16[4,2,96,128]{3,2,1,0:T(8,128)(2,1)S(1)} %get-tuple-element.45), channel_id=1, source_target_pairs={{0,24},{2,26},{4,28},{6,30},{8,0},{10,2},{12,4},{14,6},{16,8},{18,... | collective-permute-start | bytes 589832 | tf_op jit(solution)/shard_map/ppermute | solution.py:348
  53.3 17.8 %collective-permute-start.14 = (bf16[2,160,128]{2,1,0:T(8,128)(2,1)S(1)}, bf16[2,160,128]{2,1,0:T(8,128)(2,1)S(1)}, u32[]{:S(2)}, u32[]{:S(2)}) collective-permute-start(bf16[2,160,128]{2,1,0:T(8,128)(2,1)S(1)} %get-tuple-element.54), channel_id=1, source_target_pairs={{0,8},{2,10},{4,12},{6,14},{8,16},{10,18},{12,20},{14,22},{16,24},... | collective-permute-start | bytes 245768 | tf_op jit(solution)/shard_map/ppermute | solution.py:348
  57.3 15.2 %collective-permute-start.15 = (bf16[2,160,128]{2,1,0:T(8,128)(2,1)S(1)}, bf16[2,160,128]{2,1,0:T(8,128)(2,1)S(1)}, u32[]{:S(2)}, u32[]{:S(2)}) collective-permute-start(bf16[2,160,128]{2,1,0:T(8,128)(2,1)S(1)} %get-tuple-element.55), channel_id=1, source_target_pairs={{0,16},{2,18},{4,20},{6,22},{8,24},{10,26},{12,28},{14,30},{16,0},... | collective-permute-start | bytes 245768 | tf_op jit(solution)/shard_map/ppermute | solution.py:348
  59.3 13.2 %collective-permute-start.16 = (bf16[2,160,128]{2,1,0:T(8,128)(2,1)S(1)}, bf16[2,160,128]{2,1,0:T(8,128)(2,1)S(1)}, u32[]{:S(2)}, u32[]{:S(2)}) collective-permute-start(bf16[2,160,128]{2,1,0:T(8,128)(2,1)S(1)} %get-tuple-element.56), channel_id=1, source_target_pairs={{0,24},{2,26},{4,28},{6,30},{8,0},{10,2},{12,4},{14,6},{16,8},{18,... | collective-permute-start | bytes 245768 | tf_op jit(solution)/shard_map/ppermute | solution.py:348
  59.8 5.2 %collective-permute-start.10 = (f32[32]{0:T(128)S(1)}, f32[32]{0:T(128)S(1)}, u32[]{:S(2)}, u32[]{:S(2)}) collective-permute-start(f32[32]{0:T(128)S(1)} %add_add_fusion.1), channel_id=1, source_target_pairs={{0,24},{2,26},{4,28},{6,30},{8,0},{10,2},{12,4},{14,6},{16,8},{18,... | collective-permute-start | bytes 392 | tf_op jit(solution)/shard_map/ppermute | solution.py:348
  61.7 5.3 %collective-permute-start.8 = (f32[32]{0:T(128)S(1)}, f32[32]{0:T(128)S(1)}, u32[]{:S(2)}, u32[]{:S(2)}) collective-permute-start(f32[32]{0:T(128)S(1)} %add_add_fusion.1), channel_id=1, source_target_pairs={{0,8},{2,10},{4,12},{6,14},{8,16},{10,18},{12,20},{14,22},{16,24},... | collective-permute-start | bytes 392 | tf_op jit(solution)/shard_map/ppermute | solution.py:348
  64.9 4.4 %collective-permute-start.9 = (f32[32]{0:T(128)S(1)}, f32[32]{0:T(128)S(1)}, u32[]{:S(2)}, u32[]{:S(2)}) collective-permute-start(f32[32]{0:T(128)S(1)} %add_add_fusion.1), channel_id=1, source_target_pairs={{0,16},{2,18},{4,20},{6,22},{8,24},{10,26},{12,28},{14,30},{16,0},... | collective-permute-start | bytes 392 | tf_op jit(solution)/shard_map/ppermute | solution.py:348
  67.0 5.6 %collective-permute-start.18 = (bf16[2,96,128]{2,1,0:T(8,128)(2,1)S(1)}, bf16[2,96,128]{2,1,0:T(8,128)(2,1)S(1)}, u32[]{:S(2)}, u32[]{:S(2)}) collective-permute-start(bf16[2,96,128]{2,1,0:T(8,128)(2,1)S(1)} %get-tuple-element.66), channel_id=1, source_target_pairs={{0,2},{2,0},{4,6},{6,4},{8,10},{10,8},{12,14},{14,12},{16,18},{18,... | collective-permute-start | bytes 147464 | tf_op jit(solution)/shard_map/ppermute | solution.py:345
  69.4 4.1 %collective-permute-start.19 = (bf16[2,96,128]{2,1,0:T(8,128)(2,1)S(1)}, bf16[2,96,128]{2,1,0:T(8,128)(2,1)S(1)}, u32[]{:S(2)}, u32[]{:S(2)}) collective-permute-start(bf16[2,96,128]{2,1,0:T(8,128)(2,1)S(1)} %get-tuple-element.67), channel_id=1, source_target_pairs={{0,4},{2,6},{4,0},{6,2},{8,12},{10,14},{12,8},{14,10},{16,20},{18,... | collective-permute-start | bytes 147464 | tf_op jit(solution)/shard_map/ppermute | solution.py:345
  71.1 5.0 %collective-permute-start.20 = (bf16[2,96,128]{2,1,0:T(8,128)(2,1)S(1)}, bf16[2,96,128]{2,1,0:T(8,128)(2,1)S(1)}, u32[]{:S(2)}, u32[]{:S(2)}) collective-permute-start(bf16[2,96,128]{2,1,0:T(8,128)(2,1)S(1)} %get-tuple-element.68), channel_id=1, source_target_pairs={{0,6},{2,4},{4,2},{6,0},{8,14},{10,12},{12,10},{14,8},{16,22},{18,... | collective-permute-start | bytes 147464 | tf_op jit(solution)/shard_map/ppermute | solution.py:345
  72.6 4.8 %collective-permute-start.17 = (bf16[2,160,128]{2,1,0:T(8,128)(2,1)S(1)}, bf16[2,160,128]{2,1,0:T(8,128)(2,1)S(1)}, u32[]{:S(2)}, u32[]{:S(2)}) collective-permute-start(bf16[2,160,128]{2,1,0:T(8,128)(2,1)S(1)} %multiply_convert_fusion.refs_0_), channel_id=1, source_target_pairs={{1,0},{0,1},{3,2},{2,3},{5,4},{4,5},{7,6},{6,7},{9,8},{8,9},{11,10... | collective-permute-start | bytes 245768 | tf_op jit(solution)/shard_map/ppermute | solution.py:351
  76.1 1.3 %collective-permute-start.21 = (bf16[2,96,128]{2,1,0:T(8,128)(2,1)S(1)}, bf16[2,96,128]{2,1,0:T(8,128)(2,1)S(1)}, u32[]{:S(2)}, u32[]{:S(2)}) collective-permute-start(bf16[2,96,128]{2,1,0:T(8,128)(2,1)S(1)} %multiply_convert_fusion.1.refs_2_), channel_id=1, source_target_pairs={{1,0},{0,1},{3,2},{2,3},{5,4},{4,5},{7,6},{6,7},{9,8},{8,9},{11,10... | collective-permute-start | bytes 147464 | tf_op jit(solution)/shard_map/ppermute | solution.py:351
  78.7 6.2 %collective-permute-start.28 = (bf16[2,48,128]{2,1,0:T(8,128)(2,1)S(1)}, bf16[2,48,128]{2,1,0:T(8,128)(2,1)S(1)}, u32[]{:S(2)}, u32[]{:S(2)}) collective-permute-start(bf16[2,48,128]{2,1,0:T(8,128)(2,1)S(1)} %get-tuple-element.72), channel_id=1, source_target_pairs={{0,2},{2,0},{4,6},{6,4},{8,10},{10,8},{12,14},{14,12},{16,18},{18,... | collective-permute-start | bytes 73736 | tf_op jit(solution)/shard_map/ppermute | solution.py:345
  80.2 6.1 %collective-permute-start.29 = (bf16[2,48,128]{2,1,0:T(8,128)(2,1)S(1)}, bf16[2,48,128]{2,1,0:T(8,128)(2,1)S(1)}, u32[]{:S(2)}, u32[]{:S(2)}) collective-permute-start(bf16[2,48,128]{2,1,0:T(8,128)(2,1)S(1)} %get-tuple-element.72), channel_id=1, source_target_pairs={{0,4},{2,6},{4,0},{6,2},{8,12},{10,14},{12,8},{14,10},{16,20},{18,... | collective-permute-start | bytes 73736 | tf_op jit(solution)/shard_map/ppermute | solution.py:345
  80.7 5.6 %collective-permute-start.30 = (bf16[2,48,128]{2,1,0:T(8,128)(2,1)S(1)}, bf16[2,48,128]{2,1,0:T(8,128)(2,1)S(1)}, u32[]{:S(2)}, u32[]{:S(2)}) collective-permute-start(bf16[2,48,128]{2,1,0:T(8,128)(2,1)S(1)} %get-tuple-element.72), channel_id=1, source_target_pairs={{0,6},{2,4},{4,2},{6,0},{8,14},{10,12},{12,10},{14,8},{16,22},{18,... | collective-permute-start | bytes 73736 | tf_op jit(solution)/shard_map/ppermute | solution.py:345
  82.2 6.7 %collective-permute-start.22 = (bf16[2,80,128]{2,1,0:T(8,128)(2,1)S(1)}, bf16[2,80,128]{2,1,0:T(8,128)(2,1)S(1)}, u32[]{:S(2)}, u32[]{:S(2)}) collective-permute-start(bf16[2,80,128]{2,1,0:T(8,128)(2,1)S(1)} %get-tuple-element.71), channel_id=1, source_target_pairs={{0,8},{2,10},{4,12},{6,14},{8,16},{10,18},{12,20},{14,22},{16,24},... | collective-permute-start | bytes 122888 | tf_op jit(solution)/shard_map/ppermute | solution.py:348
  83.9 7.2 %collective-permute-start.23 = (bf16[2,80,128]{2,1,0:T(8,128)(2,1)S(1)}, bf16[2,80,128]{2,1,0:T(8,128)(2,1)S(1)}, u32[]{:S(2)}, u32[]{:S(2)}) collective-permute-start(bf16[2,80,128]{2,1,0:T(8,128)(2,1)S(1)} %get-tuple-element.71), channel_id=1, source_target_pairs={{0,16},{2,18},{4,20},{6,22},{8,24},{10,26},{12,28},{14,30},{16,0},... | collective-permute-start | bytes 122888 | tf_op jit(solution)/shard_map/ppermute | solution.py:348
  84.9 6.2 %collective-permute-start.24 = (bf16[2,80,128]{2,1,0:T(8,128)(2,1)S(1)}, bf16[2,80,128]{2,1,0:T(8,128)(2,1)S(1)}, u32[]{:S(2)}, u32[]{:S(2)}) collective-permute-start(bf16[2,80,128]{2,1,0:T(8,128)(2,1)S(1)} %get-tuple-element.71), channel_id=1, source_target_pairs={{0,24},{2,26},{4,28},{6,30},{8,0},{10,2},{12,4},{14,6},{16,8},{18,... | collective-permute-start | bytes 122888 | tf_op jit(solution)/shard_map/ppermute | solution.py:348
  86.3 7.6 %collective-permute-start.31 = (bf16[4,2,48,128]{3,2,1,0:T(8,128)(2,1)S(1)}, bf16[4,2,48,128]{3,2,1,0:T(8,128)(2,1)S(1)}, u32[]{:S(2)}, u32[]{:S(2)}) collective-permute-start(bf16[4,2,48,128]{3,2,1,0:T(8,128)(2,1)S(1)} %pad_maximum_fusion.1.refs_4_), channel_id=1, source_target_pairs={{0,8},{2,10},{4,12},{6,14},{8,16},{10,18},{12,20},{14,22},{16,24},... | collective-permute-start | bytes 294920 | tf_op jit(solution)/shard_map/ppermute | solution.py:348
  87.3 9.6 %collective-permute-start.32 = (bf16[4,2,48,128]{3,2,1,0:T(8,128)(2,1)S(1)}, bf16[4,2,48,128]{3,2,1,0:T(8,128)(2,1)S(1)}, u32[]{:S(2)}, u32[]{:S(2)}) collective-permute-start(bf16[4,2,48,128]{3,2,1,0:T(8,128)(2,1)S(1)} %pad_maximum_fusion.1.refs_4_), channel_id=1, source_target_pairs={{0,16},{2,18},{4,20},{6,22},{8,24},{10,26},{12,28},{14,30},{16,0},... | collective-permute-start | bytes 294920 | tf_op jit(solution)/shard_map/ppermute | solution.py:348
  89.0 7.8 %collective-permute-start.33 = (bf16[4,2,48,128]{3,2,1,0:T(8,128)(2,1)S(1)}, bf16[4,2,48,128]{3,2,1,0:T(8,128)(2,1)S(1)}, u32[]{:S(2)}, u32[]{:S(2)}) collective-permute-start(bf16[4,2,48,128]{3,2,1,0:T(8,128)(2,1)S(1)} %pad_maximum_fusion.1.refs_4_), channel_id=1, source_target_pairs={{0,24},{2,26},{4,28},{6,30},{8,0},{10,2},{12,4},{14,6},{16,8},{18,... | collective-permute-start | bytes 294920 | tf_op jit(solution)/shard_map/ppermute | solution.py:348
  91.1 6.2 %collective-permute-start.25 = (bf16[4,2,80,128]{3,2,1,0:T(8,128)(2,1)S(1)}, bf16[4,2,80,128]{3,2,1,0:T(8,128)(2,1)S(1)}, u32[]{:S(2)}, u32[]{:S(2)}) collective-permute-start(bf16[4,2,80,128]{3,2,1,0:T(8,128)(2,1)S(1)} %pad_maximum_fusion.refs_0_), channel_id=1, source_target_pairs={{0,2},{2,0},{4,6},{6,4},{8,10},{10,8},{12,14},{14,12},{16,18},{18,... | collective-permute-start | bytes 491528 | tf_op jit(solution)/shard_map/ppermute | solution.py:345
  92.7 7.8 %collective-permute-start.26 = (bf16[4,2,80,128]{3,2,1,0:T(8,128)(2,1)S(1)}, bf16[4,2,80,128]{3,2,1,0:T(8,128)(2,1)S(1)}, u32[]{:S(2)}, u32[]{:S(2)}) collective-permute-start(bf16[4,2,80,128]{3,2,1,0:T(8,128)(2,1)S(1)} %pad_maximum_fusion.refs_0_), channel_id=1, source_target_pairs={{0,4},{2,6},{4,0},{6,2},{8,12},{10,14},{12,8},{14,10},{16,20},{18,... | collective-permute-start | bytes 491528 | tf_op jit(solution)/shard_map/ppermute | solution.py:345
  94.0 6.5 %collective-permute-start.27 = (bf16[4,2,80,128]{3,2,1,0:T(8,128)(2,1)S(1)}, bf16[4,2,80,128]{3,2,1,0:T(8,128)(2,1)S(1)}, u32[]{:S(2)}, u32[]{:S(2)}) collective-permute-start(bf16[4,2,80,128]{3,2,1,0:T(8,128)(2,1)S(1)} %pad_maximum_fusion.refs_0_), channel_id=1, source_target_pairs={{0,6},{2,4},{4,2},{6,0},{8,14},{10,12},{12,10},{14,8},{16,22},{18,... | collective-permute-start | bytes 491528 | tf_op jit(solution)/shard_map/ppermute | solution.py:345

commit v3 on v2

--- a/solution.py
+++ b/solution.py
@@ -23,6 +23,10 @@
     return [pltpu.with_memory_space_constraint(a, pltpu.VMEM) for a in arrays]
 
 
+def in_hbm(*arrays):
+    return [pltpu.with_memory_space_constraint(a, pltpu.HBM) for a in arrays]
+
+
 def swap_matrix():
     to = lax.broadcasted_iota(jnp.int32, (CHUNK * CHUNK, CHUNK * CHUNK), 0)
     at = lax.broadcasted_iota(jnp.int32, (CHUNK * CHUNK, CHUNK * CHUNK), 1)
@@ -39,7 +43,8 @@
     return [cols == column for column in column_order(row)[1:]]
 
 
-def bias_kernel(vals_hbm, greens_hbm, cols_ref, turned_ref, bias_ref, vals, greens, swap, gs, acc, vsem, gsem):
+def bias_kernel(vals_hbm, greens_hbm, walkers_hbm, cols_ref, turned_ref, bias_ref, mine_ref, vals, greens, swap, gs, acc, vsem,
+                gsem, wsem):
     total_steps, vectors = turned_ref.shape[:2]
     walk = bias_ref.shape[0]
     steps = BLOCK // CHUNK
@@ -56,7 +61,10 @@
             copy.start()
         return carry
 
+    own = mine_ref.shape[0]
     lax.fori_loop(0, total_steps, begin, 0)
+    take = pltpu.make_async_copy(walkers_hbm.at[pl.ds(lax.axis_index("chol") * own, own)], mine_ref, wsem)
+    take.start()
     swap[...] = swap_matrix()
     bias_ref[...] = jnp.zeros_like(bias_ref)
     first = lax.broadcasted_iota(jnp.int32, (CHUNK * CHUNK, LANES), 1) < BLOCK
@@ -112,9 +120,10 @@
 
     acc[...] = jnp.zeros_like(acc)
     lax.fori_loop(0, total_steps, step, 0)
-
-
-def bias_call(vals, greens, cols):
+    take.wait()
+
+
+def bias_call(vals, greens, walkers, cols, own):
     vectors, rowblocks = vals.shape[:2]
     walk, half_rows, norb = greens.shape
     steps = half_rows // CHUNK
@@ -122,14 +131,14 @@
     return pl.pallas_call(
         bias_kernel,
         in_specs=[
-            pl.BlockSpec(memory_space=pl.ANY),
-            pl.BlockSpec(memory_space=pl.ANY),
+            *[pl.BlockSpec(memory_space=pl.ANY)] * 3,
             pl.BlockSpec(memory_space=pltpu.VMEM),
         ],
-        out_specs=[pl.BlockSpec(memory_space=pltpu.VMEM)] * 2,
+        out_specs=[pl.BlockSpec(memory_space=pltpu.VMEM)] * 3,
         out_shape=[
             pltpu.VMEM((steps, vectors, wide), jnp.bfloat16),
             pltpu.VMEM((walk, vectors), jnp.float32),
+            pltpu.VMEM((own, *walkers.shape[1:]), jnp.bfloat16),
         ],
         scratch_shapes=[
             pltpu.VMEM((steps, vectors, CHUNK, LANES), jnp.bfloat16),
@@ -139,10 +148,11 @@
             pltpu.VMEM((vectors, 4 * walk), jnp.float32),
             pltpu.SemaphoreType.DMA((steps,)),
             pltpu.SemaphoreType.DMA((steps,)),
+            pltpu.SemaphoreType.DMA,
         ],
         compiler_params=params(24),
         name="force_bias",
-    )(vals, greens, cols)
+    )(*in_hbm(vals, greens, walkers), cols)
 
 
 def potential_kernel(start, steps, layout, by_plane, fields_ref, own_ref, *refs):
@@ -339,7 +349,6 @@
     own = walk // chips
     layout = (nz, plane, own)
     step_factor = 72.0 / float(vectors * chips * BLOCK) ** 0.5
-    me = lax.axis_index("chol")
 
     def to_plane(a, dp):
         return lax.ppermute(a, "chol", [(c, (c // plane) * plane + ((c % plane) ^ dp)) for c in range(chips)])
@@ -351,10 +360,8 @@
         return [a] + [lax.ppermute(a, "orb", [((c + d) % n_orb, c) for c in range(n_orb)]) for d in range(1, n_orb)]
 
     cols = jnp.transpose(chol_cols, (1, 2, 0))
-    mine = lax.dynamic_slice_in_dim(walkers, me * own, own, 0)
+    turned, partial_bias, mine = bias_call(chol_vals, greens, walkers, cols, own)
     start = around_orb(mine)
-
-    turned, partial_bias = bias_call(chol_vals, greens, cols)
     bias, *others = around_orb(partial_bias)
 
     total_steps = rowblocks * BLOCK // CHUNK

time: 102 us -> 107 us (1.049)
  waiting for transfers between devices: 26.5 us -> 42 us
  local copies, waits for them, and re-layouts: 12.5 us -> 0.8 us
  starting transfers between devices: 44.3 us -> 46.1 us
    ppermute x15, waiting for transfers between devices: 7.13 us -> 22.4 us  [to_plane(): lax.ppermute(a, 'chol', [(c, c // plane * plane + (c % plane ^ dp)) for c...]
    unnamed x16 -> x4, local copies, waits for them, and re-layouts: 12.4 us -> 0.69 us
    ppermute x15, starting transfers between devices: 18.7 us -> 20.5 us  [to_plane(): lax.ppermute(a, 'chol', [(c, c // plane * plane + (c % plane ^ dp)) for c...]
  transfers between devices with their start and end apart: 34 -> 34, of which waited for: 13 -> 16; matrix products, arithmetic and copies ran while one was open for 1% -> 1% of each run, Pallas kernels for 4% -> 4%
where the time goes in v3:
time: 107 us
  starting transfers between devices  46.1 us (43%)
  waiting for transfers between devices  42 us (39%)
  Pallas kernels  16.7 us (16%)
    ppermute x15, starting transfers between devices, to_z(): lax.ppermute(a, 'chol', [(c, (c // plane + dz) % nz * plane + c % plane)...  24.9 us
    ppermute x15, waiting for transfers between devices, to_plane(): lax.ppermute(a, 'chol', [(c, c // plane * plane + (c % plane ^ dp)) for c...  22.4 us
    ppermute x15, starting transfers between devices, to_plane(): lax.ppermute(a, 'chol', [(c, c // plane * plane + (c % plane ^ dp)) for c...  20.5 us
    ppermute x15, waiting for transfers between devices, to_z(): lax.ppermute(a, 'chol', [(c, (c // plane + dz) % nz * plane + c % plane)...  16.2 us
    pallas_call x1, Pallas kernels, bias_call(): pl.pallas_call(bias_kernel, in_specs=[*[pl.BlockSpec(memory_space=pl.ANY)...  8.49 us
    pallas_call x2, Pallas kernels, potential_call(): pl.pallas_call(functools.partial(potential_kernel, start, steps, layout,...  5.64 us
    ppermute x4, waiting for transfers between devices, around_orb(): lax.ppermute(a, 'orb', [((c + d) % n_orb, c) for c in range(n_orb)])  3.33 us
  transfers between devices with their start and end apart: 34, of which 16 were waited for; matrix products, arithmetic and copies ran while one was open for 1% of the time, Pallas kernels for 4%

profile of v3, /device:TPU:0, one launch (start us, length us, event | category | flops | bytes accessed | tf_op | source)
XLA Modules:
  0.0 107.0 jit_solution(16851246089141841121)
XLA Ops:
  0.7 0.7 copy-done.1
  1.3 8.5 %force_bias.1 = (bf16[8,256,2048]{2,1,0:T(8,128)(2,1)S(1)}, f32[32,256]{1,0:T(8,128)S(1)}, bf16[2,128,128]{2,1,0:T(8,128)(2,1)S(1)}) custom-call(bf16[256,2,64,128]{3,2,1,0:T(8,128)(2,1)} %vals_hbm.1, bf16[32,128,256]{2,1,0:T(8,128)(2,1)} %greens_hbm.1, bf16[32,128,128]{2,1,0:T(8,128)(2,1)} %walkers_hbm.1, s32[2,2,256]{2,1,0:T(2,128)S(1)} %bitcast.13), custom_call_target="tpu_custom_call" | custom-call | tf_op jit(solution)/shard_map/force_bias/pallas_call | solution.py:131
  9.8 0.5 collective-permute-start
  10.3 0.9 collective-permute-done.refs_0_
  11.2 1.9 %potential.2 = (bf16[4,2,96,128]{3,2,1,0:T(8,128)(2,1)S(1)}, bf16[4,2,96,128]{3,2,1,0:T(8,128)(2,1)S(1)}, bf16[4,2,96,128]{3,2,1,0:T(8,128)(2,1)S(1)}, bf16[4,2,96,128]{3,2,1,0:T(8,128)(2,1)S(1)}, f32[32,128]{1,0:T(8,128)S(1)}) custom-call(f32[32,256]{1,0:T(8,128)S(1)} %bitcast.10, f32[32,256]{1,0:T(8,128)S(1)} %get-tuple-element.40.own_ref, ...), custom_call_target="tpu_custom_call" | custom-call | tf_op jit(solution)/shard_map/potential/pallas_call | solution.py:224
  13.2 3.0 %collective-permute-start.5 = (bf16[4,2,96,128]{3,2,1,0:T(8,128)(2,1)S(1)}, bf16[4,2,96,128]{3,2,1,0:T(8,128)(2,1)S(1)}, u32[]{:S(2)}, u32[]{:S(2)}) collective-permute-start(bf16[4,2,96,128]{3,2,1,0:T(8,128)(2,1)S(1)} %get-tuple-element.45), channel_id=1, source_target_pairs={{0,8},{2,10},{4,12},{6,14},{8,16},{10,18},{12,20},{14,22},{16,24},... | collective-permute-start | bytes 589832 | tf_op jit(solution)/shard_map/ppermute | solution.py:357
  16.1 3.7 %potential.3 = (bf16[4,2,160,128]{3,2,1,0:T(8,128)(2,1)S(1)}, bf16[4,2,160,128]{3,2,1,0:T(8,128)(2,1)S(1)}, bf16[4,2,160,128]{3,2,1,0:T(8,128)(2,1)S(1)}, bf16[4,2,160,128]{3,2,1,0:T(8,128)(2,1)S(1)}, f32[32,128]{1,0:T(8,128)}) custom-call(f32[32,256]{1,0:T(8,128)S(1)} %bitcast.11, f32[32,256]{1,0:T(8,128)S(1)} %get-tuple-element.40.own_ref, ...), custom_call_target="tpu_custom_call" | custom-call | tf_op jit(solution)/shard_map/potential/pallas_call | solution.py:224
  19.8 1.5 %collective-permute-start.11 = (bf16[4,2,160,128]{3,2,1,0:T(8,128)(2,1)S(1)}, bf16[4,2,160,128]{3,2,1,0:T(8,128)(2,1)S(1)}, u32[]{:S(2)}, u32[]{:S(2)}) collective-permute-start(bf16[4,2,160,128]{3,2,1,0:T(8,128)(2,1)S(1)} %get-tuple-element.52), channel_id=1, source_target_pairs={{0,2},{2,0},{4,6},{6,4},{8,10},{10,8},{12,14},{14,12},{16,18},{18,... | collective-permute-start | bytes 983048 | tf_op jit(solution)/shard_map/ppermute | solution.py:354
  21.3 1.5 %collective-permute-start.12 = (bf16[4,2,160,128]{3,2,1,0:T(8,128)(2,1)S(1)}, bf16[4,2,160,128]{3,2,1,0:T(8,128)(2,1)S(1)}, u32[]{:S(2)}, u32[]{:S(2)}) collective-permute-start(bf16[4,2,160,128]{3,2,1,0:T(8,128)(2,1)S(1)} %get-tuple-element.53), channel_id=1, source_target_pairs={{0,4},{2,6},{4,0},{6,2},{8,12},{10,14},{12,8},{14,10},{16,20},{18,... | collective-permute-start | bytes 983048 | tf_op jit(solution)/shard_map/ppermute | solution.py:354
  22.9 0.5 collective-permute-start.13
  23.3 0.1 slice_reduce_fusion
  23.4 1.6 %collective-permute-start.2 = (f32[32]{0:T(128)S(1)}, f32[32]{0:T(128)S(1)}, u32[]{:S(2)}, u32[]{:S(2)}) collective-permute-start(f32[32]{0:T(128)S(1)} %slice_reduce_fusion), channel_id=1, source_target_pairs={{0,2},{2,0},{4,6},{6,4},{8,10},{10,8},{12,14},{14,12},{16,18},{18,... | collective-permute-start | bytes 392 | tf_op jit(solution)/shard_map/ppermute | solution.py:354
  25.0 11.4 %collective-permute-done.2 = f32[32]{0:T(128)S(1)} collective-permute-done((f32[32]{0:T(128)S(1)}, f32[32]{0:T(128)S(1)}, u32[]{:S(2)}, u32[]{:S(2)}) %collective-permute-start.2) | collective-permute-done | bytes 160 | tf_op jit(solution)/shard_map/ppermute | solution.py:354
  36.4 1.5 %collective-permute-start.3 = (f32[32]{0:T(128)S(1)}, f32[32]{0:T(128)S(1)}, u32[]{:S(2)}, u32[]{:S(2)}) collective-permute-start(f32[32]{0:T(128)S(1)} %slice_reduce_fusion), channel_id=1, source_target_pairs={{0,4},{2,6},{4,0},{6,2},{8,12},{10,14},{12,8},{14,10},{16,20},{18,... | collective-permute-start | bytes 392 | tf_op jit(solution)/shard_map/ppermute | solution.py:354
  37.9 2.0 %collective-permute-done.3 = f32[32]{0:T(128)S(1)} collective-permute-done((f32[32]{0:T(128)S(1)}, f32[32]{0:T(128)S(1)}, u32[]{:S(2)}, u32[]{:S(2)}) %collective-permute-start.3) | collective-permute-done | bytes 160 | tf_op jit(solution)/shard_map/ppermute | solution.py:354
  39.9 2.4 %collective-permute-start.4 = (f32[32]{0:T(128)S(1)}, f32[32]{0:T(128)S(1)}, u32[]{:S(2)}, u32[]{:S(2)}) collective-permute-start(f32[32]{0:T(128)S(1)} %slice_reduce_fusion), channel_id=1, source_target_pairs={{0,6},{2,4},{4,2},{6,0},{8,14},{10,12},{12,10},{14,8},{16,22},{18,... | collective-permute-start | bytes 392 | tf_op jit(solution)/shard_map/ppermute | solution.py:354
  42.3 2.0 %collective-permute-done.4 = f32[32]{0:T(128)S(1)} collective-permute-done((f32[32]{0:T(128)S(1)}, f32[32]{0:T(128)S(1)}, u32[]{:S(2)}, u32[]{:S(2)}) %collective-permute-start.4) | collective-permute-done | bytes 160 | tf_op jit(solution)/shard_map/ppermute | solution.py:354
  44.4 0.0 collective-permute-start.1
  44.4 1.3 %collective-permute-done.1.refs_5_ = bf16[2,128,128]{2,1,0:T(8,128)(2,1)S(1)} collective-permute-done((bf16[2,128,128]{2,1,0:T(8,128)(2,1)S(1)}, bf16[2,128,128]{2,1,0:T(8,128)(2,1)S(1)}, u32[]{:S(2)}, u32[]{:S(2)}) %collective-permute-start.1) | collective-permute-done | bytes 65568 | tf_op jit(solution)/shard_map/ppermute | solution.py:360
  45.6 2.6 %collective-permute-start.6 = (bf16[4,2,96,128]{3,2,1,0:T(8,128)(2,1)S(1)}, bf16[4,2,96,128]{3,2,1,0:T(8,128)(2,1)S(1)}, u32[]{:S(2)}, u32[]{:S(2)}) collective-permute-start(bf16[4,2,96,128]{3,2,1,0:T(8,128)(2,1)S(1)} %get-tuple-element.46), channel_id=1, source_target_pairs={{0,16},{2,18},{4,20},{6,22},{8,24},{10,26},{12,28},{14,30},{16,0},... | collective-permute-start | bytes 589832 | tf_op jit(solution)/shard_map/ppermute | solution.py:357
  48.2 1.3 %collective-permute-start.7 = (bf16[4,2,96,128]{3,2,1,0:T(8,128)(2,1)S(1)}, bf16[4,2,96,128]{3,2,1,0:T(8,128)(2,1)S(1)}, u32[]{:S(2)}, u32[]{:S(2)}) collective-permute-start(bf16[4,2,96,128]{3,2,1,0:T(8,128)(2,1)S(1)} %get-tuple-element.47), channel_id=1, source_target_pairs={{0,24},{2,26},{4,28},{6,30},{8,0},{10,2},{12,4},{14,6},{16,8},{18,... | collective-permute-start | bytes 589832 | tf_op jit(solution)/shard_map/ppermute | solution.py:357
  49.6 9.0 %collective-permute-done.6.refs_2_ = bf16[4,2,96,128]{3,2,1,0:T(8,128)(2,1)S(1)} collective-permute-done((bf16[4,2,96,128]{3,2,1,0:T(8,128)(2,1)S(1)}, bf16[4,2,96,128]{3,2,1,0:T(8,128)(2,1)S(1)}, u32[]{:S(2)}, u32[]{:S(2)}) %collective-permute-start.6) | collective-permute-done | bytes 196640 | tf_op jit(solution)/shard_map/ppermute | solution.py:357
  58.5 0.0 collective-permute-done.7.refs_3_
  58.5 0.0 collective-permute-done.11.refs_1_
  58.5 0.2 sum_parts.2
  58.7 4.0 %collective-permute-start.14 = (bf16[2,160,128]{2,1,0:T(8,128)(2,1)S(1)}, bf16[2,160,128]{2,1,0:T(8,128)(2,1)S(1)}, u32[]{:S(2)}, u32[]{:S(2)}) collective-permute-start(bf16[2,160,128]{2,1,0:T(8,128)(2,1)S(1)} %get-tuple-element.56), channel_id=1, source_target_pairs={{0,8},{2,10},{4,12},{6,14},{8,16},{10,18},{12,20},{14,22},{16,24},... | collective-permute-start | bytes 245768 | tf_op jit(solution)/shard_map/ppermute | solution.py:357
  62.8 2.3 %collective-permute-start.15 = (bf16[2,160,128]{2,1,0:T(8,128)(2,1)S(1)}, bf16[2,160,128]{2,1,0:T(8,128)(2,1)S(1)}, u32[]{:S(2)}, u32[]{:S(2)}) collective-permute-start(bf16[2,160,128]{2,1,0:T(8,128)(2,1)S(1)} %get-tuple-element.57), channel_id=1, source_target_pairs={{0,16},{2,18},{4,20},{6,22},{8,24},{10,26},{12,28},{14,30},{16,0},... | collective-permute-start | bytes 245768 | tf_op jit(solution)/shard_map/ppermute | solution.py:357
  65.0 0.1 collective-permute-start.16
  65.2 1.9 %collective-permute-start.10 = (f32[32]{0:T(128)S(1)}, f32[32]{0:T(128)S(1)}, u32[]{:S(2)}, u32[]{:S(2)}) collective-permute-start(f32[32]{0:T(128)S(1)} %add_add_fusion.1), channel_id=1, source_target_pairs={{0,24},{2,26},{4,28},{6,30},{8,0},{10,2},{12,4},{14,6},{16,8},{18,... | collective-permute-start | bytes 392 | tf_op jit(solution)/shard_map/ppermute | solution.py:357
  67.1 0.1 collective-permute-start.8
  67.2 0.1 sum_parts.3
  67.3 3.3 %collective-permute-done.10 = f32[32]{0:T(128)S(1)} collective-permute-done((f32[32]{0:T(128)S(1)}, f32[32]{0:T(128)S(1)}, u32[]{:S(2)}, u32[]{:S(2)}) %collective-permute-start.10) | collective-permute-done | bytes 160 | tf_op jit(solution)/shard_map/ppermute | solution.py:357
  70.6 0.7 collective-permute-start.9
  71.3 1.2 %collective-permute-done.8 = f32[32]{0:T(128)S(1)} collective-permute-done((f32[32]{0:T(128)S(1)}, f32[32]{0:T(128)S(1)}, u32[]{:S(2)}, u32[]{:S(2)}) %collective-permute-start.8) | collective-permute-done | bytes 160 | tf_op jit(solution)/shard_map/ppermute | solution.py:357
  72.5 1.5 %collective-permute-start.18 = (bf16[2,96,128]{2,1,0:T(8,128)(2,1)S(1)}, bf16[2,96,128]{2,1,0:T(8,128)(2,1)S(1)}, u32[]{:S(2)}, u32[]{:S(2)}) collective-permute-start(bf16[2,96,128]{2,1,0:T(8,128)(2,1)S(1)} %get-tuple-element.68), channel_id=1, source_target_pairs={{0,2},{2,0},{4,6},{6,4},{8,10},{10,8},{12,14},{14,12},{16,18},{18,... | collective-permute-start | bytes 147464 | tf_op jit(solution)/shard_map/ppermute | solution.py:354
  74.0 1.1 %collective-permute-done.9 = f32[32]{0:T(128)S(1)} collective-permute-done((f32[32]{0:T(128)S(1)}, f32[32]{0:T(128)S(1)}, u32[]{:S(2)}, u32[]{:S(2)}) %collective-permute-start.9) | collective-permute-done | bytes 160 | tf_op jit(solution)/shard_map/ppermute | solution.py:357
  75.1 1.5 %collective-permute-start.19 = (bf16[2,96,128]{2,1,0:T(8,128)(2,1)S(1)}, bf16[2,96,128]{2,1,0:T(8,128)(2,1)S(1)}, u32[]{:S(2)}, u32[]{:S(2)}) collective-permute-start(bf16[2,96,128]{2,1,0:T(8,128)(2,1)S(1)} %get-tuple-element.69), channel_id=1, source_target_pairs={{0,4},{2,6},{4,0},{6,2},{8,12},{10,14},{12,8},{14,10},{16,20},{18,... | collective-permute-start | bytes 147464 | tf_op jit(solution)/shard_map/ppermute | solution.py:354
  76.6 0.0 collective-permute-done.14
  76.6 1.4 %collective-permute-start.20 = (bf16[2,96,128]{2,1,0:T(8,128)(2,1)S(1)}, bf16[2,96,128]{2,1,0:T(8,128)(2,1)S(1)}, u32[]{:S(2)}, u32[]{:S(2)}) collective-permute-start(bf16[2,96,128]{2,1,0:T(8,128)(2,1)S(1)} %get-tuple-element.70), channel_id=1, source_target_pairs={{0,6},{2,4},{4,2},{6,0},{8,14},{10,12},{12,10},{14,8},{16,22},{18,... | collective-permute-start | bytes 147464 | tf_op jit(solution)/shard_map/ppermute | solution.py:354
  78.0 0.1 multiply_convert_fusion.refs_0_
  78.1 0.1 collective-permute-start.17
  78.2 1.0 collective-permute-done.19
  79.2 2.4 %collective-permute-done.20 = bf16[2,96,128]{2,1,0:T(8,128)(2,1)S(1)} collective-permute-done((bf16[2,96,128]{2,1,0:T(8,128)(2,1)S(1)}, bf16[2,96,128]{2,1,0:T(8,128)(2,1)S(1)}, u32[]{:S(2)}, u32[]{:S(2)}) %collective-permute-start.20) | collective-permute-done | bytes 49184 | tf_op jit(solution)/shard_map/ppermute | solution.py:354
  81.6 0.1 collective-permute-start.21
  81.7 1.2 %collective-permute-done.21.refs_3_ = bf16[2,96,128]{2,1,0:T(8,128)(2,1)S(1)} collective-permute-done((bf16[2,96,128]{2,1,0:T(8,128)(2,1)S(1)}, bf16[2,96,128]{2,1,0:T(8,128)(2,1)S(1)}, u32[]{:S(2)}, u32[]{:S(2)}) %collective-permute-start.21) | collective-permute-done | bytes 49184 | tf_op jit(solution)/shard_map/ppermute | solution.py:360
  82.9 1.3 %series.1 = (bf16[2,48,128]{2,1,0:T(8,128)(2,1)S(1)}, bf16[2,80,128]{2,1,0:T(8,128)(2,1)S(1)}) custom-call(bf16[2,160,128]{2,1,0:T(8,128)(2,1)S(1)} %multiply_convert_fusion.refs_0_, bf16[2,160,128]{2,1,0:T(8,128)(2,1)S(1)} %collective-permute-done.17.refs_1_, bf16[2,96,128]{2,1,0:T(8,128)(2,1)S(1)} %multiply_convert_fusion.1.refs_2_, ...), custom_call_target="tpu_custom_call" | custom-call | tf_op jit(solution)/shard_map/series/pallas_call | solution.py:301
  84.2 1.5 %collective-permute-start.28 = (bf16[2,48,128]{2,1,0:T(8,128)(2,1)S(1)}, bf16[2,48,128]{2,1,0:T(8,128)(2,1)S(1)}, u32[]{:S(2)}, u32[]{:S(2)}) collective-permute-start(bf16[2,48,128]{2,1,0:T(8,128)(2,1)S(1)} %get-tuple-element.74), channel_id=1, source_target_pairs={{0,2},{2,0},{4,6},{6,4},{8,10},{10,8},{12,14},{14,12},{16,18},{18,... | collective-permute-start | bytes 73736 | tf_op jit(solution)/shard_map/ppermute | solution.py:354
  85.7 0.5 collective-permute-start.29
  86.3 1.5 %collective-permute-start.30 = (bf16[2,48,128]{2,1,0:T(8,128)(2,1)S(1)}, bf16[2,48,128]{2,1,0:T(8,128)(2,1)S(1)}, u32[]{:S(2)}, u32[]{:S(2)}) collective-permute-start(bf16[2,48,128]{2,1,0:T(8,128)(2,1)S(1)} %get-tuple-element.74), channel_id=1, source_target_pairs={{0,6},{2,4},{4,2},{6,0},{8,14},{10,12},{12,10},{14,8},{16,22},{18,... | collective-permute-start | bytes 73736 | tf_op jit(solution)/shard_map/ppermute | solution.py:354
  87.8 1.7 %collective-permute-start.22 = (bf16[2,80,128]{2,1,0:T(8,128)(2,1)S(1)}, bf16[2,80,128]{2,1,0:T(8,128)(2,1)S(1)}, u32[]{:S(2)}, u32[]{:S(2)}) collective-permute-start(bf16[2,80,128]{2,1,0:T(8,128)(2,1)S(1)} %get-tuple-element.73), channel_id=1, source_target_pairs={{0,8},{2,10},{4,12},{6,14},{8,16},{10,18},{12,20},{14,22},{16,24},... | collective-permute-start | bytes 122888 | tf_op jit(solution)/shard_map/ppermute | solution.py:357
  89.5 0.9 collective-permute-start.23
  90.4 1.5 %collective-permute-start.24 = (bf16[2,80,128]{2,1,0:T(8,128)(2,1)S(1)}, bf16[2,80,128]{2,1,0:T(8,128)(2,1)S(1)}, u32[]{:S(2)}, u32[]{:S(2)}) collective-permute-start(bf16[2,80,128]{2,1,0:T(8,128)(2,1)S(1)} %get-tuple-element.73), channel_id=1, source_target_pairs={{0,24},{2,26},{4,28},{6,30},{8,0},{10,2},{12,4},{14,6},{16,8},{18,... | collective-permute-start | bytes 122888 | tf_op jit(solution)/shard_map/ppermute | solution.py:357
  91.9 0.9 collective-permute-start.31
  92.8 1.7 %collective-permute-start.32 = (bf16[4,2,48,128]{3,2,1,0:T(8,128)(2,1)S(1)}, bf16[4,2,48,128]{3,2,1,0:T(8,128)(2,1)S(1)}, u32[]{:S(2)}, u32[]{:S(2)}) collective-permute-start(bf16[4,2,48,128]{3,2,1,0:T(8,128)(2,1)S(1)} %pad_maximum_fusion.1.refs_4_), channel_id=1, source_target_pairs={{0,16},{2,18},{4,20},{6,22},{8,24},{10,26},{12,28},{14,30},{16,0},... | collective-permute-start | bytes 294920 | tf_op jit(solution)/shard_map/ppermute | solution.py:357
  94.5 2.1 %collective-permute-start.33 = (bf16[4,2,48,128]{3,2,1,0:T(8,128)(2,1)S(1)}, bf16[4,2,48,128]{3,2,1,0:T(8,128)(2,1)S(1)}, u32[]{:S(2)}, u32[]{:S(2)}) collective-permute-start(bf16[4,2,48,128]{3,2,1,0:T(8,128)(2,1)S(1)} %pad_maximum_fusion.1.refs_4_), channel_id=1, source_target_pairs={{0,24},{2,26},{4,28},{6,30},{8,0},{10,2},{12,4},{14,6},{16,8},{18,... | collective-permute-start | bytes 294920 | tf_op jit(solution)/shard_map/ppermute | solution.py:357
  96.7 1.5 %collective-permute-start.25 = (bf16[4,2,80,128]{3,2,1,0:T(8,128)(2,1)S(1)}, bf16[4,2,80,128]{3,2,1,0:T(8,128)(2,1)S(1)}, u32[]{:S(2)}, u32[]{:S(2)}) collective-permute-start(bf16[4,2,80,128]{3,2,1,0:T(8,128)(2,1)S(1)} %pad_maximum_fusion.refs_0_), channel_id=1, source_target_pairs={{0,2},{2,0},{4,6},{6,4},{8,10},{10,8},{12,14},{14,12},{16,18},{18,... | collective-permute-start | bytes 491528 | tf_op jit(solution)/shard_map/ppermute | solution.py:354
  98.2 0.5 collective-permute-start.26
  98.7 0.8 collective-permute-done.31.refs_5_
  99.5 1.4 %collective-permute-start.27 = (bf16[4,2,80,128]{3,2,1,0:T(8,128)(2,1)S(1)}, bf16[4,2,80,128]{3,2,1,0:T(8,128)(2,1)S(1)}, u32[]{:S(2)}, u32[]{:S(2)}) collective-permute-start(bf16[4,2,80,128]{3,2,1,0:T(8,128)(2,1)S(1)} %pad_maximum_fusion.refs_0_), channel_id=1, source_target_pairs={{0,6},{2,4},{4,2},{6,0},{8,14},{10,12},{12,10},{14,8},{16,22},{18,... | collective-permute-start | bytes 491528 | tf_op jit(solution)/shard_map/ppermute | solution.py:354
  100.9 0.5 add_add_fusion
  101.5 0.9 collective-permute-done.32.refs_6_
  102.4 0.5 collective-permute-done.25.refs_1_
  102.8 3.1 %collective-permute-done.26.refs_2_ = bf16[4,2,80,128]{3,2,1,0:T(8,128)(2,1)S(1)} collective-permute-done((bf16[4,2,80,128]{3,2,1,0:T(8,128)(2,1)S(1)}, bf16[4,2,80,128]{3,2,1,0:T(8,128)(2,1)S(1)}, u32[]{:S(2)}, u32[]{:S(2)}) %collective-permute-start.26) | collective-permute-done | bytes 163872 | tf_op jit(solution)/shard_map/ppermute | solution.py:354
  105.9 1.1 place_walkers.1
  (22 shorter events, 0.1 us)
Async XLA Ops:
  0.6 10.6 %copy-start = (f32[256,32]{0,1:T(8,128)S(1)}, f32[256,32]{0,1:T(8,128)}, u32[]{:S(2)}) copy-start(f32[256,32]{0,1:T(8,128)} %param.9) | copy-start | bytes 98308
  0.6 0.7 copy-start.1
  9.8 1.4 %collective-permute-start = (f32[32,256]{1,0:T(8,128)S(1)}, f32[32,256]{1,0:T(8,128)S(1)}, u32[]{:S(2)}, u32[]{:S(2)}) collective-permute-start(f32[32,256]{1,0:T(8,128)S(1)} %get-tuple-element.40.own_ref), channel_id=1, source_target_pairs={{1,0},{0,1},{3,2},{2,3},{5,4},{4,5},{7,6},{6,7},{9,8},{8,9},{11,10... | collective-permute-start | bytes 98312 | tf_op jit(solution)/shard_map/ppermute | solution.py:360
  13.2 35.0 %collective-permute-start.5 = (bf16[4,2,96,128]{3,2,1,0:T(8,128)(2,1)S(1)}, bf16[4,2,96,128]{3,2,1,0:T(8,128)(2,1)S(1)}, u32[]{:S(2)}, u32[]{:S(2)}) collective-permute-start(bf16[4,2,96,128]{3,2,1,0:T(8,128)(2,1)S(1)} %get-tuple-element.45), channel_id=1, source_target_pairs={{0,8},{2,10},{4,12},{6,14},{8,16},{10,18},{12,20},{14,22},{16,24},... | collective-permute-start | bytes 589832 | tf_op jit(solution)/shard_map/ppermute | solution.py:357
  19.8 38.7 %collective-permute-start.11 = (bf16[4,2,160,128]{3,2,1,0:T(8,128)(2,1)S(1)}, bf16[4,2,160,128]{3,2,1,0:T(8,128)(2,1)S(1)}, u32[]{:S(2)}, u32[]{:S(2)}) collective-permute-start(bf16[4,2,160,128]{3,2,1,0:T(8,128)(2,1)S(1)} %get-tuple-element.52), channel_id=1, source_target_pairs={{0,2},{2,0},{4,6},{6,4},{8,10},{10,8},{12,14},{14,12},{16,18},{18,... | collective-permute-start | bytes 983048 | tf_op jit(solution)/shard_map/ppermute | solution.py:354
  21.3 37.2 %collective-permute-start.12 = (bf16[4,2,160,128]{3,2,1,0:T(8,128)(2,1)S(1)}, bf16[4,2,160,128]{3,2,1,0:T(8,128)(2,1)S(1)}, u32[]{:S(2)}, u32[]{:S(2)}) collective-permute-start(bf16[4,2,160,128]{3,2,1,0:T(8,128)(2,1)S(1)} %get-tuple-element.53), channel_id=1, source_target_pairs={{0,4},{2,6},{4,0},{6,2},{8,12},{10,14},{12,8},{14,10},{16,20},{18,... | collective-permute-start | bytes 983048 | tf_op jit(solution)/shard_map/ppermute | solution.py:354
  22.9 35.7 %collective-permute-start.13 = (bf16[4,2,160,128]{3,2,1,0:T(8,128)(2,1)S(1)}, bf16[4,2,160,128]{3,2,1,0:T(8,128)(2,1)S(1)}, u32[]{:S(2)}, u32[]{:S(2)}) collective-permute-start(bf16[4,2,160,128]{3,2,1,0:T(8,128)(2,1)S(1)} %get-tuple-element.54), channel_id=1, source_target_pairs={{0,6},{2,4},{4,2},{6,0},{8,14},{10,12},{12,10},{14,8},{16,22},{18,... | collective-permute-start | bytes 983048 | tf_op jit(solution)/shard_map/ppermute | solution.py:354
  23.4 12.9 %collective-permute-start.2 = (f32[32]{0:T(128)S(1)}, f32[32]{0:T(128)S(1)}, u32[]{:S(2)}, u32[]{:S(2)}) collective-permute-start(f32[32]{0:T(128)S(1)} %slice_reduce_fusion), channel_id=1, source_target_pairs={{0,2},{2,0},{4,6},{6,4},{8,10},{10,8},{12,14},{14,12},{16,18},{18,... | collective-permute-start | bytes 392 | tf_op jit(solution)/shard_map/ppermute | solution.py:354
  36.4 3.5 %collective-permute-start.3 = (f32[32]{0:T(128)S(1)}, f32[32]{0:T(128)S(1)}, u32[]{:S(2)}, u32[]{:S(2)}) collective-permute-start(f32[32]{0:T(128)S(1)} %slice_reduce_fusion), channel_id=1, source_target_pairs={{0,4},{2,6},{4,0},{6,2},{8,12},{10,14},{12,8},{14,10},{16,20},{18,... | collective-permute-start | bytes 392 | tf_op jit(solution)/shard_map/ppermute | solution.py:354
  39.9 4.4 %collective-permute-start.4 = (f32[32]{0:T(128)S(1)}, f32[32]{0:T(128)S(1)}, u32[]{:S(2)}, u32[]{:S(2)}) collective-permute-start(f32[32]{0:T(128)S(1)} %slice_reduce_fusion), channel_id=1, source_target_pairs={{0,6},{2,4},{4,2},{6,0},{8,14},{10,12},{12,10},{14,8},{16,22},{18,... | collective-permute-start | bytes 392 | tf_op jit(solution)/shard_map/ppermute | solution.py:354
  44.4 1.3 %collective-permute-start.1 = (bf16[2,128,128]{2,1,0:T(8,128)(2,1)S(1)}, bf16[2,128,128]{2,1,0:T(8,128)(2,1)S(1)}, u32[]{:S(2)}, u32[]{:S(2)}) collective-permute-start(bf16[2,128,128]{2,1,0:T(8,128)(2,1)S(1)} %get-tuple-element.71.refs_4_), channel_id=1, source_target_pairs={{1,0},{0,1},{3,2},{2,3},{5,4},{4,5},{7,6},{6,7},{9,8},{8,9},{11,10... | collective-permute-start | bytes 196616 | tf_op jit(solution)/shard_map/ppermute | solution.py:360
  45.6 12.9 %collective-permute-start.6 = (bf16[4,2,96,128]{3,2,1,0:T(8,128)(2,1)S(1)}, bf16[4,2,96,128]{3,2,1,0:T(8,128)(2,1)S(1)}, u32[]{:S(2)}, u32[]{:S(2)}) collective-permute-start(bf16[4,2,96,128]{3,2,1,0:T(8,128)(2,1)S(1)} %get-tuple-element.46), channel_id=1, source_target_pairs={{0,16},{2,18},{4,20},{6,22},{8,24},{10,26},{12,28},{14,30},{16,0},... | collective-permute-start | bytes 589832 | tf_op jit(solution)/shard_map/ppermute | solution.py:357
  48.2 10.3 %collective-permute-start.7 = (bf16[4,2,96,128]{3,2,1,0:T(8,128)(2,1)S(1)}, bf16[4,2,96,128]{3,2,1,0:T(8,128)(2,1)S(1)}, u32[]{:S(2)}, u32[]{:S(2)}) collective-permute-start(bf16[4,2,96,128]{3,2,1,0:T(8,128)(2,1)S(1)} %get-tuple-element.47), channel_id=1, source_target_pairs={{0,24},{2,26},{4,28},{6,30},{8,0},{10,2},{12,4},{14,6},{16,8},{18,... | collective-permute-start | bytes 589832 | tf_op jit(solution)/shard_map/ppermute | solution.py:357
  58.7 17.9 %collective-permute-start.14 = (bf16[2,160,128]{2,1,0:T(8,128)(2,1)S(1)}, bf16[2,160,128]{2,1,0:T(8,128)(2,1)S(1)}, u32[]{:S(2)}, u32[]{:S(2)}) collective-permute-start(bf16[2,160,128]{2,1,0:T(8,128)(2,1)S(1)} %get-tuple-element.56), channel_id=1, source_target_pairs={{0,8},{2,10},{4,12},{6,14},{8,16},{10,18},{12,20},{14,22},{16,24},... | collective-permute-start | bytes 245768 | tf_op jit(solution)/shard_map/ppermute | solution.py:357
  62.8 15.3 %collective-permute-start.15 = (bf16[2,160,128]{2,1,0:T(8,128)(2,1)S(1)}, bf16[2,160,128]{2,1,0:T(8,128)(2,1)S(1)}, u32[]{:S(2)}, u32[]{:S(2)}) collective-permute-start(bf16[2,160,128]{2,1,0:T(8,128)(2,1)S(1)} %get-tuple-element.57), channel_id=1, source_target_pairs={{0,16},{2,18},{4,20},{6,22},{8,24},{10,26},{12,28},{14,30},{16,0},... | collective-permute-start | bytes 245768 | tf_op jit(solution)/shard_map/ppermute | solution.py:357
  65.0 13.0 %collective-permute-start.16 = (bf16[2,160,128]{2,1,0:T(8,128)(2,1)S(1)}, bf16[2,160,128]{2,1,0:T(8,128)(2,1)S(1)}, u32[]{:S(2)}, u32[]{:S(2)}) collective-permute-start(bf16[2,160,128]{2,1,0:T(8,128)(2,1)S(1)} %get-tuple-element.58), channel_id=1, source_target_pairs={{0,24},{2,26},{4,28},{6,30},{8,0},{10,2},{12,4},{14,6},{16,8},{18,... | collective-permute-start | bytes 245768 | tf_op jit(solution)/shard_map/ppermute | solution.py:357
  65.2 5.5 %collective-permute-start.10 = (f32[32]{0:T(128)S(1)}, f32[32]{0:T(128)S(1)}, u32[]{:S(2)}, u32[]{:S(2)}) collective-permute-start(f32[32]{0:T(128)S(1)} %add_add_fusion.1), channel_id=1, source_target_pairs={{0,24},{2,26},{4,28},{6,30},{8,0},{10,2},{12,4},{14,6},{16,8},{18,... | collective-permute-start | bytes 392 | tf_op jit(solution)/shard_map/ppermute | solution.py:357
  67.1 5.3 %collective-permute-start.8 = (f32[32]{0:T(128)S(1)}, f32[32]{0:T(128)S(1)}, u32[]{:S(2)}, u32[]{:S(2)}) collective-permute-start(f32[32]{0:T(128)S(1)} %add_add_fusion.1), channel_id=1, source_target_pairs={{0,8},{2,10},{4,12},{6,14},{8,16},{10,18},{12,20},{14,22},{16,24},... | collective-permute-start | bytes 392 | tf_op jit(solution)/shard_map/ppermute | solution.py:357
  70.6 4.4 %collective-permute-start.9 = (f32[32]{0:T(128)S(1)}, f32[32]{0:T(128)S(1)}, u32[]{:S(2)}, u32[]{:S(2)}) collective-permute-start(f32[32]{0:T(128)S(1)} %add_add_fusion.1), channel_id=1, source_target_pairs={{0,16},{2,18},{4,20},{6,22},{8,24},{10,26},{12,28},{14,30},{16,0},... | collective-permute-start | bytes 392 | tf_op jit(solution)/shard_map/ppermute | solution.py:357
  72.5 5.7 %collective-permute-start.18 = (bf16[2,96,128]{2,1,0:T(8,128)(2,1)S(1)}, bf16[2,96,128]{2,1,0:T(8,128)(2,1)S(1)}, u32[]{:S(2)}, u32[]{:S(2)}) collective-permute-start(bf16[2,96,128]{2,1,0:T(8,128)(2,1)S(1)} %get-tuple-element.68), channel_id=1, source_target_pairs={{0,2},{2,0},{4,6},{6,4},{8,10},{10,8},{12,14},{14,12},{16,18},{18,... | collective-permute-start | bytes 147464 | tf_op jit(solution)/shard_map/ppermute | solution.py:354
  75.1 4.1 %collective-permute-start.19 = (bf16[2,96,128]{2,1,0:T(8,128)(2,1)S(1)}, bf16[2,96,128]{2,1,0:T(8,128)(2,1)S(1)}, u32[]{:S(2)}, u32[]{:S(2)}) collective-permute-start(bf16[2,96,128]{2,1,0:T(8,128)(2,1)S(1)} %get-tuple-element.69), channel_id=1, source_target_pairs={{0,4},{2,6},{4,0},{6,2},{8,12},{10,14},{12,8},{14,10},{16,20},{18,... | collective-permute-start | bytes 147464 | tf_op jit(solution)/shard_map/ppermute | solution.py:354
  76.6 5.0 %collective-permute-start.20 = (bf16[2,96,128]{2,1,0:T(8,128)(2,1)S(1)}, bf16[2,96,128]{2,1,0:T(8,128)(2,1)S(1)}, u32[]{:S(2)}, u32[]{:S(2)}) collective-permute-start(bf16[2,96,128]{2,1,0:T(8,128)(2,1)S(1)} %get-tuple-element.70), channel_id=1, source_target_pairs={{0,6},{2,4},{4,2},{6,0},{8,14},{10,12},{12,10},{14,8},{16,22},{18,... | collective-permute-start | bytes 147464 | tf_op jit(solution)/shard_map/ppermute | solution.py:354
  78.1 4.8 %collective-permute-start.17 = (bf16[2,160,128]{2,1,0:T(8,128)(2,1)S(1)}, bf16[2,160,128]{2,1,0:T(8,128)(2,1)S(1)}, u32[]{:S(2)}, u32[]{:S(2)}) collective-permute-start(bf16[2,160,128]{2,1,0:T(8,128)(2,1)S(1)} %multiply_convert_fusion.refs_0_), channel_id=1, source_target_pairs={{1,0},{0,1},{3,2},{2,3},{5,4},{4,5},{7,6},{6,7},{9,8},{8,9},{11,10... | collective-permute-start | bytes 245768 | tf_op jit(solution)/shard_map/ppermute | solution.py:360
  81.6 1.3 %collective-permute-start.21 = (bf16[2,96,128]{2,1,0:T(8,128)(2,1)S(1)}, bf16[2,96,128]{2,1,0:T(8,128)(2,1)S(1)}, u32[]{:S(2)}, u32[]{:S(2)}) collective-permute-start(bf16[2,96,128]{2,1,0:T(8,128)(2,1)S(1)} %multiply_convert_fusion.1.refs_2_), channel_id=1, source_target_pairs={{1,0},{0,1},{3,2},{2,3},{5,4},{4,5},{7,6},{6,7},{9,8},{8,9},{11,10... | collective-permute-start | bytes 147464 | tf_op jit(solution)/shard_map/ppermute | solution.py:360
  84.2 6.2 %collective-permute-start.28 = (bf16[2,48,128]{2,1,0:T(8,128)(2,1)S(1)}, bf16[2,48,128]{2,1,0:T(8,128)(2,1)S(1)}, u32[]{:S(2)}, u32[]{:S(2)}) collective-permute-start(bf16[2,48,128]{2,1,0:T(8,128)(2,1)S(1)} %get-tuple-element.74), channel_id=1, source_target_pairs={{0,2},{2,0},{4,6},{6,4},{8,10},{10,8},{12,14},{14,12},{16,18},{18,... | collective-permute-start | bytes 73736 | tf_op jit(solution)/shard_map/ppermute | solution.py:354
  85.7 6.1 %collective-permute-start.29 = (bf16[2,48,128]{2,1,0:T(8,128)(2,1)S(1)}, bf16[2,48,128]{2,1,0:T(8,128)(2,1)S(1)}, u32[]{:S(2)}, u32[]{:S(2)}) collective-permute-start(bf16[2,48,128]{2,1,0:T(8,128)(2,1)S(1)} %get-tuple-element.74), channel_id=1, source_target_pairs={{0,4},{2,6},{4,0},{6,2},{8,12},{10,14},{12,8},{14,10},{16,20},{18,... | collective-permute-start | bytes 73736 | tf_op jit(solution)/shard_map/ppermute | solution.py:354
  86.3 5.6 %collective-permute-start.30 = (bf16[2,48,128]{2,1,0:T(8,128)(2,1)S(1)}, bf16[2,48,128]{2,1,0:T(8,128)(2,1)S(1)}, u32[]{:S(2)}, u32[]{:S(2)}) collective-permute-start(bf16[2,48,128]{2,1,0:T(8,128)(2,1)S(1)} %get-tuple-element.74), channel_id=1, source_target_pairs={{0,6},{2,4},{4,2},{6,0},{8,14},{10,12},{12,10},{14,8},{16,22},{18,... | collective-permute-start | bytes 73736 | tf_op jit(solution)/shard_map/ppermute | solution.py:354
  87.8 6.7 %collective-permute-start.22 = (bf16[2,80,128]{2,1,0:T(8,128)(2,1)S(1)}, bf16[2,80,128]{2,1,0:T(8,128)(2,1)S(1)}, u32[]{:S(2)}, u32[]{:S(2)}) collective-permute-start(bf16[2,80,128]{2,1,0:T(8,128)(2,1)S(1)} %get-tuple-element.73), channel_id=1, source_target_pairs={{0,8},{2,10},{4,12},{6,14},{8,16},{10,18},{12,20},{14,22},{16,24},... | collective-permute-start | bytes 122888 | tf_op jit(solution)/shard_map/ppermute | solution.py:357
  89.5 7.2 %collective-permute-start.23 = (bf16[2,80,128]{2,1,0:T(8,128)(2,1)S(1)}, bf16[2,80,128]{2,1,0:T(8,128)(2,1)S(1)}, u32[]{:S(2)}, u32[]{:S(2)}) collective-permute-start(bf16[2,80,128]{2,1,0:T(8,128)(2,1)S(1)} %get-tuple-element.73), channel_id=1, source_target_pairs={{0,16},{2,18},{4,20},{6,22},{8,24},{10,26},{12,28},{14,30},{16,0},... | collective-permute-start | bytes 122888 | tf_op jit(solution)/shard_map/ppermute | solution.py:357
  90.4 6.3 %collective-permute-start.24 = (bf16[2,80,128]{2,1,0:T(8,128)(2,1)S(1)}, bf16[2,80,128]{2,1,0:T(8,128)(2,1)S(1)}, u32[]{:S(2)}, u32[]{:S(2)}) collective-permute-start(bf16[2,80,128]{2,1,0:T(8,128)(2,1)S(1)} %get-tuple-element.73), channel_id=1, source_target_pairs={{0,24},{2,26},{4,28},{6,30},{8,0},{10,2},{12,4},{14,6},{16,8},{18,... | collective-permute-start | bytes 122888 | tf_op jit(solution)/shard_map/ppermute | solution.py:357
  91.9 7.6 %collective-permute-start.31 = (bf16[4,2,48,128]{3,2,1,0:T(8,128)(2,1)S(1)}, bf16[4,2,48,128]{3,2,1,0:T(8,128)(2,1)S(1)}, u32[]{:S(2)}, u32[]{:S(2)}) collective-permute-start(bf16[4,2,48,128]{3,2,1,0:T(8,128)(2,1)S(1)} %pad_maximum_fusion.1.refs_4_), channel_id=1, source_target_pairs={{0,8},{2,10},{4,12},{6,14},{8,16},{10,18},{12,20},{14,22},{16,24},... | collective-permute-start | bytes 294920 | tf_op jit(solution)/shard_map/ppermute | solution.py:357
  92.8 9.6 %collective-permute-start.32 = (bf16[4,2,48,128]{3,2,1,0:T(8,128)(2,1)S(1)}, bf16[4,2,48,128]{3,2,1,0:T(8,128)(2,1)S(1)}, u32[]{:S(2)}, u32[]{:S(2)}) collective-permute-start(bf16[4,2,48,128]{3,2,1,0:T(8,128)(2,1)S(1)} %pad_maximum_fusion.1.refs_4_), channel_id=1, source_target_pairs={{0,16},{2,18},{4,20},{6,22},{8,24},{10,26},{12,28},{14,30},{16,0},... | collective-permute-start | bytes 294920 | tf_op jit(solution)/shard_map/ppermute | solution.py:357
  94.5 7.8 %collective-permute-start.33 = (bf16[4,2,48,128]{3,2,1,0:T(8,128)(2,1)S(1)}, bf16[4,2,48,128]{3,2,1,0:T(8,128)(2,1)S(1)}, u32[]{:S(2)}, u32[]{:S(2)}) collective-permute-start(bf16[4,2,48,128]{3,2,1,0:T(8,128)(2,1)S(1)} %pad_maximum_fusion.1.refs_4_), channel_id=1, source_target_pairs={{0,24},{2,26},{4,28},{6,30},{8,0},{10,2},{12,4},{14,6},{16,8},{18,... | collective-permute-start | bytes 294920 | tf_op jit(solution)/shard_map/ppermute | solution.py:357
  96.7 6.2 %collective-permute-start.25 = (bf16[4,2,80,128]{3,2,1,0:T(8,128)(2,1)S(1)}, bf16[4,2,80,128]{3,2,1,0:T(8,128)(2,1)S(1)}, u32[]{:S(2)}, u32[]{:S(2)}) collective-permute-start(bf16[4,2,80,128]{3,2,1,0:T(8,128)(2,1)S(1)} %pad_maximum_fusion.refs_0_), channel_id=1, source_target_pairs={{0,2},{2,0},{4,6},{6,4},{8,10},{10,8},{12,14},{14,12},{16,18},{18,... | collective-permute-start | bytes 491528 | tf_op jit(solution)/shard_map/ppermute | solution.py:354
  98.2 7.7 %collective-permute-start.26 = (bf16[4,2,80,128]{3,2,1,0:T(8,128)(2,1)S(1)}, bf16[4,2,80,128]{3,2,1,0:T(8,128)(2,1)S(1)}, u32[]{:S(2)}, u32[]{:S(2)}) collective-permute-start(bf16[4,2,80,128]{3,2,1,0:T(8,128)(2,1)S(1)} %pad_maximum_fusion.refs_0_), channel_id=1, source_target_pairs={{0,4},{2,6},{4,0},{6,2},{8,12},{10,14},{12,8},{14,10},{16,20},{18,... | collective-permute-start | bytes 491528 | tf_op jit(solution)/shard_map/ppermute | solution.py:354
  99.5 6.4 %collective-permute-start.27 = (bf16[4,2,80,128]{3,2,1,0:T(8,128)(2,1)S(1)}, bf16[4,2,80,128]{3,2,1,0:T(8,128)(2,1)S(1)}, u32[]{:S(2)}, u32[]{:S(2)}) collective-permute-start(bf16[4,2,80,128]{3,2,1,0:T(8,128)(2,1)S(1)} %pad_maximum_fusion.refs_0_), channel_id=1, source_target_pairs={{0,6},{2,4},{4,2},{6,0},{8,14},{10,12},{12,10},{14,8},{16,22},{18,... | collective-permute-start | bytes 491528 | tf_op jit(solution)/shard_map/ppermute | solution.py:354

commit v4 on v3

--- a/solution.py
+++ b/solution.py
@@ -155,77 +155,68 @@
     )(*in_hbm(vals, greens, walkers), cols)
 
 
-def potential_kernel(start, steps, layout, by_plane, fields_ref, own_ref, *refs):
+def potential_kernel(early_steps, layout, fields_ref, own_ref, *refs):
     nz, plane, own = layout
     others = refs[:lax.axis_size("orb") - 1]
-    cols_ref, turned_ref = refs[len(others):len(others) + 2]
-    groups = plane if by_plane else nz
-    outs = refs[len(others) + 2:len(others) + 2 + groups]
-    energy_ref, s_ref, swap = refs[len(others) + 2 + groups:]
+    cols_ref, turned_ref, early_ref, late_ref, energy_ref, s_ref, swap = refs[len(others):]
     walk, vectors = fields_ref.shape
     rowblocks = cols_ref.shape[0]
 
-    me = lax.axis_index("chol")
     bias = own_ref[...]
     for other in others:
         bias = bias + other[...]
     energy = 0.5 * jnp.sum(bias * bias, axis=1, keepdims=True)
-    energy_ref[...] = jnp.broadcast_to(energy, energy_ref.shape)
-    shifted = (fields_ref[...] - bias).astype(jnp.bfloat16)
-    at = lax.broadcasted_iota(jnp.int32, (walk, walk), 0)
-    source = lax.broadcasted_iota(jnp.int32, (walk, walk), 1)
-    chip = at // own
-    z = (me // plane + chip // plane) % nz
-    p = (me % plane) ^ (chip % plane)
-    wanted = (z * plane + p) * own + at % own
-    pick = (wanted == source).astype(jnp.float32).astype(jnp.bfloat16)
-    ordered = jnp.dot(pick, shifted, preferred_element_type=jnp.float32)
+    energy_ref[...] = jnp.zeros_like(energy_ref)
+    energy_ref[:, :walk] = jnp.broadcast_to(energy, (walk, LANES)).T[:CHUNK]
+    shifted = (fields_ref[...] - bias).astype(jnp.bfloat16).astype(jnp.float32)
     for local in range(rowblocks):
         row = lax.axis_index("orb") * rowblocks + local
-        s_ref[local, 0:walk] = ordered.astype(jnp.bfloat16)
+        s_ref[local, 0:walk] = shifted.astype(jnp.bfloat16)
         for k, mask in enumerate(slot_masks(cols_ref[local, 1:2, :], row)):
-            s_ref[local, (k + 1) * walk:(k + 2) * walk] = jnp.where(mask, ordered, 0.0).astype(jnp.bfloat16)
+            s_ref[local, (k + 1) * walk:(k + 2) * walk] = jnp.where(mask, shifted, 0.0).astype(jnp.bfloat16)
     swap[...] = swap_matrix()
     first = lax.broadcasted_iota(jnp.int32, (walk, LANES), 1) < BLOCK
 
-    def step(t, carry):
-        left = s_ref[lax.div(start + t, BLOCK // CHUNK)]
-        tiles = []
-        for i in range(0, CHUNK, 2):
-            both = jnp.dot(
-                left, turned_ref[start + t, :, i * LANES:(i + 2) * LANES], preferred_element_type=jnp.float32
-            )
-            for side in range(2):
-                out = both[:, side * LANES:(side + 1) * LANES]
-                near = jnp.where(first, out[0:walk], out[walk:2 * walk])
-                far = jnp.where(first, pltpu.roll(out[2 * walk:3 * walk], BLOCK, 1), out[3 * walk:])
-                tiles.append(jnp.concatenate([near, far], axis=1).astype(jnp.bfloat16))
-        for w0 in range(0, walk, CHUNK):
-            mixed = jnp.concatenate([tile[w0:w0 + CHUNK] for tile in tiles], axis=0)
-            mixed = jnp.dot(swap[...], mixed, preferred_element_type=jnp.float32).astype(jnp.bfloat16)
-            for w in range(CHUNK):
-                chip, j = (w0 + w) // own, (w0 + w) % own
-                group, inner = (chip % plane, chip // plane) if by_plane else (chip // plane, chip % plane)
-                for half in range(2):
-                    rows = pl.ds(pl.multiple_of((2 * t + half) * CHUNK, CHUNK), CHUNK)
-                    outs[group][inner, j, rows, :] = (
-                        mixed[w * CHUNK:(w + 1) * CHUNK, half * LANES:(half + 1) * LANES]
-                    )
-        return carry
-
-    lax.fori_loop(0, steps, step, 0)
-
-
-def potential_call(start, steps, layout, by_plane, fields, bias, others, cols, turned):
+    def steps(out_ref, start, count, by_plane):
+        def step(t, carry):
+            left = s_ref[lax.div(start + t, BLOCK // CHUNK)]
+            tiles = []
+            for i in range(0, CHUNK, 2):
+                both = jnp.dot(
+                    left, turned_ref[start + t, :, i * LANES:(i + 2) * LANES], preferred_element_type=jnp.float32
+                )
+                for side in range(2):
+                    out = both[:, side * LANES:(side + 1) * LANES]
+                    near = jnp.where(first, out[0:walk], out[walk:2 * walk])
+                    far = jnp.where(first, pltpu.roll(out[2 * walk:3 * walk], BLOCK, 1), out[3 * walk:])
+                    tiles.append(jnp.concatenate([near, far], axis=1).astype(jnp.bfloat16))
+            for w0 in range(0, walk, CHUNK):
+                mixed = jnp.concatenate([tile[w0:w0 + CHUNK] for tile in tiles], axis=0)
+                mixed = jnp.dot(swap[...], mixed, preferred_element_type=jnp.float32).astype(jnp.bfloat16)
+                for w in range(CHUNK):
+                    chip, j = (w0 + w) // own, (w0 + w) % own
+                    at = (chip % plane, chip // plane) if by_plane else (chip // plane, chip % plane)
+                    for half in range(2):
+                        rows = pl.ds(pl.multiple_of((2 * t + half) * CHUNK, CHUNK), CHUNK)
+                        out_ref[(*at, j, rows)] = mixed[w * CHUNK:(w + 1) * CHUNK, half * LANES:(half + 1) * LANES]
+            return carry
+
+        lax.fori_loop(0, count, step, 0)
+
+    steps(early_ref, 0, early_steps, False)
+    steps(late_ref, early_steps, turned_ref.shape[0] - early_steps, True)
+
+
+def potential_call(early_steps, layout, fields, bias, others, cols, turned):
     nz, plane, own = layout
     walk, vectors = fields.shape
-    groups, inner = (plane, nz) if by_plane else (nz, plane)
     rows = 2 * CHUNK
-    *parts, energy = pl.pallas_call(
-        functools.partial(potential_kernel, start, steps, layout, by_plane),
+    return pl.pallas_call(
+        functools.partial(potential_kernel, early_steps, layout),
         out_shape=[
-            *[pltpu.VMEM((inner, own, steps * rows, LANES), jnp.bfloat16)] * groups,
-            pltpu.VMEM((walk, LANES), jnp.float32),
+            pltpu.VMEM((nz, plane, own, early_steps * rows, LANES), jnp.bfloat16),
+            pltpu.VMEM((plane, nz, own, (turned.shape[0] - early_steps) * rows, LANES), jnp.bfloat16),
+            pltpu.VMEM((CHUNK, LANES), jnp.float32),
         ],
         scratch_shapes=[
             pltpu.VMEM((cols.shape[0], 4 * walk, vectors), jnp.bfloat16),
@@ -234,33 +225,37 @@
         compiler_params=params(16),
         name="potential",
     )(fields, *in_vmem(bias, *others), cols, *in_vmem(turned))
-    return parts, energy
-
-
-def sum_kernel(count, *refs):
-    ins, outs = refs[:count], refs[count:]
-    for k, out in enumerate(outs):
-        total = ins[0][k].astype(jnp.float32)
-        for ref in ins[1:]:
-            total = total + ref[k].astype(jnp.float32)
-        out[...] = total.astype(out.dtype)
-
-
-def sum_call(arrays):
-    pieces = arrays[0].shape[0]
-    shape = pltpu.VMEM(arrays[0].shape[1:], jnp.bfloat16)
+
+
+def sum_kernel(in_ref, out_ref):
+    for k in range(out_ref.shape[0]):
+        total = in_ref[0, k].astype(jnp.float32)
+        for source in range(1, in_ref.shape[0]):
+            total = total + in_ref[source, k].astype(jnp.float32)
+        out_ref[k] = total.astype(out_ref.dtype)
+
+
+def sum_call(array):
     return pl.pallas_call(
-        functools.partial(sum_kernel, len(arrays)),
-        out_shape=[shape] * pieces,
+        sum_kernel,
+        out_shape=pltpu.VMEM(array.shape[1:], jnp.bfloat16),
         compiler_params=params(16),
         name="sum_parts",
-    )(*in_vmem(*arrays))
+    )(*in_vmem(array))
+
+
+def split(value):
+    parts = []
+    for _ in range(3):
+        parts.append(value.astype(jnp.bfloat16))
+        value = value - parts[-1].astype(jnp.float32)
+    return parts
 
 
 def series_kernel(sizes, *refs):
     n_orb, late_steps, early_steps = sizes
     late, early, start = refs[:n_orb], refs[n_orb:2 * n_orb], refs[2 * n_orb:3 * n_orb]
-    plane_ref, z_ref, pot, term, total = refs[3 * n_orb:]
+    energy_ref, plane_ref, z_ref, pot, term, total = refs[3 * n_orb:]
     me = lax.axis_index("orb")
     own, half_rows = start[0].shape[:2]
     rowblocks = half_rows // BLOCK
@@ -290,19 +285,27 @@
             moved = begin[r].astype(jnp.float32) + sums[r]
             total[r // rowblocks, j, (r % rowblocks) * BLOCK:(r % rowblocks + 1) * BLOCK] = moved.astype(jnp.bfloat16)
     mine = total[pl.ds(me, 1)][0]
-    cut = z_ref.shape[1]
-    z_ref[...] = mine[:, :cut]
-    plane_ref[...] = mine[:, cut:]
-
-
-def series_call(sizes, cut, late, early, start):
+    cut = (z_ref.shape[1] - CHUNK) // own
+    tile = lax.broadcasted_iota(jnp.int32, (CHUNK, LANES), 0)
+    high, middle, low = (part.astype(jnp.float32) for part in split(energy_ref[...]))
+    tile = jnp.where(tile == 0, high, jnp.where(tile == 1, middle, jnp.where(tile == 2, low, 0.0))).astype(jnp.bfloat16)
+    for to in range(z_ref.shape[0]):
+        for j in range(own):
+            z_ref[to, j * cut:(j + 1) * cut] = mine[j, :cut]
+        z_ref[to, own * cut:] = tile
+    for to in range(plane_ref.shape[0]):
+        plane_ref[to] = mine[:, cut:]
+
+
+def series_call(sizes, cut, layout, late, early, start, energy):
+    nz, plane, _ = layout
     n_orb = sizes[0]
     own, half_rows, nocc = start[0].shape
     return pl.pallas_call(
         functools.partial(series_kernel, sizes),
         out_shape=[
-            pltpu.VMEM((own, half_rows - cut, nocc), jnp.bfloat16),
-            pltpu.VMEM((own, cut, nocc), jnp.bfloat16),
+            pltpu.VMEM((plane, own, half_rows - cut, nocc), jnp.bfloat16),
+            pltpu.VMEM((nz, own * cut + CHUNK, nocc), jnp.bfloat16),
         ],
         scratch_shapes=[
             pltpu.VMEM((ROWBLK, own, BLOCK, 2 * LANES), jnp.bfloat16),
@@ -311,32 +314,37 @@
         ],
         compiler_params=params(16),
         name="series",
-    )(*in_vmem(*late, *early, *start))
-
-
-def place_kernel(layout, *refs):
+    )(*in_vmem(*late, *early, *start, energy))
+
+
+def place_kernel(layout, z_first, plane_first, out, energy_ref):
     nz, plane, own = layout
-    z_first, plane_first = refs[:plane], refs[plane:plane + nz]
-    out = refs[plane + nz]
-    me = lax.axis_index("chol")
-    cut = z_first[0].shape[2]
-    for dp in range(plane):
-        for dz in range(nz):
-            chip = lax.rem(me // plane + nz - dz, nz) * plane + (lax.rem(me, plane) ^ dp)
-            to = pl.ds(chip * own, own)
-            out[to, :cut, :] = z_first[dp][dz]
-            out[to, cut:, :] = plane_first[dz][dp]
+    cut = out.shape[1] - plane_first.shape[3]
+    energy = jnp.zeros((CHUNK, LANES), jnp.float32)
+    for p in range(plane):
+        for z in range(nz):
+            for j in range(own):
+                w = (z * plane + p) * own + j
+                out[w, :cut] = z_first[p, z, j * cut:(j + 1) * cut]
+                out[w, cut:] = plane_first[z, p, j]
+            energy = energy + z_first[p, z, own * cut:].astype(jnp.float32)
+    energy_ref[...] = (energy[0:1] + energy[1:2] + energy[2:3])[:, :energy_ref.shape[1]]
 
 
 def place_call(layout, z_first, plane_first):
     nz, plane, own = layout
-    cut, rest, nocc = z_first[0].shape[2], plane_first[0].shape[2], z_first[0].shape[3]
+    rest, nocc = plane_first.shape[3:]
+    walk = nz * plane * own
+    cut = (z_first.shape[2] - CHUNK) // own
     return pl.pallas_call(
         functools.partial(place_kernel, layout),
-        out_shape=jax.ShapeDtypeStruct((nz * plane * own, cut + rest, nocc), jnp.bfloat16),
+        out_shape=[
+            jax.ShapeDtypeStruct((walk, cut + rest, nocc), jnp.bfloat16),
+            jax.ShapeDtypeStruct((1, walk), jnp.float32),
+        ],
         compiler_params=params(16),
         name="place_walkers",
-    )(*in_vmem(*z_first, *plane_first))
+    )(*in_vmem(z_first, plane_first))
 
 
 def per_device(chol_vals, chol_cols, greens, walkers, fields):
@@ -350,11 +358,11 @@
     layout = (nz, plane, own)
     step_factor = 72.0 / float(vectors * chips * BLOCK) ** 0.5
 
-    def to_plane(a, dp):
-        return lax.ppermute(a, "chol", [(c, (c // plane) * plane + ((c % plane) ^ dp)) for c in range(chips)])
-
-    def to_z(a, dz):
-        return lax.ppermute(a, "chol", [(c, ((c // plane + dz) % nz) * plane + c % plane) for c in range(chips)])
+    plane_groups = [[z * plane + p for p in range(plane)] for z in range(nz)]
+    z_groups = [[z * plane + p for z in range(nz)] for p in range(plane)]
+
+    def swap(a, groups):
+        return lax.all_to_all(a, "chol", 0, 0, axis_index_groups=groups, tiled=True)
 
     def around_orb(a):
         return [a] + [lax.ppermute(a, "orb", [((c + d) % n_orb, c) for c in range(n_orb)]) for d in range(1, n_orb)]
@@ -363,42 +371,30 @@
     turned, partial_bias, mine = bias_call(chol_vals, greens, walkers, cols, own)
     start = around_orb(mine)
     bias, *others = around_orb(partial_bias)
+    start, others = lax.optimization_barrier((start, others))
 
     total_steps = rowblocks * BLOCK // CHUNK
     early_steps = total_steps * 3 // 8
     late_steps = total_steps - early_steps
-    fields_t = fields.T
-    early, energy = potential_call(0, early_steps, layout, False, fields_t, bias, others, cols, turned)
-    early_in = [early[0]] + [to_z(early[dz], dz) for dz in range(1, nz)]
-    late, _ = potential_call(early_steps, late_steps, layout, True, fields_t, bias, others, cols, turned)
-    late_in = [late[0]] + [to_plane(late[dp], dp) for dp in range(1, plane)]
-    energy = energy[:, 0]
-    energy_in = [to_plane(energy, dp) for dp in range(1, plane)]
-    start, energy_in, early_in = lax.optimization_barrier((start, energy_in, early_in))
-    energy = energy + sum(energy_in)
-    early_sums = sum_call(early_in)
-    early_in = [early_sums[0]] + [to_plane(early_sums[dp], dp) for dp in range(1, plane)]
-    late_sums = sum_call(late_in)
-    late_in = [late_sums[0]] + [to_z(late_sums[dz], dz) for dz in range(1, nz)]
-
-    energy_in = [to_z(energy, dz) for dz in range(1, nz)]
-    energy_in, late_in = lax.optimization_barrier((energy_in, late_in))
-    energy = energy + sum(energy_in)
-
-    def finish(arrays):
-        total = arrays[0].astype(jnp.float32)
-        for a in arrays[1:]:
-            total = total + a.astype(jnp.float32)
+    early, late, energy = potential_call(early_steps, layout, fields.T, bias, others, cols, turned)
+    early = sum_call(swap(early, z_groups))
+    late = sum_call(swap(late, plane_groups))
+
+    def finish(array):
+        total = jnp.sum(array.astype(jnp.float32), axis=0)
         return around_orb((step_factor * total).astype(jnp.bfloat16))
 
+    early = finish(swap(early, plane_groups))
+    late = finish(swap(late, z_groups))
     cut = half_rows // CHUNK * 5 // 8 * CHUNK
-    b_part, a_part = series_call((n_orb, late_steps, early_steps), cut, finish(late_in), finish(early_in), start)
-
-    a_all = jnp.stack([a_part] + [to_z(a_part, dz) for dz in range(1, nz)])
-    b_all = jnp.stack([b_part] + [to_plane(b_part, dp) for dp in range(1, plane)])
-    z_first = [a_all] + [to_plane(a_all, dp) for dp in range(1, plane)]
-    plane_first = [b_all] + [to_z(b_all, dz) for dz in range(1, nz)]
-    return place_call(layout, z_first, plane_first), energy
+    b_part, a_part = series_call((n_orb, late_steps, early_steps), cut, layout, late, early, start, energy)
+
+    a_all = swap(a_part, z_groups)
+    b_all = swap(b_part, plane_groups)
+    z_first = swap(jnp.broadcast_to(a_all[None], (plane, *a_all.shape)), plane_groups)
+    plane_first = swap(jnp.broadcast_to(b_all[None], (nz, *b_all.shape)), z_groups)
+    moved, energy = place_call(layout, z_first, plane_first)
+    return moved, energy.reshape(walk)
 
 
 def solution(mesh):

time: 107 us -> 131 us (1.22)
  blocking collectives: 0 us -> 68.2 us
  starting transfers between devices: 46.1 us -> 11.8 us
  waiting for transfers between devices: 42 us -> 30 us
  Pallas kernels: 16.7 us -> 18.4 us
    all_to_all x0 -> x5, blocking collectives: none -> 68.2 us  [swap(): return lax.all_to_all(a, 'chol', 0, 0, axis_index_groups=groups, tiled=True)]
    ppermute x30 -> x0, starting transfers between devices: 45.4 us -> none  [the longest x15 24.9 us: to_z(): lax.ppermute(a, 'chol', [(c, (c // plane + dz) % nz * plane + c % plane)...]
    ppermute x30 -> x0, waiting for transfers between devices: 38.7 us -> none  [the longest x15 22.4 us: to_plane(): lax.ppermute(a, 'chol', [(c, c // plane * plane + (c % plane ^ dp)) for c...]
    all_to_all x0 -> x3, waiting for transfers between devices: none -> 28 us  [swap(): return lax.all_to_all(a, 'chol', 0, 0, axis_index_groups=groups, tiled=True)]
    all_to_all x0 -> x3, starting transfers between devices: none -> 10.5 us  [swap(): return lax.all_to_all(a, 'chol', 0, 0, axis_index_groups=groups, tiled=True)]
    pallas_call x5 -> x4, Pallas kernels: 6.97 us -> 8.64 us  [the longest x1 5.95 us: potential_call(): pl.pallas_call(functools.partial(potential_kernel, early_steps, layout),...]
    ppermute x4, waiting for transfers between devices: 3.33 us -> 2.02 us  [around_orb(): lax.ppermute(a, 'orb', [((c + d) % n_orb, c) for c in range(n_orb)])]
  transfers between devices with their start and end apart: 34 -> 7, of which waited for: 16 -> 5; matrix products, arithmetic and copies ran while one was open for 1% -> 0% of each run, Pallas kernels for 4% -> 1%
where the time goes in v4:
time: 131 us; the launch traced here: 130 us
  blocking collectives  68.2 us (52%)
  waiting for transfers between devices  30 us (23%)
  Pallas kernels  18.4 us (14%)
  starting transfers between devices  11.8 us (9%)
    all_to_all x5, blocking collectives, swap(): return lax.all_to_all(a, 'chol', 0, 0, axis_index_groups=groups, tiled=True)  68.2 us
    all_to_all x3, waiting for transfers between devices, swap(): return lax.all_to_all(a, 'chol', 0, 0, axis_index_groups=groups, tiled=True)  28 us
    all_to_all x3, starting transfers between devices, swap(): return lax.all_to_all(a, 'chol', 0, 0, axis_index_groups=groups, tiled=True)  10.5 us
    pallas_call x1, Pallas kernels, bias_call(): pl.pallas_call(bias_kernel, in_specs=[*[pl.BlockSpec(memory_space=pl.ANY)...  8.49 us
    pallas_call x1, Pallas kernels, potential_call(): pl.pallas_call(functools.partial(potential_kernel, early_steps, layout),...  5.95 us
  transfers between devices with their start and end apart: 7, of which 5 were waited for; matrix products, arithmetic and copies ran while one was open for 0% of the time, Pallas kernels for 1%

profile of v4, /device:TPU:0, one launch (start us, length us, event | category | flops | bytes accessed | tf_op | source)
XLA Modules:
  0.0 130.0 jit_solution(4108337746508121557)
XLA Ops:
  0.6 0.0 copy-start.1
  0.6 0.7 copy-done.1
  1.3 0.0 copy-start
  1.3 8.5 %force_bias.1 = (bf16[8,256,2048]{2,1,0:T(8,128)(2,1)S(1)}, f32[32,256]{1,0:T(8,128)S(1)}, bf16[2,128,128]{2,1,0:T(8,128)(2,1)S(1)}) custom-call(bf16[256,2,64,128]{3,2,1,0:T(8,128)(2,1)} %vals_hbm.1, bf16[32,128,256]{2,1,0:T(8,128)(2,1)} %greens_hbm.1, bf16[32,128,128]{2,1,0:T(8,128)(2,1)} %walkers_hbm.1, s32[2,2,256]{2,1,0:T(2,128)S(1)} %bitcast.4), custom_call_target="tpu_custom_call" | custom-call | tf_op jit(solution)/shard_map/force_bias/pallas_call | solution.py:131
  9.8 0.5 collective-permute-start
  10.3 0.1 collective-permute-start.1
  10.4 1.1 collective-permute-done.1.refs_0_
  11.5 0.0 collective-permute-done.refs_5_
  11.6 0.0 copy-done
  11.6 5.9 %potential.1 = (bf16[4,4,2,96,128]{4,3,2,1,0:T(8,128)(2,1)S(1)}, bf16[4,4,2,160,128]{4,3,2,1,0:T(8,128)(2,1)}, f32[16,128]{1,0:T(8,128)S(1)}) custom-call(f32[32,256]{1,0:T(8,128)S(1)} %bitcast.3, f32[32,256]{1,0:T(8,128)S(1)} %get-tuple-element.15.own_ref, f32[32,256]{1,0:T(8,128)S(1)} %collective-permute-done.1.refs_0_, s32[2,2,256]{2,1,0:T(2,128)S(1)} %bitcast.5, ...), custom_call_target="tpu_custom_call" | custom-call | tf_op jit(solution)/shard_map/potential/pallas_call | solution.py:214
  17.5 26.4 %all_to_all.40.in_ref = bf16[4,4,2,96,128]{4,3,2,1,0:T(8,128)(2,1)S(1)} all-to-all(bf16[4,4,2,96,128]{4,3,2,1,0:T(8,128)(2,1)S(1)} %get-tuple-element.20), channel_id=1, replica_groups={{0,8,16,24},{2,10,18,26},{4,12,20,28},{6,14,22,30},{1,9,17,25},{3,11,19..., dimensions={0} | all-to-all | bytes 1572864 | tf_op jit(solution)/shard_map/all_to_all | solution.py:365
  43.9 3.7 %all-to-all-start = ((bf16[4,4,2,160,128]{4,3,2,1,0:T(8,128)(2,1)}), bf16[4,4,2,160,128]{4,3,2,1,0:T(8,128)(2,1)S(1)}, u32[]{:S(2)}, u32[]{:S(2)}) async-start(bf16[4,4,2,160,128]{4,3,2,1,0:T(8,128)(2,1)} %get-tuple-element.19), calls=%async_computation | async-start | bytes 2621440 | tf_op jit(solution)/shard_map/all_to_all | solution.py:365
  47.7 0.8 sum_parts.3
  48.4 15.2 %all-to-all-done.in_ref = bf16[4,4,2,160,128]{4,3,2,1,0:T(8,128)(2,1)S(1)} async-done(((bf16[4,4,2,160,128]{4,3,2,1,0:T(8,128)(2,1)}), bf16[4,4,2,160,128]{4,3,2,1,0:T(8,128)(2,1)S(1)}, u32[]{:S(2)}, u32[]{:S(2)}) %all-to-all-start) | async-done | bytes 1310752 | tf_op jit(solution)/shard_map/all_to_all | solution.py:365
  63.6 3.4 %all-to-all-start.3 = ((bf16[4,2,96,128]{3,2,1,0:T(8,128)(2,1)}), bf16[4,2,96,128]{3,2,1,0:T(8,128)(2,1)S(1)}, u32[]{:S(2)}, u32[]{:S(2)}) async-start(bf16[4,2,96,128]{3,2,1,0:T(8,128)(2,1)} %sum_parts.3), calls=%async_computation.3 | async-start | bytes 393216 | tf_op jit(solution)/shard_map/all_to_all | solution.py:365
  66.9 0.9 sum_parts.2
  67.8 4.3 %all-to-all-done.3 = bf16[4,2,96,128]{3,2,1,0:T(8,128)(2,1)S(1)} async-done(((bf16[4,2,96,128]{3,2,1,0:T(8,128)(2,1)}), bf16[4,2,96,128]{3,2,1,0:T(8,128)(2,1)S(1)}, u32[]{:S(2)}, u32[]{:S(2)}) %all-to-all-start.3) | async-done | bytes 196640 | tf_op jit(solution)/shard_map/all_to_all | solution.py:365
  72.1 3.5 %all-to-all-start.1 = ((bf16[4,2,160,128]{3,2,1,0:T(8,128)(2,1)}), bf16[4,2,160,128]{3,2,1,0:T(8,128)(2,1)S(1)}, u32[]{:S(2)}, u32[]{:S(2)}) async-start(bf16[4,2,160,128]{3,2,1,0:T(8,128)(2,1)} %sum_parts.2), calls=%async_computation.1 | async-start | bytes 655360 | tf_op jit(solution)/shard_map/all_to_all | solution.py:365
  75.6 8.5 %all-to-all-done.1 = bf16[4,2,160,128]{3,2,1,0:T(8,128)(2,1)S(1)} async-done(((bf16[4,2,160,128]{3,2,1,0:T(8,128)(2,1)}), bf16[4,2,160,128]{3,2,1,0:T(8,128)(2,1)S(1)}, u32[]{:S(2)}, u32[]{:S(2)}) %all-to-all-start.1) | async-done | bytes 327712 | tf_op jit(solution)/shard_map/all_to_all | solution.py:365
  84.2 0.1 collective-permute-start.2
  84.3 0.6 collective-permute-start.3
  84.9 0.9 collective-permute-done.3.refs_3_
  85.7 0.0 collective-permute-done.2.refs_1_
  85.7 1.3 series.1
  87.0 7.4 %all_to_all.41 = bf16[4,2,48,128]{3,2,1,0:T(8,128)(2,1)S(1)} all-to-all(bf16[4,2,48,128]{3,2,1,0:T(8,128)(2,1)S(1)} %get-tuple-element.25), channel_id=1, replica_groups={{0,2,4,6},{8,10,12,14},{16,18,20,22},{24,26,28,30},{1,3,5,7},{9,11,13,1..., dimensions={0} | all-to-all | bytes 196608 | tf_op jit(solution)/shard_map/all_to_all | solution.py:365
  94.4 9.3 %all_to_all.42 = bf16[4,176,128]{2,1,0:T(8,128)(2,1)S(1)} all-to-all(bf16[4,176,128]{2,1,0:T(8,128)(2,1)S(1)} %get-tuple-element.24), channel_id=1, replica_groups={{0,8,16,24},{2,10,18,26},{4,12,20,28},{6,14,22,30},{1,9,17,25},{3,11,19..., dimensions={0} | all-to-all | bytes 360448 | tf_op jit(solution)/shard_map/all_to_all | solution.py:365
  103.7 0.1 broadcast_in_dim.5
  103.7 13.2 %all_to_all.43.plane_first = bf16[4,4,2,48,128]{4,3,2,1,0:T(8,128)(2,1)S(1)} all-to-all(bf16[4,4,2,48,128]{4,3,2,1,0:T(8,128)(2,1)S(1)} %broadcast_in_dim.5), channel_id=1, replica_groups={{0,8,16,24},{2,10,18,26},{4,12,20,28},{6,14,22,30},{1,9,17,25},{3,11,19..., dimensions={0} | all-to-all | bytes 786432 | tf_op jit(solution)/shard_map/all_to_all | solution.py:365
  116.9 0.1 broadcast_in_dim.4
  117.0 11.9 %all_to_all.44.z_first = bf16[4,4,176,128]{3,2,1,0:T(8,128)(2,1)S(1)} all-to-all(bf16[4,4,176,128]{3,2,1,0:T(8,128)(2,1)S(1)} %broadcast_in_dim.4), channel_id=1, replica_groups={{0,2,4,6},{8,10,12,14},{16,18,20,22},{24,26,28,30},{1,3,5,7},{9,11,13,1..., dimensions={0} | all-to-all | bytes 1441792 | tf_op jit(solution)/shard_map/all_to_all | solution.py:365
  128.9 1.0 place_walkers.1
  (4 shorter events, 0.1 us)
Async XLA Ops:
  0.6 0.7 copy-start.1
  1.3 10.2 %copy-start = (f32[256,32]{0,1:T(8,128)S(1)}, f32[256,32]{0,1:T(8,128)}, u32[]{:S(2)}) copy-start(f32[256,32]{0,1:T(8,128)} %param.9) | copy-start | bytes 98308
  9.8 1.7 %collective-permute-start = (bf16[2,128,128]{2,1,0:T(8,128)(2,1)S(1)}, bf16[2,128,128]{2,1,0:T(8,128)(2,1)S(1)}, u32[]{:S(2)}, u32[]{:S(2)}) collective-permute-start(bf16[2,128,128]{2,1,0:T(8,128)(2,1)S(1)} %get-tuple-element.21.refs_4_), channel_id=1, source_target_pairs={{1,0},{0,1},{3,2},{2,3},{5,4},{4,5},{7,6},{6,7},{9,8},{8,9},{11,10... | collective-permute-start | bytes 196616 | tf_op jit(solution)/shard_map/ppermute | solution.py:368
  10.3 1.2 collective-permute-start.1
  43.9 19.6 %all-to-all-start = ((bf16[4,4,2,160,128]{4,3,2,1,0:T(8,128)(2,1)}), bf16[4,4,2,160,128]{4,3,2,1,0:T(8,128)(2,1)S(1)}, u32[]{:S(2)}, u32[]{:S(2)}) async-start(bf16[4,4,2,160,128]{4,3,2,1,0:T(8,128)(2,1)} %get-tuple-element.19), calls=%async_computation | async-start | bytes 2621440 | tf_op jit(solution)/shard_map/all_to_all | solution.py:365
  63.6 8.5 %all-to-all-start.3 = ((bf16[4,2,96,128]{3,2,1,0:T(8,128)(2,1)}), bf16[4,2,96,128]{3,2,1,0:T(8,128)(2,1)S(1)}, u32[]{:S(2)}, u32[]{:S(2)}) async-start(bf16[4,2,96,128]{3,2,1,0:T(8,128)(2,1)} %sum_parts.3), calls=%async_computation.3 | async-start | bytes 393216 | tf_op jit(solution)/shard_map/all_to_all | solution.py:365
  72.1 12.0 %all-to-all-start.1 = ((bf16[4,2,160,128]{3,2,1,0:T(8,128)(2,1)}), bf16[4,2,160,128]{3,2,1,0:T(8,128)(2,1)S(1)}, u32[]{:S(2)}, u32[]{:S(2)}) async-start(bf16[4,2,160,128]{3,2,1,0:T(8,128)(2,1)} %sum_parts.2), calls=%async_computation.1 | async-start | bytes 655360 | tf_op jit(solution)/shard_map/all_to_all | solution.py:365
  84.2 1.5 %collective-permute-start.2 = (bf16[2,160,128]{2,1,0:T(8,128)(2,1)S(1)}, bf16[2,160,128]{2,1,0:T(8,128)(2,1)S(1)}, u32[]{:S(2)}, u32[]{:S(2)}) collective-permute-start(bf16[2,160,128]{2,1,0:T(8,128)(2,1)S(1)} %multiply_convert_fusion.refs_0_), channel_id=1, source_target_pairs={{1,0},{0,1},{3,2},{2,3},{5,4},{4,5},{7,6},{6,7},{9,8},{8,9},{11,10... | collective-permute-start | bytes 245768 | tf_op jit(solution)/shard_map/ppermute | solution.py:368
  84.3 1.4 %collective-permute-start.3 = (bf16[2,96,128]{2,1,0:T(8,128)(2,1)S(1)}, bf16[2,96,128]{2,1,0:T(8,128)(2,1)S(1)}, u32[]{:S(2)}, u32[]{:S(2)}) collective-permute-start(bf16[2,96,128]{2,1,0:T(8,128)(2,1)S(1)} %multiply_convert_fusion.1.refs_2_), channel_id=1, source_target_pairs={{1,0},{0,1},{3,2},{2,3},{5,4},{4,5},{7,6},{6,7},{9,8},{8,9},{11,10... | collective-permute-start | bytes 147464 | tf_op jit(solution)/shard_map/ppermute | solution.py:368

commit v5 on v3

--- a/solution.py
+++ b/solution.py
@@ -15,8 +15,19 @@
 MIB = 1024 * 1024
 
 
+FREE = pl.CostEstimate(flops=0, bytes_accessed=0, transcendentals=0)
+
+
 def params(mib):
     return pltpu.CompilerParams(vmem_limit_bytes=mib * MIB)
+
+
+def split(value):
+    parts = []
+    for _ in range(3):
+        parts.append(value.astype(jnp.bfloat16))
+        value = value - parts[-1].astype(jnp.float32)
+    return parts
 
 
 def in_vmem(*arrays):
@@ -150,13 +161,15 @@
             pltpu.SemaphoreType.DMA((steps,)),
             pltpu.SemaphoreType.DMA,
         ],
+        cost_estimate=FREE,
         compiler_params=params(24),
         name="force_bias",
     )(*in_hbm(vals, greens, walkers), cols)
 
 
-def potential_kernel(start, steps, layout, by_plane, fields_ref, own_ref, *refs):
+def potential_kernel(start, steps, layout, by_plane, n_after, fields_ref, own_ref, *refs):
     nz, plane, own = layout
+    refs = refs[n_after:]
     others = refs[:lax.axis_size("orb") - 1]
     cols_ref, turned_ref = refs[len(others):len(others) + 2]
     groups = plane if by_plane else nz
@@ -170,7 +183,8 @@
     for other in others:
         bias = bias + other[...]
     energy = 0.5 * jnp.sum(bias * bias, axis=1, keepdims=True)
-    energy_ref[...] = jnp.broadcast_to(energy, energy_ref.shape)
+    energy_ref[...] = jnp.zeros_like(energy_ref)
+    energy_ref[:, :walk] = jnp.broadcast_to(energy, (walk, LANES)).T[:CHUNK]
     shifted = (fields_ref[...] - bias).astype(jnp.bfloat16)
     at = lax.broadcasted_iota(jnp.int32, (walk, walk), 0)
     source = lax.broadcasted_iota(jnp.int32, (walk, walk), 1)
@@ -216,24 +230,25 @@
     lax.fori_loop(0, steps, step, 0)
 
 
-def potential_call(start, steps, layout, by_plane, fields, bias, others, cols, turned):
+def potential_call(start, steps, layout, by_plane, fields, bias, others, cols, turned, after=()):
     nz, plane, own = layout
     walk, vectors = fields.shape
     groups, inner = (plane, nz) if by_plane else (nz, plane)
     rows = 2 * CHUNK
     *parts, energy = pl.pallas_call(
-        functools.partial(potential_kernel, start, steps, layout, by_plane),
+        functools.partial(potential_kernel, start, steps, layout, by_plane, len(after)),
         out_shape=[
             *[pltpu.VMEM((inner, own, steps * rows, LANES), jnp.bfloat16)] * groups,
-            pltpu.VMEM((walk, LANES), jnp.float32),
+            pltpu.VMEM((CHUNK, LANES), jnp.float32),
         ],
         scratch_shapes=[
             pltpu.VMEM((cols.shape[0], 4 * walk, vectors), jnp.bfloat16),
             pltpu.VMEM((CHUNK * CHUNK, CHUNK * CHUNK), jnp.bfloat16),
         ],
+        cost_estimate=FREE,
         compiler_params=params(16),
         name="potential",
-    )(fields, *in_vmem(bias, *others), cols, *in_vmem(turned))
+    )(fields, *in_vmem(bias, *after, *others), cols, *in_vmem(turned))
     return parts, energy
 
 
@@ -252,6 +267,7 @@
     return pl.pallas_call(
         functools.partial(sum_kernel, len(arrays)),
         out_shape=[shape] * pieces,
+        cost_estimate=FREE,
         compiler_params=params(16),
         name="sum_parts",
     )(*in_vmem(*arrays))
@@ -260,7 +276,7 @@
 def series_kernel(sizes, *refs):
     n_orb, late_steps, early_steps = sizes
     late, early, start = refs[:n_orb], refs[n_orb:2 * n_orb], refs[2 * n_orb:3 * n_orb]
-    plane_ref, z_ref, pot, term, total = refs[3 * n_orb:]
+    energy_ref, plane_ref, z_ref, pot, term, total = refs[3 * n_orb:]
     me = lax.axis_index("orb")
     own, half_rows = start[0].shape[:2]
     rowblocks = half_rows // BLOCK
@@ -290,50 +306,65 @@
             moved = begin[r].astype(jnp.float32) + sums[r]
             total[r // rowblocks, j, (r % rowblocks) * BLOCK:(r % rowblocks + 1) * BLOCK] = moved.astype(jnp.bfloat16)
     mine = total[pl.ds(me, 1)][0]
-    cut = z_ref.shape[1]
-    z_ref[...] = mine[:, :cut]
+    cut = (z_ref.shape[0] - CHUNK) // own
+    at = lax.broadcasted_iota(jnp.int32, (CHUNK, LANES), 0)
+    high, middle, low = (part.astype(jnp.float32) for part in split(energy_ref[...]))
+    tile = jnp.where(at == 0, high, jnp.where(at == 1, middle, jnp.where(at == 2, low, 0.0)))
+    for j in range(own):
+        z_ref[j * cut:(j + 1) * cut] = mine[j, :cut]
+    z_ref[own * cut:] = tile.astype(jnp.bfloat16)
     plane_ref[...] = mine[:, cut:]
 
 
-def series_call(sizes, cut, late, early, start):
+def series_call(sizes, cut, late, early, start, energy):
     n_orb = sizes[0]
     own, half_rows, nocc = start[0].shape
     return pl.pallas_call(
         functools.partial(series_kernel, sizes),
         out_shape=[
             pltpu.VMEM((own, half_rows - cut, nocc), jnp.bfloat16),
-            pltpu.VMEM((own, cut, nocc), jnp.bfloat16),
+            pltpu.VMEM((own * cut + CHUNK, nocc), jnp.bfloat16),
         ],
         scratch_shapes=[
             pltpu.VMEM((ROWBLK, own, BLOCK, 2 * LANES), jnp.bfloat16),
             pltpu.VMEM((n_orb, own, half_rows, nocc), jnp.bfloat16),
             pltpu.VMEM((n_orb, own, half_rows, nocc), jnp.bfloat16),
         ],
+        cost_estimate=FREE,
         compiler_params=params(16),
         name="series",
-    )(*in_vmem(*late, *early, *start))
+    )(*in_vmem(*late, *early, *start, energy))
 
 
 def place_kernel(layout, *refs):
     nz, plane, own = layout
     z_first, plane_first = refs[:plane], refs[plane:plane + nz]
-    out = refs[plane + nz]
+    out, energy_ref = refs[plane + nz:]
     me = lax.axis_index("chol")
-    cut = z_first[0].shape[2]
+    cut = out.shape[1] - plane_first[0].shape[2]
+    energy = jnp.zeros((CHUNK, LANES), jnp.float32)
     for dp in range(plane):
         for dz in range(nz):
             chip = lax.rem(me // plane + nz - dz, nz) * plane + (lax.rem(me, plane) ^ dp)
-            to = pl.ds(chip * own, own)
-            out[to, :cut, :] = z_first[dp][dz]
-            out[to, cut:, :] = plane_first[dz][dp]
+            for j in range(own):
+                out[chip * own + j, :cut] = z_first[dp][dz, j * cut:(j + 1) * cut]
+                out[chip * own + j, cut:] = plane_first[dz][dp, j]
+            energy = energy + z_first[dp][dz, own * cut:].astype(jnp.float32)
+    energy_ref[...] = (energy[0:1] + energy[1:2] + energy[2:3])[:, :energy_ref.shape[1]]
 
 
 def place_call(layout, z_first, plane_first):
     nz, plane, own = layout
-    cut, rest, nocc = z_first[0].shape[2], plane_first[0].shape[2], z_first[0].shape[3]
+    rest, nocc = plane_first[0].shape[2:]
+    walk = nz * plane * own
+    cut = (z_first[0].shape[1] - CHUNK) // own
     return pl.pallas_call(
         functools.partial(place_kernel, layout),
-        out_shape=jax.ShapeDtypeStruct((nz * plane * own, cut + rest, nocc), jnp.bfloat16),
+        out_shape=[
+            jax.ShapeDtypeStruct((walk, cut + rest, nocc), jnp.bfloat16),
+            jax.ShapeDtypeStruct((1, walk), jnp.float32),
+        ],
+        cost_estimate=FREE,
         compiler_params=params(16),
         name="place_walkers",
     )(*in_vmem(*z_first, *plane_first))
@@ -363,6 +394,7 @@
     turned, partial_bias, mine = bias_call(chol_vals, greens, walkers, cols, own)
     start = around_orb(mine)
     bias, *others = around_orb(partial_bias)
+    start, others = lax.optimization_barrier((start, others))
 
     total_steps = rowblocks * BLOCK // CHUNK
     early_steps = total_steps * 3 // 8
@@ -370,20 +402,13 @@
     fields_t = fields.T
     early, energy = potential_call(0, early_steps, layout, False, fields_t, bias, others, cols, turned)
     early_in = [early[0]] + [to_z(early[dz], dz) for dz in range(1, nz)]
-    late, _ = potential_call(early_steps, late_steps, layout, True, fields_t, bias, others, cols, turned)
+    late, _ = potential_call(early_steps, late_steps, layout, True, fields_t, bias, others, cols, turned, [energy])
     late_in = [late[0]] + [to_plane(late[dp], dp) for dp in range(1, plane)]
-    energy = energy[:, 0]
-    energy_in = [to_plane(energy, dp) for dp in range(1, plane)]
-    start, energy_in, early_in = lax.optimization_barrier((start, energy_in, early_in))
-    energy = energy + sum(energy_in)
     early_sums = sum_call(early_in)
     early_in = [early_sums[0]] + [to_plane(early_sums[dp], dp) for dp in range(1, plane)]
     late_sums = sum_call(late_in)
     late_in = [late_sums[0]] + [to_z(late_sums[dz], dz) for dz in range(1, nz)]
 
-    energy_in = [to_z(energy, dz) for dz in range(1, nz)]
-    energy_in, late_in = lax.optimization_barrier((energy_in, late_in))
-    energy = energy + sum(energy_in)
 
     def finish(arrays):
         total = arrays[0].astype(jnp.float32)
@@ -392,13 +417,14 @@
         return around_orb((step_factor * total).astype(jnp.bfloat16))
 
     cut = half_rows // CHUNK * 5 // 8 * CHUNK
-    b_part, a_part = series_call((n_orb, late_steps, early_steps), cut, finish(late_in), finish(early_in), start)
+    b_part, a_part = series_call((n_orb, late_steps, early_steps), cut, finish(late_in), finish(early_in), start, energy)
 
     a_all = jnp.stack([a_part] + [to_z(a_part, dz) for dz in range(1, nz)])
     b_all = jnp.stack([b_part] + [to_plane(b_part, dp) for dp in range(1, plane)])
     z_first = [a_all] + [to_plane(a_all, dp) for dp in range(1, plane)]
     plane_first = [b_all] + [to_z(b_all, dz) for dz in range(1, nz)]
-    return place_call(layout, z_first, plane_first), energy
+    moved, energy = place_call(layout, z_first, plane_first)
+    return moved, energy.reshape(walk)
 
 
 def solution(mesh):

time: 107 us -> 79.2 us (0.74)
  waiting for transfers between devices: 42 us -> 19.3 us
  starting transfers between devices: 46.1 us -> 41.4 us
    ppermute x15 -> x12, waiting for transfers between devices: 22.4 us -> 10.3 us  [to_plane(): lax.ppermute(a, 'chol', [(c, c // plane * plane + (c % plane ^ dp)) for c...]
    ppermute x15 -> x12, waiting for transfers between devices: 16.2 us -> 6.59 us  [to_z(): lax.ppermute(a, 'chol', [(c, (c // plane + dz) % nz * plane + c % plane)...]
    ppermute x15 -> x12, starting transfers between devices: 20.5 us -> 14.8 us  [to_plane(): lax.ppermute(a, 'chol', [(c, c // plane * plane + (c % plane ^ dp)) for c...]
    ppermute x15 -> x12, starting transfers between devices: 24.9 us -> 25.9 us  [to_z(): lax.ppermute(a, 'chol', [(c, (c // plane + dz) % nz * plane + c % plane)...]
  transfers between devices with their start and end apart: 34 -> 28, of which waited for: 16 -> 11; matrix products, arithmetic and copies ran while one was open for 1% -> 0% of each run, Pallas kernels for 4% -> 0%
where the time goes in v5:
time: 79.2 us; the launch traced here: 79 us
  starting transfers between devices  41.4 us (52%)
  waiting for transfers between devices  19.3 us (24%)
  Pallas kernels  16.7 us (21%)
    ppermute x12, starting transfers between devices, to_z(): lax.ppermute(a, 'chol', [(c, (c // plane + dz) % nz * plane + c % plane)...  25.9 us
    ppermute x12, starting transfers between devices, to_plane(): lax.ppermute(a, 'chol', [(c, c // plane * plane + (c % plane ^ dp)) for c...  14.8 us
    ppermute x12, waiting for transfers between devices, to_plane(): lax.ppermute(a, 'chol', [(c, c // plane * plane + (c % plane ^ dp)) for c...  10.3 us
    pallas_call x1, Pallas kernels, bias_call(): pl.pallas_call(bias_kernel, in_specs=[*[pl.BlockSpec(memory_space=pl.ANY)...  8.49 us
    ppermute x12, waiting for transfers between devices, to_z(): lax.ppermute(a, 'chol', [(c, (c // plane + dz) % nz * plane + c % plane)...  6.59 us
    pallas_call x2, Pallas kernels, potential_call(): pl.pallas_call(functools.partial(potential_kernel, start, steps, layout,...  5.62 us
    ppermute x4, waiting for transfers between devices, around_orb(): lax.ppermute(a, 'orb', [((c + d) % n_orb, c) for c in range(n_orb)])  2.35 us
  transfers between devices with their start and end apart: 28, of which 11 were waited for; matrix products, arithmetic and copies ran while one was open for 0% of the time, Pallas kernels for 0%

profile of v5, /device:TPU:0, one launch (start us, length us, event | category | flops | bytes accessed | tf_op | source)
XLA Modules:
  0.0 79.0 jit_solution(5240727748015000750)
XLA Ops:
  0.7 0.7 copy-done.1
  1.3 8.5 %force_bias.1 = (bf16[8,256,2048]{2,1,0:T(8,128)(2,1)S(1)}, f32[32,256]{1,0:T(8,128)S(1)}, bf16[2,128,128]{2,1,0:T(8,128)(2,1)S(1)}) custom-call(bf16[256,2,64,128]{3,2,1,0:T(8,128)(2,1)} %vals_hbm.1, bf16[32,128,256]{2,1,0:T(8,128)(2,1)} %greens_hbm.1, bf16[32,128,128]{2,1,0:T(8,128)(2,1)} %walkers_hbm.1, s32[2,2,256]{2,1,0:T(2,128)S(1)} %bitcast.14), custom_call_target="tpu_custom_call" | custom-call | tf_op jit(solution)/shard_map/force_bias/pallas_call | solution.py:142
  9.8 0.5 collective-permute-start
  10.3 0.1 collective-permute-start.1
  10.4 1.1 %collective-permute-done.1.refs_0_.refs_1_ = f32[32,256]{1,0:T(8,128)S(1)} collective-permute-done((f32[32,256]{1,0:T(8,128)S(1)}, f32[32,256]{1,0:T(8,128)S(1)}, u32[]{:S(2)}, u32[]{:S(2)}) %collective-permute-start.1) | collective-permute-done | bytes 32800 | tf_op jit(solution)/shard_map/ppermute | solution.py:391
  11.6 0.0 collective-permute-done.refs_5_
  11.6 1.9 %potential.2 = (bf16[4,2,96,128]{3,2,1,0:T(8,128)(2,1)S(1)}, bf16[4,2,96,128]{3,2,1,0:T(8,128)(2,1)S(1)}, bf16[4,2,96,128]{3,2,1,0:T(8,128)(2,1)S(1)}, bf16[4,2,96,128]{3,2,1,0:T(8,128)(2,1)S(1)}, f32[16,128]{1,0:T(8,128)S(1)}) custom-call(f32[32,256]{1,0:T(8,128)S(1)} %bitcast.11, f32[32,256]{1,0:T(8,128)S(1)} %get-tuple-element.29.own_ref, ...), custom_call_target="tpu_custom_call" | custom-call | tf_op jit(solution)/shard_map/potential/pallas_call | solution.py:238
  13.5 3.7 %potential.3 = (bf16[4,2,160,128]{3,2,1,0:T(8,128)(2,1)S(1)}, bf16[4,2,160,128]{3,2,1,0:T(8,128)(2,1)S(1)}, bf16[4,2,160,128]{3,2,1,0:T(8,128)(2,1)S(1)}, bf16[4,2,160,128]{3,2,1,0:T(8,128)(2,1)S(1)}, f32[16,128]{1,0:T(8,128)}) custom-call(f32[32,256]{1,0:T(8,128)S(1)} %bitcast.12, f32[32,256]{1,0:T(8,128)S(1)} %get-tuple-element.29.own_ref, ...), custom_call_target="tpu_custom_call" | custom-call | tf_op jit(solution)/shard_map/potential/pallas_call | solution.py:238
  17.2 2.7 %collective-permute-start.2 = (bf16[4,2,160,128]{3,2,1,0:T(8,128)(2,1)S(1)}, bf16[4,2,160,128]{3,2,1,0:T(8,128)(2,1)S(1)}, u32[]{:S(2)}, u32[]{:S(2)}) collective-permute-start(bf16[4,2,160,128]{3,2,1,0:T(8,128)(2,1)S(1)} %get-tuple-element.35), channel_id=1, source_target_pairs={{0,2},{2,0},{4,6},{6,4},{8,10},{10,8},{12,14},{14,12},{16,18},{18,... | collective-permute-start | bytes 983048 | tf_op jit(solution)/shard_map/ppermute | solution.py:385
  19.8 1.5 %collective-permute-start.3 = (bf16[4,2,160,128]{3,2,1,0:T(8,128)(2,1)S(1)}, bf16[4,2,160,128]{3,2,1,0:T(8,128)(2,1)S(1)}, u32[]{:S(2)}, u32[]{:S(2)}) collective-permute-start(bf16[4,2,160,128]{3,2,1,0:T(8,128)(2,1)S(1)} %get-tuple-element.36), channel_id=1, source_target_pairs={{0,4},{2,6},{4,0},{6,2},{8,12},{10,14},{12,8},{14,10},{16,20},{18,... | collective-permute-start | bytes 983048 | tf_op jit(solution)/shard_map/ppermute | solution.py:385
  21.4 0.0 collective-permute-start.4
  21.4 3.1 %collective-permute-start.10 = (bf16[4,2,96,128]{3,2,1,0:T(8,128)(2,1)S(1)}, bf16[4,2,96,128]{3,2,1,0:T(8,128)(2,1)S(1)}, u32[]{:S(2)}, u32[]{:S(2)}) collective-permute-start(bf16[4,2,96,128]{3,2,1,0:T(8,128)(2,1)S(1)} %get-tuple-element.44), channel_id=1, source_target_pairs={{0,16},{2,18},{4,20},{6,22},{8,24},{10,26},{12,28},{14,30},{16,0},... | collective-permute-start | bytes 589832 | tf_op jit(solution)/shard_map/ppermute | solution.py:388
  24.4 1.3 %collective-permute-start.11 = (bf16[4,2,96,128]{3,2,1,0:T(8,128)(2,1)S(1)}, bf16[4,2,96,128]{3,2,1,0:T(8,128)(2,1)S(1)}, u32[]{:S(2)}, u32[]{:S(2)}) collective-permute-start(bf16[4,2,96,128]{3,2,1,0:T(8,128)(2,1)S(1)} %get-tuple-element.45), channel_id=1, source_target_pairs={{0,24},{2,26},{4,28},{6,30},{8,0},{10,2},{12,4},{14,6},{16,8},{18,... | collective-permute-start | bytes 589832 | tf_op jit(solution)/shard_map/ppermute | solution.py:388
  25.8 2.6 %collective-permute-done.2.refs_1_ = bf16[4,2,160,128]{3,2,1,0:T(8,128)(2,1)S(1)} collective-permute-done((bf16[4,2,160,128]{3,2,1,0:T(8,128)(2,1)S(1)}, bf16[4,2,160,128]{3,2,1,0:T(8,128)(2,1)S(1)}, u32[]{:S(2)}, u32[]{:S(2)}) %collective-permute-start.2) | collective-permute-done | bytes 327712 | tf_op jit(solution)/shard_map/ppermute | solution.py:385
  28.4 2.1 %collective-permute-start.9 = (bf16[4,2,96,128]{3,2,1,0:T(8,128)(2,1)S(1)}, bf16[4,2,96,128]{3,2,1,0:T(8,128)(2,1)S(1)}, u32[]{:S(2)}, u32[]{:S(2)}) collective-permute-start(bf16[4,2,96,128]{3,2,1,0:T(8,128)(2,1)S(1)} %get-tuple-element.43), channel_id=1, source_target_pairs={{0,8},{2,10},{4,12},{6,14},{8,16},{10,18},{12,20},{14,22},{16,24},... | collective-permute-start | bytes 589832 | tf_op jit(solution)/shard_map/ppermute | solution.py:388
  30.5 6.1 %collective-permute-done.3.refs_2_ = bf16[4,2,160,128]{3,2,1,0:T(8,128)(2,1)S(1)} collective-permute-done((bf16[4,2,160,128]{3,2,1,0:T(8,128)(2,1)S(1)}, bf16[4,2,160,128]{3,2,1,0:T(8,128)(2,1)S(1)}, u32[]{:S(2)}, u32[]{:S(2)}) %collective-permute-start.3) | collective-permute-done | bytes 327712 | tf_op jit(solution)/shard_map/ppermute | solution.py:385
  36.6 0.0 collective-permute-done.4.refs_3_
  36.6 0.2 sum_parts.2
  36.7 1.6 %collective-permute-start.5 = (bf16[2,160,128]{2,1,0:T(8,128)(2,1)S(1)}, bf16[2,160,128]{2,1,0:T(8,128)(2,1)S(1)}, u32[]{:S(2)}, u32[]{:S(2)}) collective-permute-start(bf16[2,160,128]{2,1,0:T(8,128)(2,1)S(1)} %get-tuple-element.39), channel_id=1, source_target_pairs={{0,8},{2,10},{4,12},{6,14},{8,16},{10,18},{12,20},{14,22},{16,24},... | collective-permute-start | bytes 245768 | tf_op jit(solution)/shard_map/ppermute | solution.py:388
  38.4 2.6 %collective-permute-start.6 = (bf16[2,160,128]{2,1,0:T(8,128)(2,1)S(1)}, bf16[2,160,128]{2,1,0:T(8,128)(2,1)S(1)}, u32[]{:S(2)}, u32[]{:S(2)}) collective-permute-start(bf16[2,160,128]{2,1,0:T(8,128)(2,1)S(1)} %get-tuple-element.40), channel_id=1, source_target_pairs={{0,16},{2,18},{4,20},{6,22},{8,24},{10,26},{12,28},{14,30},{16,0},... | collective-permute-start | bytes 245768 | tf_op jit(solution)/shard_map/ppermute | solution.py:388
  40.9 0.0 collective-permute-done.10.refs_2_
  40.9 1.4 %collective-permute-start.7 = (bf16[2,160,128]{2,1,0:T(8,128)(2,1)S(1)}, bf16[2,160,128]{2,1,0:T(8,128)(2,1)S(1)}, u32[]{:S(2)}, u32[]{:S(2)}) collective-permute-start(bf16[2,160,128]{2,1,0:T(8,128)(2,1)S(1)} %get-tuple-element.41), channel_id=1, source_target_pairs={{0,24},{2,26},{4,28},{6,30},{8,0},{10,2},{12,4},{14,6},{16,8},{18,... | collective-permute-start | bytes 245768 | tf_op jit(solution)/shard_map/ppermute | solution.py:388
  42.3 0.0 collective-permute-done.11.refs_3_
  42.3 0.0 collective-permute-done.9.refs_1_
  42.3 0.1 sum_parts.3
  42.4 1.3 %collective-permute-start.12 = (bf16[2,96,128]{2,1,0:T(8,128)(2,1)S(1)}, bf16[2,96,128]{2,1,0:T(8,128)(2,1)S(1)}, u32[]{:S(2)}, u32[]{:S(2)}) collective-permute-start(bf16[2,96,128]{2,1,0:T(8,128)(2,1)S(1)} %get-tuple-element.47), channel_id=1, source_target_pairs={{0,2},{2,0},{4,6},{6,4},{8,10},{10,8},{12,14},{14,12},{16,18},{18,... | collective-permute-start | bytes 147464 | tf_op jit(solution)/shard_map/ppermute | solution.py:385
  43.7 0.8 %collective-permute-start.13 = (bf16[2,96,128]{2,1,0:T(8,128)(2,1)S(1)}, bf16[2,96,128]{2,1,0:T(8,128)(2,1)S(1)}, u32[]{:S(2)}, u32[]{:S(2)}) collective-permute-start(bf16[2,96,128]{2,1,0:T(8,128)(2,1)S(1)} %get-tuple-element.48), channel_id=1, source_target_pairs={{0,4},{2,6},{4,0},{6,2},{8,12},{10,14},{12,8},{14,10},{16,20},{18,... | collective-permute-start | bytes 147464 | tf_op jit(solution)/shard_map/ppermute | solution.py:385
  44.5 0.0 collective-permute-done.5
  44.5 1.4 %collective-permute-start.14 = (bf16[2,96,128]{2,1,0:T(8,128)(2,1)S(1)}, bf16[2,96,128]{2,1,0:T(8,128)(2,1)S(1)}, u32[]{:S(2)}, u32[]{:S(2)}) collective-permute-start(bf16[2,96,128]{2,1,0:T(8,128)(2,1)S(1)} %get-tuple-element.49), channel_id=1, source_target_pairs={{0,6},{2,4},{4,2},{6,0},{8,14},{10,12},{12,10},{14,8},{16,22},{18,... | collective-permute-start | bytes 147464 | tf_op jit(solution)/shard_map/ppermute | solution.py:385
  46.0 1.8 %collective-permute-done.6 = bf16[2,160,128]{2,1,0:T(8,128)(2,1)S(1)} collective-permute-done((bf16[2,160,128]{2,1,0:T(8,128)(2,1)S(1)}, bf16[2,160,128]{2,1,0:T(8,128)(2,1)S(1)}, u32[]{:S(2)}, u32[]{:S(2)}) %collective-permute-start.6) | collective-permute-done | bytes 81952 | tf_op jit(solution)/shard_map/ppermute | solution.py:388
  47.8 0.0 collective-permute-done.7
  47.8 0.1 multiply_convert_fusion.refs_0_
  47.8 0.1 collective-permute-start.8
  47.9 0.0 collective-permute-done.12
  47.9 0.1 collective-permute-done.13
  48.1 1.5 %collective-permute-done.14 = bf16[2,96,128]{2,1,0:T(8,128)(2,1)S(1)} collective-permute-done((bf16[2,96,128]{2,1,0:T(8,128)(2,1)S(1)}, bf16[2,96,128]{2,1,0:T(8,128)(2,1)S(1)}, u32[]{:S(2)}, u32[]{:S(2)}) %collective-permute-start.14) | collective-permute-done | bytes 49184 | tf_op jit(solution)/shard_map/ppermute | solution.py:385
  49.6 0.1 collective-permute-start.15
  49.6 1.2 %collective-permute-done.15.refs_3_ = bf16[2,96,128]{2,1,0:T(8,128)(2,1)S(1)} collective-permute-done((bf16[2,96,128]{2,1,0:T(8,128)(2,1)S(1)}, bf16[2,96,128]{2,1,0:T(8,128)(2,1)S(1)}, u32[]{:S(2)}, u32[]{:S(2)}) %collective-permute-start.15) | collective-permute-done | bytes 49184 | tf_op jit(solution)/shard_map/ppermute | solution.py:391
  50.9 0.0 collective-permute-done.8.refs_1_
  50.9 1.3 %series.1 = (bf16[2,48,128]{2,1,0:T(8,128)(2,1)S(1)}, bf16[176,128]{1,0:T(8,128)(2,1)S(1)}) custom-call(bf16[2,160,128]{2,1,0:T(8,128)(2,1)S(1)} %multiply_convert_fusion.refs_0_, bf16[2,160,128]{2,1,0:T(8,128)(2,1)S(1)} %collective-permute-done.8.refs_1_, bf16[2,96,128]{2,1,0:T(8,128)(2,1)S(1)} %multiply_convert_fusion.1.refs_2_, ...), custom_call_target="tpu_custom_call" | custom-call | tf_op jit(solution)/shard_map/series/pallas_call | solution.py:322
  52.1 1.6 %collective-permute-start.22 = (bf16[2,48,128]{2,1,0:T(8,128)(2,1)S(1)}, bf16[2,48,128]{2,1,0:T(8,128)(2,1)S(1)}, u32[]{:S(2)}, u32[]{:S(2)}) collective-permute-start(bf16[2,48,128]{2,1,0:T(8,128)(2,1)S(1)} %get-tuple-element.53), channel_id=1, source_target_pairs={{0,2},{2,0},{4,6},{6,4},{8,10},{10,8},{12,14},{14,12},{16,18},{18,... | collective-permute-start | bytes 73736 | tf_op jit(solution)/shard_map/ppermute | solution.py:385
  53.7 0.5 collective-permute-start.23
  54.2 1.5 %collective-permute-start.24 = (bf16[2,48,128]{2,1,0:T(8,128)(2,1)S(1)}, bf16[2,48,128]{2,1,0:T(8,128)(2,1)S(1)}, u32[]{:S(2)}, u32[]{:S(2)}) collective-permute-start(bf16[2,48,128]{2,1,0:T(8,128)(2,1)S(1)} %get-tuple-element.53), channel_id=1, source_target_pairs={{0,6},{2,4},{4,2},{6,0},{8,14},{10,12},{12,10},{14,8},{16,22},{18,... | collective-permute-start | bytes 73736 | tf_op jit(solution)/shard_map/ppermute | solution.py:385
  55.7 5.6 %collective-permute-start.16 = (bf16[176,128]{1,0:T(8,128)(2,1)S(1)}, bf16[176,128]{1,0:T(8,128)(2,1)S(1)}, u32[]{:S(2)}, u32[]{:S(2)}) collective-permute-start(bf16[176,128]{1,0:T(8,128)(2,1)S(1)} %get-tuple-element.52), channel_id=1, source_target_pairs={{0,8},{2,10},{4,12},{6,14},{8,16},{10,18},{12,20},{14,22},{16,24},... | collective-permute-start | bytes 135176 | tf_op jit(solution)/shard_map/ppermute | solution.py:388
  61.3 1.0 %collective-permute-start.17 = (bf16[176,128]{1,0:T(8,128)(2,1)S(1)}, bf16[176,128]{1,0:T(8,128)(2,1)S(1)}, u32[]{:S(2)}, u32[]{:S(2)}) collective-permute-start(bf16[176,128]{1,0:T(8,128)(2,1)S(1)} %get-tuple-element.52), channel_id=1, source_target_pairs={{0,16},{2,18},{4,20},{6,22},{8,24},{10,26},{12,28},{14,30},{16,0},... | collective-permute-start | bytes 135176 | tf_op jit(solution)/shard_map/ppermute | solution.py:388
  62.3 0.0 collective-permute-done.22
  62.3 2.9 %collective-permute-start.18 = (bf16[176,128]{1,0:T(8,128)(2,1)S(1)}, bf16[176,128]{1,0:T(8,128)(2,1)S(1)}, u32[]{:S(2)}, u32[]{:S(2)}) collective-permute-start(bf16[176,128]{1,0:T(8,128)(2,1)S(1)} %get-tuple-element.52), channel_id=1, source_target_pairs={{0,24},{2,26},{4,28},{6,30},{8,0},{10,2},{12,4},{14,6},{16,8},{18,... | collective-permute-start | bytes 135176 | tf_op jit(solution)/shard_map/ppermute | solution.py:388
  65.2 0.0 collective-permute-done.23
  65.2 0.0 collective-permute-done.24
  65.2 0.1 collective-permute-start.25
  65.3 0.0 collective-permute-done.16
  65.3 1.0 %collective-permute-done.17 = bf16[176,128]{1,0:T(8,128)(2,1)S(1)} collective-permute-done((bf16[176,128]{1,0:T(8,128)(2,1)S(1)}, bf16[176,128]{1,0:T(8,128)(2,1)S(1)}, u32[]{:S(2)}, u32[]{:S(2)}) %collective-permute-start.17) | collective-permute-done | bytes 45088 | tf_op jit(solution)/shard_map/ppermute | solution.py:388
  66.3 0.6 collective-permute-done.18
  67.0 0.6 collective-permute-start.19
  67.5 1.1 %collective-permute-start.20 = (bf16[4,176,128]{2,1,0:T(8,128)(2,1)S(1)}, bf16[4,176,128]{2,1,0:T(8,128)(2,1)S(1)}, u32[]{:S(2)}, u32[]{:S(2)}) collective-permute-start(bf16[4,176,128]{2,1,0:T(8,128)(2,1)S(1)} %pad_maximum_fusion.refs_0_), channel_id=1, source_target_pairs={{0,4},{2,6},{4,0},{6,2},{8,12},{10,14},{12,8},{14,10},{16,20},{18,... | collective-permute-start | bytes 540680 | tf_op jit(solution)/shard_map/ppermute | solution.py:385
  68.6 1.9 %collective-permute-start.21 = (bf16[4,176,128]{2,1,0:T(8,128)(2,1)S(1)}, bf16[4,176,128]{2,1,0:T(8,128)(2,1)S(1)}, u32[]{:S(2)}, u32[]{:S(2)}) collective-permute-start(bf16[4,176,128]{2,1,0:T(8,128)(2,1)S(1)} %pad_maximum_fusion.refs_0_), channel_id=1, source_target_pairs={{0,6},{2,4},{4,2},{6,0},{8,14},{10,12},{12,10},{14,8},{16,22},{18,... | collective-permute-start | bytes 540680 | tf_op jit(solution)/shard_map/ppermute | solution.py:385
  70.5 1.3 %collective-permute-start.26 = (bf16[4,2,48,128]{3,2,1,0:T(8,128)(2,1)S(1)}, bf16[4,2,48,128]{3,2,1,0:T(8,128)(2,1)S(1)}, u32[]{:S(2)}, u32[]{:S(2)}) collective-permute-start(bf16[4,2,48,128]{3,2,1,0:T(8,128)(2,1)S(1)} %pad_maximum_fusion.1.refs_4_), channel_id=1, source_target_pairs={{0,16},{2,18},{4,20},{6,22},{8,24},{10,26},{12,28},{14,30},{16,0},... | collective-permute-start | bytes 294920 | tf_op jit(solution)/shard_map/ppermute | solution.py:388
  71.9 0.0 collective-permute-done.25.refs_5_
  71.9 2.9 %collective-permute-start.27 = (bf16[4,2,48,128]{3,2,1,0:T(8,128)(2,1)S(1)}, bf16[4,2,48,128]{3,2,1,0:T(8,128)(2,1)S(1)}, u32[]{:S(2)}, u32[]{:S(2)}) collective-permute-start(bf16[4,2,48,128]{3,2,1,0:T(8,128)(2,1)S(1)} %pad_maximum_fusion.1.refs_4_), channel_id=1, source_target_pairs={{0,24},{2,26},{4,28},{6,30},{8,0},{10,2},{12,4},{14,6},{16,8},{18,... | collective-permute-start | bytes 294920 | tf_op jit(solution)/shard_map/ppermute | solution.py:388
  74.7 1.3 %collective-permute-done.26.refs_6_ = bf16[4,2,48,128]{3,2,1,0:T(8,128)(2,1)S(1)} collective-permute-done((bf16[4,2,48,128]{3,2,1,0:T(8,128)(2,1)S(1)}, bf16[4,2,48,128]{3,2,1,0:T(8,128)(2,1)S(1)}, u32[]{:S(2)}, u32[]{:S(2)}) %collective-permute-start.26) | collective-permute-done | bytes 98336 | tf_op jit(solution)/shard_map/ppermute | solution.py:388
  76.0 1.9 %collective-permute-done.27.refs_7_ = bf16[4,2,48,128]{3,2,1,0:T(8,128)(2,1)S(1)} collective-permute-done((bf16[4,2,48,128]{3,2,1,0:T(8,128)(2,1)S(1)}, bf16[4,2,48,128]{3,2,1,0:T(8,128)(2,1)S(1)}, u32[]{:S(2)}, u32[]{:S(2)}) %collective-permute-start.27) | collective-permute-done | bytes 98336 | tf_op jit(solution)/shard_map/ppermute | solution.py:388
  77.9 0.0 collective-permute-done.20.refs_2_
  77.9 0.0 collective-permute-done.21.refs_3_
  77.9 1.1 %place_walkers.1 = (bf16[32,128,128]{2,1,0:T(8,128)(2,1)}, f32[1,32]{1,0:T(1,128)}) custom-call(bf16[4,176,128]{2,1,0:T(8,128)(2,1)S(1)} %pad_maximum_fusion.refs_0_, bf16[4,176,128]{2,1,0:T(8,128)(2,1)S(1)} %collective-permute-done.19.refs_1_, bf16[4,176,128]{2,1,0:T(8,128)(2,1)S(1)} %collective-permute-done.20.refs_2_, ...), custom_call_target="tpu_custom_call" | custom-call | tf_op jit(solution)/shard_map/place_walkers/pallas_call | solution.py:361
  (7 shorter events, 0.1 us)
Async XLA Ops:
  0.6 10.9 %copy-start = (f32[256,32]{0,1:T(8,128)S(1)}, f32[256,32]{0,1:T(8,128)}, u32[]{:S(2)}) copy-start(f32[256,32]{0,1:T(8,128)} %param.9) | copy-start | bytes 98308
  0.6 0.7 copy-start.1
  9.8 1.7 %collective-permute-start = (bf16[2,128,128]{2,1,0:T(8,128)(2,1)S(1)}, bf16[2,128,128]{2,1,0:T(8,128)(2,1)S(1)}, u32[]{:S(2)}, u32[]{:S(2)}) collective-permute-start(bf16[2,128,128]{2,1,0:T(8,128)(2,1)S(1)} %get-tuple-element.50.refs_4_), channel_id=1, source_target_pairs={{1,0},{0,1},{3,2},{2,3},{5,4},{4,5},{7,6},{6,7},{9,8},{8,9},{11,10... | collective-permute-start | bytes 196616 | tf_op jit(solution)/shard_map/ppermute | solution.py:391
  10.3 1.2 %collective-permute-start.1 = (f32[32,256]{1,0:T(8,128)S(1)}, f32[32,256]{1,0:T(8,128)S(1)}, u32[]{:S(2)}, u32[]{:S(2)}) collective-permute-start(f32[32,256]{1,0:T(8,128)S(1)} %get-tuple-element.29.own_ref), channel_id=1, source_target_pairs={{1,0},{0,1},{3,2},{2,3},{5,4},{4,5},{7,6},{6,7},{9,8},{8,9},{11,10... | collective-permute-start | bytes 98312 | tf_op jit(solution)/shard_map/ppermute | solution.py:391
  17.2 11.2 %collective-permute-start.2 = (bf16[4,2,160,128]{3,2,1,0:T(8,128)(2,1)S(1)}, bf16[4,2,160,128]{3,2,1,0:T(8,128)(2,1)S(1)}, u32[]{:S(2)}, u32[]{:S(2)}) collective-permute-start(bf16[4,2,160,128]{3,2,1,0:T(8,128)(2,1)S(1)} %get-tuple-element.35), channel_id=1, source_target_pairs={{0,2},{2,0},{4,6},{6,4},{8,10},{10,8},{12,14},{14,12},{16,18},{18,... | collective-permute-start | bytes 983048 | tf_op jit(solution)/shard_map/ppermute | solution.py:385
  19.8 16.7 %collective-permute-start.3 = (bf16[4,2,160,128]{3,2,1,0:T(8,128)(2,1)S(1)}, bf16[4,2,160,128]{3,2,1,0:T(8,128)(2,1)S(1)}, u32[]{:S(2)}, u32[]{:S(2)}) collective-permute-start(bf16[4,2,160,128]{3,2,1,0:T(8,128)(2,1)S(1)} %get-tuple-element.36), channel_id=1, source_target_pairs={{0,4},{2,6},{4,0},{6,2},{8,12},{10,14},{12,8},{14,10},{16,20},{18,... | collective-permute-start | bytes 983048 | tf_op jit(solution)/shard_map/ppermute | solution.py:385
  21.4 15.2 %collective-permute-start.4 = (bf16[4,2,160,128]{3,2,1,0:T(8,128)(2,1)S(1)}, bf16[4,2,160,128]{3,2,1,0:T(8,128)(2,1)S(1)}, u32[]{:S(2)}, u32[]{:S(2)}) collective-permute-start(bf16[4,2,160,128]{3,2,1,0:T(8,128)(2,1)S(1)} %get-tuple-element.37), channel_id=1, source_target_pairs={{0,6},{2,4},{4,2},{6,0},{8,14},{10,12},{12,10},{14,8},{16,22},{18,... | collective-permute-start | bytes 983048 | tf_op jit(solution)/shard_map/ppermute | solution.py:385
  21.4 19.6 %collective-permute-start.10 = (bf16[4,2,96,128]{3,2,1,0:T(8,128)(2,1)S(1)}, bf16[4,2,96,128]{3,2,1,0:T(8,128)(2,1)S(1)}, u32[]{:S(2)}, u32[]{:S(2)}) collective-permute-start(bf16[4,2,96,128]{3,2,1,0:T(8,128)(2,1)S(1)} %get-tuple-element.44), channel_id=1, source_target_pairs={{0,16},{2,18},{4,20},{6,22},{8,24},{10,26},{12,28},{14,30},{16,0},... | collective-permute-start | bytes 589832 | tf_op jit(solution)/shard_map/ppermute | solution.py:388
  24.4 17.9 %collective-permute-start.11 = (bf16[4,2,96,128]{3,2,1,0:T(8,128)(2,1)S(1)}, bf16[4,2,96,128]{3,2,1,0:T(8,128)(2,1)S(1)}, u32[]{:S(2)}, u32[]{:S(2)}) collective-permute-start(bf16[4,2,96,128]{3,2,1,0:T(8,128)(2,1)S(1)} %get-tuple-element.45), channel_id=1, source_target_pairs={{0,24},{2,26},{4,28},{6,30},{8,0},{10,2},{12,4},{14,6},{16,8},{18,... | collective-permute-start | bytes 589832 | tf_op jit(solution)/shard_map/ppermute | solution.py:388
  28.4 13.9 %collective-permute-start.9 = (bf16[4,2,96,128]{3,2,1,0:T(8,128)(2,1)S(1)}, bf16[4,2,96,128]{3,2,1,0:T(8,128)(2,1)S(1)}, u32[]{:S(2)}, u32[]{:S(2)}) collective-permute-start(bf16[4,2,96,128]{3,2,1,0:T(8,128)(2,1)S(1)} %get-tuple-element.43), channel_id=1, source_target_pairs={{0,8},{2,10},{4,12},{6,14},{8,16},{10,18},{12,20},{14,22},{16,24},... | collective-permute-start | bytes 589832 | tf_op jit(solution)/shard_map/ppermute | solution.py:388
  36.7 7.8 %collective-permute-start.5 = (bf16[2,160,128]{2,1,0:T(8,128)(2,1)S(1)}, bf16[2,160,128]{2,1,0:T(8,128)(2,1)S(1)}, u32[]{:S(2)}, u32[]{:S(2)}) collective-permute-start(bf16[2,160,128]{2,1,0:T(8,128)(2,1)S(1)} %get-tuple-element.39), channel_id=1, source_target_pairs={{0,8},{2,10},{4,12},{6,14},{8,16},{10,18},{12,20},{14,22},{16,24},... | collective-permute-start | bytes 245768 | tf_op jit(solution)/shard_map/ppermute | solution.py:388
  38.4 9.4 %collective-permute-start.6 = (bf16[2,160,128]{2,1,0:T(8,128)(2,1)S(1)}, bf16[2,160,128]{2,1,0:T(8,128)(2,1)S(1)}, u32[]{:S(2)}, u32[]{:S(2)}) collective-permute-start(bf16[2,160,128]{2,1,0:T(8,128)(2,1)S(1)} %get-tuple-element.40), channel_id=1, source_target_pairs={{0,16},{2,18},{4,20},{6,22},{8,24},{10,26},{12,28},{14,30},{16,0},... | collective-permute-start | bytes 245768 | tf_op jit(solution)/shard_map/ppermute | solution.py:388
  40.9 6.8 %collective-permute-start.7 = (bf16[2,160,128]{2,1,0:T(8,128)(2,1)S(1)}, bf16[2,160,128]{2,1,0:T(8,128)(2,1)S(1)}, u32[]{:S(2)}, u32[]{:S(2)}) collective-permute-start(bf16[2,160,128]{2,1,0:T(8,128)(2,1)S(1)} %get-tuple-element.41), channel_id=1, source_target_pairs={{0,24},{2,26},{4,28},{6,30},{8,0},{10,2},{12,4},{14,6},{16,8},{18,... | collective-permute-start | bytes 245768 | tf_op jit(solution)/shard_map/ppermute | solution.py:388
  42.4 5.5 %collective-permute-start.12 = (bf16[2,96,128]{2,1,0:T(8,128)(2,1)S(1)}, bf16[2,96,128]{2,1,0:T(8,128)(2,1)S(1)}, u32[]{:S(2)}, u32[]{:S(2)}) collective-permute-start(bf16[2,96,128]{2,1,0:T(8,128)(2,1)S(1)} %get-tuple-element.47), channel_id=1, source_target_pairs={{0,2},{2,0},{4,6},{6,4},{8,10},{10,8},{12,14},{14,12},{16,18},{18,... | collective-permute-start | bytes 147464 | tf_op jit(solution)/shard_map/ppermute | solution.py:385
  43.7 4.4 %collective-permute-start.13 = (bf16[2,96,128]{2,1,0:T(8,128)(2,1)S(1)}, bf16[2,96,128]{2,1,0:T(8,128)(2,1)S(1)}, u32[]{:S(2)}, u32[]{:S(2)}) collective-permute-start(bf16[2,96,128]{2,1,0:T(8,128)(2,1)S(1)} %get-tuple-element.48), channel_id=1, source_target_pairs={{0,4},{2,6},{4,0},{6,2},{8,12},{10,14},{12,8},{14,10},{16,20},{18,... | collective-permute-start | bytes 147464 | tf_op jit(solution)/shard_map/ppermute | solution.py:385
  44.5 5.0 %collective-permute-start.14 = (bf16[2,96,128]{2,1,0:T(8,128)(2,1)S(1)}, bf16[2,96,128]{2,1,0:T(8,128)(2,1)S(1)}, u32[]{:S(2)}, u32[]{:S(2)}) collective-permute-start(bf16[2,96,128]{2,1,0:T(8,128)(2,1)S(1)} %get-tuple-element.49), channel_id=1, source_target_pairs={{0,6},{2,4},{4,2},{6,0},{8,14},{10,12},{12,10},{14,8},{16,22},{18,... | collective-permute-start | bytes 147464 | tf_op jit(solution)/shard_map/ppermute | solution.py:385
  47.8 3.0 %collective-permute-start.8 = (bf16[2,160,128]{2,1,0:T(8,128)(2,1)S(1)}, bf16[2,160,128]{2,1,0:T(8,128)(2,1)S(1)}, u32[]{:S(2)}, u32[]{:S(2)}) collective-permute-start(bf16[2,160,128]{2,1,0:T(8,128)(2,1)S(1)} %multiply_convert_fusion.refs_0_), channel_id=1, source_target_pairs={{1,0},{0,1},{3,2},{2,3},{5,4},{4,5},{7,6},{6,7},{9,8},{8,9},{11,10... | collective-permute-start | bytes 245768 | tf_op jit(solution)/shard_map/ppermute | solution.py:391
  49.6 1.3 %collective-permute-start.15 = (bf16[2,96,128]{2,1,0:T(8,128)(2,1)S(1)}, bf16[2,96,128]{2,1,0:T(8,128)(2,1)S(1)}, u32[]{:S(2)}, u32[]{:S(2)}) collective-permute-start(bf16[2,96,128]{2,1,0:T(8,128)(2,1)S(1)} %multiply_convert_fusion.1.refs_2_), channel_id=1, source_target_pairs={{1,0},{0,1},{3,2},{2,3},{5,4},{4,5},{7,6},{6,7},{9,8},{8,9},{11,10... | collective-permute-start | bytes 147464 | tf_op jit(solution)/shard_map/ppermute | solution.py:391
  52.1 10.1 %collective-permute-start.22 = (bf16[2,48,128]{2,1,0:T(8,128)(2,1)S(1)}, bf16[2,48,128]{2,1,0:T(8,128)(2,1)S(1)}, u32[]{:S(2)}, u32[]{:S(2)}) collective-permute-start(bf16[2,48,128]{2,1,0:T(8,128)(2,1)S(1)} %get-tuple-element.53), channel_id=1, source_target_pairs={{0,2},{2,0},{4,6},{6,4},{8,10},{10,8},{12,14},{14,12},{16,18},{18,... | collective-permute-start | bytes 73736 | tf_op jit(solution)/shard_map/ppermute | solution.py:385
  53.7 11.5 %collective-permute-start.23 = (bf16[2,48,128]{2,1,0:T(8,128)(2,1)S(1)}, bf16[2,48,128]{2,1,0:T(8,128)(2,1)S(1)}, u32[]{:S(2)}, u32[]{:S(2)}) collective-permute-start(bf16[2,48,128]{2,1,0:T(8,128)(2,1)S(1)} %get-tuple-element.53), channel_id=1, source_target_pairs={{0,4},{2,6},{4,0},{6,2},{8,12},{10,14},{12,8},{14,10},{16,20},{18,... | collective-permute-start | bytes 73736 | tf_op jit(solution)/shard_map/ppermute | solution.py:385
  54.2 11.0 %collective-permute-start.24 = (bf16[2,48,128]{2,1,0:T(8,128)(2,1)S(1)}, bf16[2,48,128]{2,1,0:T(8,128)(2,1)S(1)}, u32[]{:S(2)}, u32[]{:S(2)}) collective-permute-start(bf16[2,48,128]{2,1,0:T(8,128)(2,1)S(1)} %get-tuple-element.53), channel_id=1, source_target_pairs={{0,6},{2,4},{4,2},{6,0},{8,14},{10,12},{12,10},{14,8},{16,22},{18,... | collective-permute-start | bytes 73736 | tf_op jit(solution)/shard_map/ppermute | solution.py:385
  55.7 9.6 %collective-permute-start.16 = (bf16[176,128]{1,0:T(8,128)(2,1)S(1)}, bf16[176,128]{1,0:T(8,128)(2,1)S(1)}, u32[]{:S(2)}, u32[]{:S(2)}) collective-permute-start(bf16[176,128]{1,0:T(8,128)(2,1)S(1)} %get-tuple-element.52), channel_id=1, source_target_pairs={{0,8},{2,10},{4,12},{6,14},{8,16},{10,18},{12,20},{14,22},{16,24},... | collective-permute-start | bytes 135176 | tf_op jit(solution)/shard_map/ppermute | solution.py:388
  61.3 5.0 %collective-permute-start.17 = (bf16[176,128]{1,0:T(8,128)(2,1)S(1)}, bf16[176,128]{1,0:T(8,128)(2,1)S(1)}, u32[]{:S(2)}, u32[]{:S(2)}) collective-permute-start(bf16[176,128]{1,0:T(8,128)(2,1)S(1)} %get-tuple-element.52), channel_id=1, source_target_pairs={{0,16},{2,18},{4,20},{6,22},{8,24},{10,26},{12,28},{14,30},{16,0},... | collective-permute-start | bytes 135176 | tf_op jit(solution)/shard_map/ppermute | solution.py:388
  62.3 4.6 %collective-permute-start.18 = (bf16[176,128]{1,0:T(8,128)(2,1)S(1)}, bf16[176,128]{1,0:T(8,128)(2,1)S(1)}, u32[]{:S(2)}, u32[]{:S(2)}) collective-permute-start(bf16[176,128]{1,0:T(8,128)(2,1)S(1)} %get-tuple-element.52), channel_id=1, source_target_pairs={{0,24},{2,26},{4,28},{6,30},{8,0},{10,2},{12,4},{14,6},{16,8},{18,... | collective-permute-start | bytes 135176 | tf_op jit(solution)/shard_map/ppermute | solution.py:388
  65.2 6.6 %collective-permute-start.25 = (bf16[4,2,48,128]{3,2,1,0:T(8,128)(2,1)S(1)}, bf16[4,2,48,128]{3,2,1,0:T(8,128)(2,1)S(1)}, u32[]{:S(2)}, u32[]{:S(2)}) collective-permute-start(bf16[4,2,48,128]{3,2,1,0:T(8,128)(2,1)S(1)} %pad_maximum_fusion.1.refs_4_), channel_id=1, source_target_pairs={{0,8},{2,10},{4,12},{6,14},{8,16},{10,18},{12,20},{14,22},{16,24},... | collective-permute-start | bytes 294920 | tf_op jit(solution)/shard_map/ppermute | solution.py:388
  67.0 11.0 %collective-permute-start.19 = (bf16[4,176,128]{2,1,0:T(8,128)(2,1)S(1)}, bf16[4,176,128]{2,1,0:T(8,128)(2,1)S(1)}, u32[]{:S(2)}, u32[]{:S(2)}) collective-permute-start(bf16[4,176,128]{2,1,0:T(8,128)(2,1)S(1)} %pad_maximum_fusion.refs_0_), channel_id=1, source_target_pairs={{0,2},{2,0},{4,6},{6,4},{8,10},{10,8},{12,14},{14,12},{16,18},{18,... | collective-permute-start | bytes 540680 | tf_op jit(solution)/shard_map/ppermute | solution.py:385
  67.5 10.4 %collective-permute-start.20 = (bf16[4,176,128]{2,1,0:T(8,128)(2,1)S(1)}, bf16[4,176,128]{2,1,0:T(8,128)(2,1)S(1)}, u32[]{:S(2)}, u32[]{:S(2)}) collective-permute-start(bf16[4,176,128]{2,1,0:T(8,128)(2,1)S(1)} %pad_maximum_fusion.refs_0_), channel_id=1, source_target_pairs={{0,4},{2,6},{4,0},{6,2},{8,12},{10,14},{12,8},{14,10},{16,20},{18,... | collective-permute-start | bytes 540680 | tf_op jit(solution)/shard_map/ppermute | solution.py:385
  68.6 9.3 %collective-permute-start.21 = (bf16[4,176,128]{2,1,0:T(8,128)(2,1)S(1)}, bf16[4,176,128]{2,1,0:T(8,128)(2,1)S(1)}, u32[]{:S(2)}, u32[]{:S(2)}) collective-permute-start(bf16[4,176,128]{2,1,0:T(8,128)(2,1)S(1)} %pad_maximum_fusion.refs_0_), channel_id=1, source_target_pairs={{0,6},{2,4},{4,2},{6,0},{8,14},{10,12},{12,10},{14,8},{16,22},{18,... | collective-permute-start | bytes 540680 | tf_op jit(solution)/shard_map/ppermute | solution.py:385
  70.5 5.5 %collective-permute-start.26 = (bf16[4,2,48,128]{3,2,1,0:T(8,128)(2,1)S(1)}, bf16[4,2,48,128]{3,2,1,0:T(8,128)(2,1)S(1)}, u32[]{:S(2)}, u32[]{:S(2)}) collective-permute-start(bf16[4,2,48,128]{3,2,1,0:T(8,128)(2,1)S(1)} %pad_maximum_fusion.1.refs_4_), channel_id=1, source_target_pairs={{0,16},{2,18},{4,20},{6,22},{8,24},{10,26},{12,28},{14,30},{16,0},... | collective-permute-start | bytes 294920 | tf_op jit(solution)/shard_map/ppermute | solution.py:388
  71.9 6.0 %collective-permute-start.27 = (bf16[4,2,48,128]{3,2,1,0:T(8,128)(2,1)S(1)}, bf16[4,2,48,128]{3,2,1,0:T(8,128)(2,1)S(1)}, u32[]{:S(2)}, u32[]{:S(2)}) collective-permute-start(bf16[4,2,48,128]{3,2,1,0:T(8,128)(2,1)S(1)} %pad_maximum_fusion.1.refs_4_), channel_id=1, source_target_pairs={{0,24},{2,26},{4,28},{6,30},{8,0},{10,2},{12,4},{14,6},{16,8},{18,... | collective-permute-start | bytes 294920 | tf_op jit(solution)/shard_map/ppermute | solution.py:388

commit v6 on v5

--- a/solution.py
+++ b/solution.py
@@ -36,6 +36,10 @@
 
 def in_hbm(*arrays):
     return [pltpu.with_memory_space_constraint(a, pltpu.HBM) for a in arrays]
+
+
+def hop(at, distance, count):
+    return at ^ distance if count & (count - 1) == 0 else (at + distance) % count
 
 
 def swap_matrix():
@@ -167,9 +171,8 @@
     )(*in_hbm(vals, greens, walkers), cols)
 
 
-def potential_kernel(start, steps, layout, by_plane, n_after, fields_ref, own_ref, *refs):
+def potential_kernel(start, steps, layout, by_plane, fields_ref, own_ref, *refs):
     nz, plane, own = layout
-    refs = refs[n_after:]
     others = refs[:lax.axis_size("orb") - 1]
     cols_ref, turned_ref = refs[len(others):len(others) + 2]
     groups = plane if by_plane else nz
@@ -189,8 +192,8 @@
     at = lax.broadcasted_iota(jnp.int32, (walk, walk), 0)
     source = lax.broadcasted_iota(jnp.int32, (walk, walk), 1)
     chip = at // own
-    z = (me // plane + chip // plane) % nz
-    p = (me % plane) ^ (chip % plane)
+    z = hop(me // plane, chip // plane, nz)
+    p = hop(me % plane, chip % plane, plane)
     wanted = (z * plane + p) * own + at % own
     pick = (wanted == source).astype(jnp.float32).astype(jnp.bfloat16)
     ordered = jnp.dot(pick, shifted, preferred_element_type=jnp.float32)
@@ -230,13 +233,13 @@
     lax.fori_loop(0, steps, step, 0)
 
 
-def potential_call(start, steps, layout, by_plane, fields, bias, others, cols, turned, after=()):
+def potential_call(start, steps, layout, by_plane, fields, bias, others, cols, turned):
     nz, plane, own = layout
     walk, vectors = fields.shape
     groups, inner = (plane, nz) if by_plane else (nz, plane)
     rows = 2 * CHUNK
     *parts, energy = pl.pallas_call(
-        functools.partial(potential_kernel, start, steps, layout, by_plane, len(after)),
+        functools.partial(potential_kernel, start, steps, layout, by_plane),
         out_shape=[
             *[pltpu.VMEM((inner, own, steps * rows, LANES), jnp.bfloat16)] * groups,
             pltpu.VMEM((CHUNK, LANES), jnp.float32),
@@ -248,7 +251,7 @@
         cost_estimate=FREE,
         compiler_params=params(16),
         name="potential",
-    )(fields, *in_vmem(bias, *after, *others), cols, *in_vmem(turned))
+    )(fields, *in_vmem(bias, *others), cols, *in_vmem(turned))
     return parts, energy
 
 
@@ -276,7 +279,7 @@
 def series_kernel(sizes, *refs):
     n_orb, late_steps, early_steps = sizes
     late, early, start = refs[:n_orb], refs[n_orb:2 * n_orb], refs[2 * n_orb:3 * n_orb]
-    energy_ref, plane_ref, z_ref, pot, term, total = refs[3 * n_orb:]
+    energy_ref, moved_ref, pot, term, total = refs[3 * n_orb:]
     me = lax.axis_index("orb")
     own, half_rows = start[0].shape[:2]
     rowblocks = half_rows // BLOCK
@@ -306,25 +309,19 @@
             moved = begin[r].astype(jnp.float32) + sums[r]
             total[r // rowblocks, j, (r % rowblocks) * BLOCK:(r % rowblocks + 1) * BLOCK] = moved.astype(jnp.bfloat16)
     mine = total[pl.ds(me, 1)][0]
-    cut = (z_ref.shape[0] - CHUNK) // own
     at = lax.broadcasted_iota(jnp.int32, (CHUNK, LANES), 0)
     high, middle, low = (part.astype(jnp.float32) for part in split(energy_ref[...]))
     tile = jnp.where(at == 0, high, jnp.where(at == 1, middle, jnp.where(at == 2, low, 0.0)))
-    for j in range(own):
-        z_ref[j * cut:(j + 1) * cut] = mine[j, :cut]
-    z_ref[own * cut:] = tile.astype(jnp.bfloat16)
-    plane_ref[...] = mine[:, cut:]
-
-
-def series_call(sizes, cut, late, early, start, energy):
+    moved_ref[:own * half_rows] = mine.reshape(own * half_rows, mine.shape[2])
+    moved_ref[own * half_rows:] = tile.astype(jnp.bfloat16)
+
+
+def series_call(sizes, late, early, start, energy):
     n_orb = sizes[0]
     own, half_rows, nocc = start[0].shape
     return pl.pallas_call(
         functools.partial(series_kernel, sizes),
-        out_shape=[
-            pltpu.VMEM((own, half_rows - cut, nocc), jnp.bfloat16),
-            pltpu.VMEM((own * cut + CHUNK, nocc), jnp.bfloat16),
-        ],
+        out_shape=pltpu.VMEM((own * half_rows + CHUNK, nocc), jnp.bfloat16),
         scratch_shapes=[
             pltpu.VMEM((ROWBLK, own, BLOCK, 2 * LANES), jnp.bfloat16),
             pltpu.VMEM((n_orb, own, half_rows, nocc), jnp.bfloat16),
@@ -338,36 +335,35 @@
 
 def place_kernel(layout, *refs):
     nz, plane, own = layout
-    z_first, plane_first = refs[:plane], refs[plane:plane + nz]
-    out, energy_ref = refs[plane + nz:]
+    gathered = refs[:plane]
+    out, energy_ref = refs[plane:]
     me = lax.axis_index("chol")
-    cut = out.shape[1] - plane_first[0].shape[2]
+    rows = out.shape[1]
     energy = jnp.zeros((CHUNK, LANES), jnp.float32)
     for dp in range(plane):
         for dz in range(nz):
-            chip = lax.rem(me // plane + nz - dz, nz) * plane + (lax.rem(me, plane) ^ dp)
+            z = hop(lax.div(me, plane), -dz if nz & (nz - 1) else dz, nz)
+            p = hop(lax.rem(me, plane), -dp if plane & (plane - 1) else dp, plane)
             for j in range(own):
-                out[chip * own + j, :cut] = z_first[dp][dz, j * cut:(j + 1) * cut]
-                out[chip * own + j, cut:] = plane_first[dz][dp, j]
-            energy = energy + z_first[dp][dz, own * cut:].astype(jnp.float32)
+                out[(z * plane + p) * own + j] = gathered[dp][dz, j * rows:(j + 1) * rows]
+            energy = energy + gathered[dp][dz, own * rows:].astype(jnp.float32)
     energy_ref[...] = (energy[0:1] + energy[1:2] + energy[2:3])[:, :energy_ref.shape[1]]
 
 
-def place_call(layout, z_first, plane_first):
+def place_call(layout, gathered):
     nz, plane, own = layout
-    rest, nocc = plane_first[0].shape[2:]
     walk = nz * plane * own
-    cut = (z_first[0].shape[1] - CHUNK) // own
+    rows = (gathered[0].shape[1] - CHUNK) // own
     return pl.pallas_call(
         functools.partial(place_kernel, layout),
         out_shape=[
-            jax.ShapeDtypeStruct((walk, cut + rest, nocc), jnp.bfloat16),
+            jax.ShapeDtypeStruct((walk, rows, gathered[0].shape[2]), jnp.bfloat16),
             jax.ShapeDtypeStruct((1, walk), jnp.float32),
         ],
         cost_estimate=FREE,
         compiler_params=params(16),
         name="place_walkers",
-    )(*in_vmem(*z_first, *plane_first))
+    )(*in_vmem(*gathered))
 
 
 def per_device(chol_vals, chol_cols, greens, walkers, fields):
@@ -382,10 +378,10 @@
     step_factor = 72.0 / float(vectors * chips * BLOCK) ** 0.5
 
     def to_plane(a, dp):
-        return lax.ppermute(a, "chol", [(c, (c // plane) * plane + ((c % plane) ^ dp)) for c in range(chips)])
+        return lax.ppermute(a, "chol", [(c, (c // plane) * plane + hop(c % plane, dp, plane)) for c in range(chips)])
 
     def to_z(a, dz):
-        return lax.ppermute(a, "chol", [(c, ((c // plane + dz) % nz) * plane + c % plane) for c in range(chips)])
+        return lax.ppermute(a, "chol", [(c, hop(c // plane, dz, nz) * plane + c % plane) for c in range(chips)])
 
     def around_orb(a):
         return [a] + [lax.ppermute(a, "orb", [((c + d) % n_orb, c) for c in range(n_orb)]) for d in range(1, n_orb)]
@@ -397,12 +393,12 @@
     start, others = lax.optimization_barrier((start, others))
 
     total_steps = rowblocks * BLOCK // CHUNK
-    early_steps = total_steps * 3 // 8
+    early_steps = total_steps // 4
     late_steps = total_steps - early_steps
     fields_t = fields.T
     early, energy = potential_call(0, early_steps, layout, False, fields_t, bias, others, cols, turned)
     early_in = [early[0]] + [to_z(early[dz], dz) for dz in range(1, nz)]
-    late, _ = potential_call(early_steps, late_steps, layout, True, fields_t, bias, others, cols, turned, [energy])
+    late, _ = potential_call(early_steps, late_steps, layout, True, fields_t, bias, others, cols, turned)
     late_in = [late[0]] + [to_plane(late[dp], dp) for dp in range(1, plane)]
     early_sums = sum_call(early_in)
     early_in = [early_sums[0]] + [to_plane(early_sums[dp], dp) for dp in range(1, plane)]
@@ -416,14 +412,10 @@
             total = total + a.astype(jnp.float32)
         return around_orb((step_factor * total).astype(jnp.bfloat16))
 
-    cut = half_rows // CHUNK * 5 // 8 * CHUNK
-    b_part, a_part = series_call((n_orb, late_steps, early_steps), cut, finish(late_in), finish(early_in), start, energy)
-
-    a_all = jnp.stack([a_part] + [to_z(a_part, dz) for dz in range(1, nz)])
-    b_all = jnp.stack([b_part] + [to_plane(b_part, dp) for dp in range(1, plane)])
-    z_first = [a_all] + [to_plane(a_all, dp) for dp in range(1, plane)]
-    plane_first = [b_all] + [to_z(b_all, dz) for dz in range(1, nz)]
-    moved, energy = place_call(layout, z_first, plane_first)
+    piece = series_call((n_orb, late_steps, early_steps), finish(late_in), finish(early_in), start, energy)
+    pieces = jnp.stack([piece] + [to_z(piece, dz) for dz in range(1, nz)])
+    gathered = [pieces] + [to_plane(pieces, dp) for dp in range(1, plane)]
+    moved, energy = place_call(layout, gathered)
     return moved, energy.reshape(walk)
 
 

time: 79.2 us -> 78.4 us (0.990)
  starting transfers between devices: 41.4 us -> 27.9 us
  waiting for transfers between devices: 19.3 us -> 32.1 us
    ppermute x24 -> x18, starting transfers between devices: 40.7 us -> 26.7 us  [the longest x9 15.4 us: to_z(): lax.ppermute(a, 'chol', [(c, hop(c // plane, dz, nz) * plane + c % plane)...]
    ppermute x24 -> x18, waiting for transfers between devices: 16.9 us -> 30.1 us  [the longest x9 20.7 us: to_plane(): lax.ppermute(a, 'chol', [(c, c // plane * plane + hop(c % plane, dp, plan...]
  transfers between devices with their start and end apart: 28 -> 22, of which waited for: 11 -> 8; matrix products, arithmetic and copies ran while one was open for 0% -> 0% of each run, Pallas kernels for 0% -> 2%
where the time goes in v6:
time: 78.4 us; the launch traced here: 78.2 us
  waiting for transfers between devices  32.1 us (41%)
  starting transfers between devices  27.9 us (36%)
  Pallas kernels  16.7 us (21%)
    ppermute x9, waiting for transfers between devices, to_plane(): lax.ppermute(a, 'chol', [(c, c // plane * plane + hop(c % plane, dp, plan...  20.7 us
    ppermute x9, starting transfers between devices, to_z(): lax.ppermute(a, 'chol', [(c, hop(c // plane, dz, nz) * plane + c % plane)...  15.4 us
    ppermute x9, starting transfers between devices, to_plane(): lax.ppermute(a, 'chol', [(c, c // plane * plane + hop(c % plane, dp, plan...  11.3 us
    ppermute x9, waiting for transfers between devices, to_z(): lax.ppermute(a, 'chol', [(c, hop(c // plane, dz, nz) * plane + c % plane)...  9.38 us
    pallas_call x1, Pallas kernels, bias_call(): pl.pallas_call(bias_kernel, in_specs=[*[pl.BlockSpec(memory_space=pl.ANY)...  8.49 us
    pallas_call x2, Pallas kernels, potential_call(): pl.pallas_call(functools.partial(potential_kernel, start, steps, layout,...  5.59 us
    ppermute x4, waiting for transfers between devices, around_orb(): lax.ppermute(a, 'orb', [((c + d) % n_orb, c) for c in range(n_orb)])  1.99 us
  transfers between devices with their start and end apart: 22, of which 8 were waited for; matrix products, arithmetic and copies ran while one was open for 0% of the time, Pallas kernels for 2%

profile of v6, /device:TPU:0, one launch (start us, length us, event | category | flops | bytes accessed | tf_op | source)
XLA Modules:
  0.0 78.2 jit_solution(12596291577893964397)
XLA Ops:
  0.6 0.0 copy-start
  0.6 0.0 copy-start.1
  0.7 0.7 copy-done.1
  1.3 8.5 %force_bias.1 = (bf16[8,256,2048]{2,1,0:T(8,128)(2,1)S(1)}, f32[32,256]{1,0:T(8,128)S(1)}, bf16[2,128,128]{2,1,0:T(8,128)(2,1)S(1)}) custom-call(bf16[256,2,64,128]{3,2,1,0:T(8,128)(2,1)} %vals_hbm.1, bf16[32,128,256]{2,1,0:T(8,128)(2,1)} %greens_hbm.1, bf16[32,128,128]{2,1,0:T(8,128)(2,1)} %walkers_hbm.1, s32[2,2,256]{2,1,0:T(2,128)S(1)} %bitcast.10), custom_call_target="tpu_custom_call" | custom-call | tf_op jit(solution)/shard_map/force_bias/pallas_call | solution.py:146
  9.8 0.5 collective-permute-start
  10.3 0.1 collective-permute-start.1
  10.4 1.1 %collective-permute-done.1.refs_0_ = f32[32,256]{1,0:T(8,128)S(1)} collective-permute-done((f32[32,256]{1,0:T(8,128)S(1)}, f32[32,256]{1,0:T(8,128)S(1)}, u32[]{:S(2)}, u32[]{:S(2)}) %collective-permute-start.1) | collective-permute-done | bytes 32800 | tf_op jit(solution)/shard_map/ppermute | solution.py:387
  11.6 0.0 collective-permute-done.refs_5_
  11.6 0.0 copy-done
  11.6 4.2 %potential.2 = (bf16[4,2,192,128]{3,2,1,0:T(8,128)(2,1)S(1)}, bf16[4,2,192,128]{3,2,1,0:T(8,128)(2,1)S(1)}, bf16[4,2,192,128]{3,2,1,0:T(8,128)(2,1)S(1)}, bf16[4,2,192,128]{3,2,1,0:T(8,128)(2,1)S(1)}, f32[16,128]{1,0:T(8,128)}) custom-call(f32[32,256]{1,0:T(8,128)S(1)} %bitcast.8, f32[32,256]{1,0:T(8,128)S(1)} %get-tuple-element.27.own_ref, ...), custom_call_target="tpu_custom_call" | custom-call | tf_op jit(solution)/shard_map/potential/pallas_call | solution.py:241
  15.8 2.7 %collective-permute-start.2 = (bf16[4,2,192,128]{3,2,1,0:T(8,128)(2,1)S(1)}, bf16[4,2,192,128]{3,2,1,0:T(8,128)(2,1)S(1)}, u32[]{:S(2)}, u32[]{:S(2)}) collective-permute-start(bf16[4,2,192,128]{3,2,1,0:T(8,128)(2,1)S(1)} %get-tuple-element.32), channel_id=1, source_target_pairs={{0,2},{2,0},{4,6},{6,4},{8,10},{10,8},{12,14},{14,12},{16,18},{18,... | collective-permute-start | bytes 1179656 | tf_op jit(solution)/shard_map/ppermute | solution.py:381
  18.5 1.5 %collective-permute-start.3 = (bf16[4,2,192,128]{3,2,1,0:T(8,128)(2,1)S(1)}, bf16[4,2,192,128]{3,2,1,0:T(8,128)(2,1)S(1)}, u32[]{:S(2)}, u32[]{:S(2)}) collective-permute-start(bf16[4,2,192,128]{3,2,1,0:T(8,128)(2,1)S(1)} %get-tuple-element.33), channel_id=1, source_target_pairs={{0,4},{2,6},{4,0},{6,2},{8,12},{10,14},{12,8},{14,10},{16,20},{18,... | collective-permute-start | bytes 1179656 | tf_op jit(solution)/shard_map/ppermute | solution.py:381
  20.0 0.0 collective-permute-start.4
  20.0 1.3 %potential.3 = (bf16[4,2,64,128]{3,2,1,0:T(8,128)(2,1)S(1)}, bf16[4,2,64,128]{3,2,1,0:T(8,128)(2,1)S(1)}, bf16[4,2,64,128]{3,2,1,0:T(8,128)(2,1)S(1)}, bf16[4,2,64,128]{3,2,1,0:T(8,128)(2,1)S(1)}, f32[16,128]{1,0:T(8,128)S(1)}) custom-call(f32[32,256]{1,0:T(8,128)S(1)} %bitcast.9, f32[32,256]{1,0:T(8,128)S(1)} %get-tuple-element.27.own_ref, ...), custom_call_target="tpu_custom_call" | custom-call | tf_op jit(solution)/shard_map/potential/pallas_call | solution.py:241
  21.3 3.1 %collective-permute-start.10 = (bf16[4,2,64,128]{3,2,1,0:T(8,128)(2,1)S(1)}, bf16[4,2,64,128]{3,2,1,0:T(8,128)(2,1)S(1)}, u32[]{:S(2)}, u32[]{:S(2)}) collective-permute-start(bf16[4,2,64,128]{3,2,1,0:T(8,128)(2,1)S(1)} %get-tuple-element.41), channel_id=1, source_target_pairs={{0,16},{2,18},{4,20},{6,22},{8,24},{10,26},{12,28},{14,30},{16,0},... | collective-permute-start | bytes 393224 | tf_op jit(solution)/shard_map/ppermute | solution.py:384
  24.5 1.3 %collective-permute-start.11 = (bf16[4,2,64,128]{3,2,1,0:T(8,128)(2,1)S(1)}, bf16[4,2,64,128]{3,2,1,0:T(8,128)(2,1)S(1)}, u32[]{:S(2)}, u32[]{:S(2)}) collective-permute-start(bf16[4,2,64,128]{3,2,1,0:T(8,128)(2,1)S(1)} %get-tuple-element.42), channel_id=1, source_target_pairs={{0,24},{2,26},{4,28},{6,30},{8,16},{10,18},{12,20},{14,22},{16,8},... | collective-permute-start | bytes 393224 | tf_op jit(solution)/shard_map/ppermute | solution.py:384
  25.8 2.6 %collective-permute-done.2.refs_1_ = bf16[4,2,192,128]{3,2,1,0:T(8,128)(2,1)S(1)} collective-permute-done((bf16[4,2,192,128]{3,2,1,0:T(8,128)(2,1)S(1)}, bf16[4,2,192,128]{3,2,1,0:T(8,128)(2,1)S(1)}, u32[]{:S(2)}, u32[]{:S(2)}) %collective-permute-start.2) | collective-permute-done | bytes 393248 | tf_op jit(solution)/shard_map/ppermute | solution.py:381
  28.4 2.1 %collective-permute-start.9 = (bf16[4,2,64,128]{3,2,1,0:T(8,128)(2,1)S(1)}, bf16[4,2,64,128]{3,2,1,0:T(8,128)(2,1)S(1)}, u32[]{:S(2)}, u32[]{:S(2)}) collective-permute-start(bf16[4,2,64,128]{3,2,1,0:T(8,128)(2,1)S(1)} %get-tuple-element.40), channel_id=1, source_target_pairs={{0,8},{2,10},{4,12},{6,14},{8,0},{10,2},{12,4},{14,6},{16,24},{18,... | collective-permute-start | bytes 393224 | tf_op jit(solution)/shard_map/ppermute | solution.py:384
  30.5 7.5 %collective-permute-done.3.refs_2_ = bf16[4,2,192,128]{3,2,1,0:T(8,128)(2,1)S(1)} collective-permute-done((bf16[4,2,192,128]{3,2,1,0:T(8,128)(2,1)S(1)}, bf16[4,2,192,128]{3,2,1,0:T(8,128)(2,1)S(1)}, u32[]{:S(2)}, u32[]{:S(2)}) %collective-permute-start.3) | collective-permute-done | bytes 393248 | tf_op jit(solution)/shard_map/ppermute | solution.py:381
  38.0 0.0 collective-permute-done.4.refs_3_
  38.0 0.2 sum_parts.2
  38.2 1.6 %collective-permute-start.5 = (bf16[2,192,128]{2,1,0:T(8,128)(2,1)S(1)}, bf16[2,192,128]{2,1,0:T(8,128)(2,1)S(1)}, u32[]{:S(2)}, u32[]{:S(2)}) collective-permute-start(bf16[2,192,128]{2,1,0:T(8,128)(2,1)S(1)} %get-tuple-element.36), channel_id=1, source_target_pairs={{0,8},{2,10},{4,12},{6,14},{8,0},{10,2},{12,4},{14,6},{16,24},{18,... | collective-permute-start | bytes 294920 | tf_op jit(solution)/shard_map/ppermute | solution.py:384
  39.8 2.6 %collective-permute-start.6 = (bf16[2,192,128]{2,1,0:T(8,128)(2,1)S(1)}, bf16[2,192,128]{2,1,0:T(8,128)(2,1)S(1)}, u32[]{:S(2)}, u32[]{:S(2)}) collective-permute-start(bf16[2,192,128]{2,1,0:T(8,128)(2,1)S(1)} %get-tuple-element.37), channel_id=1, source_target_pairs={{0,16},{2,18},{4,20},{6,22},{8,24},{10,26},{12,28},{14,30},{16,0},... | collective-permute-start | bytes 294920 | tf_op jit(solution)/shard_map/ppermute | solution.py:384
  42.4 0.0 collective-permute-done.10.refs_2_
  42.4 0.2 collective-permute-start.7
  42.7 0.0 collective-permute-done.11.refs_3_
  42.7 0.0 collective-permute-done.9.refs_1_
  42.7 0.1 sum_parts.3
  42.7 1.3 %collective-permute-start.12 = (bf16[2,64,128]{2,1,0:T(8,128)(2,1)S(1)}, bf16[2,64,128]{2,1,0:T(8,128)(2,1)S(1)}, u32[]{:S(2)}, u32[]{:S(2)}) collective-permute-start(bf16[2,64,128]{2,1,0:T(8,128)(2,1)S(1)} %get-tuple-element.44), channel_id=1, source_target_pairs={{0,2},{2,0},{4,6},{6,4},{8,10},{10,8},{12,14},{14,12},{16,18},{18,... | collective-permute-start | bytes 98312 | tf_op jit(solution)/shard_map/ppermute | solution.py:381
  44.0 0.8 %collective-permute-start.13 = (bf16[2,64,128]{2,1,0:T(8,128)(2,1)S(1)}, bf16[2,64,128]{2,1,0:T(8,128)(2,1)S(1)}, u32[]{:S(2)}, u32[]{:S(2)}) collective-permute-start(bf16[2,64,128]{2,1,0:T(8,128)(2,1)S(1)} %get-tuple-element.45), channel_id=1, source_target_pairs={{0,4},{2,6},{4,0},{6,2},{8,12},{10,14},{12,8},{14,10},{16,20},{18,... | collective-permute-start | bytes 98312 | tf_op jit(solution)/shard_map/ppermute | solution.py:381
  44.9 0.0 collective-permute-done.5
  44.9 1.4 %collective-permute-start.14 = (bf16[2,64,128]{2,1,0:T(8,128)(2,1)S(1)}, bf16[2,64,128]{2,1,0:T(8,128)(2,1)S(1)}, u32[]{:S(2)}, u32[]{:S(2)}) collective-permute-start(bf16[2,64,128]{2,1,0:T(8,128)(2,1)S(1)} %get-tuple-element.46), channel_id=1, source_target_pairs={{0,6},{2,4},{4,2},{6,0},{8,14},{10,12},{12,10},{14,8},{16,22},{18,... | collective-permute-start | bytes 98312 | tf_op jit(solution)/shard_map/ppermute | solution.py:381
  46.3 3.5 %collective-permute-done.6 = bf16[2,192,128]{2,1,0:T(8,128)(2,1)S(1)} collective-permute-done((bf16[2,192,128]{2,1,0:T(8,128)(2,1)S(1)}, bf16[2,192,128]{2,1,0:T(8,128)(2,1)S(1)}, u32[]{:S(2)}, u32[]{:S(2)}) %collective-permute-start.6) | collective-permute-done | bytes 98336 | tf_op jit(solution)/shard_map/ppermute | solution.py:384
  49.8 0.0 collective-permute-done.7
  49.8 0.1 multiply_convert_fusion.refs_0_
  49.8 0.1 collective-permute-start.8
  49.9 0.0 collective-permute-done.12
  49.9 0.0 collective-permute-done.13
  49.9 0.0 collective-permute-done.14
  50.0 0.5 collective-permute-start.15
  50.5 0.9 %collective-permute-done.15.refs_3_ = bf16[2,64,128]{2,1,0:T(8,128)(2,1)S(1)} collective-permute-done((bf16[2,64,128]{2,1,0:T(8,128)(2,1)S(1)}, bf16[2,64,128]{2,1,0:T(8,128)(2,1)S(1)}, u32[]{:S(2)}, u32[]{:S(2)}) %collective-permute-start.15) | collective-permute-done | bytes 32800 | tf_op jit(solution)/shard_map/ppermute | solution.py:387
  51.4 0.0 collective-permute-done.8.refs_1_
  51.4 1.3 %series.1 = bf16[272,128]{1,0:T(8,128)(2,1)S(1)} custom-call(bf16[2,192,128]{2,1,0:T(8,128)(2,1)S(1)} %multiply_convert_fusion.refs_0_, bf16[2,192,128]{2,1,0:T(8,128)(2,1)S(1)} %collective-permute-done.8.refs_1_, bf16[2,64,128]{2,1,0:T(8,128)(2,1)S(1)} %multiply_convert_fusion.1.refs_2_, bf16[2,64,128]{2,1,0:T(8,128)(2,1)S(1)} %collective-permute-done.15.refs_3_, ...), custom_call_target="tpu_custom_call" | custom-call | tf_op jit(solution)/shard_map/series/pallas_call | solution.py:322
  52.6 1.7 %collective-permute-start.16 = (bf16[272,128]{1,0:T(8,128)(2,1)S(1)}, bf16[272,128]{1,0:T(8,128)(2,1)S(1)}, u32[]{:S(2)}, u32[]{:S(2)}) collective-permute-start(bf16[272,128]{1,0:T(8,128)(2,1)S(1)} %series.1), channel_id=1, source_target_pairs={{0,8},{2,10},{4,12},{6,14},{8,0},{10,2},{12,4},{14,6},{16,24},{18,... | collective-permute-start | bytes 208904 | tf_op jit(solution)/shard_map/ppermute | solution.py:384
  54.3 2.1 %collective-permute-start.17 = (bf16[272,128]{1,0:T(8,128)(2,1)S(1)}, bf16[272,128]{1,0:T(8,128)(2,1)S(1)}, u32[]{:S(2)}, u32[]{:S(2)}) collective-permute-start(bf16[272,128]{1,0:T(8,128)(2,1)S(1)} %series.1), channel_id=1, source_target_pairs={{0,16},{2,18},{4,20},{6,22},{8,24},{10,26},{12,28},{14,30},{16,0},... | collective-permute-start | bytes 208904 | tf_op jit(solution)/shard_map/ppermute | solution.py:384
  56.5 0.6 collective-permute-start.18
  57.1 0.0 collective-permute-done.16
  57.2 5.8 %collective-permute-done.17 = bf16[272,128]{1,0:T(8,128)(2,1)S(1)} collective-permute-done((bf16[272,128]{1,0:T(8,128)(2,1)S(1)}, bf16[272,128]{1,0:T(8,128)(2,1)S(1)}, u32[]{:S(2)}, u32[]{:S(2)}) %collective-permute-start.17) | collective-permute-done | bytes 69664 | tf_op jit(solution)/shard_map/ppermute | solution.py:384
  63.0 0.0 collective-permute-done.18
  63.0 1.5 %collective-permute-start.19 = (bf16[4,272,128]{2,1,0:T(8,128)(2,1)S(1)}, bf16[4,272,128]{2,1,0:T(8,128)(2,1)S(1)}, u32[]{:S(2)}, u32[]{:S(2)}) collective-permute-start(bf16[4,272,128]{2,1,0:T(8,128)(2,1)S(1)} %pad_maximum_fusion.refs_0_), channel_id=1, source_target_pairs={{0,2},{2,0},{4,6},{6,4},{8,10},{10,8},{12,14},{14,12},{16,18},{18,... | collective-permute-start | bytes 835592 | tf_op jit(solution)/shard_map/ppermute | solution.py:381
  64.6 0.5 collective-permute-start.20
  65.1 1.5 %collective-permute-start.21 = (bf16[4,272,128]{2,1,0:T(8,128)(2,1)S(1)}, bf16[4,272,128]{2,1,0:T(8,128)(2,1)S(1)}, u32[]{:S(2)}, u32[]{:S(2)}) collective-permute-start(bf16[4,272,128]{2,1,0:T(8,128)(2,1)S(1)} %pad_maximum_fusion.refs_0_), channel_id=1, source_target_pairs={{0,6},{2,4},{4,2},{6,0},{8,14},{10,12},{12,10},{14,8},{16,22},{18,... | collective-permute-start | bytes 835592 | tf_op jit(solution)/shard_map/ppermute | solution.py:381
  66.6 6.1 %collective-permute-done.19.refs_1_ = bf16[4,272,128]{2,1,0:T(8,128)(2,1)S(1)} collective-permute-done((bf16[4,272,128]{2,1,0:T(8,128)(2,1)S(1)}, bf16[4,272,128]{2,1,0:T(8,128)(2,1)S(1)}, u32[]{:S(2)}, u32[]{:S(2)}) %collective-permute-start.19) | collective-permute-done | bytes 278560 | tf_op jit(solution)/shard_map/ppermute | solution.py:381
  72.7 4.5 %collective-permute-done.20.refs_2_ = bf16[4,272,128]{2,1,0:T(8,128)(2,1)S(1)} collective-permute-done((bf16[4,272,128]{2,1,0:T(8,128)(2,1)S(1)}, bf16[4,272,128]{2,1,0:T(8,128)(2,1)S(1)}, u32[]{:S(2)}, u32[]{:S(2)}) %collective-permute-start.20) | collective-permute-done | bytes 278560 | tf_op jit(solution)/shard_map/ppermute | solution.py:381
  77.2 0.0 collective-permute-done.21.refs_3_
  77.2 1.1 %place_walkers.1 = (bf16[32,128,128]{2,1,0:T(8,128)(2,1)}, f32[1,32]{1,0:T(1,128)}) custom-call(bf16[4,272,128]{2,1,0:T(8,128)(2,1)S(1)} %pad_maximum_fusion.refs_0_, bf16[4,272,128]{2,1,0:T(8,128)(2,1)S(1)} %collective-permute-done.19.refs_1_, bf16[4,272,128]{2,1,0:T(8,128)(2,1)S(1)} %collective-permute-done.20.refs_2_, ...), custom_call_target="tpu_custom_call" | custom-call | tf_op jit(solution)/shard_map/place_walkers/pallas_call | solution.py:357
  (2 shorter events, 0.1 us)
Async XLA Ops:
  0.6 10.9 %copy-start = (f32[256,32]{0,1:T(8,128)S(1)}, f32[256,32]{0,1:T(8,128)}, u32[]{:S(2)}) copy-start(f32[256,32]{0,1:T(8,128)} %param.9) | copy-start | bytes 98308
  0.6 0.7 copy-start.1
  9.8 1.7 %collective-permute-start = (bf16[2,128,128]{2,1,0:T(8,128)(2,1)S(1)}, bf16[2,128,128]{2,1,0:T(8,128)(2,1)S(1)}, u32[]{:S(2)}, u32[]{:S(2)}) collective-permute-start(bf16[2,128,128]{2,1,0:T(8,128)(2,1)S(1)} %get-tuple-element.47.refs_4_), channel_id=1, source_target_pairs={{1,0},{0,1},{3,2},{2,3},{5,4},{4,5},{7,6},{6,7},{9,8},{8,9},{11,10... | collective-permute-start | bytes 196616 | tf_op jit(solution)/shard_map/ppermute | solution.py:387
  10.3 1.2 %collective-permute-start.1 = (f32[32,256]{1,0:T(8,128)S(1)}, f32[32,256]{1,0:T(8,128)S(1)}, u32[]{:S(2)}, u32[]{:S(2)}) collective-permute-start(f32[32,256]{1,0:T(8,128)S(1)} %get-tuple-element.27.own_ref), channel_id=1, source_target_pairs={{1,0},{0,1},{3,2},{2,3},{5,4},{4,5},{7,6},{6,7},{9,8},{8,9},{11,10... | collective-permute-start | bytes 98312 | tf_op jit(solution)/shard_map/ppermute | solution.py:387
  15.8 12.6 %collective-permute-start.2 = (bf16[4,2,192,128]{3,2,1,0:T(8,128)(2,1)S(1)}, bf16[4,2,192,128]{3,2,1,0:T(8,128)(2,1)S(1)}, u32[]{:S(2)}, u32[]{:S(2)}) collective-permute-start(bf16[4,2,192,128]{3,2,1,0:T(8,128)(2,1)S(1)} %get-tuple-element.32), channel_id=1, source_target_pairs={{0,2},{2,0},{4,6},{6,4},{8,10},{10,8},{12,14},{14,12},{16,18},{18,... | collective-permute-start | bytes 1179656 | tf_op jit(solution)/shard_map/ppermute | solution.py:381
  18.5 19.5 %collective-permute-start.3 = (bf16[4,2,192,128]{3,2,1,0:T(8,128)(2,1)S(1)}, bf16[4,2,192,128]{3,2,1,0:T(8,128)(2,1)S(1)}, u32[]{:S(2)}, u32[]{:S(2)}) collective-permute-start(bf16[4,2,192,128]{3,2,1,0:T(8,128)(2,1)S(1)} %get-tuple-element.33), channel_id=1, source_target_pairs={{0,4},{2,6},{4,0},{6,2},{8,12},{10,14},{12,8},{14,10},{16,20},{18,... | collective-permute-start | bytes 1179656 | tf_op jit(solution)/shard_map/ppermute | solution.py:381
  20.0 18.0 %collective-permute-start.4 = (bf16[4,2,192,128]{3,2,1,0:T(8,128)(2,1)S(1)}, bf16[4,2,192,128]{3,2,1,0:T(8,128)(2,1)S(1)}, u32[]{:S(2)}, u32[]{:S(2)}) collective-permute-start(bf16[4,2,192,128]{3,2,1,0:T(8,128)(2,1)S(1)} %get-tuple-element.34), channel_id=1, source_target_pairs={{0,6},{2,4},{4,2},{6,0},{8,14},{10,12},{12,10},{14,8},{16,22},{18,... | collective-permute-start | bytes 1179656 | tf_op jit(solution)/shard_map/ppermute | solution.py:381
  21.3 21.1 %collective-permute-start.10 = (bf16[4,2,64,128]{3,2,1,0:T(8,128)(2,1)S(1)}, bf16[4,2,64,128]{3,2,1,0:T(8,128)(2,1)S(1)}, u32[]{:S(2)}, u32[]{:S(2)}) collective-permute-start(bf16[4,2,64,128]{3,2,1,0:T(8,128)(2,1)S(1)} %get-tuple-element.41), channel_id=1, source_target_pairs={{0,16},{2,18},{4,20},{6,22},{8,24},{10,26},{12,28},{14,30},{16,0},... | collective-permute-start | bytes 393224 | tf_op jit(solution)/shard_map/ppermute | solution.py:384
  24.5 18.2 %collective-permute-start.11 = (bf16[4,2,64,128]{3,2,1,0:T(8,128)(2,1)S(1)}, bf16[4,2,64,128]{3,2,1,0:T(8,128)(2,1)S(1)}, u32[]{:S(2)}, u32[]{:S(2)}) collective-permute-start(bf16[4,2,64,128]{3,2,1,0:T(8,128)(2,1)S(1)} %get-tuple-element.42), channel_id=1, source_target_pairs={{0,24},{2,26},{4,28},{6,30},{8,16},{10,18},{12,20},{14,22},{16,8},... | collective-permute-start | bytes 393224 | tf_op jit(solution)/shard_map/ppermute | solution.py:384
  28.4 14.2 %collective-permute-start.9 = (bf16[4,2,64,128]{3,2,1,0:T(8,128)(2,1)S(1)}, bf16[4,2,64,128]{3,2,1,0:T(8,128)(2,1)S(1)}, u32[]{:S(2)}, u32[]{:S(2)}) collective-permute-start(bf16[4,2,64,128]{3,2,1,0:T(8,128)(2,1)S(1)} %get-tuple-element.40), channel_id=1, source_target_pairs={{0,8},{2,10},{4,12},{6,14},{8,0},{10,2},{12,4},{14,6},{16,24},{18,... | collective-permute-start | bytes 393224 | tf_op jit(solution)/shard_map/ppermute | solution.py:384
  38.2 6.7 %collective-permute-start.5 = (bf16[2,192,128]{2,1,0:T(8,128)(2,1)S(1)}, bf16[2,192,128]{2,1,0:T(8,128)(2,1)S(1)}, u32[]{:S(2)}, u32[]{:S(2)}) collective-permute-start(bf16[2,192,128]{2,1,0:T(8,128)(2,1)S(1)} %get-tuple-element.36), channel_id=1, source_target_pairs={{0,8},{2,10},{4,12},{6,14},{8,0},{10,2},{12,4},{14,6},{16,24},{18,... | collective-permute-start | bytes 294920 | tf_op jit(solution)/shard_map/ppermute | solution.py:384
  39.8 9.9 %collective-permute-start.6 = (bf16[2,192,128]{2,1,0:T(8,128)(2,1)S(1)}, bf16[2,192,128]{2,1,0:T(8,128)(2,1)S(1)}, u32[]{:S(2)}, u32[]{:S(2)}) collective-permute-start(bf16[2,192,128]{2,1,0:T(8,128)(2,1)S(1)} %get-tuple-element.37), channel_id=1, source_target_pairs={{0,16},{2,18},{4,20},{6,22},{8,24},{10,26},{12,28},{14,30},{16,0},... | collective-permute-start | bytes 294920 | tf_op jit(solution)/shard_map/ppermute | solution.py:384
  42.4 7.3 %collective-permute-start.7 = (bf16[2,192,128]{2,1,0:T(8,128)(2,1)S(1)}, bf16[2,192,128]{2,1,0:T(8,128)(2,1)S(1)}, u32[]{:S(2)}, u32[]{:S(2)}) collective-permute-start(bf16[2,192,128]{2,1,0:T(8,128)(2,1)S(1)} %get-tuple-element.38), channel_id=1, source_target_pairs={{0,24},{2,26},{4,28},{6,30},{8,16},{10,18},{12,20},{14,22},{16,8},... | collective-permute-start | bytes 294920 | tf_op jit(solution)/shard_map/ppermute | solution.py:384
  42.7 7.2 %collective-permute-start.12 = (bf16[2,64,128]{2,1,0:T(8,128)(2,1)S(1)}, bf16[2,64,128]{2,1,0:T(8,128)(2,1)S(1)}, u32[]{:S(2)}, u32[]{:S(2)}) collective-permute-start(bf16[2,64,128]{2,1,0:T(8,128)(2,1)S(1)} %get-tuple-element.44), channel_id=1, source_target_pairs={{0,2},{2,0},{4,6},{6,4},{8,10},{10,8},{12,14},{14,12},{16,18},{18,... | collective-permute-start | bytes 98312 | tf_op jit(solution)/shard_map/ppermute | solution.py:381
  44.0 5.9 %collective-permute-start.13 = (bf16[2,64,128]{2,1,0:T(8,128)(2,1)S(1)}, bf16[2,64,128]{2,1,0:T(8,128)(2,1)S(1)}, u32[]{:S(2)}, u32[]{:S(2)}) collective-permute-start(bf16[2,64,128]{2,1,0:T(8,128)(2,1)S(1)} %get-tuple-element.45), channel_id=1, source_target_pairs={{0,4},{2,6},{4,0},{6,2},{8,12},{10,14},{12,8},{14,10},{16,20},{18,... | collective-permute-start | bytes 98312 | tf_op jit(solution)/shard_map/ppermute | solution.py:381
  44.9 5.1 %collective-permute-start.14 = (bf16[2,64,128]{2,1,0:T(8,128)(2,1)S(1)}, bf16[2,64,128]{2,1,0:T(8,128)(2,1)S(1)}, u32[]{:S(2)}, u32[]{:S(2)}) collective-permute-start(bf16[2,64,128]{2,1,0:T(8,128)(2,1)S(1)} %get-tuple-element.46), channel_id=1, source_target_pairs={{0,6},{2,4},{4,2},{6,0},{8,14},{10,12},{12,10},{14,8},{16,22},{18,... | collective-permute-start | bytes 98312 | tf_op jit(solution)/shard_map/ppermute | solution.py:381
  49.8 1.5 %collective-permute-start.8 = (bf16[2,192,128]{2,1,0:T(8,128)(2,1)S(1)}, bf16[2,192,128]{2,1,0:T(8,128)(2,1)S(1)}, u32[]{:S(2)}, u32[]{:S(2)}) collective-permute-start(bf16[2,192,128]{2,1,0:T(8,128)(2,1)S(1)} %multiply_convert_fusion.refs_0_), channel_id=1, source_target_pairs={{1,0},{0,1},{3,2},{2,3},{5,4},{4,5},{7,6},{6,7},{9,8},{8,9},{11,10... | collective-permute-start | bytes 294920 | tf_op jit(solution)/shard_map/ppermute | solution.py:387
  50.0 1.4 %collective-permute-start.15 = (bf16[2,64,128]{2,1,0:T(8,128)(2,1)S(1)}, bf16[2,64,128]{2,1,0:T(8,128)(2,1)S(1)}, u32[]{:S(2)}, u32[]{:S(2)}) collective-permute-start(bf16[2,64,128]{2,1,0:T(8,128)(2,1)S(1)} %multiply_convert_fusion.1.refs_2_), channel_id=1, source_target_pairs={{1,0},{0,1},{3,2},{2,3},{5,4},{4,5},{7,6},{6,7},{9,8},{8,9},{11,10... | collective-permute-start | bytes 98312 | tf_op jit(solution)/shard_map/ppermute | solution.py:387
  52.6 4.5 %collective-permute-start.16 = (bf16[272,128]{1,0:T(8,128)(2,1)S(1)}, bf16[272,128]{1,0:T(8,128)(2,1)S(1)}, u32[]{:S(2)}, u32[]{:S(2)}) collective-permute-start(bf16[272,128]{1,0:T(8,128)(2,1)S(1)} %series.1), channel_id=1, source_target_pairs={{0,8},{2,10},{4,12},{6,14},{8,0},{10,2},{12,4},{14,6},{16,24},{18,... | collective-permute-start | bytes 208904 | tf_op jit(solution)/shard_map/ppermute | solution.py:384
  54.3 8.7 %collective-permute-start.17 = (bf16[272,128]{1,0:T(8,128)(2,1)S(1)}, bf16[272,128]{1,0:T(8,128)(2,1)S(1)}, u32[]{:S(2)}, u32[]{:S(2)}) collective-permute-start(bf16[272,128]{1,0:T(8,128)(2,1)S(1)} %series.1), channel_id=1, source_target_pairs={{0,16},{2,18},{4,20},{6,22},{8,24},{10,26},{12,28},{14,30},{16,0},... | collective-permute-start | bytes 208904 | tf_op jit(solution)/shard_map/ppermute | solution.py:384
  56.5 6.5 %collective-permute-start.18 = (bf16[272,128]{1,0:T(8,128)(2,1)S(1)}, bf16[272,128]{1,0:T(8,128)(2,1)S(1)}, u32[]{:S(2)}, u32[]{:S(2)}) collective-permute-start(bf16[272,128]{1,0:T(8,128)(2,1)S(1)} %series.1), channel_id=1, source_target_pairs={{0,24},{2,26},{4,28},{6,30},{8,16},{10,18},{12,20},{14,22},{16,8},... | collective-permute-start | bytes 208904 | tf_op jit(solution)/shard_map/ppermute | solution.py:384
  63.0 9.7 %collective-permute-start.19 = (bf16[4,272,128]{2,1,0:T(8,128)(2,1)S(1)}, bf16[4,272,128]{2,1,0:T(8,128)(2,1)S(1)}, u32[]{:S(2)}, u32[]{:S(2)}) collective-permute-start(bf16[4,272,128]{2,1,0:T(8,128)(2,1)S(1)} %pad_maximum_fusion.refs_0_), channel_id=1, source_target_pairs={{0,2},{2,0},{4,6},{6,4},{8,10},{10,8},{12,14},{14,12},{16,18},{18,... | collective-permute-start | bytes 835592 | tf_op jit(solution)/shard_map/ppermute | solution.py:381
  64.6 12.6 %collective-permute-start.20 = (bf16[4,272,128]{2,1,0:T(8,128)(2,1)S(1)}, bf16[4,272,128]{2,1,0:T(8,128)(2,1)S(1)}, u32[]{:S(2)}, u32[]{:S(2)}) collective-permute-start(bf16[4,272,128]{2,1,0:T(8,128)(2,1)S(1)} %pad_maximum_fusion.refs_0_), channel_id=1, source_target_pairs={{0,4},{2,6},{4,0},{6,2},{8,12},{10,14},{12,8},{14,10},{16,20},{18,... | collective-permute-start | bytes 835592 | tf_op jit(solution)/shard_map/ppermute | solution.py:381
  65.1 12.1 %collective-permute-start.21 = (bf16[4,272,128]{2,1,0:T(8,128)(2,1)S(1)}, bf16[4,272,128]{2,1,0:T(8,128)(2,1)S(1)}, u32[]{:S(2)}, u32[]{:S(2)}) collective-permute-start(bf16[4,272,128]{2,1,0:T(8,128)(2,1)S(1)} %pad_maximum_fusion.refs_0_), channel_id=1, source_target_pairs={{0,6},{2,4},{4,2},{6,0},{8,14},{10,12},{12,10},{14,8},{16,22},{18,... | collective-permute-start | bytes 835592 | tf_op jit(solution)/shard_map/ppermute | solution.py:381

commit v7 on v6

--- a/solution.py
+++ b/solution.py
@@ -38,8 +38,16 @@
     return [pltpu.with_memory_space_constraint(a, pltpu.HBM) for a in arrays]
 
 
-def hop(at, distance, count):
-    return at ^ distance if count & (count - 1) == 0 else (at + distance) % count
+def orders(chips, early):
+    bits = list(range(chips.bit_length() - 1))
+    assert chips == 1 << len(bits)
+    if early:
+        bits = bits[len(bits) // 2:] + bits[:len(bits) // 2]
+    return bits, [bits[k ^ 1] if k ^ 1 < len(bits) else bits[k] for k in range(len(bits))]
+
+
+def flips(chips, early, core):
+    return [jnp.where(core % 2 == 0, 1 << even, 1 << odd) for even, odd in zip(*orders(chips, early))]
 
 
 def swap_matrix():
@@ -171,14 +179,14 @@
     )(*in_hbm(vals, greens, walkers), cols)
 
 
-def potential_kernel(start, steps, layout, by_plane, fields_ref, own_ref, *refs):
-    nz, plane, own = layout
+def potential_kernel(start, steps, chips, early, fields_ref, own_ref, *refs):
     others = refs[:lax.axis_size("orb") - 1]
     cols_ref, turned_ref = refs[len(others):len(others) + 2]
-    groups = plane if by_plane else nz
-    outs = refs[len(others) + 2:len(others) + 2 + groups]
-    energy_ref, s_ref, swap = refs[len(others) + 2 + groups:]
+    outs = refs[len(others) + 2:len(others) + 4]
+    energy_ref, s_ref, swap = refs[len(others) + 4:]
     walk, vectors = fields_ref.shape
+    own = walk // chips
+    bits = chips.bit_length() - 1
     rowblocks = cols_ref.shape[0]
 
     me = lax.axis_index("chol")
@@ -192,9 +200,10 @@
     at = lax.broadcasted_iota(jnp.int32, (walk, walk), 0)
     source = lax.broadcasted_iota(jnp.int32, (walk, walk), 1)
     chip = at // own
-    z = hop(me // plane, chip // plane, nz)
-    p = hop(me % plane, chip % plane, plane)
-    wanted = (z * plane + p) * own + at % own
+    to = jnp.broadcast_to(me, chip.shape)
+    for k, flip in enumerate(flips(chips, early, lax.axis_index("orb"))):
+        to = to ^ (((chip >> (bits - 1 - k)) & 1) * flip)
+    wanted = to * own + at % own
     pick = (wanted == source).astype(jnp.float32).astype(jnp.bfloat16)
     ordered = jnp.dot(pick, shifted, preferred_element_type=jnp.float32)
     for local in range(rowblocks):
@@ -203,7 +212,7 @@
         for k, mask in enumerate(slot_masks(cols_ref[local, 1:2, :], row)):
             s_ref[local, (k + 1) * walk:(k + 2) * walk] = jnp.where(mask, ordered, 0.0).astype(jnp.bfloat16)
     swap[...] = swap_matrix()
-    first = lax.broadcasted_iota(jnp.int32, (walk, LANES), 1) < BLOCK
+    lower = lax.broadcasted_iota(jnp.int32, (walk, LANES), 1) < BLOCK
 
     def step(t, carry):
         left = s_ref[lax.div(start + t, BLOCK // CHUNK)]
@@ -214,18 +223,18 @@
             )
             for side in range(2):
                 out = both[:, side * LANES:(side + 1) * LANES]
-                near = jnp.where(first, out[0:walk], out[walk:2 * walk])
-                far = jnp.where(first, pltpu.roll(out[2 * walk:3 * walk], BLOCK, 1), out[3 * walk:])
+                near = jnp.where(lower, out[0:walk], out[walk:2 * walk])
+                far = jnp.where(lower, pltpu.roll(out[2 * walk:3 * walk], BLOCK, 1), out[3 * walk:])
                 tiles.append(jnp.concatenate([near, far], axis=1).astype(jnp.bfloat16))
         for w0 in range(0, walk, CHUNK):
             mixed = jnp.concatenate([tile[w0:w0 + CHUNK] for tile in tiles], axis=0)
             mixed = jnp.dot(swap[...], mixed, preferred_element_type=jnp.float32).astype(jnp.bfloat16)
             for w in range(CHUNK):
                 chip, j = (w0 + w) // own, (w0 + w) % own
-                group, inner = (chip % plane, chip // plane) if by_plane else (chip // plane, chip % plane)
+                place = [(chip >> (bits - 1 - k)) & 1 for k in range(bits)]
                 for half in range(2):
                     rows = pl.ds(pl.multiple_of((2 * t + half) * CHUNK, CHUNK), CHUNK)
-                    outs[group][inner, j, rows, :] = (
+                    outs[place[0]][(*place[1:], j, rows)] = (
                         mixed[w * CHUNK:(w + 1) * CHUNK, half * LANES:(half + 1) * LANES]
                     )
         return carry
@@ -233,15 +242,14 @@
     lax.fori_loop(0, steps, step, 0)
 
 
-def potential_call(start, steps, layout, by_plane, fields, bias, others, cols, turned):
-    nz, plane, own = layout
+def potential_call(start, steps, chips, early, fields, bias, others, cols, turned):
     walk, vectors = fields.shape
-    groups, inner = (plane, nz) if by_plane else (nz, plane)
+    inner = (2,) * (chips.bit_length() - 2)
     rows = 2 * CHUNK
     *parts, energy = pl.pallas_call(
-        functools.partial(potential_kernel, start, steps, layout, by_plane),
+        functools.partial(potential_kernel, start, steps, chips, early),
         out_shape=[
-            *[pltpu.VMEM((inner, own, steps * rows, LANES), jnp.bfloat16)] * groups,
+            *[pltpu.VMEM((*inner, walk // chips, steps * rows, LANES), jnp.bfloat16)] * 2,
             pltpu.VMEM((CHUNK, LANES), jnp.float32),
         ],
         scratch_shapes=[
@@ -255,8 +263,8 @@
     return parts, energy
 
 
-def sum_kernel(count, *refs):
-    ins, outs = refs[:count], refs[count:]
+def sum_kernel(count, skip, *refs):
+    ins, outs = refs[:count], refs[count + skip:]
     for k, out in enumerate(outs):
         total = ins[0][k].astype(jnp.float32)
         for ref in ins[1:]:
@@ -264,16 +272,16 @@
         out[...] = total.astype(out.dtype)
 
 
-def sum_call(arrays):
+def sum_call(arrays, after=()):
     pieces = arrays[0].shape[0]
     shape = pltpu.VMEM(arrays[0].shape[1:], jnp.bfloat16)
     return pl.pallas_call(
-        functools.partial(sum_kernel, len(arrays)),
+        functools.partial(sum_kernel, len(arrays), len(after)),
         out_shape=[shape] * pieces,
         cost_estimate=FREE,
         compiler_params=params(16),
         name="sum_parts",
-    )(*in_vmem(*arrays))
+    )(*in_vmem(*arrays, *after))
 
 
 def series_kernel(sizes, *refs):
@@ -333,37 +341,37 @@
     )(*in_vmem(*late, *early, *start, energy))
 
 
-def place_kernel(layout, *refs):
-    nz, plane, own = layout
-    gathered = refs[:plane]
-    out, energy_ref = refs[plane:]
+def place_kernel(chips, mine_ref, theirs_ref, out, energy_ref):
+    bits = chips.bit_length() - 1
+    own = out.shape[0] // chips
+    rows = out.shape[1]
     me = lax.axis_index("chol")
-    rows = out.shape[1]
+    flip = flips(chips, False, lax.axis_index("orb"))
     energy = jnp.zeros((CHUNK, LANES), jnp.float32)
-    for dp in range(plane):
-        for dz in range(nz):
-            z = hop(lax.div(me, plane), -dz if nz & (nz - 1) else dz, nz)
-            p = hop(lax.rem(me, plane), -dp if plane & (plane - 1) else dp, plane)
-            for j in range(own):
-                out[(z * plane + p) * own + j] = gathered[dp][dz, j * rows:(j + 1) * rows]
-            energy = energy + gathered[dp][dz, own * rows:].astype(jnp.float32)
+    for n in range(chips):
+        place = [(n >> (bits - 1 - k)) & 1 for k in range(bits)]
+        chip = me
+        for k in range(bits):
+            chip = chip ^ (place[k] * flip[k])
+        piece = (theirs_ref if place[0] else mine_ref).at[*place[1:]]
+        for j in range(own):
+            out[chip * own + j] = piece[j * rows:(j + 1) * rows]
+        energy = energy + piece[own * rows:].astype(jnp.float32)
     energy_ref[...] = (energy[0:1] + energy[1:2] + energy[2:3])[:, :energy_ref.shape[1]]
 
 
-def place_call(layout, gathered):
-    nz, plane, own = layout
-    walk = nz * plane * own
-    rows = (gathered[0].shape[1] - CHUNK) // own
+def place_call(chips, own, mine, theirs):
+    rows = (mine.shape[-2] - CHUNK) // own
     return pl.pallas_call(
-        functools.partial(place_kernel, layout),
+        functools.partial(place_kernel, chips),
         out_shape=[
-            jax.ShapeDtypeStruct((walk, rows, gathered[0].shape[2]), jnp.bfloat16),
-            jax.ShapeDtypeStruct((1, walk), jnp.float32),
+            jax.ShapeDtypeStruct((chips * own, rows, mine.shape[-1]), jnp.bfloat16),
+            jax.ShapeDtypeStruct((1, chips * own), jnp.float32),
         ],
         cost_estimate=FREE,
         compiler_params=params(16),
         name="place_walkers",
-    )(*in_vmem(*gathered))
+    )(*in_vmem(mine, theirs))
 
 
 def per_device(chol_vals, chol_cols, greens, walkers, fields):
@@ -371,17 +379,14 @@
     walk, half_rows = greens.shape[:2]
     chips = lax.axis_size("chol")
     n_orb = lax.axis_size("orb")
-    plane = 4 if chips % 4 == 0 else 1
-    nz = chips // plane
     own = walk // chips
-    layout = (nz, plane, own)
+    bits = chips.bit_length() - 1
     step_factor = 72.0 / float(vectors * chips * BLOCK) ** 0.5
 
-    def to_plane(a, dp):
-        return lax.ppermute(a, "chol", [(c, (c // plane) * plane + hop(c % plane, dp, plane)) for c in range(chips)])
-
-    def to_z(a, dz):
-        return lax.ppermute(a, "chol", [(c, hop(c // plane, dz, nz) * plane + c % plane) for c in range(chips)])
+    def exchange(a, step, early):
+        order = orders(chips, early)
+        pairs = [(c, c ^ (1 << order[core % 2][step]), core) for c in range(chips) for core in range(n_orb)]
+        return lax.ppermute(a, ("chol", "orb"), [(c * n_orb + core, to * n_orb + core) for c, to, core in pairs])
 
     def around_orb(a):
         return [a] + [lax.ppermute(a, "orb", [((c + d) % n_orb, c) for c in range(n_orb)]) for d in range(1, n_orb)]
@@ -393,18 +398,17 @@
     start, others = lax.optimization_barrier((start, others))
 
     total_steps = rowblocks * BLOCK // CHUNK
-    early_steps = total_steps // 4
+    early_steps = total_steps * 3 // 8
     late_steps = total_steps - early_steps
     fields_t = fields.T
-    early, energy = potential_call(0, early_steps, layout, False, fields_t, bias, others, cols, turned)
-    early_in = [early[0]] + [to_z(early[dz], dz) for dz in range(1, nz)]
-    late, _ = potential_call(early_steps, late_steps, layout, True, fields_t, bias, others, cols, turned)
-    late_in = [late[0]] + [to_plane(late[dp], dp) for dp in range(1, plane)]
-    early_sums = sum_call(early_in)
-    early_in = [early_sums[0]] + [to_plane(early_sums[dp], dp) for dp in range(1, plane)]
-    late_sums = sum_call(late_in)
-    late_in = [late_sums[0]] + [to_z(late_sums[dz], dz) for dz in range(1, nz)]
-
+    late, energy = potential_call(early_steps, late_steps, chips, False, fields_t, bias, others, cols, turned)
+    early, again = potential_call(0, early_steps, chips, True, fields_t, bias, others, cols, turned)
+    for step in range(bits - 1):
+        late = sum_call([late[0], exchange(late[1], step, False)], after=[again] if step == 0 else [])
+    for step in range(bits - 1):
+        early = sum_call([early[0], exchange(early[1], step, True)])
+    late_in = [late[0], exchange(late[1], bits - 1, False)]
+    early_in = [early[0], exchange(early[1], bits - 1, True)]
 
     def finish(arrays):
         total = arrays[0].astype(jnp.float32)
@@ -413,9 +417,9 @@
         return around_orb((step_factor * total).astype(jnp.bfloat16))
 
     piece = series_call((n_orb, late_steps, early_steps), finish(late_in), finish(early_in), start, energy)
-    pieces = jnp.stack([piece] + [to_z(piece, dz) for dz in range(1, nz)])
-    gathered = [pieces] + [to_plane(pieces, dp) for dp in range(1, plane)]
-    moved, energy = place_call(layout, gathered)
+    for step in reversed(range(1, bits)):
+        piece = jnp.stack([piece, exchange(piece, step, False)])
+    moved, energy = place_call(chips, own, piece, exchange(piece, 0, False))
     return moved, energy.reshape(walk)
 
 

time: 78.4 us -> 84.2 us (1.074)
  waiting for transfers between devices: 32.1 us -> 53.7 us
  starting transfers between devices: 27.9 us -> 12.4 us
    ppermute x18 -> x12, waiting for transfers between devices: 30.1 us -> 51.4 us  [exchange(): lax.ppermute(a, ('chol', 'orb'), [(c * n_orb + core, to * n_orb + core) f...]
    ppermute x18 -> x12, starting transfers between devices: 26.7 us -> 11.6 us  [exchange(): lax.ppermute(a, ('chol', 'orb'), [(c * n_orb + core, to * n_orb + core) f...]
    pallas_call x5 -> x9, Pallas kernels: 6.92 us -> 6.51 us  [the longest x2 5.03 us: potential_call(): pl.pallas_call(functools.partial(potential_kernel, start, steps, chips, e...]
  transfers between devices with their start and end apart: 22 -> 16, of which waited for: 8 -> 13; matrix products, arithmetic and copies ran while one was open for 0% -> 0% of each run, Pallas kernels for 2% -> 3%
where the time goes in v7:
time: 84.2 us; the launch traced here: 84 us
  waiting for transfers between devices  53.7 us (64%)
  Pallas kernels  16.3 us (19%)
  starting transfers between devices  12.4 us (15%)
    ppermute x12, waiting for transfers between devices, exchange(): lax.ppermute(a, ('chol', 'orb'), [(c * n_orb + core, to * n_orb + core) f...  51.4 us
    ppermute x12, starting transfers between devices, exchange(): lax.ppermute(a, ('chol', 'orb'), [(c * n_orb + core, to * n_orb + core) f...  11.6 us
    pallas_call x1, Pallas kernels, bias_call(): pl.pallas_call(bias_kernel, in_specs=[*[pl.BlockSpec(memory_space=pl.ANY)...  8.49 us
    pallas_call x2, Pallas kernels, potential_call(): pl.pallas_call(functools.partial(potential_kernel, start, steps, chips, e...  5.03 us
    ppermute x4, waiting for transfers between devices, around_orb(): lax.ppermute(a, 'orb', [((c + d) % n_orb, c) for c in range(n_orb)])  2.35 us
  transfers between devices with their start and end apart: 16, of which 13 were waited for; matrix products, arithmetic and copies ran while one was open for 0% of the time, Pallas kernels for 3%

profile of v7, /device:TPU:0, one launch (start us, length us, event | category | flops | bytes accessed | tf_op | source)
XLA Modules:
  0.0 84.0 jit_solution(6816360018634368322)
XLA Ops:
  0.6 0.0 copy-start
  0.6 0.0 copy-start.1
  0.7 0.7 copy-done.1
  1.3 8.5 %force_bias.1 = (bf16[8,256,2048]{2,1,0:T(8,128)(2,1)S(1)}, f32[32,256]{1,0:T(8,128)S(1)}, bf16[2,128,128]{2,1,0:T(8,128)(2,1)S(1)}) custom-call(bf16[256,2,64,128]{3,2,1,0:T(8,128)(2,1)} %vals_hbm.1, bf16[32,128,256]{2,1,0:T(8,128)(2,1)} %greens_hbm.1, bf16[32,128,128]{2,1,0:T(8,128)(2,1)} %walkers_hbm.1, s32[2,2,256]{2,1,0:T(2,128)S(1)} %bitcast.14), custom_call_target="tpu_custom_call" | custom-call | tf_op jit(solution)/shard_map/force_bias/pallas_call | solution.py:154
  9.8 0.5 collective-permute-start
  10.3 0.1 collective-permute-start.1
  10.4 1.1 %collective-permute-done.1.refs_0_ = f32[32,256]{1,0:T(8,128)S(1)} collective-permute-done((f32[32,256]{1,0:T(8,128)S(1)}, f32[32,256]{1,0:T(8,128)S(1)}, u32[]{:S(2)}, u32[]{:S(2)}) %collective-permute-start.1) | collective-permute-done | bytes 32800 | tf_op jit(solution)/shard_map/ppermute | solution.py:392
  11.6 0.0 collective-permute-done.refs_5_
  11.6 0.0 copy-done
  11.6 3.1 %potential.2 = (bf16[2,2,2,2,160,128]{5,4,3,2,1,0:T(8,128)(2,1)S(1)}, bf16[2,2,2,2,160,128]{5,4,3,2,1,0:T(8,128)(2,1)S(1)}, f32[16,128]{1,0:T(8,128)S(1)}) custom-call(f32[32,256]{1,0:T(8,128)S(1)} %bitcast.12, f32[32,256]{1,0:T(8,128)S(1)} %get-tuple-element.28.own_ref, f32[32,256]{1,0:T(8,128)S(1)} %collective-permute-done.1.refs_0_, ...), custom_call_target="tpu_custom_call" | custom-call | tf_op jit(solution)/shard_map/potential/pallas_call | solution.py:249
  14.7 2.7 %collective-permute-start.2 = (bf16[2,2,2,2,160,128]{5,4,3,2,1,0:T(8,128)(2,1)S(1)}, bf16[2,2,2,2,160,128]{5,4,3,2,1,0:T(8,128)(2,1)S(1)}, u32[]{:S(2)}, u32[]{:S(2)}) collective-permute-start(bf16[2,2,2,2,160,128]{5,4,3,2,1,0:T(8,128)(2,1)S(1)} %get-tuple-element.33), channel_id=1, source_target_pairs={{0,2},{1,5},{2,0},{3,7},{4,6},{5,1},{6,4},{7,3},{8,10},{9,13},{10,... | collective-permute-start | bytes 1966088 | tf_op jit(solution)/shard_map/ppermute | solution.py:389
  17.4 1.9 %potential.3 = (bf16[2,2,2,2,96,128]{5,4,3,2,1,0:T(8,128)(2,1)S(1)}, bf16[2,2,2,2,96,128]{5,4,3,2,1,0:T(8,128)(2,1)S(1)}, f32[16,128]{1,0:T(8,128)S(1)}) custom-call(f32[32,256]{1,0:T(8,128)S(1)} %bitcast.13, f32[32,256]{1,0:T(8,128)S(1)} %get-tuple-element.28.own_ref, f32[32,256]{1,0:T(8,128)S(1)} %collective-permute-done.1.refs_0_, ...), custom_call_target="tpu_custom_call" | custom-call | tf_op jit(solution)/shard_map/potential/pallas_call | solution.py:249
  19.3 1.6 %collective-permute-start.7 = (bf16[2,2,2,2,96,128]{5,4,3,2,1,0:T(8,128)(2,1)S(1)}, bf16[2,2,2,2,96,128]{5,4,3,2,1,0:T(8,128)(2,1)S(1)}, u32[]{:S(2)}, u32[]{:S(2)}) collective-permute-start(bf16[2,2,2,2,96,128]{5,4,3,2,1,0:T(8,128)(2,1)S(1)} %get-tuple-element.42), channel_id=1, source_target_pairs={{0,8},{1,17},{2,10},{3,19},{4,12},{5,21},{6,14},{7,23},{8,0},{9,25... | collective-permute-start | bytes 1179656 | tf_op jit(solution)/shard_map/ppermute | solution.py:389
  21.0 5.0 %collective-permute-done.2.refs_1_ = bf16[2,2,2,2,160,128]{5,4,3,2,1,0:T(8,128)(2,1)S(1)} collective-permute-done((bf16[2,2,2,2,160,128]{5,4,3,2,1,0:T(8,128)(2,1)S(1)}, bf16[2,2,2,2,160,128]{5,4,3,2,1,0:T(8,128)(2,1)S(1)}, u32[]{:S(2)}, u32[]{:S(2)}) %collective-permute-start.2) | collective-permute-done | bytes 655392 | tf_op jit(solution)/shard_map/ppermute | solution.py:389
  25.9 0.2 sum_parts.6
  26.1 2.1 %collective-permute-start.3 = (bf16[2,2,2,160,128]{4,3,2,1,0:T(8,128)(2,1)S(1)}, bf16[2,2,2,160,128]{4,3,2,1,0:T(8,128)(2,1)S(1)}, u32[]{:S(2)}, u32[]{:S(2)}) collective-permute-start(bf16[2,2,2,160,128]{4,3,2,1,0:T(8,128)(2,1)S(1)} %get-tuple-element.36), channel_id=1, source_target_pairs={{0,4},{1,3},{2,6},{3,1},{4,0},{5,7},{6,2},{7,5},{8,12},{9,11},{10,... | collective-permute-start | bytes 983048 | tf_op jit(solution)/shard_map/ppermute | solution.py:389
  28.2 3.1 %collective-permute-done.7.refs_1_ = bf16[2,2,2,2,96,128]{5,4,3,2,1,0:T(8,128)(2,1)S(1)} collective-permute-done((bf16[2,2,2,2,96,128]{5,4,3,2,1,0:T(8,128)(2,1)S(1)}, bf16[2,2,2,2,96,128]{5,4,3,2,1,0:T(8,128)(2,1)S(1)}, u32[]{:S(2)}, u32[]{:S(2)}) %collective-permute-start.7) | collective-permute-done | bytes 393248 | tf_op jit(solution)/shard_map/ppermute | solution.py:389
  31.3 0.1 sum_parts.9
  31.4 1.7 %collective-permute-start.8 = (bf16[2,2,2,96,128]{4,3,2,1,0:T(8,128)(2,1)S(1)}, bf16[2,2,2,96,128]{4,3,2,1,0:T(8,128)(2,1)S(1)}, u32[]{:S(2)}, u32[]{:S(2)}) collective-permute-start(bf16[2,2,2,96,128]{4,3,2,1,0:T(8,128)(2,1)S(1)} %get-tuple-element.44), channel_id=1, source_target_pairs={{0,16},{1,9},{2,18},{3,11},{4,20},{5,13},{6,22},{7,15},{8,24},{9,1... | collective-permute-start | bytes 589832 | tf_op jit(solution)/shard_map/ppermute | solution.py:389
  33.2 0.1 collective-permute-done.3.refs_1_
  33.3 0.1 sum_parts.7
  33.3 2.5 %collective-permute-start.4 = (bf16[2,2,160,128]{3,2,1,0:T(8,128)(2,1)S(1)}, bf16[2,2,160,128]{3,2,1,0:T(8,128)(2,1)S(1)}, u32[]{:S(2)}, u32[]{:S(2)}) collective-permute-start(bf16[2,2,160,128]{3,2,1,0:T(8,128)(2,1)S(1)} %get-tuple-element.38), channel_id=1, source_target_pairs={{0,8},{1,17},{2,10},{3,19},{4,12},{5,21},{6,14},{7,23},{8,0},{9,25... | collective-permute-start | bytes 491528 | tf_op jit(solution)/shard_map/ppermute | solution.py:389
  35.9 7.8 %collective-permute-done.8.refs_1_ = bf16[2,2,2,96,128]{4,3,2,1,0:T(8,128)(2,1)S(1)} collective-permute-done((bf16[2,2,2,96,128]{4,3,2,1,0:T(8,128)(2,1)S(1)}, bf16[2,2,2,96,128]{4,3,2,1,0:T(8,128)(2,1)S(1)}, u32[]{:S(2)}, u32[]{:S(2)}) %collective-permute-start.8) | collective-permute-done | bytes 196640 | tf_op jit(solution)/shard_map/ppermute | solution.py:389
  43.7 0.1 collective-permute-start.9
  43.8 0.0 collective-permute-done.4.refs_1_
  43.9 0.5 collective-permute-start.5
  44.4 4.1 %collective-permute-done.9.refs_1_ = bf16[2,2,96,128]{3,2,1,0:T(8,128)(2,1)S(1)} collective-permute-done((bf16[2,2,96,128]{3,2,1,0:T(8,128)(2,1)S(1)}, bf16[2,2,96,128]{3,2,1,0:T(8,128)(2,1)S(1)}, u32[]{:S(2)}, u32[]{:S(2)}) %collective-permute-start.9) | collective-permute-done | bytes 98336 | tf_op jit(solution)/shard_map/ppermute | solution.py:389
  48.5 0.1 collective-permute-start.10
  48.5 1.6 %collective-permute-done.5 = bf16[2,160,128]{2,1,0:T(8,128)(2,1)S(1)} collective-permute-done((bf16[2,160,128]{2,1,0:T(8,128)(2,1)S(1)}, bf16[2,160,128]{2,1,0:T(8,128)(2,1)S(1)}, u32[]{:S(2)}, u32[]{:S(2)}) %collective-permute-start.5) | collective-permute-done | bytes 81952 | tf_op jit(solution)/shard_map/ppermute | solution.py:389
  50.2 0.1 collective-permute-start.6
  50.3 2.3 %collective-permute-done.10 = bf16[2,96,128]{2,1,0:T(8,128)(2,1)S(1)} collective-permute-done((bf16[2,96,128]{2,1,0:T(8,128)(2,1)S(1)}, bf16[2,96,128]{2,1,0:T(8,128)(2,1)S(1)}, u32[]{:S(2)}, u32[]{:S(2)}) %collective-permute-start.10) | collective-permute-done | bytes 49184 | tf_op jit(solution)/shard_map/ppermute | solution.py:389
  52.6 0.1 collective-permute-start.11
  52.7 1.2 %collective-permute-done.11.refs_3_ = bf16[2,96,128]{2,1,0:T(8,128)(2,1)S(1)} collective-permute-done((bf16[2,96,128]{2,1,0:T(8,128)(2,1)S(1)}, bf16[2,96,128]{2,1,0:T(8,128)(2,1)S(1)}, u32[]{:S(2)}, u32[]{:S(2)}) %collective-permute-start.11) | collective-permute-done | bytes 49184 | tf_op jit(solution)/shard_map/ppermute | solution.py:392
  53.9 0.0 collective-permute-done.6.refs_1_
  53.9 1.3 %series.1 = bf16[272,128]{1,0:T(8,128)(2,1)S(1)} custom-call(bf16[2,160,128]{2,1,0:T(8,128)(2,1)S(1)} %multiply_convert_fusion.refs_0_, bf16[2,160,128]{2,1,0:T(8,128)(2,1)S(1)} %collective-permute-done.6.refs_1_, bf16[2,96,128]{2,1,0:T(8,128)(2,1)S(1)} %multiply_convert_fusion.1.refs_2_, bf16[2,96,128]{2,1,0:T(8,128)(2,1)S(1)} %collective-permute-done.11.refs_3_, ...), custom_call_target="tpu_custom_call" | custom-call | tf_op jit(solution)/shard_map/series/pallas_call | solution.py:330
  55.2 0.1 collective-permute-start.12
  55.3 5.9 %collective-permute-done.12 = bf16[272,128]{1,0:T(8,128)(2,1)S(1)} collective-permute-done((bf16[272,128]{1,0:T(8,128)(2,1)S(1)}, bf16[272,128]{1,0:T(8,128)(2,1)S(1)}, u32[]{:S(2)}, u32[]{:S(2)}) %collective-permute-start.12) | collective-permute-done | bytes 69664 | tf_op jit(solution)/shard_map/ppermute | solution.py:389
  61.3 0.1 collective-permute-start.13
  61.3 5.3 %collective-permute-done.13 = bf16[2,272,128]{2,1,0:T(8,128)(2,1)S(1)} collective-permute-done((bf16[2,272,128]{2,1,0:T(8,128)(2,1)S(1)}, bf16[2,272,128]{2,1,0:T(8,128)(2,1)S(1)}, u32[]{:S(2)}, u32[]{:S(2)}) %collective-permute-start.13) | collective-permute-done | bytes 139296 | tf_op jit(solution)/shard_map/ppermute | solution.py:389
  66.7 0.1 collective-permute-start.14
  66.8 6.5 %collective-permute-done.14 = bf16[2,2,272,128]{3,2,1,0:T(8,128)(2,1)S(1)} collective-permute-done((bf16[2,2,272,128]{3,2,1,0:T(8,128)(2,1)S(1)}, bf16[2,2,272,128]{3,2,1,0:T(8,128)(2,1)S(1)}, u32[]{:S(2)}, u32[]{:S(2)}) %collective-permute-start.14) | collective-permute-done | bytes 278560 | tf_op jit(solution)/shard_map/ppermute | solution.py:389
  73.3 0.1 pad_maximum_fusion.mine_ref
  73.4 0.1 collective-permute-start.15
  73.5 9.5 %collective-permute-done.15.theirs_ref = bf16[2,2,2,272,128]{4,3,2,1,0:T(8,128)(2,1)S(1)} collective-permute-done((bf16[2,2,2,272,128]{4,3,2,1,0:T(8,128)(2,1)S(1)}, bf16[2,2,2,272,128]{4,3,2,1,0:T(8,128)(2,1)S(1)}, u32[]{:S(2)}, u32[]{:S(2)}) %collective-permute-start.15) | collective-permute-done | bytes 557088 | tf_op jit(solution)/shard_map/ppermute | solution.py:389
  83.0 1.1 %place_walkers.1 = (bf16[32,128,128]{2,1,0:T(8,128)(2,1)}, f32[1,32]{1,0:T(1,128)}) custom-call(bf16[2,2,2,272,128]{4,3,2,1,0:T(8,128)(2,1)S(1)} %pad_maximum_fusion.mine_ref, bf16[2,2,2,272,128]{4,3,2,1,0:T(8,128)(2,1)S(1)} %collective-permute-done.15.theirs_ref), custom_call_target="tpu_custom_call" | custom-call | tf_op jit(solution)/shard_map/place_walkers/pallas_call | solution.py:365
  (7 shorter events, 0.2 us)
Async XLA Ops:
  0.6 10.9 %copy-start = (f32[256,32]{0,1:T(8,128)S(1)}, f32[256,32]{0,1:T(8,128)}, u32[]{:S(2)}) copy-start(f32[256,32]{0,1:T(8,128)} %param.9) | copy-start | bytes 98308
  0.6 0.7 copy-start.1
  9.8 1.7 %collective-permute-start = (bf16[2,128,128]{2,1,0:T(8,128)(2,1)S(1)}, bf16[2,128,128]{2,1,0:T(8,128)(2,1)S(1)}, u32[]{:S(2)}, u32[]{:S(2)}) collective-permute-start(bf16[2,128,128]{2,1,0:T(8,128)(2,1)S(1)} %get-tuple-element.49.refs_4_), channel_id=1, source_target_pairs={{1,0},{0,1},{3,2},{2,3},{5,4},{4,5},{7,6},{6,7},{9,8},{8,9},{11,10... | collective-permute-start | bytes 196616 | tf_op jit(solution)/shard_map/ppermute | solution.py:392
  10.3 1.2 %collective-permute-start.1 = (f32[32,256]{1,0:T(8,128)S(1)}, f32[32,256]{1,0:T(8,128)S(1)}, u32[]{:S(2)}, u32[]{:S(2)}) collective-permute-start(f32[32,256]{1,0:T(8,128)S(1)} %get-tuple-element.28.own_ref), channel_id=1, source_target_pairs={{1,0},{0,1},{3,2},{2,3},{5,4},{4,5},{7,6},{6,7},{9,8},{8,9},{11,10... | collective-permute-start | bytes 98312 | tf_op jit(solution)/shard_map/ppermute | solution.py:392
  14.7 11.3 %collective-permute-start.2 = (bf16[2,2,2,2,160,128]{5,4,3,2,1,0:T(8,128)(2,1)S(1)}, bf16[2,2,2,2,160,128]{5,4,3,2,1,0:T(8,128)(2,1)S(1)}, u32[]{:S(2)}, u32[]{:S(2)}) collective-permute-start(bf16[2,2,2,2,160,128]{5,4,3,2,1,0:T(8,128)(2,1)S(1)} %get-tuple-element.33), channel_id=1, source_target_pairs={{0,2},{1,5},{2,0},{3,7},{4,6},{5,1},{6,4},{7,3},{8,10},{9,13},{10,... | collective-permute-start | bytes 1966088 | tf_op jit(solution)/shard_map/ppermute | solution.py:389
  19.3 12.0 %collective-permute-start.7 = (bf16[2,2,2,2,96,128]{5,4,3,2,1,0:T(8,128)(2,1)S(1)}, bf16[2,2,2,2,96,128]{5,4,3,2,1,0:T(8,128)(2,1)S(1)}, u32[]{:S(2)}, u32[]{:S(2)}) collective-permute-start(bf16[2,2,2,2,96,128]{5,4,3,2,1,0:T(8,128)(2,1)S(1)} %get-tuple-element.42), channel_id=1, source_target_pairs={{0,8},{1,17},{2,10},{3,19},{4,12},{5,21},{6,14},{7,23},{8,0},{9,25... | collective-permute-start | bytes 1179656 | tf_op jit(solution)/shard_map/ppermute | solution.py:389
  26.1 7.2 %collective-permute-start.3 = (bf16[2,2,2,160,128]{4,3,2,1,0:T(8,128)(2,1)S(1)}, bf16[2,2,2,160,128]{4,3,2,1,0:T(8,128)(2,1)S(1)}, u32[]{:S(2)}, u32[]{:S(2)}) collective-permute-start(bf16[2,2,2,160,128]{4,3,2,1,0:T(8,128)(2,1)S(1)} %get-tuple-element.36), channel_id=1, source_target_pairs={{0,4},{1,3},{2,6},{3,1},{4,0},{5,7},{6,2},{7,5},{8,12},{9,11},{10,... | collective-permute-start | bytes 983048 | tf_op jit(solution)/shard_map/ppermute | solution.py:389
  31.4 12.3 %collective-permute-start.8 = (bf16[2,2,2,96,128]{4,3,2,1,0:T(8,128)(2,1)S(1)}, bf16[2,2,2,96,128]{4,3,2,1,0:T(8,128)(2,1)S(1)}, u32[]{:S(2)}, u32[]{:S(2)}) collective-permute-start(bf16[2,2,2,96,128]{4,3,2,1,0:T(8,128)(2,1)S(1)} %get-tuple-element.44), channel_id=1, source_target_pairs={{0,16},{1,9},{2,18},{3,11},{4,20},{5,13},{6,22},{7,15},{8,24},{9,1... | collective-permute-start | bytes 589832 | tf_op jit(solution)/shard_map/ppermute | solution.py:389
  33.3 10.5 %collective-permute-start.4 = (bf16[2,2,160,128]{3,2,1,0:T(8,128)(2,1)S(1)}, bf16[2,2,160,128]{3,2,1,0:T(8,128)(2,1)S(1)}, u32[]{:S(2)}, u32[]{:S(2)}) collective-permute-start(bf16[2,2,160,128]{3,2,1,0:T(8,128)(2,1)S(1)} %get-tuple-element.38), channel_id=1, source_target_pairs={{0,8},{1,17},{2,10},{3,19},{4,12},{5,21},{6,14},{7,23},{8,0},{9,25... | collective-permute-start | bytes 491528 | tf_op jit(solution)/shard_map/ppermute | solution.py:389
  43.7 4.7 %collective-permute-start.9 = (bf16[2,2,96,128]{3,2,1,0:T(8,128)(2,1)S(1)}, bf16[2,2,96,128]{3,2,1,0:T(8,128)(2,1)S(1)}, u32[]{:S(2)}, u32[]{:S(2)}) collective-permute-start(bf16[2,2,96,128]{3,2,1,0:T(8,128)(2,1)S(1)} %get-tuple-element.46), channel_id=1, source_target_pairs={{0,2},{1,5},{2,0},{3,7},{4,6},{5,1},{6,4},{7,3},{8,10},{9,13},{10,... | collective-permute-start | bytes 294920 | tf_op jit(solution)/shard_map/ppermute | solution.py:389
  43.9 6.3 %collective-permute-start.5 = (bf16[2,160,128]{2,1,0:T(8,128)(2,1)S(1)}, bf16[2,160,128]{2,1,0:T(8,128)(2,1)S(1)}, u32[]{:S(2)}, u32[]{:S(2)}) collective-permute-start(bf16[2,160,128]{2,1,0:T(8,128)(2,1)S(1)} %get-tuple-element.40), channel_id=1, source_target_pairs={{0,16},{1,9},{2,18},{3,11},{4,20},{5,13},{6,22},{7,15},{8,24},{9,1... | collective-permute-start | bytes 245768 | tf_op jit(solution)/shard_map/ppermute | solution.py:389
  48.5 4.2 %collective-permute-start.10 = (bf16[2,96,128]{2,1,0:T(8,128)(2,1)S(1)}, bf16[2,96,128]{2,1,0:T(8,128)(2,1)S(1)}, u32[]{:S(2)}, u32[]{:S(2)}) collective-permute-start(bf16[2,96,128]{2,1,0:T(8,128)(2,1)S(1)} %get-tuple-element.48), channel_id=1, source_target_pairs={{0,4},{1,3},{2,6},{3,1},{4,0},{5,7},{6,2},{7,5},{8,12},{9,11},{10,... | collective-permute-start | bytes 147464 | tf_op jit(solution)/shard_map/ppermute | solution.py:389
  50.2 3.7 %collective-permute-start.6 = (bf16[2,160,128]{2,1,0:T(8,128)(2,1)S(1)}, bf16[2,160,128]{2,1,0:T(8,128)(2,1)S(1)}, u32[]{:S(2)}, u32[]{:S(2)}) collective-permute-start(bf16[2,160,128]{2,1,0:T(8,128)(2,1)S(1)} %multiply_convert_fusion.refs_0_), channel_id=1, source_target_pairs={{1,0},{0,1},{3,2},{2,3},{5,4},{4,5},{7,6},{6,7},{9,8},{8,9},{11,10... | collective-permute-start | bytes 245768 | tf_op jit(solution)/shard_map/ppermute | solution.py:392
  52.6 1.3 %collective-permute-start.11 = (bf16[2,96,128]{2,1,0:T(8,128)(2,1)S(1)}, bf16[2,96,128]{2,1,0:T(8,128)(2,1)S(1)}, u32[]{:S(2)}, u32[]{:S(2)}) collective-permute-start(bf16[2,96,128]{2,1,0:T(8,128)(2,1)S(1)} %multiply_convert_fusion.1.refs_2_), channel_id=1, source_target_pairs={{1,0},{0,1},{3,2},{2,3},{5,4},{4,5},{7,6},{6,7},{9,8},{8,9},{11,10... | collective-permute-start | bytes 147464 | tf_op jit(solution)/shard_map/ppermute | solution.py:392
  55.2 6.0 %collective-permute-start.12 = (bf16[272,128]{1,0:T(8,128)(2,1)S(1)}, bf16[272,128]{1,0:T(8,128)(2,1)S(1)}, u32[]{:S(2)}, u32[]{:S(2)}) collective-permute-start(bf16[272,128]{1,0:T(8,128)(2,1)S(1)} %series.1), channel_id=1, source_target_pairs={{0,16},{1,9},{2,18},{3,11},{4,20},{5,13},{6,22},{7,15},{8,24},{9,1... | collective-permute-start | bytes 208904 | tf_op jit(solution)/shard_map/ppermute | solution.py:389
  61.3 5.4 %collective-permute-start.13 = (bf16[2,272,128]{2,1,0:T(8,128)(2,1)S(1)}, bf16[2,272,128]{2,1,0:T(8,128)(2,1)S(1)}, u32[]{:S(2)}, u32[]{:S(2)}) collective-permute-start(bf16[2,272,128]{2,1,0:T(8,128)(2,1)S(1)} %get-tuple-element.57), channel_id=1, source_target_pairs={{0,8},{1,17},{2,10},{3,19},{4,12},{5,21},{6,14},{7,23},{8,0},{9,25... | collective-permute-start | bytes 417800 | tf_op jit(solution)/shard_map/ppermute | solution.py:389
  66.7 6.6 %collective-permute-start.14 = (bf16[2,2,272,128]{3,2,1,0:T(8,128)(2,1)S(1)}, bf16[2,2,272,128]{3,2,1,0:T(8,128)(2,1)S(1)}, u32[]{:S(2)}, u32[]{:S(2)}) collective-permute-start(bf16[2,2,272,128]{3,2,1,0:T(8,128)(2,1)S(1)} %get-tuple-element.55), channel_id=1, source_target_pairs={{0,4},{1,3},{2,6},{3,1},{4,0},{5,7},{6,2},{7,5},{8,12},{9,11},{10,... | collective-permute-start | bytes 835592 | tf_op jit(solution)/shard_map/ppermute | solution.py:389
  73.4 9.6 %collective-permute-start.15 = (bf16[2,2,2,272,128]{4,3,2,1,0:T(8,128)(2,1)S(1)}, bf16[2,2,2,272,128]{4,3,2,1,0:T(8,128)(2,1)S(1)}, u32[]{:S(2)}, u32[]{:S(2)}) collective-permute-start(bf16[2,2,2,272,128]{4,3,2,1,0:T(8,128)(2,1)S(1)} %pad_maximum_fusion.mine_ref), channel_id=1, source_target_pairs={{0,2},{1,5},{2,0},{3,7},{4,6},{5,1},{6,4},{7,3},{8,10},{9,13},{10,... | collective-permute-start | bytes 1671176 | tf_op jit(solution)/shard_map/ppermute | solution.py:389

commit v8 on v6

--- a/solution.py
+++ b/solution.py
@@ -58,8 +58,8 @@
     return [cols == column for column in column_order(row)[1:]]
 
 
-def bias_kernel(vals_hbm, greens_hbm, walkers_hbm, cols_ref, turned_ref, bias_ref, mine_ref, vals, greens, swap, gs, acc, vsem,
-                gsem, wsem):
+def bias_kernel(vals_hbm, greens_hbm, walkers_hbm, cols_hbm, turned_ref, bias_ref, mine_ref, cols_ref, vals, greens, swap, gs,
+                acc, vsem, gsem, wsem, csem):
     total_steps, vectors = turned_ref.shape[:2]
     walk = bias_ref.shape[0]
     steps = BLOCK // CHUNK
@@ -80,15 +80,17 @@
     lax.fori_loop(0, total_steps, begin, 0)
     take = pltpu.make_async_copy(walkers_hbm.at[pl.ds(lax.axis_index("chol") * own, own)], mine_ref, wsem)
     take.start()
+    take_cols = pltpu.make_async_copy(cols_hbm, cols_ref, csem)
+    take_cols.start()
     swap[...] = swap_matrix()
     bias_ref[...] = jnp.zeros_like(bias_ref)
     first = lax.broadcasted_iota(jnp.int32, (CHUNK * CHUNK, LANES), 1) < BLOCK
 
-    def step(t, carry):
+    def turn(t):
         for copy in copies(t):
             copy.wait()
-        local = lax.div(t, steps)
-        row = lax.axis_index("orb") * cols_ref.shape[0] + local
+        slot = lax.rem(t, 2)
+        row = lax.axis_index("orb") * cols_ref.shape[0] + lax.div(t, steps)
         upper = row // 2 == 1
         odd = row % 2 == 1
         for w in range(0, walk, CHUNK):
@@ -106,7 +108,9 @@
             for k, piece in enumerate(pieces):
                 piece = piece.astype(jnp.bfloat16)
                 for i in range(CHUNK):
-                    gs[k * walk + w:k * walk + w + CHUNK, i * LANES:(i + 1) * LANES] = piece[i * CHUNK:(i + 1) * CHUNK]
+                    gs[slot, k * walk + w:k * walk + w + CHUNK, i * LANES:(i + 1) * LANES] = (
+                        piece[i * CHUNK:(i + 1) * CHUNK]
+                    )
         for g in range(0, vectors, 2 * CHUNK):
             both = [vals[t, g + side * CHUNK:g + (side + 1) * CHUNK].reshape(CHUNK * CHUNK, LANES) for side in range(2)]
             both = jnp.dot(swap[...], jnp.concatenate(both, axis=1), preferred_element_type=jnp.float32)
@@ -116,25 +120,38 @@
                     turned_ref[t, g + side * CHUNK:g + (side + 1) * CHUNK, i * LANES:(i + 1) * LANES] = (
                         both[i * CHUNK:(i + 1) * CHUNK, side * LANES:(side + 1) * LANES]
                     )
-        part = lax.dot_general(
-            turned_ref[t], gs[...], (((1,), (1,)), ((), ())), preferred_element_type=jnp.float32
+
+    def product(t):
+        return lax.dot_general(
+            turned_ref[t], gs[lax.rem(t, 2)], (((1,), (1,)), ((), ())), preferred_element_type=jnp.float32
         )
-        begins = lax.rem(t, steps) == 0
-        acc[...] = jnp.where(begins, 0.0, acc[...]) + part
-
-        @pl.when(lax.rem(t, steps) == steps - 1)
+
+    def close(t):
+        local = lax.div(t, steps)
+        row = lax.axis_index("orb") * cols_ref.shape[0] + local
+        flat = acc[...].T
+        total = flat[0:walk]
+        for k, mask in enumerate(slot_masks(cols_ref[local, 1:2, :], row)):
+            total = total + jnp.where(mask, flat[(k + 1) * walk:(k + 2) * walk], 0.0)
+        bias_ref[...] += total
+
+    def step(t, carry):
+        part = product(t - 1)
+        turn(t)
+        acc[...] = jnp.where(lax.rem(t - 1, steps) == 0, 0.0, acc[...]) + part
+
+        @pl.when(lax.rem(t, steps) == 0)
         def _():
-            flat = acc[...].T
-            total = flat[0:walk]
-            cols = cols_ref[local, 1:2, :]
-            for k, mask in enumerate(slot_masks(cols, row)):
-                total = total + jnp.where(mask, flat[(k + 1) * walk:(k + 2) * walk], 0.0)
-            bias_ref[...] += total
+            close(t - 1)
 
         return carry
 
     acc[...] = jnp.zeros_like(acc)
-    lax.fori_loop(0, total_steps, step, 0)
+    turn(0)
+    take_cols.wait()
+    lax.fori_loop(1, total_steps, step, 0)
+    acc[...] += product(total_steps - 1)
+    close(total_steps - 1)
     take.wait()
 
 
@@ -146,29 +163,30 @@
     return pl.pallas_call(
         bias_kernel,
         in_specs=[
-            *[pl.BlockSpec(memory_space=pl.ANY)] * 3,
-            pl.BlockSpec(memory_space=pltpu.VMEM),
-        ],
-        out_specs=[pl.BlockSpec(memory_space=pltpu.VMEM)] * 3,
+            *[pl.BlockSpec(memory_space=pl.ANY)] * 4,
+        ],
+        out_specs=[pl.BlockSpec(memory_space=pltpu.VMEM)] * 4,
         out_shape=[
             pltpu.VMEM((steps, vectors, wide), jnp.bfloat16),
             pltpu.VMEM((walk, vectors), jnp.float32),
             pltpu.VMEM((own, *walkers.shape[1:]), jnp.bfloat16),
+            pltpu.VMEM(cols.shape, jnp.int32),
         ],
         scratch_shapes=[
             pltpu.VMEM((steps, vectors, CHUNK, LANES), jnp.bfloat16),
             pltpu.VMEM((steps, walk, CHUNK, norb), jnp.bfloat16),
             pltpu.VMEM((CHUNK * CHUNK, CHUNK * CHUNK), jnp.bfloat16),
-            pltpu.VMEM((4 * walk, wide), jnp.bfloat16),
+            pltpu.VMEM((2, 4 * walk, wide), jnp.bfloat16),
             pltpu.VMEM((vectors, 4 * walk), jnp.float32),
             pltpu.SemaphoreType.DMA((steps,)),
             pltpu.SemaphoreType.DMA((steps,)),
             pltpu.SemaphoreType.DMA,
+            pltpu.SemaphoreType.DMA,
         ],
         cost_estimate=FREE,
         compiler_params=params(24),
         name="force_bias",
-    )(*in_hbm(vals, greens, walkers), cols)
+    )(*in_hbm(vals, greens, walkers, cols))
 
 
 def potential_kernel(start, steps, layout, by_plane, fields_ref, own_ref, *refs):
@@ -222,15 +240,16 @@
             mixed = jnp.dot(swap[...], mixed, preferred_element_type=jnp.float32).astype(jnp.bfloat16)
             for w in range(CHUNK):
                 chip, j = (w0 + w) // own, (w0 + w) % own
-                group, inner = (chip % plane, chip // plane) if by_plane else (chip // plane, chip % plane)
+                dz, dp = chip // plane, chip % plane
+                out, inner = (outs[dp], dz) if by_plane else (outs[dz], dp)
                 for half in range(2):
                     rows = pl.ds(pl.multiple_of((2 * t + half) * CHUNK, CHUNK), CHUNK)
-                    outs[group][inner, j, rows, :] = (
-                        mixed[w * CHUNK:(w + 1) * CHUNK, half * LANES:(half + 1) * LANES]
-                    )
+                    out[inner, j, rows] = mixed[w * CHUNK:(w + 1) * CHUNK, half * LANES:(half + 1) * LANES]
         return carry
 
-    lax.fori_loop(0, steps, step, 0)
+    lax.fori_loop(0, steps // 2, lambda t, carry: step(2 * t + 1, step(2 * t, carry)), 0)
+    if steps % 2:
+        step(steps - 1, 0)
 
 
 def potential_call(start, steps, layout, by_plane, fields, bias, others, cols, turned):
@@ -251,35 +270,60 @@
         cost_estimate=FREE,
         compiler_params=params(16),
         name="potential",
-    )(fields, *in_vmem(bias, *others), cols, *in_vmem(turned))
+    )(fields, *in_vmem(bias, *others, cols, turned))
     return parts, energy
 
 
-def sum_kernel(count, *refs):
-    ins, outs = refs[:count], refs[count:]
-    for k, out in enumerate(outs):
-        total = ins[0][k].astype(jnp.float32)
-        for ref in ins[1:]:
-            total = total + ref[k].astype(jnp.float32)
-        out[...] = total.astype(out.dtype)
+def add(refs, *at):
+    total = refs[0][at].astype(jnp.float32)
+    for ref in refs[1:]:
+        total = total + ref[at].astype(jnp.float32)
+    return total
+
+
+def vmem_call(kernel, name, out_shape, *arrays):
+    return pl.pallas_call(
+        kernel, out_shape=out_shape, cost_estimate=FREE, compiler_params=params(16), name=name
+    )(*in_vmem(*arrays))
 
 
 def sum_call(arrays):
-    pieces = arrays[0].shape[0]
-    shape = pltpu.VMEM(arrays[0].shape[1:], jnp.bfloat16)
-    return pl.pallas_call(
-        functools.partial(sum_kernel, len(arrays)),
-        out_shape=[shape] * pieces,
-        cost_estimate=FREE,
-        compiler_params=params(16),
-        name="sum_parts",
-    )(*in_vmem(*arrays))
-
-
-def series_kernel(sizes, *refs):
-    n_orb, late_steps, early_steps = sizes
-    late, early, start = refs[:n_orb], refs[n_orb:2 * n_orb], refs[2 * n_orb:3 * n_orb]
-    energy_ref, moved_ref, pot, term, total = refs[3 * n_orb:]
+    def kernel(*refs):
+        for k, out in enumerate(refs[len(arrays):]):
+            out[...] = add(refs[:len(arrays)], k).astype(out.dtype)
+
+    out_shape = [pltpu.VMEM(arrays[0].shape[1:], jnp.bfloat16)] * arrays[0].shape[0]
+    return vmem_call(kernel, "sum_parts", out_shape, *arrays)
+
+
+def finish_call(factor, early, late):
+    own, rows, lanes = early[0].shape
+
+    def kernel(*refs):
+        out = refs[-1]
+        out[:, :rows] = (factor * add(refs[:len(early)], Ellipsis)).astype(out.dtype)
+        out[:, rows:] = (factor * add(refs[len(early):-1], Ellipsis)).astype(out.dtype)
+
+    out_shape = pltpu.VMEM((own, rows + late[0].shape[1], lanes), jnp.bfloat16)
+    return vmem_call(kernel, "finish", out_shape, *early, *late)
+
+
+def stack_call(pieces, slots, near):
+    def kernel(*refs):
+        ins, outs = refs[:len(pieces) + len(near)], refs[len(pieces) + len(near):]
+        for ref, slot in zip(ins, slots):
+            outs[0][slot] = ref[...]
+        for ref, out in zip(ins[len(pieces):], outs[1:]):
+            out[...] = ref[...]
+
+    one = pltpu.VMEM(pieces[0].shape, jnp.bfloat16)
+    out_shape = [pltpu.VMEM((len(pieces), *pieces[0].shape), jnp.bfloat16)] + [one] * len(near)
+    return vmem_call(kernel, "stack_pieces", out_shape, *pieces, *near)
+
+
+def series_kernel(n_orb, *refs):
+    found, start = refs[:n_orb], refs[n_orb:2 * n_orb]
+    energy_ref, moved_ref, pot, term, total = refs[2 * n_orb:]
     me = lax.axis_index("orb")
     own, half_rows = start[0].shape[:2]
     rowblocks = half_rows // BLOCK
@@ -288,11 +332,10 @@
         at = lax.rem(me + d, n_orb)
         term[pl.ds(at, 1)] = start[d][...][None]
         for t in range(rowblocks * per):
-            ref, k = (early[d], t) if t < early_steps else (late[d], t - early_steps)
             for half in range(2):
-                rows = slice((2 * k + half) * CHUNK, (2 * k + half + 1) * CHUNK)
+                rows = slice((2 * t + half) * CHUNK, (2 * t + half + 1) * CHUNK)
                 pot[pl.ds(at * rowblocks + t // per, 1), :, (t % per) * CHUNK:(t % per + 1) * CHUNK,
-                    half * LANES:(half + 1) * LANES] = ref[:, rows, :][None]
+                    half * LANES:(half + 1) * LANES] = found[d][:, rows, :][None]
     for j in range(own):
         blocks = [term[r // rowblocks, j, (r % rowblocks) * BLOCK:(r % rowblocks + 1) * BLOCK] for r in range(ROWBLK)]
         sums = [jnp.zeros(blocks[0].shape, jnp.float32)] * ROWBLK
@@ -316,11 +359,11 @@
     moved_ref[own * half_rows:] = tile.astype(jnp.bfloat16)
 
 
-def series_call(sizes, late, early, start, energy):
-    n_orb = sizes[0]
+def series_call(found, start, energy):
+    n_orb = len(found)
     own, half_rows, nocc = start[0].shape
     return pl.pallas_call(
-        functools.partial(series_kernel, sizes),
+        functools.partial(series_kernel, n_orb),
         out_shape=pltpu.VMEM((own * half_rows + CHUNK, nocc), jnp.bfloat16),
         scratch_shapes=[
             pltpu.VMEM((ROWBLK, own, BLOCK, 2 * LANES), jnp.bfloat16),
@@ -330,13 +373,13 @@
         cost_estimate=FREE,
         compiler_params=params(16),
         name="series",
-    )(*in_vmem(*late, *early, *start, energy))
+    )(*in_vmem(*found, *start, energy))
 
 
 def place_kernel(layout, *refs):
     nz, plane, own = layout
-    gathered = refs[:plane]
-    out, energy_ref = refs[plane:]
+    near, far = refs[:plane], refs[plane:2 * plane]
+    out, energy_ref = refs[2 * plane:]
     me = lax.axis_index("chol")
     rows = out.shape[1]
     energy = jnp.zeros((CHUNK, LANES), jnp.float32)
@@ -344,26 +387,27 @@
         for dz in range(nz):
             z = hop(lax.div(me, plane), -dz if nz & (nz - 1) else dz, nz)
             p = hop(lax.rem(me, plane), -dp if plane & (plane - 1) else dp, plane)
+            piece = far[dp].at[dz - 1] if dz else near[dp]
             for j in range(own):
-                out[(z * plane + p) * own + j] = gathered[dp][dz, j * rows:(j + 1) * rows]
-            energy = energy + gathered[dp][dz, own * rows:].astype(jnp.float32)
+                out[(z * plane + p) * own + j] = piece[j * rows:(j + 1) * rows]
+            energy = energy + piece[own * rows:].astype(jnp.float32)
     energy_ref[...] = (energy[0:1] + energy[1:2] + energy[2:3])[:, :energy_ref.shape[1]]
 
 
-def place_call(layout, gathered):
+def place_call(layout, near, far):
     nz, plane, own = layout
     walk = nz * plane * own
-    rows = (gathered[0].shape[1] - CHUNK) // own
+    rows = (near[0].shape[0] - CHUNK) // own
     return pl.pallas_call(
         functools.partial(place_kernel, layout),
         out_shape=[
-            jax.ShapeDtypeStruct((walk, rows, gathered[0].shape[2]), jnp.bfloat16),
+            jax.ShapeDtypeStruct((walk, rows, near[0].shape[1]), jnp.bfloat16),
             jax.ShapeDtypeStruct((1, walk), jnp.float32),
         ],
         cost_estimate=FREE,
         compiler_params=params(16),
         name="place_walkers",
-    )(*in_vmem(*gathered))
+    )(*in_vmem(*near, *far))
 
 
 def per_device(chol_vals, chol_cols, greens, walkers, fields):
@@ -387,7 +431,7 @@
         return [a] + [lax.ppermute(a, "orb", [((c + d) % n_orb, c) for c in range(n_orb)]) for d in range(1, n_orb)]
 
     cols = jnp.transpose(chol_cols, (1, 2, 0))
-    turned, partial_bias, mine = bias_call(chol_vals, greens, walkers, cols, own)
+    turned, partial_bias, mine, cols = bias_call(chol_vals, greens, walkers, cols, own)
     start = around_orb(mine)
     bias, *others = around_orb(partial_bias)
     start, others = lax.optimization_barrier((start, others))
@@ -396,26 +440,28 @@
     early_steps = total_steps // 4
     late_steps = total_steps - early_steps
     fields_t = fields.T
-    early, energy = potential_call(0, early_steps, layout, False, fields_t, bias, others, cols, turned)
-    early_in = [early[0]] + [to_z(early[dz], dz) for dz in range(1, nz)]
-    late, _ = potential_call(early_steps, late_steps, layout, True, fields_t, bias, others, cols, turned)
-    late_in = [late[0]] + [to_plane(late[dp], dp) for dp in range(1, plane)]
-    early_sums = sum_call(early_in)
-    early_in = [early_sums[0]] + [to_plane(early_sums[dp], dp) for dp in range(1, plane)]
-    late_sums = sum_call(late_in)
-    late_in = [late_sums[0]] + [to_z(late_sums[dz], dz) for dz in range(1, nz)]
-
-
-    def finish(arrays):
-        total = arrays[0].astype(jnp.float32)
-        for a in arrays[1:]:
-            total = total + a.astype(jnp.float32)
-        return around_orb((step_factor * total).astype(jnp.bfloat16))
-
-    piece = series_call((n_orb, late_steps, early_steps), finish(late_in), finish(early_in), start, energy)
-    pieces = jnp.stack([piece] + [to_z(piece, dz) for dz in range(1, nz)])
-    gathered = [pieces] + [to_plane(pieces, dp) for dp in range(1, plane)]
-    moved, energy = place_call(layout, gathered)
+    def all_plane(arrays):
+        return [to_plane(arrays[dp - 1], dp) for dp in reversed(range(1, plane))]
+
+    z_order = [*range(2, nz), 1]
+
+    def all_z(arrays):
+        return [to_z(arrays[dz - 1], dz) for dz in z_order]
+
+    late, energy = potential_call(early_steps, late_steps, layout, True, fields_t, bias, others, cols, turned)
+    early, _ = potential_call(0, early_steps, layout, False, fields_t, bias, others, cols, turned)
+    early_came = all_z(early[1:])
+    late = sum_call([late[0], *all_plane(late[1:])])
+    late_came = all_z(late[1:])
+    early = sum_call([early[0], *early_came])
+    found = finish_call(step_factor, [early[0], *all_plane(early[1:])], [late[0], *late_came])
+
+    piece = series_call(around_orb(found), start, energy)
+    near = [piece, *(to_plane(piece, dp) for dp in range(1, plane))]
+    came = all_z([piece] * (nz - 1))
+    pieces, *near[1:] = stack_call(came, [dz - 1 for dz in z_order], near[1:])
+    far = {dp: to_plane(pieces, dp) for dp in reversed(range(1, plane))}
+    moved, energy = place_call(layout, near, [pieces, *(far[dp] for dp in range(1, plane))])
     return moved, energy.reshape(walk)
 
 

time: 78.4 us -> 78.8 us (level)
  waiting for transfers between devices: 32.1 us -> 27.1 us
  starting transfers between devices: 27.9 us -> 31.8 us
  Pallas kernels: 16.7 us -> 19 us
    ppermute x9, waiting for transfers between devices: 9.38 us -> 1.63 us  [to_z(): lax.ppermute(a, 'chol', [(c, hop(c // plane, dz, nz) * plane + c % plane)...]
    ppermute x9 -> x12, starting transfers between devices: 11.3 us -> 16.2 us  [to_plane(): lax.ppermute(a, 'chol', [(c, c // plane * plane + hop(c % plane, dp, plan...]
    pallas_call x1, Pallas kernels: 8.49 us -> 11.5 us  [bias_call(): pl.pallas_call(bias_kernel, in_specs=[*[pl.BlockSpec(memory_space=pl.ANY)...]
    ppermute x9 -> x12, waiting for transfers between devices: 20.7 us -> 23 us  [to_plane(): lax.ppermute(a, 'chol', [(c, c // plane * plane + hop(c % plane, dp, plan...]
    pallas_call x2, Pallas kernels: 5.59 us -> 4.8 us  [potential_call(): pl.pallas_call(functools.partial(potential_kernel, start, steps, layout,...]
    ppermute x4 -> x3, waiting for transfers between devices: 1.99 us -> 2.47 us  [around_orb(): lax.ppermute(a, 'orb', [((c + d) % n_orb, c) for c in range(n_orb)])]
    pallas_call x3 -> x5, Pallas kernels: 1.55 us -> 1.64 us  [the longest x1 1.27 us: series_call(): pl.pallas_call(functools.partial(series_kernel, n_orb), out_shape=pltpu.V...]
  transfers between devices with their start and end apart: 22 -> 24, of which waited for: 8 -> 14; matrix products, arithmetic and copies ran while one was open for 0% -> 0% of each run, Pallas kernels for 2% -> 2%
where the time goes in v8:
time: 78.8 us; the launch traced here: 78.6 us
  starting transfers between devices  31.8 us (40%)
  waiting for transfers between devices  27.1 us (34%)
  Pallas kernels  19 us (24%)
    ppermute x12, waiting for transfers between devices, to_plane(): lax.ppermute(a, 'chol', [(c, c // plane * plane + hop(c % plane, dp, plan...  23 us
    ppermute x12, starting transfers between devices, to_plane(): lax.ppermute(a, 'chol', [(c, c // plane * plane + hop(c % plane, dp, plan...  16.2 us
    ppermute x9, starting transfers between devices, to_z(): lax.ppermute(a, 'chol', [(c, hop(c // plane, dz, nz) * plane + c % plane)...  14.9 us
    pallas_call x1, Pallas kernels, bias_call(): pl.pallas_call(bias_kernel, in_specs=[*[pl.BlockSpec(memory_space=pl.ANY)...  11.5 us
    pallas_call x2, Pallas kernels, potential_call(): pl.pallas_call(functools.partial(potential_kernel, start, steps, layout,...  4.8 us
    ppermute x3, waiting for transfers between devices, around_orb(): lax.ppermute(a, 'orb', [((c + d) % n_orb, c) for c in range(n_orb)])  2.47 us
    ppermute x9, waiting for transfers between devices, to_z(): lax.ppermute(a, 'chol', [(c, hop(c // plane, dz, nz) * plane + c % plane)...  1.63 us
  transfers between devices with their start and end apart: 24, of which 14 were waited for; matrix products, arithmetic and copies ran while one was open for 0% of the time, Pallas kernels for 2%

profile of v8, /device:TPU:0, one launch (start us, length us, event | category | flops | bytes accessed | tf_op | source)
XLA Modules:
  0.0 78.6 jit_solution(16947624993623446814)
XLA Ops:
  0.6 0.0 copy-start
  0.6 11.5 %force_bias.1 = (bf16[8,256,2048]{2,1,0:T(8,128)(2,1)S(1)}, f32[32,256]{1,0:T(8,128)S(1)}, bf16[2,128,128]{2,1,0:T(8,128)(2,1)S(1)}, s32[2,2,256]{2,1,0:T(2,128)S(1)}) custom-call(bf16[256,2,64,128]{3,2,1,0:T(8,128)(2,1)} %vals_hbm.1, bf16[32,128,256]{2,1,0:T(8,128)(2,1)} %greens_hbm.1, bf16[32,128,128]{2,1,0:T(8,128)(2,1)} %walkers_hbm.1, s32[2,2,256]{2,1,0:T(2,128)} %bitcast.5), custom_call_target="tpu_custom_call" | custom-call | tf_op jit(solution)/shard_map/force_bias/pallas_call | solution.py:163
  12.2 0.5 collective-permute-start
  12.7 0.1 collective-permute-start.1
  12.8 1.1 %collective-permute-done.1.refs_0_ = f32[32,256]{1,0:T(8,128)S(1)} collective-permute-done((f32[32,256]{1,0:T(8,128)S(1)}, f32[32,256]{1,0:T(8,128)S(1)}, u32[]{:S(2)}, u32[]{:S(2)}) %collective-permute-start.1) | collective-permute-done | bytes 32800 | tf_op jit(solution)/shard_map/ppermute | solution.py:431
  13.9 0.0 collective-permute-done.refs_3_
  13.9 0.0 copy-done
  13.9 3.2 %potential.3 = (bf16[4,2,192,128]{3,2,1,0:T(8,128)(2,1)S(1)}, bf16[4,2,192,128]{3,2,1,0:T(8,128)(2,1)S(1)}, bf16[4,2,192,128]{3,2,1,0:T(8,128)(2,1)S(1)}, bf16[4...) custom-call(f32[32,256]{1,0:T(8,128)S(1)} %bitcast.3, f32[32,256]{1,0:T(8,128)S(1)} %get-tuple-element.32.own_ref, ...), custom_call_target="tpu_custom_call" | custom-call | tf_op jit(solution)/shard_map/potential/pallas_call | solution.py:260
  17.1 3.7 %collective-permute-start.8 = (bf16[4,2,192,128]{3,2,1,0:T(8,128)(2,1)S(1)}, bf16[4,2,192,128]{3,2,1,0:T(8,128)(2,1)S(1)}, u32[]{:S(2)}, u32[]{:S(2)}) collective-permute-start(bf16[4,2,192,128]{3,2,1,0:T(8,128)(2,1)S(1)} %get-tuple-element.46), channel_id=1, source_target_pairs={{0,6},{2,4},{4,2},{6,0},{8,14},{10,12},{12,10},{14,8},{16,22},{18,... | collective-permute-start | bytes 1179656 | tf_op jit(solution)/shard_map/ppermute | solution.py:425
  20.8 0.5 collective-permute-start.9
  21.3 0.1 collective-permute-start.10
  21.4 1.6 %potential.2 = (bf16[4,2,64,128]{3,2,1,0:T(8,128)(2,1)S(1)}, bf16[4,2,64,128]{3,2,1,0:T(8,128)(2,1)S(1)}, bf16[4,2,64,128]{3,2,1,0:T(8,128)(2,1)S(1)}, bf16[4,2,64,128]{3,2,1,0:T(8,128)(2,1)S(1)}, f32[16,128]{1,0:T(8,128)}) custom-call(f32[32,256]{1,0:T(8,128)S(1)} %bitcast.4, f32[32,256]{1,0:T(8,128)S(1)} %get-tuple-element.32.own_ref, ...), custom_call_target="tpu_custom_call" | custom-call | tf_op jit(solution)/shard_map/potential/pallas_call | solution.py:260
  23.0 3.0 %collective-permute-start.2 = (bf16[4,2,64,128]{3,2,1,0:T(8,128)(2,1)S(1)}, bf16[4,2,64,128]{3,2,1,0:T(8,128)(2,1)S(1)}, u32[]{:S(2)}, u32[]{:S(2)}) collective-permute-start(bf16[4,2,64,128]{3,2,1,0:T(8,128)(2,1)S(1)} %get-tuple-element.38), channel_id=1, source_target_pairs={{0,16},{2,18},{4,20},{6,22},{8,24},{10,26},{12,28},{14,30},{16,0},... | collective-permute-start | bytes 393224 | tf_op jit(solution)/shard_map/ppermute | solution.py:428
  26.0 1.3 %collective-permute-start.3 = (bf16[4,2,64,128]{3,2,1,0:T(8,128)(2,1)S(1)}, bf16[4,2,64,128]{3,2,1,0:T(8,128)(2,1)S(1)}, u32[]{:S(2)}, u32[]{:S(2)}) collective-permute-start(bf16[4,2,64,128]{3,2,1,0:T(8,128)(2,1)S(1)} %get-tuple-element.39), channel_id=1, source_target_pairs={{0,24},{2,26},{4,28},{6,30},{8,16},{10,18},{12,20},{14,22},{16,8},... | collective-permute-start | bytes 393224 | tf_op jit(solution)/shard_map/ppermute | solution.py:428
  27.4 3.3 %collective-permute-done.8.refs_1_ = bf16[4,2,192,128]{3,2,1,0:T(8,128)(2,1)S(1)} collective-permute-done((bf16[4,2,192,128]{3,2,1,0:T(8,128)(2,1)S(1)}, bf16[4,2,192,128]{3,2,1,0:T(8,128)(2,1)S(1)}, u32[]{:S(2)}, u32[]{:S(2)}) %collective-permute-start.8) | collective-permute-done | bytes 393248 | tf_op jit(solution)/shard_map/ppermute | solution.py:425
  30.7 2.1 %collective-permute-start.4 = (bf16[4,2,64,128]{3,2,1,0:T(8,128)(2,1)S(1)}, bf16[4,2,64,128]{3,2,1,0:T(8,128)(2,1)S(1)}, u32[]{:S(2)}, u32[]{:S(2)}) collective-permute-start(bf16[4,2,64,128]{3,2,1,0:T(8,128)(2,1)S(1)} %get-tuple-element.40), channel_id=1, source_target_pairs={{0,8},{2,10},{4,12},{6,14},{8,0},{10,2},{12,4},{14,6},{16,24},{18,... | collective-permute-start | bytes 393224 | tf_op jit(solution)/shard_map/ppermute | solution.py:428
  32.8 6.0 %collective-permute-done.9.refs_2_ = bf16[4,2,192,128]{3,2,1,0:T(8,128)(2,1)S(1)} collective-permute-done((bf16[4,2,192,128]{3,2,1,0:T(8,128)(2,1)S(1)}, bf16[4,2,192,128]{3,2,1,0:T(8,128)(2,1)S(1)}, u32[]{:S(2)}, u32[]{:S(2)}) %collective-permute-start.9) | collective-permute-done | bytes 393248 | tf_op jit(solution)/shard_map/ppermute | solution.py:425
  38.8 0.3 collective-permute-done.10.refs_3_
  39.1 0.2 sum_parts.3
  39.3 2.7 %collective-permute-start.11 = (bf16[2,192,128]{2,1,0:T(8,128)(2,1)S(1)}, bf16[2,192,128]{2,1,0:T(8,128)(2,1)S(1)}, u32[]{:S(2)}, u32[]{:S(2)}) collective-permute-start(bf16[2,192,128]{2,1,0:T(8,128)(2,1)S(1)} %get-tuple-element.50), channel_id=1, source_target_pairs={{0,16},{2,18},{4,20},{6,22},{8,24},{10,26},{12,28},{14,30},{16,0},... | collective-permute-start | bytes 294920 | tf_op jit(solution)/shard_map/ppermute | solution.py:428
  42.0 1.3 %collective-permute-start.12 = (bf16[2,192,128]{2,1,0:T(8,128)(2,1)S(1)}, bf16[2,192,128]{2,1,0:T(8,128)(2,1)S(1)}, u32[]{:S(2)}, u32[]{:S(2)}) collective-permute-start(bf16[2,192,128]{2,1,0:T(8,128)(2,1)S(1)} %get-tuple-element.51), channel_id=1, source_target_pairs={{0,24},{2,26},{4,28},{6,30},{8,16},{10,18},{12,20},{14,22},{16,8},... | collective-permute-start | bytes 294920 | tf_op jit(solution)/shard_map/ppermute | solution.py:428
  43.3 0.0 collective-permute-done.2.refs_1_
  43.3 0.2 collective-permute-start.13
  43.5 0.0 collective-permute-done.3.refs_2_
  43.6 0.0 collective-permute-done.4.refs_3_
  43.6 0.1 sum_parts.2
  43.6 1.7 %collective-permute-start.5 = (bf16[2,64,128]{2,1,0:T(8,128)(2,1)S(1)}, bf16[2,64,128]{2,1,0:T(8,128)(2,1)S(1)}, u32[]{:S(2)}, u32[]{:S(2)}) collective-permute-start(bf16[2,64,128]{2,1,0:T(8,128)(2,1)S(1)} %get-tuple-element.42), channel_id=1, source_target_pairs={{0,6},{2,4},{4,2},{6,0},{8,14},{10,12},{12,10},{14,8},{16,22},{18,... | collective-permute-start | bytes 98312 | tf_op jit(solution)/shard_map/ppermute | solution.py:425
  45.3 1.3 %collective-permute-start.6 = (bf16[2,64,128]{2,1,0:T(8,128)(2,1)S(1)}, bf16[2,64,128]{2,1,0:T(8,128)(2,1)S(1)}, u32[]{:S(2)}, u32[]{:S(2)}) collective-permute-start(bf16[2,64,128]{2,1,0:T(8,128)(2,1)S(1)} %get-tuple-element.43), channel_id=1, source_target_pairs={{0,4},{2,6},{4,0},{6,2},{8,12},{10,14},{12,8},{14,10},{16,20},{18,... | collective-permute-start | bytes 98312 | tf_op jit(solution)/shard_map/ppermute | solution.py:425
  46.6 1.9 %collective-permute-done.5.refs_1_ = bf16[2,64,128]{2,1,0:T(8,128)(2,1)S(1)} collective-permute-done((bf16[2,64,128]{2,1,0:T(8,128)(2,1)S(1)}, bf16[2,64,128]{2,1,0:T(8,128)(2,1)S(1)}, u32[]{:S(2)}, u32[]{:S(2)}) %collective-permute-start.5) | collective-permute-done | bytes 32800 | tf_op jit(solution)/shard_map/ppermute | solution.py:425
  48.5 1.5 %collective-permute-start.7 = (bf16[2,64,128]{2,1,0:T(8,128)(2,1)S(1)}, bf16[2,64,128]{2,1,0:T(8,128)(2,1)S(1)}, u32[]{:S(2)}, u32[]{:S(2)}) collective-permute-start(bf16[2,64,128]{2,1,0:T(8,128)(2,1)S(1)} %get-tuple-element.44), channel_id=1, source_target_pairs={{0,2},{2,0},{4,6},{6,4},{8,10},{10,8},{12,14},{14,12},{16,18},{18,... | collective-permute-start | bytes 98312 | tf_op jit(solution)/shard_map/ppermute | solution.py:425
  50.0 0.0 collective-permute-done.6.refs_2_
  50.0 2.4 %collective-permute-done.7.refs_3_ = bf16[2,64,128]{2,1,0:T(8,128)(2,1)S(1)} collective-permute-done((bf16[2,64,128]{2,1,0:T(8,128)(2,1)S(1)}, bf16[2,64,128]{2,1,0:T(8,128)(2,1)S(1)}, u32[]{:S(2)}, u32[]{:S(2)}) %collective-permute-start.7) | collective-permute-done | bytes 32800 | tf_op jit(solution)/shard_map/ppermute | solution.py:425
  52.4 0.0 collective-permute-done.11.refs_5_
  52.4 0.0 collective-permute-done.12.refs_6_
  52.4 0.0 collective-permute-done.13.refs_7_
  52.4 0.1 finish.1.refs_0_
  52.5 0.1 collective-permute-start.14
  52.6 1.3 %collective-permute-done.14.refs_1_ = bf16[2,256,128]{2,1,0:T(8,128)(2,1)S(1)} collective-permute-done((bf16[2,256,128]{2,1,0:T(8,128)(2,1)S(1)}, bf16[2,256,128]{2,1,0:T(8,128)(2,1)S(1)}, u32[]{:S(2)}, u32[]{:S(2)}) %collective-permute-start.14) | collective-permute-done | bytes 131104 | tf_op jit(solution)/shard_map/ppermute | solution.py:431
  53.9 1.3 %series.1.refs_0_ = bf16[272,128]{1,0:T(8,128)(2,1)S(1)} custom-call(bf16[2,256,128]{2,1,0:T(8,128)(2,1)S(1)} %finish.1.refs_0_, bf16[2,256,128]{2,1,0:T(8,128)(2,1)S(1)} %collective-permute-done.14.refs_1_, bf16[2,128,128]{2,1,0:T(8,128)(2,1)S(1)} %get-tuple-element.53.refs_2_, bf16[2,128,128]{2,1,0:T(8,128)(2,1)S(1)} %collective-permute-done.refs_3_, ...), custom_call_target="tpu_custom_call" | custom-call | tf_op jit(solution)/shard_map/series/pallas_call | solution.py:365
  55.2 2.9 %collective-permute-start.15 = (bf16[272,128]{1,0:T(8,128)(2,1)S(1)}, bf16[272,128]{1,0:T(8,128)(2,1)S(1)}, u32[]{:S(2)}, u32[]{:S(2)}) collective-permute-start(bf16[272,128]{1,0:T(8,128)(2,1)S(1)} %series.1.refs_0_), channel_id=1, source_target_pairs={{0,16},{2,18},{4,20},{6,22},{8,24},{10,26},{12,28},{14,30},{16,0},... | collective-permute-start | bytes 208904 | tf_op jit(solution)/shard_map/ppermute | solution.py:428
  58.1 1.3 %collective-permute-start.16 = (bf16[272,128]{1,0:T(8,128)(2,1)S(1)}, bf16[272,128]{1,0:T(8,128)(2,1)S(1)}, u32[]{:S(2)}, u32[]{:S(2)}) collective-permute-start(bf16[272,128]{1,0:T(8,128)(2,1)S(1)} %series.1.refs_0_), channel_id=1, source_target_pairs={{0,24},{2,26},{4,28},{6,30},{8,16},{10,18},{12,20},{14,22},{16,8},... | collective-permute-start | bytes 208904 | tf_op jit(solution)/shard_map/ppermute | solution.py:428
  59.4 0.0 collective-permute-start.17
  59.4 1.5 %collective-permute-start.18 = (bf16[272,128]{1,0:T(8,128)(2,1)S(1)}, bf16[272,128]{1,0:T(8,128)(2,1)S(1)}, u32[]{:S(2)}, u32[]{:S(2)}) collective-permute-start(bf16[272,128]{1,0:T(8,128)(2,1)S(1)} %series.1.refs_0_), channel_id=1, source_target_pairs={{0,2},{2,0},{4,6},{6,4},{8,10},{10,8},{12,14},{14,12},{16,18},{18,... | collective-permute-start | bytes 208904 | tf_op jit(solution)/shard_map/ppermute | solution.py:425
  60.9 0.7 collective-permute-start.19
  61.6 0.8 %collective-permute-done.15.refs_0_ = bf16[272,128]{1,0:T(8,128)(2,1)S(1)} collective-permute-done((bf16[272,128]{1,0:T(8,128)(2,1)S(1)}, bf16[272,128]{1,0:T(8,128)(2,1)S(1)}, u32[]{:S(2)}, u32[]{:S(2)}) %collective-permute-start.15) | collective-permute-done | bytes 69664 | tf_op jit(solution)/shard_map/ppermute | solution.py:428
  62.5 1.7 %collective-permute-start.20 = (bf16[272,128]{1,0:T(8,128)(2,1)S(1)}, bf16[272,128]{1,0:T(8,128)(2,1)S(1)}, u32[]{:S(2)}, u32[]{:S(2)}) collective-permute-start(bf16[272,128]{1,0:T(8,128)(2,1)S(1)} %series.1.refs_0_), channel_id=1, source_target_pairs={{0,6},{2,4},{4,2},{6,0},{8,14},{10,12},{12,10},{14,8},{16,22},{18,... | collective-permute-start | bytes 208904 | tf_op jit(solution)/shard_map/ppermute | solution.py:425
  64.1 0.5 collective-permute-done.16.refs_1_
  64.6 0.3 collective-permute-done.17.refs_2_
  64.9 0.0 collective-permute-done.18.refs_3_
  64.9 0.9 %collective-permute-done.19.refs_4_ = bf16[272,128]{1,0:T(8,128)(2,1)S(1)} collective-permute-done((bf16[272,128]{1,0:T(8,128)(2,1)S(1)}, bf16[272,128]{1,0:T(8,128)(2,1)S(1)}, u32[]{:S(2)}, u32[]{:S(2)}) %collective-permute-start.19) | collective-permute-done | bytes 69664 | tf_op jit(solution)/shard_map/ppermute | solution.py:425
  65.8 1.9 %collective-permute-done.20.refs_5_ = bf16[272,128]{1,0:T(8,128)(2,1)S(1)} collective-permute-done((bf16[272,128]{1,0:T(8,128)(2,1)S(1)}, bf16[272,128]{1,0:T(8,128)(2,1)S(1)}, u32[]{:S(2)}, u32[]{:S(2)}) %collective-permute-start.20) | collective-permute-done | bytes 69664 | tf_op jit(solution)/shard_map/ppermute | solution.py:425
  67.7 1.6 %collective-permute-start.21 = (bf16[3,272,128]{2,1,0:T(8,128)(2,1)S(1)}, bf16[3,272,128]{2,1,0:T(8,128)(2,1)S(1)}, u32[]{:S(2)}, u32[]{:S(2)}) collective-permute-start(bf16[3,272,128]{2,1,0:T(8,128)(2,1)S(1)} %get-tuple-element.59.refs_4_), channel_id=1, source_target_pairs={{0,2},{2,0},{4,6},{6,4},{8,10},{10,8},{12,14},{14,12},{16,18},{18,... | collective-permute-start | bytes 626696 | tf_op jit(solution)/shard_map/ppermute | solution.py:425
  69.3 0.7 collective-permute-start.22
  70.0 1.3 %collective-permute-start.23 = (bf16[3,272,128]{2,1,0:T(8,128)(2,1)S(1)}, bf16[3,272,128]{2,1,0:T(8,128)(2,1)S(1)}, u32[]{:S(2)}, u32[]{:S(2)}) collective-permute-start(bf16[3,272,128]{2,1,0:T(8,128)(2,1)S(1)} %get-tuple-element.59.refs_4_), channel_id=1, source_target_pairs={{0,6},{2,4},{4,2},{6,0},{8,14},{10,12},{12,10},{14,8},{16,22},{18,... | collective-permute-start | bytes 626696 | tf_op jit(solution)/shard_map/ppermute | solution.py:425
  71.3 3.4 %collective-permute-done.21.refs_5_ = bf16[3,272,128]{2,1,0:T(8,128)(2,1)S(1)} collective-permute-done((bf16[3,272,128]{2,1,0:T(8,128)(2,1)S(1)}, bf16[3,272,128]{2,1,0:T(8,128)(2,1)S(1)}, u32[]{:S(2)}, u32[]{:S(2)}) %collective-permute-start.21) | collective-permute-done | bytes 208928 | tf_op jit(solution)/shard_map/ppermute | solution.py:425
  74.7 2.8 %collective-permute-done.22.refs_6_ = bf16[3,272,128]{2,1,0:T(8,128)(2,1)S(1)} collective-permute-done((bf16[3,272,128]{2,1,0:T(8,128)(2,1)S(1)}, bf16[3,272,128]{2,1,0:T(8,128)(2,1)S(1)}, u32[]{:S(2)}, u32[]{:S(2)}) %collective-permute-start.22) | collective-permute-done | bytes 208928 | tf_op jit(solution)/shard_map/ppermute | solution.py:425
  77.6 0.0 collective-permute-done.23.refs_7_
  77.6 1.1 %place_walkers.1 = (bf16[32,128,128]{2,1,0:T(8,128)(2,1)}, f32[1,32]{1,0:T(1,128)}) custom-call(bf16[272,128]{1,0:T(8,128)(2,1)S(1)} %series.1.refs_0_, bf16[272,128]{1,0:T(8,128)(2,1)S(1)} %get-tuple-element.56.refs_1_, bf16[272,128]{1,0:T(8,128)(2,1)S(1)} %get-tuple-element.57.refs_2_, bf16[272,128]{1,0:T(8,128)(2,1)S(1)} %get-tuple-element.58.refs_3_, ...), custom_call_target="tpu_custom_call" | custom-call | tf_op jit(solution)/shard_map/place_walkers/pallas_call | solution.py:401
  (1 shorter events, 0.0 us)
Async XLA Ops:
  0.6 13.3 %copy-start = (f32[256,32]{0,1:T(8,128)S(1)}, f32[256,32]{0,1:T(8,128)}, u32[]{:S(2)}) copy-start(f32[256,32]{0,1:T(8,128)} %param.9) | copy-start | bytes 98308
  12.2 1.7 %collective-permute-start = (bf16[2,128,128]{2,1,0:T(8,128)(2,1)S(1)}, bf16[2,128,128]{2,1,0:T(8,128)(2,1)S(1)}, u32[]{:S(2)}, u32[]{:S(2)}) collective-permute-start(bf16[2,128,128]{2,1,0:T(8,128)(2,1)S(1)} %get-tuple-element.53.refs_2_), channel_id=1, source_target_pairs={{1,0},{0,1},{3,2},{2,3},{5,4},{4,5},{7,6},{6,7},{9,8},{8,9},{11,10... | collective-permute-start | bytes 196616 | tf_op jit(solution)/shard_map/ppermute | solution.py:431
  12.7 1.2 %collective-permute-start.1 = (f32[32,256]{1,0:T(8,128)S(1)}, f32[32,256]{1,0:T(8,128)S(1)}, u32[]{:S(2)}, u32[]{:S(2)}) collective-permute-start(f32[32,256]{1,0:T(8,128)S(1)} %get-tuple-element.32.own_ref), channel_id=1, source_target_pairs={{1,0},{0,1},{3,2},{2,3},{5,4},{4,5},{7,6},{6,7},{9,8},{8,9},{11,10... | collective-permute-start | bytes 98312 | tf_op jit(solution)/shard_map/ppermute | solution.py:431
  17.1 13.6 %collective-permute-start.8 = (bf16[4,2,192,128]{3,2,1,0:T(8,128)(2,1)S(1)}, bf16[4,2,192,128]{3,2,1,0:T(8,128)(2,1)S(1)}, u32[]{:S(2)}, u32[]{:S(2)}) collective-permute-start(bf16[4,2,192,128]{3,2,1,0:T(8,128)(2,1)S(1)} %get-tuple-element.46), channel_id=1, source_target_pairs={{0,6},{2,4},{4,2},{6,0},{8,14},{10,12},{12,10},{14,8},{16,22},{18,... | collective-permute-start | bytes 1179656 | tf_op jit(solution)/shard_map/ppermute | solution.py:425
  20.8 18.0 %collective-permute-start.9 = (bf16[4,2,192,128]{3,2,1,0:T(8,128)(2,1)S(1)}, bf16[4,2,192,128]{3,2,1,0:T(8,128)(2,1)S(1)}, u32[]{:S(2)}, u32[]{:S(2)}) collective-permute-start(bf16[4,2,192,128]{3,2,1,0:T(8,128)(2,1)S(1)} %get-tuple-element.47), channel_id=1, source_target_pairs={{0,4},{2,6},{4,0},{6,2},{8,12},{10,14},{12,8},{14,10},{16,20},{18,... | collective-permute-start | bytes 1179656 | tf_op jit(solution)/shard_map/ppermute | solution.py:425
  21.3 17.8 %collective-permute-start.10 = (bf16[4,2,192,128]{3,2,1,0:T(8,128)(2,1)S(1)}, bf16[4,2,192,128]{3,2,1,0:T(8,128)(2,1)S(1)}, u32[]{:S(2)}, u32[]{:S(2)}) collective-permute-start(bf16[4,2,192,128]{3,2,1,0:T(8,128)(2,1)S(1)} %get-tuple-element.48), channel_id=1, source_target_pairs={{0,2},{2,0},{4,6},{6,4},{8,10},{10,8},{12,14},{14,12},{16,18},{18,... | collective-permute-start | bytes 1179656 | tf_op jit(solution)/shard_map/ppermute | solution.py:425
  23.0 20.3 %collective-permute-start.2 = (bf16[4,2,64,128]{3,2,1,0:T(8,128)(2,1)S(1)}, bf16[4,2,64,128]{3,2,1,0:T(8,128)(2,1)S(1)}, u32[]{:S(2)}, u32[]{:S(2)}) collective-permute-start(bf16[4,2,64,128]{3,2,1,0:T(8,128)(2,1)S(1)} %get-tuple-element.38), channel_id=1, source_target_pairs={{0,16},{2,18},{4,20},{6,22},{8,24},{10,26},{12,28},{14,30},{16,0},... | collective-permute-start | bytes 393224 | tf_op jit(solution)/shard_map/ppermute | solution.py:428
  26.0 17.5 %collective-permute-start.3 = (bf16[4,2,64,128]{3,2,1,0:T(8,128)(2,1)S(1)}, bf16[4,2,64,128]{3,2,1,0:T(8,128)(2,1)S(1)}, u32[]{:S(2)}, u32[]{:S(2)}) collective-permute-start(bf16[4,2,64,128]{3,2,1,0:T(8,128)(2,1)S(1)} %get-tuple-element.39), channel_id=1, source_target_pairs={{0,24},{2,26},{4,28},{6,30},{8,16},{10,18},{12,20},{14,22},{16,8},... | collective-permute-start | bytes 393224 | tf_op jit(solution)/shard_map/ppermute | solution.py:428
  30.7 12.9 %collective-permute-start.4 = (bf16[4,2,64,128]{3,2,1,0:T(8,128)(2,1)S(1)}, bf16[4,2,64,128]{3,2,1,0:T(8,128)(2,1)S(1)}, u32[]{:S(2)}, u32[]{:S(2)}) collective-permute-start(bf16[4,2,64,128]{3,2,1,0:T(8,128)(2,1)S(1)} %get-tuple-element.40), channel_id=1, source_target_pairs={{0,8},{2,10},{4,12},{6,14},{8,0},{10,2},{12,4},{14,6},{16,24},{18,... | collective-permute-start | bytes 393224 | tf_op jit(solution)/shard_map/ppermute | solution.py:428
  39.3 13.1 %collective-permute-start.11 = (bf16[2,192,128]{2,1,0:T(8,128)(2,1)S(1)}, bf16[2,192,128]{2,1,0:T(8,128)(2,1)S(1)}, u32[]{:S(2)}, u32[]{:S(2)}) collective-permute-start(bf16[2,192,128]{2,1,0:T(8,128)(2,1)S(1)} %get-tuple-element.50), channel_id=1, source_target_pairs={{0,16},{2,18},{4,20},{6,22},{8,24},{10,26},{12,28},{14,30},{16,0},... | collective-permute-start | bytes 294920 | tf_op jit(solution)/shard_map/ppermute | solution.py:428
  42.0 10.5 %collective-permute-start.12 = (bf16[2,192,128]{2,1,0:T(8,128)(2,1)S(1)}, bf16[2,192,128]{2,1,0:T(8,128)(2,1)S(1)}, u32[]{:S(2)}, u32[]{:S(2)}) collective-permute-start(bf16[2,192,128]{2,1,0:T(8,128)(2,1)S(1)} %get-tuple-element.51), channel_id=1, source_target_pairs={{0,24},{2,26},{4,28},{6,30},{8,16},{10,18},{12,20},{14,22},{16,8},... | collective-permute-start | bytes 294920 | tf_op jit(solution)/shard_map/ppermute | solution.py:428
  43.3 9.1 %collective-permute-start.13 = (bf16[2,192,128]{2,1,0:T(8,128)(2,1)S(1)}, bf16[2,192,128]{2,1,0:T(8,128)(2,1)S(1)}, u32[]{:S(2)}, u32[]{:S(2)}) collective-permute-start(bf16[2,192,128]{2,1,0:T(8,128)(2,1)S(1)} %get-tuple-element.52), channel_id=1, source_target_pairs={{0,8},{2,10},{4,12},{6,14},{8,0},{10,2},{12,4},{14,6},{16,24},{18,... | collective-permute-start | bytes 294920 | tf_op jit(solution)/shard_map/ppermute | solution.py:428
  43.6 4.9 %collective-permute-start.5 = (bf16[2,64,128]{2,1,0:T(8,128)(2,1)S(1)}, bf16[2,64,128]{2,1,0:T(8,128)(2,1)S(1)}, u32[]{:S(2)}, u32[]{:S(2)}) collective-permute-start(bf16[2,64,128]{2,1,0:T(8,128)(2,1)S(1)} %get-tuple-element.42), channel_id=1, source_target_pairs={{0,6},{2,4},{4,2},{6,0},{8,14},{10,12},{12,10},{14,8},{16,22},{18,... | collective-permute-start | bytes 98312 | tf_op jit(solution)/shard_map/ppermute | solution.py:425
  45.3 4.6 %collective-permute-start.6 = (bf16[2,64,128]{2,1,0:T(8,128)(2,1)S(1)}, bf16[2,64,128]{2,1,0:T(8,128)(2,1)S(1)}, u32[]{:S(2)}, u32[]{:S(2)}) collective-permute-start(bf16[2,64,128]{2,1,0:T(8,128)(2,1)S(1)} %get-tuple-element.43), channel_id=1, source_target_pairs={{0,4},{2,6},{4,0},{6,2},{8,12},{10,14},{12,8},{14,10},{16,20},{18,... | collective-permute-start | bytes 98312 | tf_op jit(solution)/shard_map/ppermute | solution.py:425
  48.5 3.9 %collective-permute-start.7 = (bf16[2,64,128]{2,1,0:T(8,128)(2,1)S(1)}, bf16[2,64,128]{2,1,0:T(8,128)(2,1)S(1)}, u32[]{:S(2)}, u32[]{:S(2)}) collective-permute-start(bf16[2,64,128]{2,1,0:T(8,128)(2,1)S(1)} %get-tuple-element.44), channel_id=1, source_target_pairs={{0,2},{2,0},{4,6},{6,4},{8,10},{10,8},{12,14},{14,12},{16,18},{18,... | collective-permute-start | bytes 98312 | tf_op jit(solution)/shard_map/ppermute | solution.py:425
  52.5 1.4 %collective-permute-start.14 = (bf16[2,256,128]{2,1,0:T(8,128)(2,1)S(1)}, bf16[2,256,128]{2,1,0:T(8,128)(2,1)S(1)}, u32[]{:S(2)}, u32[]{:S(2)}) collective-permute-start(bf16[2,256,128]{2,1,0:T(8,128)(2,1)S(1)} %finish.1.refs_0_), channel_id=1, source_target_pairs={{1,0},{0,1},{3,2},{2,3},{5,4},{4,5},{7,6},{6,7},{9,8},{8,9},{11,10... | collective-permute-start | bytes 393224 | tf_op jit(solution)/shard_map/ppermute | solution.py:431
  55.2 7.3 %collective-permute-start.15 = (bf16[272,128]{1,0:T(8,128)(2,1)S(1)}, bf16[272,128]{1,0:T(8,128)(2,1)S(1)}, u32[]{:S(2)}, u32[]{:S(2)}) collective-permute-start(bf16[272,128]{1,0:T(8,128)(2,1)S(1)} %series.1.refs_0_), channel_id=1, source_target_pairs={{0,16},{2,18},{4,20},{6,22},{8,24},{10,26},{12,28},{14,30},{16,0},... | collective-permute-start | bytes 208904 | tf_op jit(solution)/shard_map/ppermute | solution.py:428
  58.1 6.5 %collective-permute-start.16 = (bf16[272,128]{1,0:T(8,128)(2,1)S(1)}, bf16[272,128]{1,0:T(8,128)(2,1)S(1)}, u32[]{:S(2)}, u32[]{:S(2)}) collective-permute-start(bf16[272,128]{1,0:T(8,128)(2,1)S(1)} %series.1.refs_0_), channel_id=1, source_target_pairs={{0,24},{2,26},{4,28},{6,30},{8,16},{10,18},{12,20},{14,22},{16,8},... | collective-permute-start | bytes 208904 | tf_op jit(solution)/shard_map/ppermute | solution.py:428
  59.4 5.5 %collective-permute-start.17 = (bf16[272,128]{1,0:T(8,128)(2,1)S(1)}, bf16[272,128]{1,0:T(8,128)(2,1)S(1)}, u32[]{:S(2)}, u32[]{:S(2)}) collective-permute-start(bf16[272,128]{1,0:T(8,128)(2,1)S(1)} %series.1.refs_0_), channel_id=1, source_target_pairs={{0,8},{2,10},{4,12},{6,14},{8,0},{10,2},{12,4},{14,6},{16,24},{18,... | collective-permute-start | bytes 208904 | tf_op jit(solution)/shard_map/ppermute | solution.py:428
  59.4 5.5 %collective-permute-start.18 = (bf16[272,128]{1,0:T(8,128)(2,1)S(1)}, bf16[272,128]{1,0:T(8,128)(2,1)S(1)}, u32[]{:S(2)}, u32[]{:S(2)}) collective-permute-start(bf16[272,128]{1,0:T(8,128)(2,1)S(1)} %series.1.refs_0_), channel_id=1, source_target_pairs={{0,2},{2,0},{4,6},{6,4},{8,10},{10,8},{12,14},{14,12},{16,18},{18,... | collective-permute-start | bytes 208904 | tf_op jit(solution)/shard_map/ppermute | solution.py:425
  60.9 4.9 %collective-permute-start.19 = (bf16[272,128]{1,0:T(8,128)(2,1)S(1)}, bf16[272,128]{1,0:T(8,128)(2,1)S(1)}, u32[]{:S(2)}, u32[]{:S(2)}) collective-permute-start(bf16[272,128]{1,0:T(8,128)(2,1)S(1)} %series.1.refs_0_), channel_id=1, source_target_pairs={{0,4},{2,6},{4,0},{6,2},{8,12},{10,14},{12,8},{14,10},{16,20},{18,... | collective-permute-start | bytes 208904 | tf_op jit(solution)/shard_map/ppermute | solution.py:425
  62.5 5.2 %collective-permute-start.20 = (bf16[272,128]{1,0:T(8,128)(2,1)S(1)}, bf16[272,128]{1,0:T(8,128)(2,1)S(1)}, u32[]{:S(2)}, u32[]{:S(2)}) collective-permute-start(bf16[272,128]{1,0:T(8,128)(2,1)S(1)} %series.1.refs_0_), channel_id=1, source_target_pairs={{0,6},{2,4},{4,2},{6,0},{8,14},{10,12},{12,10},{14,8},{16,22},{18,... | collective-permute-start | bytes 208904 | tf_op jit(solution)/shard_map/ppermute | solution.py:425
  67.7 7.0 %collective-permute-start.21 = (bf16[3,272,128]{2,1,0:T(8,128)(2,1)S(1)}, bf16[3,272,128]{2,1,0:T(8,128)(2,1)S(1)}, u32[]{:S(2)}, u32[]{:S(2)}) collective-permute-start(bf16[3,272,128]{2,1,0:T(8,128)(2,1)S(1)} %get-tuple-element.59.refs_4_), channel_id=1, source_target_pairs={{0,2},{2,0},{4,6},{6,4},{8,10},{10,8},{12,14},{14,12},{16,18},{18,... | collective-permute-start | bytes 626696 | tf_op jit(solution)/shard_map/ppermute | solution.py:425
  69.3 8.3 %collective-permute-start.22 = (bf16[3,272,128]{2,1,0:T(8,128)(2,1)S(1)}, bf16[3,272,128]{2,1,0:T(8,128)(2,1)S(1)}, u32[]{:S(2)}, u32[]{:S(2)}) collective-permute-start(bf16[3,272,128]{2,1,0:T(8,128)(2,1)S(1)} %get-tuple-element.59.refs_4_), channel_id=1, source_target_pairs={{0,4},{2,6},{4,0},{6,2},{8,12},{10,14},{12,8},{14,10},{16,20},{18,... | collective-permute-start | bytes 626696 | tf_op jit(solution)/shard_map/ppermute | solution.py:425
  70.0 7.5 %collective-permute-start.23 = (bf16[3,272,128]{2,1,0:T(8,128)(2,1)S(1)}, bf16[3,272,128]{2,1,0:T(8,128)(2,1)S(1)}, u32[]{:S(2)}, u32[]{:S(2)}) collective-permute-start(bf16[3,272,128]{2,1,0:T(8,128)(2,1)S(1)} %get-tuple-element.59.refs_4_), channel_id=1, source_target_pairs={{0,6},{2,4},{4,2},{6,0},{8,14},{10,12},{12,10},{14,8},{16,22},{18,... | collective-permute-start | bytes 626696 | tf_op jit(solution)/shard_map/ppermute | solution.py:425

commit v9 on v8

--- a/solution.py
+++ b/solution.py
@@ -86,11 +86,11 @@
     bias_ref[...] = jnp.zeros_like(bias_ref)
     first = lax.broadcasted_iota(jnp.int32, (CHUNK * CHUNK, LANES), 1) < BLOCK
 
-    def turn(t):
+    def step(t, carry):
         for copy in copies(t):
             copy.wait()
-        slot = lax.rem(t, 2)
-        row = lax.axis_index("orb") * cols_ref.shape[0] + lax.div(t, steps)
+        local = lax.div(t, steps)
+        row = lax.axis_index("orb") * cols_ref.shape[0] + local
         upper = row // 2 == 1
         odd = row % 2 == 1
         for w in range(0, walk, CHUNK):
@@ -108,9 +108,7 @@
             for k, piece in enumerate(pieces):
                 piece = piece.astype(jnp.bfloat16)
                 for i in range(CHUNK):
-                    gs[slot, k * walk + w:k * walk + w + CHUNK, i * LANES:(i + 1) * LANES] = (
-                        piece[i * CHUNK:(i + 1) * CHUNK]
-                    )
+                    gs[k * walk + w:k * walk + w + CHUNK, i * LANES:(i + 1) * LANES] = piece[i * CHUNK:(i + 1) * CHUNK]
         for g in range(0, vectors, 2 * CHUNK):
             both = [vals[t, g + side * CHUNK:g + (side + 1) * CHUNK].reshape(CHUNK * CHUNK, LANES) for side in range(2)]
             both = jnp.dot(swap[...], jnp.concatenate(both, axis=1), preferred_element_type=jnp.float32)
@@ -120,38 +118,26 @@
                     turned_ref[t, g + side * CHUNK:g + (side + 1) * CHUNK, i * LANES:(i + 1) * LANES] = (
                         both[i * CHUNK:(i + 1) * CHUNK, side * LANES:(side + 1) * LANES]
                     )
-
-    def product(t):
-        return lax.dot_general(
-            turned_ref[t], gs[lax.rem(t, 2)], (((1,), (1,)), ((), ())), preferred_element_type=jnp.float32
+        part = lax.dot_general(
+            turned_ref[t], gs[...], (((1,), (1,)), ((), ())), preferred_element_type=jnp.float32
         )
-
-    def close(t):
-        local = lax.div(t, steps)
-        row = lax.axis_index("orb") * cols_ref.shape[0] + local
-        flat = acc[...].T
-        total = flat[0:walk]
-        for k, mask in enumerate(slot_masks(cols_ref[local, 1:2, :], row)):
-            total = total + jnp.where(mask, flat[(k + 1) * walk:(k + 2) * walk], 0.0)
-        bias_ref[...] += total
-
-    def step(t, carry):
-        part = product(t - 1)
-        turn(t)
-        acc[...] = jnp.where(lax.rem(t - 1, steps) == 0, 0.0, acc[...]) + part
-
-        @pl.when(lax.rem(t, steps) == 0)
+        begins = lax.rem(t, steps) == 0
+        acc[...] = jnp.where(begins, 0.0, acc[...]) + part
+
+        @pl.when(lax.rem(t, steps) == steps - 1)
         def _():
-            close(t - 1)
+            flat = acc[...].T
+            total = flat[0:walk]
+            cols = cols_ref[local, 1:2, :]
+            for k, mask in enumerate(slot_masks(cols, row)):
+                total = total + jnp.where(mask, flat[(k + 1) * walk:(k + 2) * walk], 0.0)
+            bias_ref[...] += total
 
         return carry
 
     acc[...] = jnp.zeros_like(acc)
-    turn(0)
     take_cols.wait()
-    lax.fori_loop(1, total_steps, step, 0)
-    acc[...] += product(total_steps - 1)
-    close(total_steps - 1)
+    lax.fori_loop(0, total_steps, step, 0)
     take.wait()
 
 
@@ -176,7 +162,7 @@
             pltpu.VMEM((steps, vectors, CHUNK, LANES), jnp.bfloat16),
             pltpu.VMEM((steps, walk, CHUNK, norb), jnp.bfloat16),
             pltpu.VMEM((CHUNK * CHUNK, CHUNK * CHUNK), jnp.bfloat16),
-            pltpu.VMEM((2, 4 * walk, wide), jnp.bfloat16),
+            pltpu.VMEM((4 * walk, wide), jnp.bfloat16),
             pltpu.VMEM((vectors, 4 * walk), jnp.float32),
             pltpu.SemaphoreType.DMA((steps,)),
             pltpu.SemaphoreType.DMA((steps,)),
@@ -189,13 +175,12 @@
     )(*in_hbm(vals, greens, walkers, cols))
 
 
-def potential_kernel(start, steps, layout, by_plane, fields_ref, own_ref, *refs):
+def potential_kernel(layout, fields_ref, own_ref, *refs):
     nz, plane, own = layout
     others = refs[:lax.axis_size("orb") - 1]
     cols_ref, turned_ref = refs[len(others):len(others) + 2]
-    groups = plane if by_plane else nz
-    outs = refs[len(others) + 2:len(others) + 2 + groups]
-    energy_ref, s_ref, swap = refs[len(others) + 2 + groups:]
+    *outs, energy_ref, s_ref, swap = refs[len(others) + 2:]
+    steps = turned_ref.shape[0]
     walk, vectors = fields_ref.shape
     rowblocks = cols_ref.shape[0]
 
@@ -224,11 +209,11 @@
     first = lax.broadcasted_iota(jnp.int32, (walk, LANES), 1) < BLOCK
 
     def step(t, carry):
-        left = s_ref[lax.div(start + t, BLOCK // CHUNK)]
+        left = s_ref[lax.div(t, BLOCK // CHUNK)]
         tiles = []
         for i in range(0, CHUNK, 2):
             both = jnp.dot(
-                left, turned_ref[start + t, :, i * LANES:(i + 2) * LANES], preferred_element_type=jnp.float32
+                left, turned_ref[t, :, i * LANES:(i + 2) * LANES], preferred_element_type=jnp.float32
             )
             for side in range(2):
                 out = both[:, side * LANES:(side + 1) * LANES]
@@ -241,10 +226,9 @@
             for w in range(CHUNK):
                 chip, j = (w0 + w) // own, (w0 + w) % own
                 dz, dp = chip // plane, chip % plane
-                out, inner = (outs[dp], dz) if by_plane else (outs[dz], dp)
                 for half in range(2):
                     rows = pl.ds(pl.multiple_of((2 * t + half) * CHUNK, CHUNK), CHUNK)
-                    out[inner, j, rows] = mixed[w * CHUNK:(w + 1) * CHUNK, half * LANES:(half + 1) * LANES]
+                    outs[j * plane + dp][dz, rows] = mixed[w * CHUNK:(w + 1) * CHUNK, half * LANES:(half + 1) * LANES]
         return carry
 
     lax.fori_loop(0, steps // 2, lambda t, carry: step(2 * t + 1, step(2 * t, carry)), 0)
@@ -252,15 +236,14 @@
         step(steps - 1, 0)
 
 
-def potential_call(start, steps, layout, by_plane, fields, bias, others, cols, turned):
+def potential_call(layout, fields, bias, others, cols, turned):
     nz, plane, own = layout
     walk, vectors = fields.shape
-    groups, inner = (plane, nz) if by_plane else (nz, plane)
-    rows = 2 * CHUNK
+    rows = turned.shape[0] * 2 * CHUNK
     *parts, energy = pl.pallas_call(
-        functools.partial(potential_kernel, start, steps, layout, by_plane),
+        functools.partial(potential_kernel, layout),
         out_shape=[
-            *[pltpu.VMEM((inner, own, steps * rows, LANES), jnp.bfloat16)] * groups,
+            *[pltpu.VMEM((nz, rows, LANES), jnp.bfloat16)] * (own * plane),
             pltpu.VMEM((CHUNK, LANES), jnp.float32),
         ],
         scratch_shapes=[
@@ -271,7 +254,7 @@
         compiler_params=params(16),
         name="potential",
     )(fields, *in_vmem(bias, *others, cols, turned))
-    return parts, energy
+    return [parts[j * plane:(j + 1) * plane] for j in range(own)], energy
 
 
 def add(refs, *at):
@@ -296,90 +279,79 @@
     return vmem_call(kernel, "sum_parts", out_shape, *arrays)
 
 
-def finish_call(factor, early, late):
-    own, rows, lanes = early[0].shape
-
+def finish_call(factor, arrays):
     def kernel(*refs):
-        out = refs[-1]
-        out[:, :rows] = (factor * add(refs[:len(early)], Ellipsis)).astype(out.dtype)
-        out[:, rows:] = (factor * add(refs[len(early):-1], Ellipsis)).astype(out.dtype)
-
-    out_shape = pltpu.VMEM((own, rows + late[0].shape[1], lanes), jnp.bfloat16)
-    return vmem_call(kernel, "finish", out_shape, *early, *late)
-
-
-def stack_call(pieces, slots, near):
+        refs[-1][...] = (factor * add(refs[:-1], Ellipsis)).astype(jnp.bfloat16)
+
+    return vmem_call(kernel, "finish", pltpu.VMEM(arrays[0].shape, jnp.bfloat16), *arrays)
+
+
+def stack_call(pieces, slots, after):
     def kernel(*refs):
-        ins, outs = refs[:len(pieces) + len(near)], refs[len(pieces) + len(near):]
-        for ref, slot in zip(ins, slots):
-            outs[0][slot] = ref[...]
-        for ref, out in zip(ins[len(pieces):], outs[1:]):
-            out[...] = ref[...]
-
-    one = pltpu.VMEM(pieces[0].shape, jnp.bfloat16)
-    out_shape = [pltpu.VMEM((len(pieces), *pieces[0].shape), jnp.bfloat16)] + [one] * len(near)
-    return vmem_call(kernel, "stack_pieces", out_shape, *pieces, *near)
-
-
-def series_kernel(n_orb, *refs):
+        for ref, slot in zip(refs, slots):
+            refs[-1][slot] = ref[...]
+
+    out_shape = pltpu.VMEM((len(pieces), *pieces[0].shape), jnp.bfloat16)
+    return vmem_call(kernel, "stack_pieces", out_shape, *pieces, *after)
+
+
+def series_kernel(n_orb, j, *refs):
     found, start = refs[:n_orb], refs[n_orb:2 * n_orb]
-    energy_ref, moved_ref, pot, term, total = refs[2 * n_orb:]
+    energy_refs, (moved_ref, pot, term, total) = refs[2 * n_orb:-4], refs[-4:]
     me = lax.axis_index("orb")
-    own, half_rows = start[0].shape[:2]
+    half_rows = start[0].shape[1]
     rowblocks = half_rows // BLOCK
     per = BLOCK // CHUNK
     for d in range(n_orb):
         at = lax.rem(me + d, n_orb)
-        term[pl.ds(at, 1)] = start[d][...][None]
+        term[at] = start[d][j]
         for t in range(rowblocks * per):
             for half in range(2):
                 rows = slice((2 * t + half) * CHUNK, (2 * t + half + 1) * CHUNK)
-                pot[pl.ds(at * rowblocks + t // per, 1), :, (t % per) * CHUNK:(t % per + 1) * CHUNK,
-                    half * LANES:(half + 1) * LANES] = found[d][:, rows, :][None]
-    for j in range(own):
-        blocks = [term[r // rowblocks, j, (r % rowblocks) * BLOCK:(r % rowblocks + 1) * BLOCK] for r in range(ROWBLK)]
-        sums = [jnp.zeros(blocks[0].shape, jnp.float32)] * ROWBLK
-        begin = blocks
-        for degree in range(1, TAYLOR + 1):
-            after = []
-            for r in range(ROWBLK):
-                right = jnp.concatenate([blocks[c] for c in column_order(r)], axis=0)
-                product = jnp.dot(pot[r, j], right, preferred_element_type=jnp.float32)
-                after.append((product / degree).astype(jnp.bfloat16))
-            blocks = after
-            sums = [s + b.astype(jnp.float32) for s, b in zip(sums, blocks)]
+                pot[at * rowblocks + t // per, (t % per) * CHUNK:(t % per + 1) * CHUNK,
+                    half * LANES:(half + 1) * LANES] = found[d][rows, :]
+    blocks = [term[r // rowblocks, (r % rowblocks) * BLOCK:(r % rowblocks + 1) * BLOCK] for r in range(ROWBLK)]
+    sums = [jnp.zeros(blocks[0].shape, jnp.float32)] * ROWBLK
+    begin = blocks
+    for degree in range(1, TAYLOR + 1):
+        after = []
         for r in range(ROWBLK):
-            moved = begin[r].astype(jnp.float32) + sums[r]
-            total[r // rowblocks, j, (r % rowblocks) * BLOCK:(r % rowblocks + 1) * BLOCK] = moved.astype(jnp.bfloat16)
-    mine = total[pl.ds(me, 1)][0]
-    at = lax.broadcasted_iota(jnp.int32, (CHUNK, LANES), 0)
-    high, middle, low = (part.astype(jnp.float32) for part in split(energy_ref[...]))
-    tile = jnp.where(at == 0, high, jnp.where(at == 1, middle, jnp.where(at == 2, low, 0.0)))
-    moved_ref[:own * half_rows] = mine.reshape(own * half_rows, mine.shape[2])
-    moved_ref[own * half_rows:] = tile.astype(jnp.bfloat16)
-
-
-def series_call(found, start, energy):
+            right = jnp.concatenate([blocks[c] for c in column_order(r)], axis=0)
+            product = jnp.dot(pot[r], right, preferred_element_type=jnp.float32)
+            after.append((product / degree).astype(jnp.bfloat16))
+        blocks = after
+        sums = [s + b.astype(jnp.float32) for s, b in zip(sums, blocks)]
+    for r in range(ROWBLK):
+        moved = begin[r].astype(jnp.float32) + sums[r]
+        total[r // rowblocks, (r % rowblocks) * BLOCK:(r % rowblocks + 1) * BLOCK] = moved.astype(jnp.bfloat16)
+    moved_ref[:half_rows] = total[me]
+    for energy_ref in energy_refs:
+        at = lax.broadcasted_iota(jnp.int32, (CHUNK, LANES), 0)
+        high, middle, low = (part.astype(jnp.float32) for part in split(energy_ref[...]))
+        tile = jnp.where(at == 0, high, jnp.where(at == 1, middle, jnp.where(at == 2, low, 0.0)))
+        moved_ref[half_rows:] = tile.astype(jnp.bfloat16)
+
+
+def series_call(j, found, start, energies):
     n_orb = len(found)
-    own, half_rows, nocc = start[0].shape
+    half_rows, nocc = start[0].shape[1:]
     return pl.pallas_call(
-        functools.partial(series_kernel, n_orb),
-        out_shape=pltpu.VMEM((own * half_rows + CHUNK, nocc), jnp.bfloat16),
+        functools.partial(series_kernel, n_orb, j),
+        out_shape=pltpu.VMEM((half_rows + CHUNK * len(energies), nocc), jnp.bfloat16),
         scratch_shapes=[
-            pltpu.VMEM((ROWBLK, own, BLOCK, 2 * LANES), jnp.bfloat16),
-            pltpu.VMEM((n_orb, own, half_rows, nocc), jnp.bfloat16),
-            pltpu.VMEM((n_orb, own, half_rows, nocc), jnp.bfloat16),
+            pltpu.VMEM((ROWBLK, BLOCK, 2 * LANES), jnp.bfloat16),
+            pltpu.VMEM((n_orb, half_rows, nocc), jnp.bfloat16),
+            pltpu.VMEM((n_orb, half_rows, nocc), jnp.bfloat16),
         ],
         cost_estimate=FREE,
         compiler_params=params(16),
         name="series",
-    )(*in_vmem(*found, *start, energy))
+    )(*in_vmem(*found, *start, *energies))
 
 
 def place_kernel(layout, *refs):
     nz, plane, own = layout
-    near, far = refs[:plane], refs[plane:2 * plane]
-    out, energy_ref = refs[2 * plane:]
+    *gathered, out, energy_ref = refs
     me = lax.axis_index("chol")
     rows = out.shape[1]
     energy = jnp.zeros((CHUNK, LANES), jnp.float32)
@@ -387,27 +359,20 @@
         for dz in range(nz):
             z = hop(lax.div(me, plane), -dz if nz & (nz - 1) else dz, nz)
             p = hop(lax.rem(me, plane), -dp if plane & (plane - 1) else dp, plane)
-            piece = far[dp].at[dz - 1] if dz else near[dp]
             for j in range(own):
-                out[(z * plane + p) * own + j] = piece[j * rows:(j + 1) * rows]
-            energy = energy + piece[own * rows:].astype(jnp.float32)
+                out[(z * plane + p) * own + j] = gathered[j * plane + dp][dz, :rows]
+            energy = energy + gathered[dp][dz, rows:].astype(jnp.float32)
     energy_ref[...] = (energy[0:1] + energy[1:2] + energy[2:3])[:, :energy_ref.shape[1]]
 
 
-def place_call(layout, near, far):
+def place_call(layout, rows, gathered):
     nz, plane, own = layout
     walk = nz * plane * own
-    rows = (near[0].shape[0] - CHUNK) // own
-    return pl.pallas_call(
-        functools.partial(place_kernel, layout),
-        out_shape=[
-            jax.ShapeDtypeStruct((walk, rows, near[0].shape[1]), jnp.bfloat16),
-            jax.ShapeDtypeStruct((1, walk), jnp.float32),
-        ],
-        cost_estimate=FREE,
-        compiler_params=params(16),
-        name="place_walkers",
-    )(*in_vmem(*near, *far))
+    out_shape = [
+        jax.ShapeDtypeStruct((walk, rows, gathered[0].shape[2]), jnp.bfloat16),
+        jax.ShapeDtypeStruct((1, walk), jnp.float32),
+    ]
+    return vmem_call(functools.partial(place_kernel, layout), "place_walkers", out_shape, *gathered)
 
 
 def per_device(chol_vals, chol_cols, greens, walkers, fields):
@@ -436,10 +401,6 @@
     bias, *others = around_orb(partial_bias)
     start, others = lax.optimization_barrier((start, others))
 
-    total_steps = rowblocks * BLOCK // CHUNK
-    early_steps = total_steps // 4
-    late_steps = total_steps - early_steps
-    fields_t = fields.T
     def all_plane(arrays):
         return [to_plane(arrays[dp - 1], dp) for dp in reversed(range(1, plane))]
 
@@ -448,20 +409,16 @@
     def all_z(arrays):
         return [to_z(arrays[dz - 1], dz) for dz in z_order]
 
-    late, energy = potential_call(early_steps, late_steps, layout, True, fields_t, bias, others, cols, turned)
-    early, _ = potential_call(0, early_steps, layout, False, fields_t, bias, others, cols, turned)
-    early_came = all_z(early[1:])
-    late = sum_call([late[0], *all_plane(late[1:])])
-    late_came = all_z(late[1:])
-    early = sum_call([early[0], *early_came])
-    found = finish_call(step_factor, [early[0], *all_plane(early[1:])], [late[0], *late_came])
-
-    piece = series_call(around_orb(found), start, energy)
-    near = [piece, *(to_plane(piece, dp) for dp in range(1, plane))]
-    came = all_z([piece] * (nz - 1))
-    pieces, *near[1:] = stack_call(came, [dz - 1 for dz in z_order], near[1:])
-    far = {dp: to_plane(pieces, dp) for dp in reversed(range(1, plane))}
-    moved, energy = place_call(layout, near, [pieces, *(far[dp] for dp in range(1, plane))])
+    parts, energy = potential_call(layout, fields.T, bias, others, cols, turned)
+    sums = [sum_call([part[0], *all_plane(part[1:])]) for part in parts]
+    gathered = {}
+    for j in reversed(range(own)):
+        found = finish_call(step_factor, [sums[j][0], *all_z(sums[j][1:])])
+        piece = series_call(j, around_orb(found), start, [] if j else [energy])
+        came = all_z([piece] * (nz - 1))
+        pieces = stack_call([piece, *reversed(came)], [0, *reversed(z_order)], gathered.get(j + 1, [])[1:])
+        gathered[j] = [pieces, *reversed(all_plane([pieces] * (plane - 1)))]
+    moved, energy = place_call(layout, half_rows, sum((gathered[j] for j in range(own)), []))
     return moved, energy.reshape(walk)
 
 

time: 78.8 us -> 83.6 us (1.061)
  waiting for transfers between devices: 27.1 us -> 30.6 us
  starting transfers between devices: 31.8 us -> 34 us
  Pallas kernels: 19 us -> 18.1 us
    ppermute x9 -> x12, waiting for transfers between devices: 1.63 us -> 17.5 us  [to_z(): lax.ppermute(a, 'chol', [(c, hop(c // plane, dz, nz) * plane + c % plane)...]
    ppermute x12, waiting for transfers between devices: 23 us -> 11.9 us  [to_plane(): lax.ppermute(a, 'chol', [(c, c // plane * plane + hop(c % plane, dp, plan...]
    ppermute x9 -> x12, starting transfers between devices: 14.9 us -> 16.5 us  [to_z(): lax.ppermute(a, 'chol', [(c, hop(c // plane, dz, nz) * plane + c % plane)...]
    pallas_call x4 -> x3, Pallas kernels: 7.12 us -> 5.59 us  [the longest x1 4.16 us: potential_call(): pl.pallas_call(functools.partial(potential_kernel, layout), out_shape=[*[...]
    ppermute x3 -> x4, waiting for transfers between devices: 2.47 us -> 1.14 us  [around_orb(): lax.ppermute(a, 'orb', [((c + d) % n_orb, c) for c in range(n_orb)])]
    pallas_call x4 -> x7, Pallas kernels: 0.37 us -> 1.42 us  [vmem_call(): pl.pallas_call(kernel, out_shape=out_shape, cost_estimate=FREE, compiler_...]
  transfers between devices with their start and end apart: 24 -> 28, of which waited for: 14 -> 16; matrix products, arithmetic and copies ran while one was open for 0% -> 0% of each run, Pallas kernels for 2% -> 2%
where the time goes in v9:
time: 83.6 us; the launch traced here: 83.5 us
  starting transfers between devices  34 us (41%)
  waiting for transfers between devices  30.6 us (37%)
  Pallas kernels  18.1 us (22%)
    ppermute x12, waiting for transfers between devices, to_z(): lax.ppermute(a, 'chol', [(c, hop(c // plane, dz, nz) * plane + c % plane)...  17.5 us
    ppermute x12, starting transfers between devices, to_plane(): lax.ppermute(a, 'chol', [(c, c // plane * plane + hop(c % plane, dp, plan...  16.8 us
    ppermute x12, starting transfers between devices, to_z(): lax.ppermute(a, 'chol', [(c, hop(c // plane, dz, nz) * plane + c % plane)...  16.5 us
    ppermute x12, waiting for transfers between devices, to_plane(): lax.ppermute(a, 'chol', [(c, c // plane * plane + hop(c % plane, dp, plan...  11.9 us
    pallas_call x1, Pallas kernels, bias_call(): pl.pallas_call(bias_kernel, in_specs=[*[pl.BlockSpec(memory_space=pl.ANY)...  11.1 us
    pallas_call x1, Pallas kernels, potential_call(): pl.pallas_call(functools.partial(potential_kernel, layout), out_shape=[*[...  4.16 us
  transfers between devices with their start and end apart: 28, of which 16 were waited for; matrix products, arithmetic and copies ran while one was open for 0% of the time, Pallas kernels for 2%

profile of v9, /device:TPU:0, one launch (start us, length us, event | category | flops | bytes accessed | tf_op | source)
XLA Modules:
  0.0 83.5 jit_solution(783102785324297704)
XLA Ops:
  0.6 0.0 copy-start
  0.6 11.1 %force_bias.1 = (bf16[8,256,2048]{2,1,0:T(8,128)(2,1)S(1)}, f32[32,256]{1,0:T(8,128)S(1)}, bf16[2,128,128]{2,1,0:T(8,128)(2,1)S(1)}, s32[2,2,256]{2,1,0:T(2,128)S(1)}) custom-call(bf16[256,2,64,128]{3,2,1,0:T(8,128)(2,1)} %vals_hbm.1, bf16[32,128,256]{2,1,0:T(8,128)(2,1)} %greens_hbm.1, bf16[32,128,128]{2,1,0:T(8,128)(2,1)} %walkers_hbm.1, s32[2,2,256]{2,1,0:T(2,128)} %bitcast.4), custom_call_target="tpu_custom_call" | custom-call | tf_op jit(solution)/shard_map/force_bias/pallas_call | solution.py:149
  11.8 0.5 collective-permute-start
  12.3 0.1 collective-permute-start.1
  12.4 1.1 %collective-permute-done.1.refs_0_ = f32[32,256]{1,0:T(8,128)S(1)} collective-permute-done((f32[32,256]{1,0:T(8,128)S(1)}, f32[32,256]{1,0:T(8,128)S(1)}, u32[]{:S(2)}, u32[]{:S(2)}) %collective-permute-start.1) | collective-permute-done | bytes 32800 | tf_op jit(solution)/shard_map/ppermute | solution.py:396
  13.5 0.0 collective-permute-done.refs_3_
  13.5 4.2 %potential.1 = (bf16[4,256,128]{2,1,0:T(8,128)(2,1)S(1)}, bf16[4,256,128]{2,1,0:T(8,128)(2,1)S(1)}, bf16[4,256,128]{2,1,0:T(8,128)(2,1)S(1)}, bf16[4,256,128]{2,...) custom-call(f32[32,256]{1,0:T(8,128)S(1)} %bitcast.3, ...), custom_call_target="tpu_custom_call" | custom-call | tf_op jit(solution)/shard_map/potential/pallas_call | solution.py:243
  17.7 3.7 %collective-permute-start.12 = (bf16[4,256,128]{2,1,0:T(8,128)(2,1)S(1)}, bf16[4,256,128]{2,1,0:T(8,128)(2,1)S(1)}, u32[]{:S(2)}, u32[]{:S(2)}) collective-permute-start(bf16[4,256,128]{2,1,0:T(8,128)(2,1)S(1)} %get-tuple-element.45), channel_id=1, source_target_pairs={{0,6},{2,4},{4,2},{6,0},{8,14},{10,12},{12,10},{14,8},{16,22},{18,... | collective-permute-start | bytes 786440 | tf_op jit(solution)/shard_map/ppermute | solution.py:390
  21.4 0.5 collective-permute-start.13
  21.9 0.1 collective-permute-start.14
  22.0 2.8 %collective-permute-start.2 = (bf16[4,256,128]{2,1,0:T(8,128)(2,1)S(1)}, bf16[4,256,128]{2,1,0:T(8,128)(2,1)S(1)}, u32[]{:S(2)}, u32[]{:S(2)}) collective-permute-start(bf16[4,256,128]{2,1,0:T(8,128)(2,1)S(1)} %get-tuple-element.34), channel_id=1, source_target_pairs={{0,6},{2,4},{4,2},{6,0},{8,14},{10,12},{12,10},{14,8},{16,22},{18,... | collective-permute-start | bytes 786440 | tf_op jit(solution)/shard_map/ppermute | solution.py:390
  24.8 0.5 collective-permute-start.3
  25.4 3.1 %collective-permute-done.12.refs_1_ = bf16[4,256,128]{2,1,0:T(8,128)(2,1)S(1)} collective-permute-done((bf16[4,256,128]{2,1,0:T(8,128)(2,1)S(1)}, bf16[4,256,128]{2,1,0:T(8,128)(2,1)S(1)}, u32[]{:S(2)}, u32[]{:S(2)}) %collective-permute-start.12) | collective-permute-done | bytes 262176 | tf_op jit(solution)/shard_map/ppermute | solution.py:390
  28.5 2.0 %collective-permute-start.4 = (bf16[4,256,128]{2,1,0:T(8,128)(2,1)S(1)}, bf16[4,256,128]{2,1,0:T(8,128)(2,1)S(1)}, u32[]{:S(2)}, u32[]{:S(2)}) collective-permute-start(bf16[4,256,128]{2,1,0:T(8,128)(2,1)S(1)} %get-tuple-element.36), channel_id=1, source_target_pairs={{0,2},{2,0},{4,6},{6,4},{8,10},{10,8},{12,14},{14,12},{16,18},{18,... | collective-permute-start | bytes 786440 | tf_op jit(solution)/shard_map/ppermute | solution.py:390
  30.5 3.7 %collective-permute-done.13.refs_2_ = bf16[4,256,128]{2,1,0:T(8,128)(2,1)S(1)} collective-permute-done((bf16[4,256,128]{2,1,0:T(8,128)(2,1)S(1)}, bf16[4,256,128]{2,1,0:T(8,128)(2,1)S(1)}, u32[]{:S(2)}, u32[]{:S(2)}) %collective-permute-start.13) | collective-permute-done | bytes 262176 | tf_op jit(solution)/shard_map/ppermute | solution.py:390
  34.1 0.5 collective-permute-done.14.refs_3_
  34.6 0.1 sum_parts.3
  34.8 2.7 %collective-permute-start.15 = (bf16[256,128]{1,0:T(8,128)(2,1)S(1)}, bf16[256,128]{1,0:T(8,128)(2,1)S(1)}, u32[]{:S(2)}, u32[]{:S(2)}) collective-permute-start(bf16[256,128]{1,0:T(8,128)(2,1)S(1)} %get-tuple-element.49), channel_id=1, source_target_pairs={{0,16},{2,18},{4,20},{6,22},{8,24},{10,26},{12,28},{14,30},{16,0},... | collective-permute-start | bytes 196616 | tf_op jit(solution)/shard_map/ppermute | solution.py:393
  37.4 1.3 %collective-permute-start.16 = (bf16[256,128]{1,0:T(8,128)(2,1)S(1)}, bf16[256,128]{1,0:T(8,128)(2,1)S(1)}, u32[]{:S(2)}, u32[]{:S(2)}) collective-permute-start(bf16[256,128]{1,0:T(8,128)(2,1)S(1)} %get-tuple-element.50), channel_id=1, source_target_pairs={{0,24},{2,26},{4,28},{6,30},{8,16},{10,18},{12,20},{14,22},{16,8},... | collective-permute-start | bytes 196616 | tf_op jit(solution)/shard_map/ppermute | solution.py:393
  38.8 3.4 %collective-permute-done.15.refs_1_ = bf16[256,128]{1,0:T(8,128)(2,1)S(1)} collective-permute-done((bf16[256,128]{1,0:T(8,128)(2,1)S(1)}, bf16[256,128]{1,0:T(8,128)(2,1)S(1)}, u32[]{:S(2)}, u32[]{:S(2)}) %collective-permute-start.15) | collective-permute-done | bytes 65568 | tf_op jit(solution)/shard_map/ppermute | solution.py:393
  42.2 1.3 %collective-permute-start.17 = (bf16[256,128]{1,0:T(8,128)(2,1)S(1)}, bf16[256,128]{1,0:T(8,128)(2,1)S(1)}, u32[]{:S(2)}, u32[]{:S(2)}) collective-permute-start(bf16[256,128]{1,0:T(8,128)(2,1)S(1)} %get-tuple-element.51), channel_id=1, source_target_pairs={{0,8},{2,10},{4,12},{6,14},{8,0},{10,2},{12,4},{14,6},{16,24},{18,... | collective-permute-start | bytes 196616 | tf_op jit(solution)/shard_map/ppermute | solution.py:393
  43.4 0.2 collective-permute-done.16.refs_2_
  43.6 2.8 %collective-permute-done.17.refs_3_ = bf16[256,128]{1,0:T(8,128)(2,1)S(1)} collective-permute-done((bf16[256,128]{1,0:T(8,128)(2,1)S(1)}, bf16[256,128]{1,0:T(8,128)(2,1)S(1)}, u32[]{:S(2)}, u32[]{:S(2)}) %collective-permute-start.17) | collective-permute-done | bytes 65568 | tf_op jit(solution)/shard_map/ppermute | solution.py:393
  46.5 0.1 collective-permute-start.18
  46.5 0.0 collective-permute-done.2.refs_1_
  46.6 0.0 collective-permute-done.3.refs_2_
  46.6 0.0 collective-permute-done.4.refs_3_
  46.6 0.1 sum_parts.2
  46.7 2.7 %collective-permute-start.5 = (bf16[256,128]{1,0:T(8,128)(2,1)S(1)}, bf16[256,128]{1,0:T(8,128)(2,1)S(1)}, u32[]{:S(2)}, u32[]{:S(2)}) collective-permute-start(bf16[256,128]{1,0:T(8,128)(2,1)S(1)} %get-tuple-element.38), channel_id=1, source_target_pairs={{0,16},{2,18},{4,20},{6,22},{8,24},{10,26},{12,28},{14,30},{16,0},... | collective-permute-start | bytes 196616 | tf_op jit(solution)/shard_map/ppermute | solution.py:393
  49.4 1.5 %collective-permute-start.6 = (bf16[256,128]{1,0:T(8,128)(2,1)S(1)}, bf16[256,128]{1,0:T(8,128)(2,1)S(1)}, u32[]{:S(2)}, u32[]{:S(2)}) collective-permute-start(bf16[256,128]{1,0:T(8,128)(2,1)S(1)} %get-tuple-element.39), channel_id=1, source_target_pairs={{0,24},{2,26},{4,28},{6,30},{8,16},{10,18},{12,20},{14,22},{16,8},... | collective-permute-start | bytes 196616 | tf_op jit(solution)/shard_map/ppermute | solution.py:393
  51.0 0.5 collective-permute-start.7
  51.4 0.0 collective-permute-done.18.refs_1_
  51.4 0.7 series.3.refs_0_
  52.2 2.4 %collective-permute-start.21 = (bf16[128,128]{1,0:T(8,128)(2,1)S(1)}, bf16[128,128]{1,0:T(8,128)(2,1)S(1)}, u32[]{:S(2)}, u32[]{:S(2)}) collective-permute-start(bf16[128,128]{1,0:T(8,128)(2,1)S(1)} %series.3.refs_0_), channel_id=1, source_target_pairs={{0,16},{2,18},{4,20},{6,22},{8,24},{10,26},{12,28},{14,30},{16,0},... | collective-permute-start | bytes 98312 | tf_op jit(solution)/shard_map/ppermute | solution.py:393
  54.6 1.5 %collective-permute-start.20 = (bf16[128,128]{1,0:T(8,128)(2,1)S(1)}, bf16[128,128]{1,0:T(8,128)(2,1)S(1)}, u32[]{:S(2)}, u32[]{:S(2)}) collective-permute-start(bf16[128,128]{1,0:T(8,128)(2,1)S(1)} %series.3.refs_0_), channel_id=1, source_target_pairs={{0,24},{2,26},{4,28},{6,30},{8,16},{10,18},{12,20},{14,22},{16,8},... | collective-permute-start | bytes 98312 | tf_op jit(solution)/shard_map/ppermute | solution.py:393
  56.1 0.0 collective-permute-done.5.refs_1_
  56.1 0.0 collective-permute-start.19
  56.1 0.0 collective-permute-done.6.refs_2_
  56.1 0.8 collective-permute-done.7.refs_3_
  57.0 0.1 collective-permute-start.8
  57.0 1.1 %collective-permute-done.21.refs_3_ = bf16[128,128]{1,0:T(8,128)(2,1)S(1)} collective-permute-done((bf16[128,128]{1,0:T(8,128)(2,1)S(1)}, bf16[128,128]{1,0:T(8,128)(2,1)S(1)}, u32[]{:S(2)}, u32[]{:S(2)}) %collective-permute-start.21) | collective-permute-done | bytes 32800 | tf_op jit(solution)/shard_map/ppermute | solution.py:393
  58.1 2.3 %collective-permute-done.20.refs_2_ = bf16[128,128]{1,0:T(8,128)(2,1)S(1)} collective-permute-done((bf16[128,128]{1,0:T(8,128)(2,1)S(1)}, bf16[128,128]{1,0:T(8,128)(2,1)S(1)}, u32[]{:S(2)}, u32[]{:S(2)}) %collective-permute-start.20) | collective-permute-done | bytes 32800 | tf_op jit(solution)/shard_map/ppermute | solution.py:393
  60.4 0.0 collective-permute-done.19.refs_1_
  60.4 0.8 collective-permute-start.24
  61.2 2.2 %collective-permute-start.23 = (bf16[4,128,128]{2,1,0:T(8,128)(2,1)S(1)}, bf16[4,128,128]{2,1,0:T(8,128)(2,1)S(1)}, u32[]{:S(2)}, u32[]{:S(2)}) collective-permute-start(bf16[4,128,128]{2,1,0:T(8,128)(2,1)S(1)} %stack_pieces.2.refs_4_), channel_id=1, source_target_pairs={{0,4},{2,6},{4,0},{6,2},{8,12},{10,14},{12,8},{14,10},{16,20},{18,... | collective-permute-start | bytes 393224 | tf_op jit(solution)/shard_map/ppermute | solution.py:390
  63.4 0.5 collective-permute-start.22
  64.0 0.0 collective-permute-done.8.refs_1_
  64.0 0.7 series.2.refs_0_
  64.7 1.5 %collective-permute-start.11 = (bf16[144,128]{1,0:T(8,128)(2,1)S(1)}, bf16[144,128]{1,0:T(8,128)(2,1)S(1)}, u32[]{:S(2)}, u32[]{:S(2)}) collective-permute-start(bf16[144,128]{1,0:T(8,128)(2,1)S(1)} %series.2.refs_0_), channel_id=1, source_target_pairs={{0,16},{2,18},{4,20},{6,22},{8,24},{10,26},{12,28},{14,30},{16,0},... | collective-permute-start | bytes 110600 | tf_op jit(solution)/shard_map/ppermute | solution.py:393
  66.2 1.0 %collective-permute-start.10 = (bf16[144,128]{1,0:T(8,128)(2,1)S(1)}, bf16[144,128]{1,0:T(8,128)(2,1)S(1)}, u32[]{:S(2)}, u32[]{:S(2)}) collective-permute-start(bf16[144,128]{1,0:T(8,128)(2,1)S(1)} %series.2.refs_0_), channel_id=1, source_target_pairs={{0,24},{2,26},{4,28},{6,30},{8,16},{10,18},{12,20},{14,22},{16,8},... | collective-permute-start | bytes 110600 | tf_op jit(solution)/shard_map/ppermute | solution.py:393
  67.2 3.1 %collective-permute-done.11.refs_3_ = bf16[144,128]{1,0:T(8,128)(2,1)S(1)} collective-permute-done((bf16[144,128]{1,0:T(8,128)(2,1)S(1)}, bf16[144,128]{1,0:T(8,128)(2,1)S(1)}, u32[]{:S(2)}, u32[]{:S(2)}) %collective-permute-start.11) | collective-permute-done | bytes 36896 | tf_op jit(solution)/shard_map/ppermute | solution.py:393
  70.3 0.0 collective-permute-start.9
  70.3 1.9 %collective-permute-done.10.refs_2_ = bf16[144,128]{1,0:T(8,128)(2,1)S(1)} collective-permute-done((bf16[144,128]{1,0:T(8,128)(2,1)S(1)}, bf16[144,128]{1,0:T(8,128)(2,1)S(1)}, u32[]{:S(2)}, u32[]{:S(2)}) %collective-permute-start.10) | collective-permute-done | bytes 36896 | tf_op jit(solution)/shard_map/ppermute | solution.py:393
  72.2 2.1 %collective-permute-done.9.refs_1_ = bf16[144,128]{1,0:T(8,128)(2,1)S(1)} collective-permute-done((bf16[144,128]{1,0:T(8,128)(2,1)S(1)}, bf16[144,128]{1,0:T(8,128)(2,1)S(1)}, u32[]{:S(2)}, u32[]{:S(2)}) %collective-permute-start.9) | collective-permute-done | bytes 36896 | tf_op jit(solution)/shard_map/ppermute | solution.py:393
  74.2 0.0 collective-permute-done.24.refs_6_.refs_7_
  74.2 0.0 collective-permute-done.23.refs_5_.refs_6_
  74.2 0.0 collective-permute-done.22.refs_4_.refs_5_
  74.3 1.3 %collective-permute-start.27 = (bf16[4,144,128]{2,1,0:T(8,128)(2,1)S(1)}, bf16[4,144,128]{2,1,0:T(8,128)(2,1)S(1)}, u32[]{:S(2)}, u32[]{:S(2)}) collective-permute-start(bf16[4,144,128]{2,1,0:T(8,128)(2,1)S(1)} %stack_pieces.3.refs_0_), channel_id=1, source_target_pairs={{0,6},{2,4},{4,2},{6,0},{8,14},{10,12},{12,10},{14,8},{16,22},{18,... | collective-permute-start | bytes 442376 | tf_op jit(solution)/shard_map/ppermute | solution.py:390
  75.5 1.7 %collective-permute-start.26 = (bf16[4,144,128]{2,1,0:T(8,128)(2,1)S(1)}, bf16[4,144,128]{2,1,0:T(8,128)(2,1)S(1)}, u32[]{:S(2)}, u32[]{:S(2)}) collective-permute-start(bf16[4,144,128]{2,1,0:T(8,128)(2,1)S(1)} %stack_pieces.3.refs_0_), channel_id=1, source_target_pairs={{0,4},{2,6},{4,0},{6,2},{8,12},{10,14},{12,8},{14,10},{16,20},{18,... | collective-permute-start | bytes 442376 | tf_op jit(solution)/shard_map/ppermute | solution.py:390
  77.3 0.5 collective-permute-start.25
  77.8 2.7 %collective-permute-done.27.refs_3_ = bf16[4,144,128]{2,1,0:T(8,128)(2,1)S(1)} collective-permute-done((bf16[4,144,128]{2,1,0:T(8,128)(2,1)S(1)}, bf16[4,144,128]{2,1,0:T(8,128)(2,1)S(1)}, u32[]{:S(2)}, u32[]{:S(2)}) %collective-permute-start.27) | collective-permute-done | bytes 147488 | tf_op jit(solution)/shard_map/ppermute | solution.py:390
  80.5 1.5 %collective-permute-done.26.refs_2_ = bf16[4,144,128]{2,1,0:T(8,128)(2,1)S(1)} collective-permute-done((bf16[4,144,128]{2,1,0:T(8,128)(2,1)S(1)}, bf16[4,144,128]{2,1,0:T(8,128)(2,1)S(1)}, u32[]{:S(2)}, u32[]{:S(2)}) %collective-permute-start.26) | collective-permute-done | bytes 147488 | tf_op jit(solution)/shard_map/ppermute | solution.py:390
  82.0 0.5 collective-permute-done.25.refs_1_
  82.4 1.1 %place_walkers.1 = (bf16[32,128,128]{2,1,0:T(8,128)(2,1)}, f32[1,32]{1,0:T(1,128)}) custom-call(bf16[4,144,128]{2,1,0:T(8,128)(2,1)S(1)} %stack_pieces.3.refs_0_, bf16[4,144,128]{2,1,0:T(8,128)(2,1)S(1)} %collective-permute-done.25.refs_1_, bf16[4,144,128]{2,1,0:T(8,128)(2,1)S(1)} %collective-permute-done.26.refs_2_, ...), custom_call_target="tpu_custom_call" | custom-call | tf_op jit(solution)/shard_map/place_walkers/pallas_call | solution.py:268
  (5 shorter events, 0.1 us)
Async XLA Ops:
  0.6 12.9 %copy-start = (f32[256,32]{0,1:T(8,128)S(1)}, f32[256,32]{0,1:T(8,128)}, u32[]{:S(2)}) copy-start(f32[256,32]{0,1:T(8,128)} %param.9) | copy-start | bytes 98308
  11.8 1.7 %collective-permute-start = (bf16[2,128,128]{2,1,0:T(8,128)(2,1)S(1)}, bf16[2,128,128]{2,1,0:T(8,128)(2,1)S(1)}, u32[]{:S(2)}, u32[]{:S(2)}) collective-permute-start(bf16[2,128,128]{2,1,0:T(8,128)(2,1)S(1)} %get-tuple-element.41.refs_2_), channel_id=1, source_target_pairs={{1,0},{0,1},{3,2},{2,3},{5,4},{4,5},{7,6},{6,7},{9,8},{8,9},{11,10... | collective-permute-start | bytes 196616 | tf_op jit(solution)/shard_map/ppermute | solution.py:396
  12.3 1.2 %collective-permute-start.1 = (f32[32,256]{1,0:T(8,128)S(1)}, f32[32,256]{1,0:T(8,128)S(1)}, u32[]{:S(2)}, u32[]{:S(2)}) collective-permute-start(f32[32,256]{1,0:T(8,128)S(1)} %get-tuple-element.28.own_ref), channel_id=1, source_target_pairs={{1,0},{0,1},{3,2},{2,3},{5,4},{4,5},{7,6},{6,7},{9,8},{8,9},{11,10... | collective-permute-start | bytes 98312 | tf_op jit(solution)/shard_map/ppermute | solution.py:396
  17.7 10.8 %collective-permute-start.12 = (bf16[4,256,128]{2,1,0:T(8,128)(2,1)S(1)}, bf16[4,256,128]{2,1,0:T(8,128)(2,1)S(1)}, u32[]{:S(2)}, u32[]{:S(2)}) collective-permute-start(bf16[4,256,128]{2,1,0:T(8,128)(2,1)S(1)} %get-tuple-element.45), channel_id=1, source_target_pairs={{0,6},{2,4},{4,2},{6,0},{8,14},{10,12},{12,10},{14,8},{16,22},{18,... | collective-permute-start | bytes 786440 | tf_op jit(solution)/shard_map/ppermute | solution.py:390
  21.4 12.8 %collective-permute-start.13 = (bf16[4,256,128]{2,1,0:T(8,128)(2,1)S(1)}, bf16[4,256,128]{2,1,0:T(8,128)(2,1)S(1)}, u32[]{:S(2)}, u32[]{:S(2)}) collective-permute-start(bf16[4,256,128]{2,1,0:T(8,128)(2,1)S(1)} %get-tuple-element.46), channel_id=1, source_target_pairs={{0,4},{2,6},{4,0},{6,2},{8,12},{10,14},{12,8},{14,10},{16,20},{18,... | collective-permute-start | bytes 786440 | tf_op jit(solution)/shard_map/ppermute | solution.py:390
  21.9 12.8 %collective-permute-start.14 = (bf16[4,256,128]{2,1,0:T(8,128)(2,1)S(1)}, bf16[4,256,128]{2,1,0:T(8,128)(2,1)S(1)}, u32[]{:S(2)}, u32[]{:S(2)}) collective-permute-start(bf16[4,256,128]{2,1,0:T(8,128)(2,1)S(1)} %get-tuple-element.47), channel_id=1, source_target_pairs={{0,2},{2,0},{4,6},{6,4},{8,10},{10,8},{12,14},{14,12},{16,18},{18,... | collective-permute-start | bytes 786440 | tf_op jit(solution)/shard_map/ppermute | solution.py:390
  22.0 24.5 %collective-permute-start.2 = (bf16[4,256,128]{2,1,0:T(8,128)(2,1)S(1)}, bf16[4,256,128]{2,1,0:T(8,128)(2,1)S(1)}, u32[]{:S(2)}, u32[]{:S(2)}) collective-permute-start(bf16[4,256,128]{2,1,0:T(8,128)(2,1)S(1)} %get-tuple-element.34), channel_id=1, source_target_pairs={{0,6},{2,4},{4,2},{6,0},{8,14},{10,12},{12,10},{14,8},{16,22},{18,... | collective-permute-start | bytes 786440 | tf_op jit(solution)/shard_map/ppermute | solution.py:390
  24.8 21.7 %collective-permute-start.3 = (bf16[4,256,128]{2,1,0:T(8,128)(2,1)S(1)}, bf16[4,256,128]{2,1,0:T(8,128)(2,1)S(1)}, u32[]{:S(2)}, u32[]{:S(2)}) collective-permute-start(bf16[4,256,128]{2,1,0:T(8,128)(2,1)S(1)} %get-tuple-element.35), channel_id=1, source_target_pairs={{0,4},{2,6},{4,0},{6,2},{8,12},{10,14},{12,8},{14,10},{16,20},{18,... | collective-permute-start | bytes 786440 | tf_op jit(solution)/shard_map/ppermute | solution.py:390
  28.5 18.1 %collective-permute-start.4 = (bf16[4,256,128]{2,1,0:T(8,128)(2,1)S(1)}, bf16[4,256,128]{2,1,0:T(8,128)(2,1)S(1)}, u32[]{:S(2)}, u32[]{:S(2)}) collective-permute-start(bf16[4,256,128]{2,1,0:T(8,128)(2,1)S(1)} %get-tuple-element.36), channel_id=1, source_target_pairs={{0,2},{2,0},{4,6},{6,4},{8,10},{10,8},{12,14},{14,12},{16,18},{18,... | collective-permute-start | bytes 786440 | tf_op jit(solution)/shard_map/ppermute | solution.py:390
  34.8 7.4 %collective-permute-start.15 = (bf16[256,128]{1,0:T(8,128)(2,1)S(1)}, bf16[256,128]{1,0:T(8,128)(2,1)S(1)}, u32[]{:S(2)}, u32[]{:S(2)}) collective-permute-start(bf16[256,128]{1,0:T(8,128)(2,1)S(1)} %get-tuple-element.49), channel_id=1, source_target_pairs={{0,16},{2,18},{4,20},{6,22},{8,24},{10,26},{12,28},{14,30},{16,0},... | collective-permute-start | bytes 196616 | tf_op jit(solution)/shard_map/ppermute | solution.py:393
  37.4 6.2 %collective-permute-start.16 = (bf16[256,128]{1,0:T(8,128)(2,1)S(1)}, bf16[256,128]{1,0:T(8,128)(2,1)S(1)}, u32[]{:S(2)}, u32[]{:S(2)}) collective-permute-start(bf16[256,128]{1,0:T(8,128)(2,1)S(1)} %get-tuple-element.50), channel_id=1, source_target_pairs={{0,24},{2,26},{4,28},{6,30},{8,16},{10,18},{12,20},{14,22},{16,8},... | collective-permute-start | bytes 196616 | tf_op jit(solution)/shard_map/ppermute | solution.py:393
  42.2 4.3 %collective-permute-start.17 = (bf16[256,128]{1,0:T(8,128)(2,1)S(1)}, bf16[256,128]{1,0:T(8,128)(2,1)S(1)}, u32[]{:S(2)}, u32[]{:S(2)}) collective-permute-start(bf16[256,128]{1,0:T(8,128)(2,1)S(1)} %get-tuple-element.51), channel_id=1, source_target_pairs={{0,8},{2,10},{4,12},{6,14},{8,0},{10,2},{12,4},{14,6},{16,24},{18,... | collective-permute-start | bytes 196616 | tf_op jit(solution)/shard_map/ppermute | solution.py:393
  46.5 5.0 %collective-permute-start.18 = (bf16[256,128]{1,0:T(8,128)(2,1)S(1)}, bf16[256,128]{1,0:T(8,128)(2,1)S(1)}, u32[]{:S(2)}, u32[]{:S(2)}) collective-permute-start(bf16[256,128]{1,0:T(8,128)(2,1)S(1)} %finish.3.refs_0_), channel_id=1, source_target_pairs={{1,0},{0,1},{3,2},{2,3},{5,4},{4,5},{7,6},{6,7},{9,8},{8,9},{11,10... | collective-permute-start | bytes 196616 | tf_op jit(solution)/shard_map/ppermute | solution.py:396
  46.7 9.4 %collective-permute-start.5 = (bf16[256,128]{1,0:T(8,128)(2,1)S(1)}, bf16[256,128]{1,0:T(8,128)(2,1)S(1)}, u32[]{:S(2)}, u32[]{:S(2)}) collective-permute-start(bf16[256,128]{1,0:T(8,128)(2,1)S(1)} %get-tuple-element.38), channel_id=1, source_target_pairs={{0,16},{2,18},{4,20},{6,22},{8,24},{10,26},{12,28},{14,30},{16,0},... | collective-permute-start | bytes 196616 | tf_op jit(solution)/shard_map/ppermute | solution.py:393
  49.4 6.7 %collective-permute-start.6 = (bf16[256,128]{1,0:T(8,128)(2,1)S(1)}, bf16[256,128]{1,0:T(8,128)(2,1)S(1)}, u32[]{:S(2)}, u32[]{:S(2)}) collective-permute-start(bf16[256,128]{1,0:T(8,128)(2,1)S(1)} %get-tuple-element.39), channel_id=1, source_target_pairs={{0,24},{2,26},{4,28},{6,30},{8,16},{10,18},{12,20},{14,22},{16,8},... | collective-permute-start | bytes 196616 | tf_op jit(solution)/shard_map/ppermute | solution.py:393
  51.0 6.0 %collective-permute-start.7 = (bf16[256,128]{1,0:T(8,128)(2,1)S(1)}, bf16[256,128]{1,0:T(8,128)(2,1)S(1)}, u32[]{:S(2)}, u32[]{:S(2)}) collective-permute-start(bf16[256,128]{1,0:T(8,128)(2,1)S(1)} %get-tuple-element.40), channel_id=1, source_target_pairs={{0,8},{2,10},{4,12},{6,14},{8,0},{10,2},{12,4},{14,6},{16,24},{18,... | collective-permute-start | bytes 196616 | tf_op jit(solution)/shard_map/ppermute | solution.py:393
  52.2 5.9 %collective-permute-start.21 = (bf16[128,128]{1,0:T(8,128)(2,1)S(1)}, bf16[128,128]{1,0:T(8,128)(2,1)S(1)}, u32[]{:S(2)}, u32[]{:S(2)}) collective-permute-start(bf16[128,128]{1,0:T(8,128)(2,1)S(1)} %series.3.refs_0_), channel_id=1, source_target_pairs={{0,16},{2,18},{4,20},{6,22},{8,24},{10,26},{12,28},{14,30},{16,0},... | collective-permute-start | bytes 98312 | tf_op jit(solution)/shard_map/ppermute | solution.py:393
  54.6 5.8 %collective-permute-start.20 = (bf16[128,128]{1,0:T(8,128)(2,1)S(1)}, bf16[128,128]{1,0:T(8,128)(2,1)S(1)}, u32[]{:S(2)}, u32[]{:S(2)}) collective-permute-start(bf16[128,128]{1,0:T(8,128)(2,1)S(1)} %series.3.refs_0_), channel_id=1, source_target_pairs={{0,24},{2,26},{4,28},{6,30},{8,16},{10,18},{12,20},{14,22},{16,8},... | collective-permute-start | bytes 98312 | tf_op jit(solution)/shard_map/ppermute | solution.py:393
  56.1 4.3 %collective-permute-start.19 = (bf16[128,128]{1,0:T(8,128)(2,1)S(1)}, bf16[128,128]{1,0:T(8,128)(2,1)S(1)}, u32[]{:S(2)}, u32[]{:S(2)}) collective-permute-start(bf16[128,128]{1,0:T(8,128)(2,1)S(1)} %series.3.refs_0_), channel_id=1, source_target_pairs={{0,8},{2,10},{4,12},{6,14},{8,0},{10,2},{12,4},{14,6},{16,24},{18,... | collective-permute-start | bytes 98312 | tf_op jit(solution)/shard_map/ppermute | solution.py:393
  57.0 7.0 %collective-permute-start.8 = (bf16[256,128]{1,0:T(8,128)(2,1)S(1)}, bf16[256,128]{1,0:T(8,128)(2,1)S(1)}, u32[]{:S(2)}, u32[]{:S(2)}) collective-permute-start(bf16[256,128]{1,0:T(8,128)(2,1)S(1)} %finish.2.refs_0_), channel_id=1, source_target_pairs={{1,0},{0,1},{3,2},{2,3},{5,4},{4,5},{7,6},{6,7},{9,8},{8,9},{11,10... | collective-permute-start | bytes 196616 | tf_op jit(solution)/shard_map/ppermute | solution.py:396
  60.4 13.8 %collective-permute-start.24 = (bf16[4,128,128]{2,1,0:T(8,128)(2,1)S(1)}, bf16[4,128,128]{2,1,0:T(8,128)(2,1)S(1)}, u32[]{:S(2)}, u32[]{:S(2)}) collective-permute-start(bf16[4,128,128]{2,1,0:T(8,128)(2,1)S(1)} %stack_pieces.2.refs_4_), channel_id=1, source_target_pairs={{0,6},{2,4},{4,2},{6,0},{8,14},{10,12},{12,10},{14,8},{16,22},{18,... | collective-permute-start | bytes 393224 | tf_op jit(solution)/shard_map/ppermute | solution.py:390
  61.2 13.0 %collective-permute-start.23 = (bf16[4,128,128]{2,1,0:T(8,128)(2,1)S(1)}, bf16[4,128,128]{2,1,0:T(8,128)(2,1)S(1)}, u32[]{:S(2)}, u32[]{:S(2)}) collective-permute-start(bf16[4,128,128]{2,1,0:T(8,128)(2,1)S(1)} %stack_pieces.2.refs_4_), channel_id=1, source_target_pairs={{0,4},{2,6},{4,0},{6,2},{8,12},{10,14},{12,8},{14,10},{16,20},{18,... | collective-permute-start | bytes 393224 | tf_op jit(solution)/shard_map/ppermute | solution.py:390
  63.4 10.8 %collective-permute-start.22 = (bf16[4,128,128]{2,1,0:T(8,128)(2,1)S(1)}, bf16[4,128,128]{2,1,0:T(8,128)(2,1)S(1)}, u32[]{:S(2)}, u32[]{:S(2)}) collective-permute-start(bf16[4,128,128]{2,1,0:T(8,128)(2,1)S(1)} %stack_pieces.2.refs_4_), channel_id=1, source_target_pairs={{0,2},{2,0},{4,6},{6,4},{8,10},{10,8},{12,14},{14,12},{16,18},{18,... | collective-permute-start | bytes 393224 | tf_op jit(solution)/shard_map/ppermute | solution.py:390
  64.7 5.6 %collective-permute-start.11 = (bf16[144,128]{1,0:T(8,128)(2,1)S(1)}, bf16[144,128]{1,0:T(8,128)(2,1)S(1)}, u32[]{:S(2)}, u32[]{:S(2)}) collective-permute-start(bf16[144,128]{1,0:T(8,128)(2,1)S(1)} %series.2.refs_0_), channel_id=1, source_target_pairs={{0,16},{2,18},{4,20},{6,22},{8,24},{10,26},{12,28},{14,30},{16,0},... | collective-permute-start | bytes 110600 | tf_op jit(solution)/shard_map/ppermute | solution.py:393
  66.2 5.9 %collective-permute-start.10 = (bf16[144,128]{1,0:T(8,128)(2,1)S(1)}, bf16[144,128]{1,0:T(8,128)(2,1)S(1)}, u32[]{:S(2)}, u32[]{:S(2)}) collective-permute-start(bf16[144,128]{1,0:T(8,128)(2,1)S(1)} %series.2.refs_0_), channel_id=1, source_target_pairs={{0,24},{2,26},{4,28},{6,30},{8,16},{10,18},{12,20},{14,22},{16,8},... | collective-permute-start | bytes 110600 | tf_op jit(solution)/shard_map/ppermute | solution.py:393
  70.3 4.0 %collective-permute-start.9 = (bf16[144,128]{1,0:T(8,128)(2,1)S(1)}, bf16[144,128]{1,0:T(8,128)(2,1)S(1)}, u32[]{:S(2)}, u32[]{:S(2)}) collective-permute-start(bf16[144,128]{1,0:T(8,128)(2,1)S(1)} %series.2.refs_0_), channel_id=1, source_target_pairs={{0,8},{2,10},{4,12},{6,14},{8,0},{10,2},{12,4},{14,6},{16,24},{18,... | collective-permute-start | bytes 110600 | tf_op jit(solution)/shard_map/ppermute | solution.py:393
  74.3 6.2 %collective-permute-start.27 = (bf16[4,144,128]{2,1,0:T(8,128)(2,1)S(1)}, bf16[4,144,128]{2,1,0:T(8,128)(2,1)S(1)}, u32[]{:S(2)}, u32[]{:S(2)}) collective-permute-start(bf16[4,144,128]{2,1,0:T(8,128)(2,1)S(1)} %stack_pieces.3.refs_0_), channel_id=1, source_target_pairs={{0,6},{2,4},{4,2},{6,0},{8,14},{10,12},{12,10},{14,8},{16,22},{18,... | collective-permute-start | bytes 442376 | tf_op jit(solution)/shard_map/ppermute | solution.py:390
  75.5 6.4 %collective-permute-start.26 = (bf16[4,144,128]{2,1,0:T(8,128)(2,1)S(1)}, bf16[4,144,128]{2,1,0:T(8,128)(2,1)S(1)}, u32[]{:S(2)}, u32[]{:S(2)}) collective-permute-start(bf16[4,144,128]{2,1,0:T(8,128)(2,1)S(1)} %stack_pieces.3.refs_0_), channel_id=1, source_target_pairs={{0,4},{2,6},{4,0},{6,2},{8,12},{10,14},{12,8},{14,10},{16,20},{18,... | collective-permute-start | bytes 442376 | tf_op jit(solution)/shard_map/ppermute | solution.py:390
  77.3 5.1 %collective-permute-start.25 = (bf16[4,144,128]{2,1,0:T(8,128)(2,1)S(1)}, bf16[4,144,128]{2,1,0:T(8,128)(2,1)S(1)}, u32[]{:S(2)}, u32[]{:S(2)}) collective-permute-start(bf16[4,144,128]{2,1,0:T(8,128)(2,1)S(1)} %stack_pieces.3.refs_0_), channel_id=1, source_target_pairs={{0,2},{2,0},{4,6},{6,4},{8,10},{10,8},{12,14},{14,12},{16,18},{18,... | collective-permute-start | bytes 442376 | tf_op jit(solution)/shard_map/ppermute | solution.py:390

commit v10 on v8

--- a/solution.py
+++ b/solution.py
@@ -77,20 +77,20 @@
         return carry
 
     own = mine_ref.shape[0]
-    lax.fori_loop(0, total_steps, begin, 0)
     take = pltpu.make_async_copy(walkers_hbm.at[pl.ds(lax.axis_index("chol") * own, own)], mine_ref, wsem)
     take.start()
     take_cols = pltpu.make_async_copy(cols_hbm, cols_ref, csem)
     take_cols.start()
+    lax.fori_loop(0, total_steps, begin, 0)
     swap[...] = swap_matrix()
     bias_ref[...] = jnp.zeros_like(bias_ref)
     first = lax.broadcasted_iota(jnp.int32, (CHUNK * CHUNK, LANES), 1) < BLOCK
 
-    def turn(t):
+    def step(t, carry):
         for copy in copies(t):
             copy.wait()
-        slot = lax.rem(t, 2)
-        row = lax.axis_index("orb") * cols_ref.shape[0] + lax.div(t, steps)
+        local = lax.div(t, steps)
+        row = lax.axis_index("orb") * cols_ref.shape[0] + local
         upper = row // 2 == 1
         odd = row % 2 == 1
         for w in range(0, walk, CHUNK):
@@ -108,9 +108,7 @@
             for k, piece in enumerate(pieces):
                 piece = piece.astype(jnp.bfloat16)
                 for i in range(CHUNK):
-                    gs[slot, k * walk + w:k * walk + w + CHUNK, i * LANES:(i + 1) * LANES] = (
-                        piece[i * CHUNK:(i + 1) * CHUNK]
-                    )
+                    gs[k * walk + w:k * walk + w + CHUNK, i * LANES:(i + 1) * LANES] = piece[i * CHUNK:(i + 1) * CHUNK]
         for g in range(0, vectors, 2 * CHUNK):
             both = [vals[t, g + side * CHUNK:g + (side + 1) * CHUNK].reshape(CHUNK * CHUNK, LANES) for side in range(2)]
             both = jnp.dot(swap[...], jnp.concatenate(both, axis=1), preferred_element_type=jnp.float32)
@@ -120,38 +118,26 @@
                     turned_ref[t, g + side * CHUNK:g + (side + 1) * CHUNK, i * LANES:(i + 1) * LANES] = (
                         both[i * CHUNK:(i + 1) * CHUNK, side * LANES:(side + 1) * LANES]
                     )
-
-    def product(t):
-        return lax.dot_general(
-            turned_ref[t], gs[lax.rem(t, 2)], (((1,), (1,)), ((), ())), preferred_element_type=jnp.float32
+        part = lax.dot_general(
+            turned_ref[t], gs[...], (((1,), (1,)), ((), ())), preferred_element_type=jnp.float32
         )
-
-    def close(t):
-        local = lax.div(t, steps)
-        row = lax.axis_index("orb") * cols_ref.shape[0] + local
-        flat = acc[...].T
-        total = flat[0:walk]
-        for k, mask in enumerate(slot_masks(cols_ref[local, 1:2, :], row)):
-            total = total + jnp.where(mask, flat[(k + 1) * walk:(k + 2) * walk], 0.0)
-        bias_ref[...] += total
-
-    def step(t, carry):
-        part = product(t - 1)
-        turn(t)
-        acc[...] = jnp.where(lax.rem(t - 1, steps) == 0, 0.0, acc[...]) + part
-
-        @pl.when(lax.rem(t, steps) == 0)
+        begins = lax.rem(t, steps) == 0
+        acc[...] = jnp.where(begins, 0.0, acc[...]) + part
+
+        @pl.when(lax.rem(t, steps) == steps - 1)
         def _():
-            close(t - 1)
+            flat = acc[...].T
+            total = flat[0:walk]
+            cols = cols_ref[local, 1:2, :]
+            for k, mask in enumerate(slot_masks(cols, row)):
+                total = total + jnp.where(mask, flat[(k + 1) * walk:(k + 2) * walk], 0.0)
+            bias_ref[...] += total
 
         return carry
 
     acc[...] = jnp.zeros_like(acc)
-    turn(0)
     take_cols.wait()
-    lax.fori_loop(1, total_steps, step, 0)
-    acc[...] += product(total_steps - 1)
-    close(total_steps - 1)
+    lax.fori_loop(0, total_steps, step, 0)
     take.wait()
 
 
@@ -176,7 +162,7 @@
             pltpu.VMEM((steps, vectors, CHUNK, LANES), jnp.bfloat16),
             pltpu.VMEM((steps, walk, CHUNK, norb), jnp.bfloat16),
             pltpu.VMEM((CHUNK * CHUNK, CHUNK * CHUNK), jnp.bfloat16),
-            pltpu.VMEM((2, 4 * walk, wide), jnp.bfloat16),
+            pltpu.VMEM((4 * walk, wide), jnp.bfloat16),
             pltpu.VMEM((vectors, 4 * walk), jnp.float32),
             pltpu.SemaphoreType.DMA((steps,)),
             pltpu.SemaphoreType.DMA((steps,)),
@@ -193,7 +179,7 @@
     nz, plane, own = layout
     others = refs[:lax.axis_size("orb") - 1]
     cols_ref, turned_ref = refs[len(others):len(others) + 2]
-    groups = plane if by_plane else nz
+    groups = 2 * plane if by_plane else nz
     outs = refs[len(others) + 2:len(others) + 2 + groups]
     energy_ref, s_ref, swap = refs[len(others) + 2 + groups:]
     walk, vectors = fields_ref.shape
@@ -241,10 +227,15 @@
             for w in range(CHUNK):
                 chip, j = (w0 + w) // own, (w0 + w) % own
                 dz, dp = chip // plane, chip % plane
-                out, inner = (outs[dp], dz) if by_plane else (outs[dz], dp)
+                if not by_plane:
+                    out, inner = outs[dz], (dp,)
+                elif dz:
+                    out, inner = outs[dp], (dz - 1,)
+                else:
+                    out, inner = outs[plane + dp], ()
                 for half in range(2):
                     rows = pl.ds(pl.multiple_of((2 * t + half) * CHUNK, CHUNK), CHUNK)
-                    out[inner, j, rows] = mixed[w * CHUNK:(w + 1) * CHUNK, half * LANES:(half + 1) * LANES]
+                    out[(*inner, j, rows)] = mixed[w * CHUNK:(w + 1) * CHUNK, half * LANES:(half + 1) * LANES]
         return carry
 
     lax.fori_loop(0, steps // 2, lambda t, carry: step(2 * t + 1, step(2 * t, carry)), 0)
@@ -255,12 +246,12 @@
 def potential_call(start, steps, layout, by_plane, fields, bias, others, cols, turned):
     nz, plane, own = layout
     walk, vectors = fields.shape
-    groups, inner = (plane, nz) if by_plane else (nz, plane)
+    leading = [(nz - 1,)] * plane + [()] * plane if by_plane else [(plane,)] * nz
     rows = 2 * CHUNK
     *parts, energy = pl.pallas_call(
         functools.partial(potential_kernel, start, steps, layout, by_plane),
         out_shape=[
-            *[pltpu.VMEM((inner, own, steps * rows, LANES), jnp.bfloat16)] * groups,
+            *[pltpu.VMEM((*inner, own, steps * rows, LANES), jnp.bfloat16) for inner in leading],
             pltpu.VMEM((CHUNK, LANES), jnp.float32),
         ],
         scratch_shapes=[
@@ -287,38 +278,52 @@
     )(*in_vmem(*arrays))
 
 
-def sum_call(arrays):
+def sum_call(arrays, after):
     def kernel(*refs):
-        for k, out in enumerate(refs[len(arrays):]):
+        for k, out in enumerate(refs[len(arrays) + len(after):]):
             out[...] = add(refs[:len(arrays)], k).astype(out.dtype)
 
     out_shape = [pltpu.VMEM(arrays[0].shape[1:], jnp.bfloat16)] * arrays[0].shape[0]
-    return vmem_call(kernel, "sum_parts", out_shape, *arrays)
-
-
-def finish_call(factor, early, late):
-    own, rows, lanes = early[0].shape
+    return vmem_call(kernel, "sum_parts", out_shape, *arrays, *after)
+
+
+def merge_call(early, near):
+    own, rows, lanes = early[0].shape[1:]
 
     def kernel(*refs):
-        out = refs[-1]
-        out[:, :rows] = (factor * add(refs[:len(early)], Ellipsis)).astype(out.dtype)
-        out[:, rows:] = (factor * add(refs[len(early):-1], Ellipsis)).astype(out.dtype)
-
-    out_shape = pltpu.VMEM((own, rows + late[0].shape[1], lanes), jnp.bfloat16)
-    return vmem_call(kernel, "finish", out_shape, *early, *late)
-
-
-def stack_call(pieces, slots, near):
+        early_refs, near_refs, outs = refs[:len(early)], refs[len(early):len(early) + len(near)], refs[-len(near):]
+        for k, (ref, out) in enumerate(zip(near_refs, outs)):
+            out[:, :rows] = add(early_refs, k).astype(out.dtype)
+            out[:, rows:] = ref[...]
+
+    out_shape = [pltpu.VMEM((own, rows + near[0].shape[1], lanes), jnp.bfloat16)] * len(near)
+    return vmem_call(kernel, "merge_parts", out_shape, *early, *near)
+
+
+def finish_call(factor, far, merged):
+    rows = merged[0].shape[1] - far[0].shape[1]
+
+    def kernel(*refs):
+        far_refs, merged_refs, out = refs[:len(far)], refs[len(far):-1], refs[-1]
+        total = add(merged_refs, slice(None), slice(0, rows))
+        out[:, :rows] = (factor * total).astype(out.dtype)
+        total = add(merged_refs, slice(None), slice(rows, None)) + add(far_refs, Ellipsis)
+        out[:, rows:] = (factor * total).astype(out.dtype)
+
+    return vmem_call(kernel, "finish", pltpu.VMEM(merged[0].shape, jnp.bfloat16), *far, *merged)
+
+
+def stack_call(near, pieces, slots):
     def kernel(*refs):
         ins, outs = refs[:len(pieces) + len(near)], refs[len(pieces) + len(near):]
-        for ref, slot in zip(ins, slots):
+        for ref, slot in zip(ins[len(near):], slots):
             outs[0][slot] = ref[...]
-        for ref, out in zip(ins[len(pieces):], outs[1:]):
+        for ref, out in zip(ins, outs[1:]):
             out[...] = ref[...]
 
     one = pltpu.VMEM(pieces[0].shape, jnp.bfloat16)
     out_shape = [pltpu.VMEM((len(pieces), *pieces[0].shape), jnp.bfloat16)] + [one] * len(near)
-    return vmem_call(kernel, "stack_pieces", out_shape, *pieces, *near)
+    return vmem_call(kernel, "stack_pieces", out_shape, *near, *pieces)
 
 
 def series_kernel(n_orb, *refs):
@@ -437,7 +442,7 @@
     start, others = lax.optimization_barrier((start, others))
 
     total_steps = rowblocks * BLOCK // CHUNK
-    early_steps = total_steps // 4
+    early_steps = total_steps // 8
     late_steps = total_steps - early_steps
     fields_t = fields.T
     def all_plane(arrays):
@@ -449,17 +454,17 @@
         return [to_z(arrays[dz - 1], dz) for dz in z_order]
 
     late, energy = potential_call(early_steps, late_steps, layout, True, fields_t, bias, others, cols, turned)
+    far, near = late[:plane], late[plane:]
     early, _ = potential_call(0, early_steps, layout, False, fields_t, bias, others, cols, turned)
     early_came = all_z(early[1:])
-    late = sum_call([late[0], *all_plane(late[1:])])
-    late_came = all_z(late[1:])
-    early = sum_call([early[0], *early_came])
-    found = finish_call(step_factor, [early[0], *all_plane(early[1:])], [late[0], *late_came])
+    merged = merge_call([early[0], *early_came], near)
+    far_came = all_z(sum_call([far[0], *all_plane(far[1:])], merged[:1]))
+    found = finish_call(step_factor, far_came, [merged[0], *all_plane(merged[1:])])
 
     piece = series_call(around_orb(found), start, energy)
     near = [piece, *(to_plane(piece, dp) for dp in range(1, plane))]
     came = all_z([piece] * (nz - 1))
-    pieces, *near[1:] = stack_call(came, [dz - 1 for dz in z_order], near[1:])
+    pieces, *near[1:] = stack_call(near[1:], came[::-1], [dz - 1 for dz in z_order[::-1]])
     far = {dp: to_plane(pieces, dp) for dp in reversed(range(1, plane))}
     moved, energy = place_call(layout, near, [pieces, *(far[dp] for dp in range(1, plane))])
     return moved, energy.reshape(walk)

time: 78.8 us -> 74.5 us (0.945)
  waiting for transfers between devices: 27.1 us -> 23.3 us
  Pallas kernels: 19 us -> 16.2 us
  starting transfers between devices: 31.8 us -> 34.2 us
    ppermute x12, waiting for transfers between devices: 23 us -> 9.57 us  [to_plane(): lax.ppermute(a, 'chol', [(c, c // plane * plane + hop(c % plane, dp, plan...]
    ppermute x9, waiting for transfers between devices: 1.63 us -> 11.2 us  [to_z(): lax.ppermute(a, 'chol', [(c, hop(c // plane, dz, nz) * plane + c % plane)...]
    pallas_call x1, Pallas kernels: 11.5 us -> 8.56 us  [bias_call(): pl.pallas_call(bias_kernel, in_specs=[*[pl.BlockSpec(memory_space=pl.ANY)...]
    ppermute x9, starting transfers between devices: 14.9 us -> 16.6 us  [to_z(): lax.ppermute(a, 'chol', [(c, hop(c // plane, dz, nz) * plane + c % plane)...]
where the time goes in v10:
time: 74.5 us; the launch traced here: 74.3 us
  starting transfers between devices  34.2 us (46%)
  waiting for transfers between devices  23.3 us (31%)
  Pallas kernels  16.2 us (22%)
    ppermute x12, starting transfers between devices, to_plane(): lax.ppermute(a, 'chol', [(c, c // plane * plane + hop(c % plane, dp, plan...  16.9 us
    ppermute x9, starting transfers between devices, to_z(): lax.ppermute(a, 'chol', [(c, hop(c // plane, dz, nz) * plane + c % plane)...  16.6 us
    ppermute x9, waiting for transfers between devices, to_z(): lax.ppermute(a, 'chol', [(c, hop(c // plane, dz, nz) * plane + c % plane)...  11.2 us
    ppermute x12, waiting for transfers between devices, to_plane(): lax.ppermute(a, 'chol', [(c, c // plane * plane + hop(c % plane, dp, plan...  9.57 us
    pallas_call x1, Pallas kernels, bias_call(): pl.pallas_call(bias_kernel, in_specs=[*[pl.BlockSpec(memory_space=pl.ANY)...  8.56 us
    pallas_call x2, Pallas kernels, potential_call(): pl.pallas_call(functools.partial(potential_kernel, start, steps, layout,...  4.95 us
    ppermute x3, waiting for transfers between devices, around_orb(): lax.ppermute(a, 'orb', [((c + d) % n_orb, c) for c in range(n_orb)])  2.47 us
  transfers between devices with their start and end apart: 24, of which 14 were waited for; matrix products, arithmetic and copies ran while one was open for 0% of the time, Pallas kernels for 2%

profile of v10, /device:TPU:0, one launch (start us, length us, event | category | flops | bytes accessed | tf_op | source)
XLA Modules:
  0.0 74.3 jit_solution(9753298717047664637)
XLA Ops:
  0.6 0.0 copy-start
  0.6 8.6 %force_bias.1 = (bf16[8,256,2048]{2,1,0:T(8,128)(2,1)S(1)}, f32[32,256]{1,0:T(8,128)S(1)}, bf16[2,128,128]{2,1,0:T(8,128)(2,1)S(1)}, s32[2,2,256]{2,1,0:T(2,128)S(1)}) custom-call(bf16[256,2,64,128]{3,2,1,0:T(8,128)(2,1)} %vals_hbm.1, bf16[32,128,256]{2,1,0:T(8,128)(2,1)} %greens_hbm.1, bf16[32,128,128]{2,1,0:T(8,128)(2,1)} %walkers_hbm.1, s32[2,2,256]{2,1,0:T(2,128)} %bitcast.5), custom_call_target="tpu_custom_call" | custom-call | tf_op jit(solution)/shard_map/force_bias/pallas_call | solution.py:149
  9.2 0.5 collective-permute-start
  9.7 0.1 collective-permute-start.1
  9.8 1.1 %collective-permute-done.1.refs_0_ = f32[32,256]{1,0:T(8,128)S(1)} collective-permute-done((f32[32,256]{1,0:T(8,128)S(1)}, f32[32,256]{1,0:T(8,128)S(1)}, u32[]{:S(2)}, u32[]{:S(2)}) %collective-permute-start.1) | collective-permute-done | bytes 32800 | tf_op jit(solution)/shard_map/ppermute | solution.py:436
  10.9 0.0 collective-permute-done.refs_3_
  10.9 0.0 copy-done
  10.9 3.7 %potential.2 = (bf16[3,2,224,128]{3,2,1,0:T(8,128)(2,1)S(1)}, bf16[3,2,224,128]{3,2,1,0:T(8,128)(2,1)S(1)}, bf16[3,2,224,128]{3,2,1,0:T(8,128)(2,1)S(1)}, bf16[3...) custom-call(f32[32,256]{1,0:T(8,128)S(1)} %bitcast.3, ...), custom_call_target="tpu_custom_call" | custom-call | tf_op jit(solution)/shard_map/potential/pallas_call | solution.py:251
  14.7 3.7 %collective-permute-start.2 = (bf16[3,2,224,128]{3,2,1,0:T(8,128)(2,1)S(1)}, bf16[3,2,224,128]{3,2,1,0:T(8,128)(2,1)S(1)}, u32[]{:S(2)}, u32[]{:S(2)}) collective-permute-start(bf16[3,2,224,128]{3,2,1,0:T(8,128)(2,1)S(1)} %get-tuple-element.41), channel_id=1, source_target_pairs={{0,6},{2,4},{4,2},{6,0},{8,14},{10,12},{12,10},{14,8},{16,22},{18,... | collective-permute-start | bytes 1032200 | tf_op jit(solution)/shard_map/ppermute | solution.py:430
  18.4 0.5 collective-permute-start.3
  18.9 0.1 collective-permute-start.4
  19.0 1.2 %potential.3 = (bf16[4,2,32,128]{3,2,1,0:T(8,128)(2,1)S(1)}, bf16[4,2,32,128]{3,2,1,0:T(8,128)(2,1)S(1)}, bf16[4,2,32,128]{3,2,1,0:T(8,128)(2,1)S(1)}, bf16[4,2,32,128]{3,2,1,0:T(8,128)(2,1)S(1)}, f32[16,128]{1,0:T(8,128)}) custom-call(f32[32,256]{1,0:T(8,128)S(1)} %bitcast.4, f32[32,256]{1,0:T(8,128)S(1)} %get-tuple-element.35.own_ref, ...), custom_call_target="tpu_custom_call" | custom-call | tf_op jit(solution)/shard_map/potential/pallas_call | solution.py:251
  20.2 3.0 %collective-permute-start.5 = (bf16[4,2,32,128]{3,2,1,0:T(8,128)(2,1)S(1)}, bf16[4,2,32,128]{3,2,1,0:T(8,128)(2,1)S(1)}, u32[]{:S(2)}, u32[]{:S(2)}) collective-permute-start(bf16[4,2,32,128]{3,2,1,0:T(8,128)(2,1)S(1)} %get-tuple-element.45), channel_id=1, source_target_pairs={{0,16},{2,18},{4,20},{6,22},{8,24},{10,26},{12,28},{14,30},{16,0},... | collective-permute-start | bytes 196616 | tf_op jit(solution)/shard_map/ppermute | solution.py:433
  23.2 1.3 %collective-permute-start.6 = (bf16[4,2,32,128]{3,2,1,0:T(8,128)(2,1)S(1)}, bf16[4,2,32,128]{3,2,1,0:T(8,128)(2,1)S(1)}, u32[]{:S(2)}, u32[]{:S(2)}) collective-permute-start(bf16[4,2,32,128]{3,2,1,0:T(8,128)(2,1)S(1)} %get-tuple-element.46), channel_id=1, source_target_pairs={{0,24},{2,26},{4,28},{6,30},{8,16},{10,18},{12,20},{14,22},{16,8},... | collective-permute-start | bytes 196616 | tf_op jit(solution)/shard_map/ppermute | solution.py:433
  24.6 1.5 %collective-permute-done.5.refs_1_ = bf16[4,2,32,128]{3,2,1,0:T(8,128)(2,1)S(1)} collective-permute-done((bf16[4,2,32,128]{3,2,1,0:T(8,128)(2,1)S(1)}, bf16[4,2,32,128]{3,2,1,0:T(8,128)(2,1)S(1)}, u32[]{:S(2)}, u32[]{:S(2)}) %collective-permute-start.5) | collective-permute-done | bytes 65568 | tf_op jit(solution)/shard_map/ppermute | solution.py:433
  26.0 2.9 %collective-permute-start.7 = (bf16[4,2,32,128]{3,2,1,0:T(8,128)(2,1)S(1)}, bf16[4,2,32,128]{3,2,1,0:T(8,128)(2,1)S(1)}, u32[]{:S(2)}, u32[]{:S(2)}) collective-permute-start(bf16[4,2,32,128]{3,2,1,0:T(8,128)(2,1)S(1)} %get-tuple-element.47), channel_id=1, source_target_pairs={{0,8},{2,10},{4,12},{6,14},{8,0},{10,2},{12,4},{14,6},{16,24},{18,... | collective-permute-start | bytes 196616 | tf_op jit(solution)/shard_map/ppermute | solution.py:433
  28.9 0.5 collective-permute-done.6.refs_2_
  29.4 1.7 %collective-permute-done.7.refs_3_ = bf16[4,2,32,128]{3,2,1,0:T(8,128)(2,1)S(1)} collective-permute-done((bf16[4,2,32,128]{3,2,1,0:T(8,128)(2,1)S(1)}, bf16[4,2,32,128]{3,2,1,0:T(8,128)(2,1)S(1)}, u32[]{:S(2)}, u32[]{:S(2)}) %collective-permute-start.7) | collective-permute-done | bytes 65568 | tf_op jit(solution)/shard_map/ppermute | solution.py:433
  31.2 2.5 %collective-permute-start.11 = (bf16[2,256,128]{2,1,0:T(8,128)(2,1)S(1)}, bf16[2,256,128]{2,1,0:T(8,128)(2,1)S(1)}, u32[]{:S(2)}, u32[]{:S(2)}) collective-permute-start(bf16[2,256,128]{2,1,0:T(8,128)(2,1)S(1)} %get-tuple-element.56), channel_id=1, source_target_pairs={{0,6},{2,4},{4,2},{6,0},{8,14},{10,12},{12,10},{14,8},{16,22},{18,... | collective-permute-start | bytes 393224 | tf_op jit(solution)/shard_map/ppermute | solution.py:430
  33.7 0.5 collective-permute-start.12
  34.2 0.0 collective-permute-done.2.refs_1_
  34.2 0.5 collective-permute-start.13
  34.8 0.0 collective-permute-done.3.refs_2_
  34.8 0.4 collective-permute-done.4.refs_3_
  35.2 0.2 sum_parts.1
  35.3 3.0 %collective-permute-start.8 = (bf16[2,224,128]{2,1,0:T(8,128)(2,1)S(1)}, bf16[2,224,128]{2,1,0:T(8,128)(2,1)S(1)}, u32[]{:S(2)}, u32[]{:S(2)}) collective-permute-start(bf16[2,224,128]{2,1,0:T(8,128)(2,1)S(1)} %get-tuple-element.53), channel_id=1, source_target_pairs={{0,16},{2,18},{4,20},{6,22},{8,24},{10,26},{12,28},{14,30},{16,0},... | collective-permute-start | bytes 344072 | tf_op jit(solution)/shard_map/ppermute | solution.py:433
  38.4 1.5 %collective-permute-start.9 = (bf16[2,224,128]{2,1,0:T(8,128)(2,1)S(1)}, bf16[2,224,128]{2,1,0:T(8,128)(2,1)S(1)}, u32[]{:S(2)}, u32[]{:S(2)}) collective-permute-start(bf16[2,224,128]{2,1,0:T(8,128)(2,1)S(1)} %get-tuple-element.54), channel_id=1, source_target_pairs={{0,24},{2,26},{4,28},{6,30},{8,16},{10,18},{12,20},{14,22},{16,8},... | collective-permute-start | bytes 344072 | tf_op jit(solution)/shard_map/ppermute | solution.py:433
  39.9 0.0 collective-permute-done.11.refs_4_
  39.9 0.5 collective-permute-start.10
  40.4 0.0 collective-permute-done.12.refs_5_
  40.4 0.0 collective-permute-done.13.refs_6_
  40.4 6.6 %collective-permute-done.8.refs_0_ = bf16[2,224,128]{2,1,0:T(8,128)(2,1)S(1)} collective-permute-done((bf16[2,224,128]{2,1,0:T(8,128)(2,1)S(1)}, bf16[2,224,128]{2,1,0:T(8,128)(2,1)S(1)}, u32[]{:S(2)}, u32[]{:S(2)}) %collective-permute-start.8) | collective-permute-done | bytes 114720 | tf_op jit(solution)/shard_map/ppermute | solution.py:433
  47.0 0.0 collective-permute-done.9.refs_1_
  47.0 0.2 collective-permute-done.10.refs_2_
  47.2 0.1 finish.1.refs_0_
  47.3 0.1 collective-permute-start.14
  47.4 1.3 %collective-permute-done.14.refs_1_ = bf16[2,256,128]{2,1,0:T(8,128)(2,1)S(1)} collective-permute-done((bf16[2,256,128]{2,1,0:T(8,128)(2,1)S(1)}, bf16[2,256,128]{2,1,0:T(8,128)(2,1)S(1)}, u32[]{:S(2)}, u32[]{:S(2)}) %collective-permute-start.14) | collective-permute-done | bytes 131104 | tf_op jit(solution)/shard_map/ppermute | solution.py:436
  48.7 1.3 %series.1.refs_0_ = bf16[272,128]{1,0:T(8,128)(2,1)S(1)} custom-call(bf16[2,256,128]{2,1,0:T(8,128)(2,1)S(1)} %finish.1.refs_0_, bf16[2,256,128]{2,1,0:T(8,128)(2,1)S(1)} %collective-permute-done.14.refs_1_, bf16[2,128,128]{2,1,0:T(8,128)(2,1)S(1)} %get-tuple-element.59.refs_2_, bf16[2,128,128]{2,1,0:T(8,128)(2,1)S(1)} %collective-permute-done.refs_3_, ...), custom_call_target="tpu_custom_call" | custom-call | tf_op jit(solution)/shard_map/series/pallas_call | solution.py:370
  50.0 3.7 %collective-permute-start.20 = (bf16[272,128]{1,0:T(8,128)(2,1)S(1)}, bf16[272,128]{1,0:T(8,128)(2,1)S(1)}, u32[]{:S(2)}, u32[]{:S(2)}) collective-permute-start(bf16[272,128]{1,0:T(8,128)(2,1)S(1)} %series.1.refs_0_), channel_id=1, source_target_pairs={{0,16},{2,18},{4,20},{6,22},{8,24},{10,26},{12,28},{14,30},{16,0},... | collective-permute-start | bytes 208904 | tf_op jit(solution)/shard_map/ppermute | solution.py:433
  53.6 0.5 collective-permute-start.19
  54.1 0.2 collective-permute-start.18
  54.3 1.3 %collective-permute-start.17 = (bf16[272,128]{1,0:T(8,128)(2,1)S(1)}, bf16[272,128]{1,0:T(8,128)(2,1)S(1)}, u32[]{:S(2)}, u32[]{:S(2)}) collective-permute-start(bf16[272,128]{1,0:T(8,128)(2,1)S(1)} %series.1.refs_0_), channel_id=1, source_target_pairs={{0,6},{2,4},{4,2},{6,0},{8,14},{10,12},{12,10},{14,8},{16,22},{18,... | collective-permute-start | bytes 208904 | tf_op jit(solution)/shard_map/ppermute | solution.py:430
  55.6 1.7 %collective-permute-start.16 = (bf16[272,128]{1,0:T(8,128)(2,1)S(1)}, bf16[272,128]{1,0:T(8,128)(2,1)S(1)}, u32[]{:S(2)}, u32[]{:S(2)}) collective-permute-start(bf16[272,128]{1,0:T(8,128)(2,1)S(1)} %series.1.refs_0_), channel_id=1, source_target_pairs={{0,4},{2,6},{4,0},{6,2},{8,12},{10,14},{12,8},{14,10},{16,20},{18,... | collective-permute-start | bytes 208904 | tf_op jit(solution)/shard_map/ppermute | solution.py:430
  57.3 0.6 collective-permute-done.20.refs_5_
  57.9 2.4 %collective-permute-start.15 = (bf16[272,128]{1,0:T(8,128)(2,1)S(1)}, bf16[272,128]{1,0:T(8,128)(2,1)S(1)}, u32[]{:S(2)}, u32[]{:S(2)}) collective-permute-start(bf16[272,128]{1,0:T(8,128)(2,1)S(1)} %series.1.refs_0_), channel_id=1, source_target_pairs={{0,2},{2,0},{4,6},{6,4},{8,10},{10,8},{12,14},{14,12},{16,18},{18,... | collective-permute-start | bytes 208904 | tf_op jit(solution)/shard_map/ppermute | solution.py:430
  60.3 0.0 collective-permute-done.19.refs_4_
  60.3 0.1 collective-permute-done.18.refs_3_
  60.5 0.0 collective-permute-done.17.refs_2_
  60.5 0.0 collective-permute-done.16.refs_1_
  60.5 2.1 %collective-permute-done.15.refs_0_ = bf16[272,128]{1,0:T(8,128)(2,1)S(1)} collective-permute-done((bf16[272,128]{1,0:T(8,128)(2,1)S(1)}, bf16[272,128]{1,0:T(8,128)(2,1)S(1)}, u32[]{:S(2)}, u32[]{:S(2)}) %collective-permute-start.15) | collective-permute-done | bytes 69664 | tf_op jit(solution)/shard_map/ppermute | solution.py:430
  62.7 1.5 %collective-permute-start.23 = (bf16[3,272,128]{2,1,0:T(8,128)(2,1)S(1)}, bf16[3,272,128]{2,1,0:T(8,128)(2,1)S(1)}, u32[]{:S(2)}, u32[]{:S(2)}) collective-permute-start(bf16[3,272,128]{2,1,0:T(8,128)(2,1)S(1)} %get-tuple-element.65.refs_4_), channel_id=1, source_target_pairs={{0,6},{2,4},{4,2},{6,0},{8,14},{10,12},{12,10},{14,8},{16,22},{18,... | collective-permute-start | bytes 626696 | tf_op jit(solution)/shard_map/ppermute | solution.py:430
  64.2 2.1 %collective-permute-start.22 = (bf16[3,272,128]{2,1,0:T(8,128)(2,1)S(1)}, bf16[3,272,128]{2,1,0:T(8,128)(2,1)S(1)}, u32[]{:S(2)}, u32[]{:S(2)}) collective-permute-start(bf16[3,272,128]{2,1,0:T(8,128)(2,1)S(1)} %get-tuple-element.65.refs_4_), channel_id=1, source_target_pairs={{0,4},{2,6},{4,0},{6,2},{8,12},{10,14},{12,8},{14,10},{16,20},{18,... | collective-permute-start | bytes 626696 | tf_op jit(solution)/shard_map/ppermute | solution.py:430
  66.3 0.0 collective-permute-start.21
  66.3 4.8 %collective-permute-done.23.refs_7_ = bf16[3,272,128]{2,1,0:T(8,128)(2,1)S(1)} collective-permute-done((bf16[3,272,128]{2,1,0:T(8,128)(2,1)S(1)}, bf16[3,272,128]{2,1,0:T(8,128)(2,1)S(1)}, u32[]{:S(2)}, u32[]{:S(2)}) %collective-permute-start.23) | collective-permute-done | bytes 208928 | tf_op jit(solution)/shard_map/ppermute | solution.py:430
  71.1 2.1 %collective-permute-done.22.refs_6_ = bf16[3,272,128]{2,1,0:T(8,128)(2,1)S(1)} collective-permute-done((bf16[3,272,128]{2,1,0:T(8,128)(2,1)S(1)}, bf16[3,272,128]{2,1,0:T(8,128)(2,1)S(1)}, u32[]{:S(2)}, u32[]{:S(2)}) %collective-permute-start.22) | collective-permute-done | bytes 208928 | tf_op jit(solution)/shard_map/ppermute | solution.py:430
  73.2 0.1 collective-permute-done.21.refs_5_
  73.3 1.1 %place_walkers.1 = (bf16[32,128,128]{2,1,0:T(8,128)(2,1)}, f32[1,32]{1,0:T(1,128)}) custom-call(bf16[272,128]{1,0:T(8,128)(2,1)S(1)} %series.1.refs_0_, bf16[272,128]{1,0:T(8,128)(2,1)S(1)} %get-tuple-element.62.refs_1_, bf16[272,128]{1,0:T(8,128)(2,1)S(1)} %get-tuple-element.63.refs_2_, bf16[272,128]{1,0:T(8,128)(2,1)S(1)} %get-tuple-element.64.refs_3_, ...), custom_call_target="tpu_custom_call" | custom-call | tf_op jit(solution)/shard_map/place_walkers/pallas_call | solution.py:406
  (2 shorter events, 0.1 us)
Async XLA Ops:
  0.6 10.3 %copy-start = (f32[256,32]{0,1:T(8,128)S(1)}, f32[256,32]{0,1:T(8,128)}, u32[]{:S(2)}) copy-start(f32[256,32]{0,1:T(8,128)} %param.9) | copy-start | bytes 98308
  9.2 1.7 %collective-permute-start = (bf16[2,128,128]{2,1,0:T(8,128)(2,1)S(1)}, bf16[2,128,128]{2,1,0:T(8,128)(2,1)S(1)}, u32[]{:S(2)}, u32[]{:S(2)}) collective-permute-start(bf16[2,128,128]{2,1,0:T(8,128)(2,1)S(1)} %get-tuple-element.59.refs_2_), channel_id=1, source_target_pairs={{1,0},{0,1},{3,2},{2,3},{5,4},{4,5},{7,6},{6,7},{9,8},{8,9},{11,10... | collective-permute-start | bytes 196616 | tf_op jit(solution)/shard_map/ppermute | solution.py:436
  9.7 1.2 %collective-permute-start.1 = (f32[32,256]{1,0:T(8,128)S(1)}, f32[32,256]{1,0:T(8,128)S(1)}, u32[]{:S(2)}, u32[]{:S(2)}) collective-permute-start(f32[32,256]{1,0:T(8,128)S(1)} %get-tuple-element.35.own_ref), channel_id=1, source_target_pairs={{1,0},{0,1},{3,2},{2,3},{5,4},{4,5},{7,6},{6,7},{9,8},{8,9},{11,10... | collective-permute-start | bytes 98312 | tf_op jit(solution)/shard_map/ppermute | solution.py:436
  14.7 19.6 %collective-permute-start.2 = (bf16[3,2,224,128]{3,2,1,0:T(8,128)(2,1)S(1)}, bf16[3,2,224,128]{3,2,1,0:T(8,128)(2,1)S(1)}, u32[]{:S(2)}, u32[]{:S(2)}) collective-permute-start(bf16[3,2,224,128]{3,2,1,0:T(8,128)(2,1)S(1)} %get-tuple-element.41), channel_id=1, source_target_pairs={{0,6},{2,4},{4,2},{6,0},{8,14},{10,12},{12,10},{14,8},{16,22},{18,... | collective-permute-start | bytes 1032200 | tf_op jit(solution)/shard_map/ppermute | solution.py:430
  18.4 16.4 %collective-permute-start.3 = (bf16[3,2,224,128]{3,2,1,0:T(8,128)(2,1)S(1)}, bf16[3,2,224,128]{3,2,1,0:T(8,128)(2,1)S(1)}, u32[]{:S(2)}, u32[]{:S(2)}) collective-permute-start(bf16[3,2,224,128]{3,2,1,0:T(8,128)(2,1)S(1)} %get-tuple-element.42), channel_id=1, source_target_pairs={{0,4},{2,6},{4,0},{6,2},{8,12},{10,14},{12,8},{14,10},{16,20},{18,... | collective-permute-start | bytes 1032200 | tf_op jit(solution)/shard_map/ppermute | solution.py:430
  18.9 16.3 %collective-permute-start.4 = (bf16[3,2,224,128]{3,2,1,0:T(8,128)(2,1)S(1)}, bf16[3,2,224,128]{3,2,1,0:T(8,128)(2,1)S(1)}, u32[]{:S(2)}, u32[]{:S(2)}) collective-permute-start(bf16[3,2,224,128]{3,2,1,0:T(8,128)(2,1)S(1)} %get-tuple-element.43), channel_id=1, source_target_pairs={{0,2},{2,0},{4,6},{6,4},{8,10},{10,8},{12,14},{14,12},{16,18},{18,... | collective-permute-start | bytes 1032200 | tf_op jit(solution)/shard_map/ppermute | solution.py:430
  20.2 5.8 %collective-permute-start.5 = (bf16[4,2,32,128]{3,2,1,0:T(8,128)(2,1)S(1)}, bf16[4,2,32,128]{3,2,1,0:T(8,128)(2,1)S(1)}, u32[]{:S(2)}, u32[]{:S(2)}) collective-permute-start(bf16[4,2,32,128]{3,2,1,0:T(8,128)(2,1)S(1)} %get-tuple-element.45), channel_id=1, source_target_pairs={{0,16},{2,18},{4,20},{6,22},{8,24},{10,26},{12,28},{14,30},{16,0},... | collective-permute-start | bytes 196616 | tf_op jit(solution)/shard_map/ppermute | solution.py:433
  23.2 6.2 %collective-permute-start.6 = (bf16[4,2,32,128]{3,2,1,0:T(8,128)(2,1)S(1)}, bf16[4,2,32,128]{3,2,1,0:T(8,128)(2,1)S(1)}, u32[]{:S(2)}, u32[]{:S(2)}) collective-permute-start(bf16[4,2,32,128]{3,2,1,0:T(8,128)(2,1)S(1)} %get-tuple-element.46), channel_id=1, source_target_pairs={{0,24},{2,26},{4,28},{6,30},{8,16},{10,18},{12,20},{14,22},{16,8},... | collective-permute-start | bytes 196616 | tf_op jit(solution)/shard_map/ppermute | solution.py:433
  26.0 5.1 %collective-permute-start.7 = (bf16[4,2,32,128]{3,2,1,0:T(8,128)(2,1)S(1)}, bf16[4,2,32,128]{3,2,1,0:T(8,128)(2,1)S(1)}, u32[]{:S(2)}, u32[]{:S(2)}) collective-permute-start(bf16[4,2,32,128]{3,2,1,0:T(8,128)(2,1)S(1)} %get-tuple-element.47), channel_id=1, source_target_pairs={{0,8},{2,10},{4,12},{6,14},{8,0},{10,2},{12,4},{14,6},{16,24},{18,... | collective-permute-start | bytes 196616 | tf_op jit(solution)/shard_map/ppermute | solution.py:433
  31.2 8.7 %collective-permute-start.11 = (bf16[2,256,128]{2,1,0:T(8,128)(2,1)S(1)}, bf16[2,256,128]{2,1,0:T(8,128)(2,1)S(1)}, u32[]{:S(2)}, u32[]{:S(2)}) collective-permute-start(bf16[2,256,128]{2,1,0:T(8,128)(2,1)S(1)} %get-tuple-element.56), channel_id=1, source_target_pairs={{0,6},{2,4},{4,2},{6,0},{8,14},{10,12},{12,10},{14,8},{16,22},{18,... | collective-permute-start | bytes 393224 | tf_op jit(solution)/shard_map/ppermute | solution.py:430
  33.7 6.7 %collective-permute-start.12 = (bf16[2,256,128]{2,1,0:T(8,128)(2,1)S(1)}, bf16[2,256,128]{2,1,0:T(8,128)(2,1)S(1)}, u32[]{:S(2)}, u32[]{:S(2)}) collective-permute-start(bf16[2,256,128]{2,1,0:T(8,128)(2,1)S(1)} %get-tuple-element.57), channel_id=1, source_target_pairs={{0,4},{2,6},{4,0},{6,2},{8,12},{10,14},{12,8},{14,10},{16,20},{18,... | collective-permute-start | bytes 393224 | tf_op jit(solution)/shard_map/ppermute | solution.py:430
  34.2 6.2 %collective-permute-start.13 = (bf16[2,256,128]{2,1,0:T(8,128)(2,1)S(1)}, bf16[2,256,128]{2,1,0:T(8,128)(2,1)S(1)}, u32[]{:S(2)}, u32[]{:S(2)}) collective-permute-start(bf16[2,256,128]{2,1,0:T(8,128)(2,1)S(1)} %get-tuple-element.58), channel_id=1, source_target_pairs={{0,2},{2,0},{4,6},{6,4},{8,10},{10,8},{12,14},{14,12},{16,18},{18,... | collective-permute-start | bytes 393224 | tf_op jit(solution)/shard_map/ppermute | solution.py:430
  35.3 11.7 %collective-permute-start.8 = (bf16[2,224,128]{2,1,0:T(8,128)(2,1)S(1)}, bf16[2,224,128]{2,1,0:T(8,128)(2,1)S(1)}, u32[]{:S(2)}, u32[]{:S(2)}) collective-permute-start(bf16[2,224,128]{2,1,0:T(8,128)(2,1)S(1)} %get-tuple-element.53), channel_id=1, source_target_pairs={{0,16},{2,18},{4,20},{6,22},{8,24},{10,26},{12,28},{14,30},{16,0},... | collective-permute-start | bytes 344072 | tf_op jit(solution)/shard_map/ppermute | solution.py:433
  38.4 8.6 %collective-permute-start.9 = (bf16[2,224,128]{2,1,0:T(8,128)(2,1)S(1)}, bf16[2,224,128]{2,1,0:T(8,128)(2,1)S(1)}, u32[]{:S(2)}, u32[]{:S(2)}) collective-permute-start(bf16[2,224,128]{2,1,0:T(8,128)(2,1)S(1)} %get-tuple-element.54), channel_id=1, source_target_pairs={{0,24},{2,26},{4,28},{6,30},{8,16},{10,18},{12,20},{14,22},{16,8},... | collective-permute-start | bytes 344072 | tf_op jit(solution)/shard_map/ppermute | solution.py:433
  39.9 7.2 %collective-permute-start.10 = (bf16[2,224,128]{2,1,0:T(8,128)(2,1)S(1)}, bf16[2,224,128]{2,1,0:T(8,128)(2,1)S(1)}, u32[]{:S(2)}, u32[]{:S(2)}) collective-permute-start(bf16[2,224,128]{2,1,0:T(8,128)(2,1)S(1)} %get-tuple-element.55), channel_id=1, source_target_pairs={{0,8},{2,10},{4,12},{6,14},{8,0},{10,2},{12,4},{14,6},{16,24},{18,... | collective-permute-start | bytes 344072 | tf_op jit(solution)/shard_map/ppermute | solution.py:433
  47.3 1.4 %collective-permute-start.14 = (bf16[2,256,128]{2,1,0:T(8,128)(2,1)S(1)}, bf16[2,256,128]{2,1,0:T(8,128)(2,1)S(1)}, u32[]{:S(2)}, u32[]{:S(2)}) collective-permute-start(bf16[2,256,128]{2,1,0:T(8,128)(2,1)S(1)} %finish.1.refs_0_), channel_id=1, source_target_pairs={{1,0},{0,1},{3,2},{2,3},{5,4},{4,5},{7,6},{6,7},{9,8},{8,9},{11,10... | collective-permute-start | bytes 393224 | tf_op jit(solution)/shard_map/ppermute | solution.py:436
  50.0 7.9 %collective-permute-start.20 = (bf16[272,128]{1,0:T(8,128)(2,1)S(1)}, bf16[272,128]{1,0:T(8,128)(2,1)S(1)}, u32[]{:S(2)}, u32[]{:S(2)}) collective-permute-start(bf16[272,128]{1,0:T(8,128)(2,1)S(1)} %series.1.refs_0_), channel_id=1, source_target_pairs={{0,16},{2,18},{4,20},{6,22},{8,24},{10,26},{12,28},{14,30},{16,0},... | collective-permute-start | bytes 208904 | tf_op jit(solution)/shard_map/ppermute | solution.py:433
  53.6 6.7 %collective-permute-start.19 = (bf16[272,128]{1,0:T(8,128)(2,1)S(1)}, bf16[272,128]{1,0:T(8,128)(2,1)S(1)}, u32[]{:S(2)}, u32[]{:S(2)}) collective-permute-start(bf16[272,128]{1,0:T(8,128)(2,1)S(1)} %series.1.refs_0_), channel_id=1, source_target_pairs={{0,24},{2,26},{4,28},{6,30},{8,16},{10,18},{12,20},{14,22},{16,8},... | collective-permute-start | bytes 208904 | tf_op jit(solution)/shard_map/ppermute | solution.py:433
  54.1 6.4 %collective-permute-start.18 = (bf16[272,128]{1,0:T(8,128)(2,1)S(1)}, bf16[272,128]{1,0:T(8,128)(2,1)S(1)}, u32[]{:S(2)}, u32[]{:S(2)}) collective-permute-start(bf16[272,128]{1,0:T(8,128)(2,1)S(1)} %series.1.refs_0_), channel_id=1, source_target_pairs={{0,8},{2,10},{4,12},{6,14},{8,0},{10,2},{12,4},{14,6},{16,24},{18,... | collective-permute-start | bytes 208904 | tf_op jit(solution)/shard_map/ppermute | solution.py:433
  54.3 6.2 %collective-permute-start.17 = (bf16[272,128]{1,0:T(8,128)(2,1)S(1)}, bf16[272,128]{1,0:T(8,128)(2,1)S(1)}, u32[]{:S(2)}, u32[]{:S(2)}) collective-permute-start(bf16[272,128]{1,0:T(8,128)(2,1)S(1)} %series.1.refs_0_), channel_id=1, source_target_pairs={{0,6},{2,4},{4,2},{6,0},{8,14},{10,12},{12,10},{14,8},{16,22},{18,... | collective-permute-start | bytes 208904 | tf_op jit(solution)/shard_map/ppermute | solution.py:430
  55.6 4.9 %collective-permute-start.16 = (bf16[272,128]{1,0:T(8,128)(2,1)S(1)}, bf16[272,128]{1,0:T(8,128)(2,1)S(1)}, u32[]{:S(2)}, u32[]{:S(2)}) collective-permute-start(bf16[272,128]{1,0:T(8,128)(2,1)S(1)} %series.1.refs_0_), channel_id=1, source_target_pairs={{0,4},{2,6},{4,0},{6,2},{8,12},{10,14},{12,8},{14,10},{16,20},{18,... | collective-permute-start | bytes 208904 | tf_op jit(solution)/shard_map/ppermute | solution.py:430
  57.9 4.7 %collective-permute-start.15 = (bf16[272,128]{1,0:T(8,128)(2,1)S(1)}, bf16[272,128]{1,0:T(8,128)(2,1)S(1)}, u32[]{:S(2)}, u32[]{:S(2)}) collective-permute-start(bf16[272,128]{1,0:T(8,128)(2,1)S(1)} %series.1.refs_0_), channel_id=1, source_target_pairs={{0,2},{2,0},{4,6},{6,4},{8,10},{10,8},{12,14},{14,12},{16,18},{18,... | collective-permute-start | bytes 208904 | tf_op jit(solution)/shard_map/ppermute | solution.py:430
  62.7 8.4 %collective-permute-start.23 = (bf16[3,272,128]{2,1,0:T(8,128)(2,1)S(1)}, bf16[3,272,128]{2,1,0:T(8,128)(2,1)S(1)}, u32[]{:S(2)}, u32[]{:S(2)}) collective-permute-start(bf16[3,272,128]{2,1,0:T(8,128)(2,1)S(1)} %get-tuple-element.65.refs_4_), channel_id=1, source_target_pairs={{0,6},{2,4},{4,2},{6,0},{8,14},{10,12},{12,10},{14,8},{16,22},{18,... | collective-permute-start | bytes 626696 | tf_op jit(solution)/shard_map/ppermute | solution.py:430
  64.2 8.9 %collective-permute-start.22 = (bf16[3,272,128]{2,1,0:T(8,128)(2,1)S(1)}, bf16[3,272,128]{2,1,0:T(8,128)(2,1)S(1)}, u32[]{:S(2)}, u32[]{:S(2)}) collective-permute-start(bf16[3,272,128]{2,1,0:T(8,128)(2,1)S(1)} %get-tuple-element.65.refs_4_), channel_id=1, source_target_pairs={{0,4},{2,6},{4,0},{6,2},{8,12},{10,14},{12,8},{14,10},{16,20},{18,... | collective-permute-start | bytes 626696 | tf_op jit(solution)/shard_map/ppermute | solution.py:430
  66.3 7.0 %collective-permute-start.21 = (bf16[3,272,128]{2,1,0:T(8,128)(2,1)S(1)}, bf16[3,272,128]{2,1,0:T(8,128)(2,1)S(1)}, u32[]{:S(2)}, u32[]{:S(2)}) collective-permute-start(bf16[3,272,128]{2,1,0:T(8,128)(2,1)S(1)} %get-tuple-element.65.refs_4_), channel_id=1, source_target_pairs={{0,2},{2,0},{4,6},{6,4},{8,10},{10,8},{12,14},{14,12},{16,18},{18,... | collective-permute-start | bytes 626696 | tf_op jit(solution)/shard_map/ppermute | solution.py:430

commit v11 on v10

--- a/solution.py
+++ b/solution.py
@@ -12,6 +12,7 @@
 ROWBLK = 4
 LANES = 2 * BLOCK
 CHUNK = 16
+EXTRA = 8
 MIB = 1024 * 1024
 
 
@@ -119,14 +120,14 @@
                         both[i * CHUNK:(i + 1) * CHUNK, side * LANES:(side + 1) * LANES]
                     )
         part = lax.dot_general(
-            turned_ref[t], gs[...], (((1,), (1,)), ((), ())), preferred_element_type=jnp.float32
+            gs[...], turned_ref[t], (((1,), (1,)), ((), ())), preferred_element_type=jnp.float32
         )
         begins = lax.rem(t, steps) == 0
         acc[...] = jnp.where(begins, 0.0, acc[...]) + part
 
         @pl.when(lax.rem(t, steps) == steps - 1)
         def _():
-            flat = acc[...].T
+            flat = acc[...]
             total = flat[0:walk]
             cols = cols_ref[local, 1:2, :]
             for k, mask in enumerate(slot_masks(cols, row)):
@@ -163,7 +164,7 @@
             pltpu.VMEM((steps, walk, CHUNK, norb), jnp.bfloat16),
             pltpu.VMEM((CHUNK * CHUNK, CHUNK * CHUNK), jnp.bfloat16),
             pltpu.VMEM((4 * walk, wide), jnp.bfloat16),
-            pltpu.VMEM((vectors, 4 * walk), jnp.float32),
+            pltpu.VMEM((4 * walk, vectors), jnp.float32),
             pltpu.SemaphoreType.DMA((steps,)),
             pltpu.SemaphoreType.DMA((steps,)),
             pltpu.SemaphoreType.DMA,
@@ -357,8 +358,8 @@
             moved = begin[r].astype(jnp.float32) + sums[r]
             total[r // rowblocks, j, (r % rowblocks) * BLOCK:(r % rowblocks + 1) * BLOCK] = moved.astype(jnp.bfloat16)
     mine = total[pl.ds(me, 1)][0]
-    at = lax.broadcasted_iota(jnp.int32, (CHUNK, LANES), 0)
-    high, middle, low = (part.astype(jnp.float32) for part in split(energy_ref[...]))
+    at = lax.broadcasted_iota(jnp.int32, (EXTRA, LANES), 0)
+    high, middle, low = (part.astype(jnp.float32) for part in split(energy_ref[:EXTRA]))
     tile = jnp.where(at == 0, high, jnp.where(at == 1, middle, jnp.where(at == 2, low, 0.0)))
     moved_ref[:own * half_rows] = mine.reshape(own * half_rows, mine.shape[2])
     moved_ref[own * half_rows:] = tile.astype(jnp.bfloat16)
@@ -369,7 +370,7 @@
     own, half_rows, nocc = start[0].shape
     return pl.pallas_call(
         functools.partial(series_kernel, n_orb),
-        out_shape=pltpu.VMEM((own * half_rows + CHUNK, nocc), jnp.bfloat16),
+        out_shape=pltpu.VMEM((own * half_rows + EXTRA, nocc), jnp.bfloat16),
         scratch_shapes=[
             pltpu.VMEM((ROWBLK, own, BLOCK, 2 * LANES), jnp.bfloat16),
             pltpu.VMEM((n_orb, own, half_rows, nocc), jnp.bfloat16),
@@ -384,31 +385,43 @@
 def place_kernel(layout, *refs):
     nz, plane, own = layout
     near, far = refs[:plane], refs[plane:2 * plane]
-    out, energy_ref = refs[2 * plane:]
+    out, energy_ref, sems = refs[2 * plane:]
     me = lax.axis_index("chol")
     rows = out.shape[1]
-    energy = jnp.zeros((CHUNK, LANES), jnp.float32)
+    copies = []
     for dp in range(plane):
         for dz in range(nz):
             z = hop(lax.div(me, plane), -dz if nz & (nz - 1) else dz, nz)
             p = hop(lax.rem(me, plane), -dp if plane & (plane - 1) else dp, plane)
             piece = far[dp].at[dz - 1] if dz else near[dp]
             for j in range(own):
-                out[(z * plane + p) * own + j] = piece[j * rows:(j + 1) * rows]
+                copy = pltpu.make_async_copy(
+                    piece.at[pl.ds(j * rows, rows)], out.at[(z * plane + p) * own + j], sems.at[len(copies)]
+                )
+                copy.start()
+                copies.append(copy)
+    energy = jnp.zeros((EXTRA, LANES), jnp.float32)
+    for dp in range(plane):
+        for dz in range(nz):
+            piece = far[dp].at[dz - 1] if dz else near[dp]
             energy = energy + piece[own * rows:].astype(jnp.float32)
     energy_ref[...] = (energy[0:1] + energy[1:2] + energy[2:3])[:, :energy_ref.shape[1]]
+    for copy in copies:
+        copy.wait()
 
 
 def place_call(layout, near, far):
     nz, plane, own = layout
     walk = nz * plane * own
-    rows = (near[0].shape[0] - CHUNK) // own
+    rows = (near[0].shape[0] - EXTRA) // own
     return pl.pallas_call(
         functools.partial(place_kernel, layout),
+        out_specs=[pl.BlockSpec(memory_space=pl.ANY), pl.BlockSpec(memory_space=pltpu.VMEM)],
         out_shape=[
-            jax.ShapeDtypeStruct((walk, rows, near[0].shape[1]), jnp.bfloat16),
+            pltpu.HBM((walk, rows, near[0].shape[1]), jnp.bfloat16),
             jax.ShapeDtypeStruct((1, walk), jnp.float32),
         ],
+        scratch_shapes=[pltpu.SemaphoreType.DMA((walk,))],
         cost_estimate=FREE,
         compiler_params=params(16),
         name="place_walkers",
@@ -464,7 +477,7 @@
     piece = series_call(around_orb(found), start, energy)
     near = [piece, *(to_plane(piece, dp) for dp in range(1, plane))]
     came = all_z([piece] * (nz - 1))
-    pieces, *near[1:] = stack_call(near[1:], came[::-1], [dz - 1 for dz in z_order[::-1]])
+    pieces, *near[2:] = stack_call(near[2:], came[::-1], [dz - 1 for dz in z_order[::-1]])
     far = {dp: to_plane(pieces, dp) for dp in reversed(range(1, plane))}
     moved, energy = place_call(layout, near, [pieces, *(far[dp] for dp in range(1, plane))])
     return moved, energy.reshape(walk)

time: 74.5 us -> 78.3 us (1.051)
  Pallas kernels: 16.2 us -> 20.1 us
  starting transfers between devices: 34.2 us -> 33.2 us
  waiting for transfers between devices: 23.3 us -> 24.1 us
    pallas_call x1, Pallas kernels: 8.56 us -> 11.8 us  [bias_call(): pl.pallas_call(bias_kernel, in_specs=[*[pl.BlockSpec(memory_space=pl.ANY)...]
    ppermute x9, waiting for transfers between devices: 11.2 us -> 13.5 us  [to_z(): lax.ppermute(a, 'chol', [(c, hop(c // plane, dz, nz) * plane + c % plane)...]
    ppermute x12, waiting for transfers between devices: 9.57 us -> 8.11 us  [to_plane(): lax.ppermute(a, 'chol', [(c, c // plane * plane + hop(c % plane, dp, plan...]
    ppermute x12, starting transfers between devices: 16.9 us -> 15.9 us  [to_plane(): lax.ppermute(a, 'chol', [(c, c // plane * plane + hop(c % plane, dp, plan...]
  transfers between devices with their start and end apart: 24 -> 24, of which waited for: 14 -> 12; matrix products, arithmetic and copies ran while one was open for 0% -> 0% of each run, Pallas kernels for 2% -> 2%
where the time goes in v11:
time: 78.3 us; the launch traced here: 78.2 us
  starting transfers between devices  33.2 us (42%)
  waiting for transfers between devices  24.1 us (31%)
  Pallas kernels  20.1 us (26%)
    ppermute x9, starting transfers between devices, to_z(): lax.ppermute(a, 'chol', [(c, hop(c // plane, dz, nz) * plane + c % plane)...  16.6 us
    ppermute x12, starting transfers between devices, to_plane(): lax.ppermute(a, 'chol', [(c, c // plane * plane + hop(c % plane, dp, plan...  15.9 us
    ppermute x9, waiting for transfers between devices, to_z(): lax.ppermute(a, 'chol', [(c, hop(c // plane, dz, nz) * plane + c % plane)...  13.5 us
    pallas_call x1, Pallas kernels, bias_call(): pl.pallas_call(bias_kernel, in_specs=[*[pl.BlockSpec(memory_space=pl.ANY)...  11.8 us
    ppermute x12, waiting for transfers between devices, to_plane(): lax.ppermute(a, 'chol', [(c, c // plane * plane + hop(c % plane, dp, plan...  8.11 us
    pallas_call x2, Pallas kernels, potential_call(): pl.pallas_call(functools.partial(potential_kernel, start, steps, layout,...  4.96 us
    ppermute x3, waiting for transfers between devices, around_orb(): lax.ppermute(a, 'orb', [((c + d) % n_orb, c) for c in range(n_orb)])  2.47 us
    pallas_call x1, Pallas kernels, place_call(): pl.pallas_call(functools.partial(place_kernel, layout), out_specs=[pl.Blo...  1.75 us
  transfers between devices with their start and end apart: 24, of which 12 were waited for; matrix products, arithmetic and copies ran while one was open for 0% of the time, Pallas kernels for 2%

profile of v11, /device:TPU:0, one launch (start us, length us, event | category | flops | bytes accessed | tf_op | source)
XLA Modules:
  0.0 78.2 jit_solution(433772984671609011)
XLA Ops:
  0.6 0.0 copy-start
  0.6 11.8 %force_bias.1 = (bf16[8,256,2048]{2,1,0:T(8,128)(2,1)S(1)}, f32[32,256]{1,0:T(8,128)S(1)}, bf16[2,128,128]{2,1,0:T(8,128)(2,1)S(1)}, s32[2,2,256]{2,1,0:T(2,128)S(1)}) custom-call(bf16[256,2,64,128]{3,2,1,0:T(8,128)(2,1)} %vals_hbm.1, bf16[32,128,256]{2,1,0:T(8,128)(2,1)} %greens_hbm.1, bf16[32,128,128]{2,1,0:T(8,128)(2,1)} %walkers_hbm.1, s32[2,2,256]{2,1,0:T(2,128)} %bitcast.5), custom_call_target="tpu_custom_call" | custom-call | tf_op jit(solution)/shard_map/force_bias/pallas_call | solution.py:150
  12.5 0.5 collective-permute-start
  13.0 0.1 collective-permute-start.1
  13.1 1.1 %collective-permute-done.1.refs_0_ = f32[32,256]{1,0:T(8,128)S(1)} collective-permute-done((f32[32,256]{1,0:T(8,128)S(1)}, f32[32,256]{1,0:T(8,128)S(1)}, u32[]{:S(2)}, u32[]{:S(2)}) %collective-permute-start.1) | collective-permute-done | bytes 32800 | tf_op jit(solution)/shard_map/ppermute | solution.py:449
  14.2 0.0 collective-permute-done.refs_3_
  14.2 0.0 copy-done
  14.2 3.7 %potential.2 = (bf16[3,2,224,128]{3,2,1,0:T(8,128)(2,1)S(1)}, bf16[3,2,224,128]{3,2,1,0:T(8,128)(2,1)S(1)}, bf16[3,2,224,128]{3,2,1,0:T(8,128)(2,1)S(1)}, bf16[3...) custom-call(f32[32,256]{1,0:T(8,128)S(1)} %bitcast.3, ...), custom_call_target="tpu_custom_call" | custom-call | tf_op jit(solution)/shard_map/potential/pallas_call | solution.py:252
  17.9 3.7 %collective-permute-start.2 = (bf16[3,2,224,128]{3,2,1,0:T(8,128)(2,1)S(1)}, bf16[3,2,224,128]{3,2,1,0:T(8,128)(2,1)S(1)}, u32[]{:S(2)}, u32[]{:S(2)}) collective-permute-start(bf16[3,2,224,128]{3,2,1,0:T(8,128)(2,1)S(1)} %get-tuple-element.40), channel_id=1, source_target_pairs={{0,6},{2,4},{4,2},{6,0},{8,14},{10,12},{12,10},{14,8},{16,22},{18,... | collective-permute-start | bytes 1032200 | tf_op jit(solution)/shard_map/ppermute | solution.py:443
  21.6 0.5 collective-permute-start.3
  22.1 0.1 collective-permute-start.4
  22.2 1.2 %potential.3 = (bf16[4,2,32,128]{3,2,1,0:T(8,128)(2,1)S(1)}, bf16[4,2,32,128]{3,2,1,0:T(8,128)(2,1)S(1)}, bf16[4,2,32,128]{3,2,1,0:T(8,128)(2,1)S(1)}, bf16[4,2,32,128]{3,2,1,0:T(8,128)(2,1)S(1)}, f32[16,128]{1,0:T(8,128)}) custom-call(f32[32,256]{1,0:T(8,128)S(1)} %bitcast.4, f32[32,256]{1,0:T(8,128)S(1)} %get-tuple-element.34.own_ref, ...), custom_call_target="tpu_custom_call" | custom-call | tf_op jit(solution)/shard_map/potential/pallas_call | solution.py:252
  23.5 3.0 %collective-permute-start.5 = (bf16[4,2,32,128]{3,2,1,0:T(8,128)(2,1)S(1)}, bf16[4,2,32,128]{3,2,1,0:T(8,128)(2,1)S(1)}, u32[]{:S(2)}, u32[]{:S(2)}) collective-permute-start(bf16[4,2,32,128]{3,2,1,0:T(8,128)(2,1)S(1)} %get-tuple-element.44), channel_id=1, source_target_pairs={{0,16},{2,18},{4,20},{6,22},{8,24},{10,26},{12,28},{14,30},{16,0},... | collective-permute-start | bytes 196616 | tf_op jit(solution)/shard_map/ppermute | solution.py:446
  26.4 1.3 %collective-permute-start.6 = (bf16[4,2,32,128]{3,2,1,0:T(8,128)(2,1)S(1)}, bf16[4,2,32,128]{3,2,1,0:T(8,128)(2,1)S(1)}, u32[]{:S(2)}, u32[]{:S(2)}) collective-permute-start(bf16[4,2,32,128]{3,2,1,0:T(8,128)(2,1)S(1)} %get-tuple-element.45), channel_id=1, source_target_pairs={{0,24},{2,26},{4,28},{6,30},{8,16},{10,18},{12,20},{14,22},{16,8},... | collective-permute-start | bytes 196616 | tf_op jit(solution)/shard_map/ppermute | solution.py:446
  27.8 1.5 %collective-permute-done.5.refs_1_ = bf16[4,2,32,128]{3,2,1,0:T(8,128)(2,1)S(1)} collective-permute-done((bf16[4,2,32,128]{3,2,1,0:T(8,128)(2,1)S(1)}, bf16[4,2,32,128]{3,2,1,0:T(8,128)(2,1)S(1)}, u32[]{:S(2)}, u32[]{:S(2)}) %collective-permute-start.5) | collective-permute-done | bytes 65568 | tf_op jit(solution)/shard_map/ppermute | solution.py:446
  29.3 2.9 %collective-permute-start.7 = (bf16[4,2,32,128]{3,2,1,0:T(8,128)(2,1)S(1)}, bf16[4,2,32,128]{3,2,1,0:T(8,128)(2,1)S(1)}, u32[]{:S(2)}, u32[]{:S(2)}) collective-permute-start(bf16[4,2,32,128]{3,2,1,0:T(8,128)(2,1)S(1)} %get-tuple-element.46), channel_id=1, source_target_pairs={{0,8},{2,10},{4,12},{6,14},{8,0},{10,2},{12,4},{14,6},{16,24},{18,... | collective-permute-start | bytes 196616 | tf_op jit(solution)/shard_map/ppermute | solution.py:446
  32.2 0.5 collective-permute-done.6.refs_2_
  32.7 1.7 %collective-permute-done.7.refs_3_ = bf16[4,2,32,128]{3,2,1,0:T(8,128)(2,1)S(1)} collective-permute-done((bf16[4,2,32,128]{3,2,1,0:T(8,128)(2,1)S(1)}, bf16[4,2,32,128]{3,2,1,0:T(8,128)(2,1)S(1)}, u32[]{:S(2)}, u32[]{:S(2)}) %collective-permute-start.7) | collective-permute-done | bytes 65568 | tf_op jit(solution)/shard_map/ppermute | solution.py:446
  34.5 2.5 %collective-permute-start.11 = (bf16[2,256,128]{2,1,0:T(8,128)(2,1)S(1)}, bf16[2,256,128]{2,1,0:T(8,128)(2,1)S(1)}, u32[]{:S(2)}, u32[]{:S(2)}) collective-permute-start(bf16[2,256,128]{2,1,0:T(8,128)(2,1)S(1)} %get-tuple-element.55), channel_id=1, source_target_pairs={{0,6},{2,4},{4,2},{6,0},{8,14},{10,12},{12,10},{14,8},{16,22},{18,... | collective-permute-start | bytes 393224 | tf_op jit(solution)/shard_map/ppermute | solution.py:443
  37.0 0.5 collective-permute-start.12
  37.5 0.0 collective-permute-done.2.refs_1_
  37.5 0.5 collective-permute-start.13
  38.0 0.0 collective-permute-done.3.refs_2_
  38.0 0.4 collective-permute-done.4.refs_3_
  38.4 0.2 sum_parts.1
  38.6 3.1 %collective-permute-start.8 = (bf16[2,224,128]{2,1,0:T(8,128)(2,1)S(1)}, bf16[2,224,128]{2,1,0:T(8,128)(2,1)S(1)}, u32[]{:S(2)}, u32[]{:S(2)}) collective-permute-start(bf16[2,224,128]{2,1,0:T(8,128)(2,1)S(1)} %get-tuple-element.52), channel_id=1, source_target_pairs={{0,16},{2,18},{4,20},{6,22},{8,24},{10,26},{12,28},{14,30},{16,0},... | collective-permute-start | bytes 344072 | tf_op jit(solution)/shard_map/ppermute | solution.py:446
  41.6 1.5 %collective-permute-start.9 = (bf16[2,224,128]{2,1,0:T(8,128)(2,1)S(1)}, bf16[2,224,128]{2,1,0:T(8,128)(2,1)S(1)}, u32[]{:S(2)}, u32[]{:S(2)}) collective-permute-start(bf16[2,224,128]{2,1,0:T(8,128)(2,1)S(1)} %get-tuple-element.53), channel_id=1, source_target_pairs={{0,24},{2,26},{4,28},{6,30},{8,16},{10,18},{12,20},{14,22},{16,8},... | collective-permute-start | bytes 344072 | tf_op jit(solution)/shard_map/ppermute | solution.py:446
  43.2 0.0 collective-permute-done.11.refs_4_
  43.2 0.5 collective-permute-start.10
  43.7 0.0 collective-permute-done.12.refs_5_
  43.7 0.0 collective-permute-done.13.refs_6_
  43.7 6.6 %collective-permute-done.8.refs_0_ = bf16[2,224,128]{2,1,0:T(8,128)(2,1)S(1)} collective-permute-done((bf16[2,224,128]{2,1,0:T(8,128)(2,1)S(1)}, bf16[2,224,128]{2,1,0:T(8,128)(2,1)S(1)}, u32[]{:S(2)}, u32[]{:S(2)}) %collective-permute-start.8) | collective-permute-done | bytes 114720 | tf_op jit(solution)/shard_map/ppermute | solution.py:446
  50.2 0.0 collective-permute-done.9.refs_1_
  50.3 0.2 collective-permute-done.10.refs_2_
  50.4 0.1 finish.1.refs_0_
  50.5 0.1 collective-permute-start.14
  50.6 1.3 %collective-permute-done.14.refs_1_ = bf16[2,256,128]{2,1,0:T(8,128)(2,1)S(1)} collective-permute-done((bf16[2,256,128]{2,1,0:T(8,128)(2,1)S(1)}, bf16[2,256,128]{2,1,0:T(8,128)(2,1)S(1)}, u32[]{:S(2)}, u32[]{:S(2)}) %collective-permute-start.14) | collective-permute-done | bytes 131104 | tf_op jit(solution)/shard_map/ppermute | solution.py:449
  51.9 1.3 %series.1.refs_0_ = bf16[264,128]{1,0:T(8,128)(2,1)S(1)} custom-call(bf16[2,256,128]{2,1,0:T(8,128)(2,1)S(1)} %finish.1.refs_0_, bf16[2,256,128]{2,1,0:T(8,128)(2,1)S(1)} %collective-permute-done.14.refs_1_, bf16[2,128,128]{2,1,0:T(8,128)(2,1)S(1)} %get-tuple-element.58.refs_2_, bf16[2,128,128]{2,1,0:T(8,128)(2,1)S(1)} %collective-permute-done.refs_3_, ...), custom_call_target="tpu_custom_call" | custom-call | tf_op jit(solution)/shard_map/series/pallas_call | solution.py:371
  53.2 3.7 %collective-permute-start.20 = (bf16[264,128]{1,0:T(8,128)(2,1)S(1)}, bf16[264,128]{1,0:T(8,128)(2,1)S(1)}, u32[]{:S(2)}, u32[]{:S(2)}) collective-permute-start(bf16[264,128]{1,0:T(8,128)(2,1)S(1)} %series.1.refs_0_), channel_id=1, source_target_pairs={{0,16},{2,18},{4,20},{6,22},{8,24},{10,26},{12,28},{14,30},{16,0},... | collective-permute-start | bytes 202760 | tf_op jit(solution)/shard_map/ppermute | solution.py:446
  56.9 0.5 collective-permute-start.19
  57.4 0.2 collective-permute-start.18
  57.5 1.3 %collective-permute-start.17 = (bf16[264,128]{1,0:T(8,128)(2,1)S(1)}, bf16[264,128]{1,0:T(8,128)(2,1)S(1)}, u32[]{:S(2)}, u32[]{:S(2)}) collective-permute-start(bf16[264,128]{1,0:T(8,128)(2,1)S(1)} %series.1.refs_0_), channel_id=1, source_target_pairs={{0,6},{2,4},{4,2},{6,0},{8,14},{10,12},{12,10},{14,8},{16,22},{18,... | collective-permute-start | bytes 202760 | tf_op jit(solution)/shard_map/ppermute | solution.py:443
  58.8 1.7 %collective-permute-start.16 = (bf16[264,128]{1,0:T(8,128)(2,1)S(1)}, bf16[264,128]{1,0:T(8,128)(2,1)S(1)}, u32[]{:S(2)}, u32[]{:S(2)}) collective-permute-start(bf16[264,128]{1,0:T(8,128)(2,1)S(1)} %series.1.refs_0_), channel_id=1, source_target_pairs={{0,4},{2,6},{4,0},{6,2},{8,12},{10,14},{12,8},{14,10},{16,20},{18,... | collective-permute-start | bytes 202760 | tf_op jit(solution)/shard_map/ppermute | solution.py:443
  60.5 0.5 collective-permute-done.20.refs_4_
  61.1 2.3 %collective-permute-done.19.refs_3_ = bf16[264,128]{1,0:T(8,128)(2,1)S(1)} collective-permute-done((bf16[264,128]{1,0:T(8,128)(2,1)S(1)}, bf16[264,128]{1,0:T(8,128)(2,1)S(1)}, u32[]{:S(2)}, u32[]{:S(2)}) %collective-permute-start.19) | collective-permute-done | bytes 67616 | tf_op jit(solution)/shard_map/ppermute | solution.py:446
  63.4 0.2 collective-permute-done.18.refs_2_
  63.6 0.0 collective-permute-done.17.refs_1_
  63.6 0.0 collective-permute-done.16.refs_0_
  63.6 1.4 %collective-permute-start.23 = (bf16[3,264,128]{2,1,0:T(8,128)(2,1)S(1)}, bf16[3,264,128]{2,1,0:T(8,128)(2,1)S(1)}, u32[]{:S(2)}, u32[]{:S(2)}) collective-permute-start(bf16[3,264,128]{2,1,0:T(8,128)(2,1)S(1)} %get-tuple-element.63.refs_4_), channel_id=1, source_target_pairs={{0,6},{2,4},{4,2},{6,0},{8,14},{10,12},{12,10},{14,8},{16,22},{18,... | collective-permute-start | bytes 608264 | tf_op jit(solution)/shard_map/ppermute | solution.py:443
  65.0 1.7 %collective-permute-start.22 = (bf16[3,264,128]{2,1,0:T(8,128)(2,1)S(1)}, bf16[3,264,128]{2,1,0:T(8,128)(2,1)S(1)}, u32[]{:S(2)}, u32[]{:S(2)}) collective-permute-start(bf16[3,264,128]{2,1,0:T(8,128)(2,1)S(1)} %get-tuple-element.63.refs_4_), channel_id=1, source_target_pairs={{0,4},{2,6},{4,0},{6,2},{8,12},{10,14},{12,8},{14,10},{16,20},{18,... | collective-permute-start | bytes 608264 | tf_op jit(solution)/shard_map/ppermute | solution.py:443
  66.7 0.5 collective-permute-start.21
  67.2 1.5 %collective-permute-start.15 = (bf16[264,128]{1,0:T(8,128)(2,1)S(1)}, bf16[264,128]{1,0:T(8,128)(2,1)S(1)}, u32[]{:S(2)}, u32[]{:S(2)}) collective-permute-start(bf16[264,128]{1,0:T(8,128)(2,1)S(1)} %series.1.refs_0_), channel_id=1, source_target_pairs={{0,2},{2,0},{4,6},{6,4},{8,10},{10,8},{12,14},{14,12},{16,18},{18,... | collective-permute-start | bytes 202760 | tf_op jit(solution)/shard_map/ppermute | solution.py:443
  68.7 7.7 %collective-permute-done.15.refs_1_ = bf16[264,128]{1,0:T(8,128)(2,1)S(1)} collective-permute-done((bf16[264,128]{1,0:T(8,128)(2,1)S(1)}, bf16[264,128]{1,0:T(8,128)(2,1)S(1)}, u32[]{:S(2)}, u32[]{:S(2)}) %collective-permute-start.15) | collective-permute-done | bytes 67616 | tf_op jit(solution)/shard_map/ppermute | solution.py:443
  76.4 0.0 collective-permute-done.23.refs_7_
  76.4 0.0 collective-permute-done.22.refs_6_
  76.4 0.0 collective-permute-done.21.refs_5_
  76.4 1.8 %place_walkers.1 = (bf16[32,128,128]{2,1,0:T(8,128)(2,1)}, f32[1,32]{1,0:T(1,128)}) custom-call(bf16[264,128]{1,0:T(8,128)(2,1)S(1)} %series.1.refs_0_, bf16[264,128]{1,0:T(8,128)(2,1)S(1)} %collective-permute-done.15.refs_1_, bf16[264,128]{1,0:T(8,128)(2,1)S(1)} %get-tuple-element.61.refs_2_, bf16[264,128]{1,0:T(8,128)(2,1)S(1)} %get-tuple-element.62.refs_3_, ...), custom_call_target="tpu_custom_call" | custom-call | tf_op jit(solution)/shard_map/place_walkers/pallas_call | solution.py:417
  (2 shorter events, 0.1 us)
Async XLA Ops:
  0.6 13.6 %copy-start = (f32[256,32]{0,1:T(8,128)S(1)}, f32[256,32]{0,1:T(8,128)}, u32[]{:S(2)}) copy-start(f32[256,32]{0,1:T(8,128)} %param.9) | copy-start | bytes 98308
  12.5 1.7 %collective-permute-start = (bf16[2,128,128]{2,1,0:T(8,128)(2,1)S(1)}, bf16[2,128,128]{2,1,0:T(8,128)(2,1)S(1)}, u32[]{:S(2)}, u32[]{:S(2)}) collective-permute-start(bf16[2,128,128]{2,1,0:T(8,128)(2,1)S(1)} %get-tuple-element.58.refs_2_), channel_id=1, source_target_pairs={{1,0},{0,1},{3,2},{2,3},{5,4},{4,5},{7,6},{6,7},{9,8},{8,9},{11,10... | collective-permute-start | bytes 196616 | tf_op jit(solution)/shard_map/ppermute | solution.py:449
  13.0 1.2 %collective-permute-start.1 = (f32[32,256]{1,0:T(8,128)S(1)}, f32[32,256]{1,0:T(8,128)S(1)}, u32[]{:S(2)}, u32[]{:S(2)}) collective-permute-start(f32[32,256]{1,0:T(8,128)S(1)} %get-tuple-element.34.own_ref), channel_id=1, source_target_pairs={{1,0},{0,1},{3,2},{2,3},{5,4},{4,5},{7,6},{6,7},{9,8},{8,9},{11,10... | collective-permute-start | bytes 98312 | tf_op jit(solution)/shard_map/ppermute | solution.py:449
  17.9 19.6 %collective-permute-start.2 = (bf16[3,2,224,128]{3,2,1,0:T(8,128)(2,1)S(1)}, bf16[3,2,224,128]{3,2,1,0:T(8,128)(2,1)S(1)}, u32[]{:S(2)}, u32[]{:S(2)}) collective-permute-start(bf16[3,2,224,128]{3,2,1,0:T(8,128)(2,1)S(1)} %get-tuple-element.40), channel_id=1, source_target_pairs={{0,6},{2,4},{4,2},{6,0},{8,14},{10,12},{12,10},{14,8},{16,22},{18,... | collective-permute-start | bytes 1032200 | tf_op jit(solution)/shard_map/ppermute | solution.py:443
  21.6 16.4 %collective-permute-start.3 = (bf16[3,2,224,128]{3,2,1,0:T(8,128)(2,1)S(1)}, bf16[3,2,224,128]{3,2,1,0:T(8,128)(2,1)S(1)}, u32[]{:S(2)}, u32[]{:S(2)}) collective-permute-start(bf16[3,2,224,128]{3,2,1,0:T(8,128)(2,1)S(1)} %get-tuple-element.41), channel_id=1, source_target_pairs={{0,4},{2,6},{4,0},{6,2},{8,12},{10,14},{12,8},{14,10},{16,20},{18,... | collective-permute-start | bytes 1032200 | tf_op jit(solution)/shard_map/ppermute | solution.py:443
  22.1 16.3 %collective-permute-start.4 = (bf16[3,2,224,128]{3,2,1,0:T(8,128)(2,1)S(1)}, bf16[3,2,224,128]{3,2,1,0:T(8,128)(2,1)S(1)}, u32[]{:S(2)}, u32[]{:S(2)}) collective-permute-start(bf16[3,2,224,128]{3,2,1,0:T(8,128)(2,1)S(1)} %get-tuple-element.42), channel_id=1, source_target_pairs={{0,2},{2,0},{4,6},{6,4},{8,10},{10,8},{12,14},{14,12},{16,18},{18,... | collective-permute-start | bytes 1032200 | tf_op jit(solution)/shard_map/ppermute | solution.py:443
  23.5 5.8 %collective-permute-start.5 = (bf16[4,2,32,128]{3,2,1,0:T(8,128)(2,1)S(1)}, bf16[4,2,32,128]{3,2,1,0:T(8,128)(2,1)S(1)}, u32[]{:S(2)}, u32[]{:S(2)}) collective-permute-start(bf16[4,2,32,128]{3,2,1,0:T(8,128)(2,1)S(1)} %get-tuple-element.44), channel_id=1, source_target_pairs={{0,16},{2,18},{4,20},{6,22},{8,24},{10,26},{12,28},{14,30},{16,0},... | collective-permute-start | bytes 196616 | tf_op jit(solution)/shard_map/ppermute | solution.py:446
  26.4 6.2 %collective-permute-start.6 = (bf16[4,2,32,128]{3,2,1,0:T(8,128)(2,1)S(1)}, bf16[4,2,32,128]{3,2,1,0:T(8,128)(2,1)S(1)}, u32[]{:S(2)}, u32[]{:S(2)}) collective-permute-start(bf16[4,2,32,128]{3,2,1,0:T(8,128)(2,1)S(1)} %get-tuple-element.45), channel_id=1, source_target_pairs={{0,24},{2,26},{4,28},{6,30},{8,16},{10,18},{12,20},{14,22},{16,8},... | collective-permute-start | bytes 196616 | tf_op jit(solution)/shard_map/ppermute | solution.py:446
  29.3 5.1 %collective-permute-start.7 = (bf16[4,2,32,128]{3,2,1,0:T(8,128)(2,1)S(1)}, bf16[4,2,32,128]{3,2,1,0:T(8,128)(2,1)S(1)}, u32[]{:S(2)}, u32[]{:S(2)}) collective-permute-start(bf16[4,2,32,128]{3,2,1,0:T(8,128)(2,1)S(1)} %get-tuple-element.46), channel_id=1, source_target_pairs={{0,8},{2,10},{4,12},{6,14},{8,0},{10,2},{12,4},{14,6},{16,24},{18,... | collective-permute-start | bytes 196616 | tf_op jit(solution)/shard_map/ppermute | solution.py:446
  34.5 8.7 %collective-permute-start.11 = (bf16[2,256,128]{2,1,0:T(8,128)(2,1)S(1)}, bf16[2,256,128]{2,1,0:T(8,128)(2,1)S(1)}, u32[]{:S(2)}, u32[]{:S(2)}) collective-permute-start(bf16[2,256,128]{2,1,0:T(8,128)(2,1)S(1)} %get-tuple-element.55), channel_id=1, source_target_pairs={{0,6},{2,4},{4,2},{6,0},{8,14},{10,12},{12,10},{14,8},{16,22},{18,... | collective-permute-start | bytes 393224 | tf_op jit(solution)/shard_map/ppermute | solution.py:443
  37.0 6.7 %collective-permute-start.12 = (bf16[2,256,128]{2,1,0:T(8,128)(2,1)S(1)}, bf16[2,256,128]{2,1,0:T(8,128)(2,1)S(1)}, u32[]{:S(2)}, u32[]{:S(2)}) collective-permute-start(bf16[2,256,128]{2,1,0:T(8,128)(2,1)S(1)} %get-tuple-element.56), channel_id=1, source_target_pairs={{0,4},{2,6},{4,0},{6,2},{8,12},{10,14},{12,8},{14,10},{16,20},{18,... | collective-permute-start | bytes 393224 | tf_op jit(solution)/shard_map/ppermute | solution.py:443
  37.5 6.2 %collective-permute-start.13 = (bf16[2,256,128]{2,1,0:T(8,128)(2,1)S(1)}, bf16[2,256,128]{2,1,0:T(8,128)(2,1)S(1)}, u32[]{:S(2)}, u32[]{:S(2)}) collective-permute-start(bf16[2,256,128]{2,1,0:T(8,128)(2,1)S(1)} %get-tuple-element.57), channel_id=1, source_target_pairs={{0,2},{2,0},{4,6},{6,4},{8,10},{10,8},{12,14},{14,12},{16,18},{18,... | collective-permute-start | bytes 393224 | tf_op jit(solution)/shard_map/ppermute | solution.py:443
  38.6 11.7 %collective-permute-start.8 = (bf16[2,224,128]{2,1,0:T(8,128)(2,1)S(1)}, bf16[2,224,128]{2,1,0:T(8,128)(2,1)S(1)}, u32[]{:S(2)}, u32[]{:S(2)}) collective-permute-start(bf16[2,224,128]{2,1,0:T(8,128)(2,1)S(1)} %get-tuple-element.52), channel_id=1, source_target_pairs={{0,16},{2,18},{4,20},{6,22},{8,24},{10,26},{12,28},{14,30},{16,0},... | collective-permute-start | bytes 344072 | tf_op jit(solution)/shard_map/ppermute | solution.py:446
  41.6 8.6 %collective-permute-start.9 = (bf16[2,224,128]{2,1,0:T(8,128)(2,1)S(1)}, bf16[2,224,128]{2,1,0:T(8,128)(2,1)S(1)}, u32[]{:S(2)}, u32[]{:S(2)}) collective-permute-start(bf16[2,224,128]{2,1,0:T(8,128)(2,1)S(1)} %get-tuple-element.53), channel_id=1, source_target_pairs={{0,24},{2,26},{4,28},{6,30},{8,16},{10,18},{12,20},{14,22},{16,8},... | collective-permute-start | bytes 344072 | tf_op jit(solution)/shard_map/ppermute | solution.py:446
  43.2 7.2 %collective-permute-start.10 = (bf16[2,224,128]{2,1,0:T(8,128)(2,1)S(1)}, bf16[2,224,128]{2,1,0:T(8,128)(2,1)S(1)}, u32[]{:S(2)}, u32[]{:S(2)}) collective-permute-start(bf16[2,224,128]{2,1,0:T(8,128)(2,1)S(1)} %get-tuple-element.54), channel_id=1, source_target_pairs={{0,8},{2,10},{4,12},{6,14},{8,0},{10,2},{12,4},{14,6},{16,24},{18,... | collective-permute-start | bytes 344072 | tf_op jit(solution)/shard_map/ppermute | solution.py:446
  50.5 1.4 %collective-permute-start.14 = (bf16[2,256,128]{2,1,0:T(8,128)(2,1)S(1)}, bf16[2,256,128]{2,1,0:T(8,128)(2,1)S(1)}, u32[]{:S(2)}, u32[]{:S(2)}) collective-permute-start(bf16[2,256,128]{2,1,0:T(8,128)(2,1)S(1)} %finish.1.refs_0_), channel_id=1, source_target_pairs={{1,0},{0,1},{3,2},{2,3},{5,4},{4,5},{7,6},{6,7},{9,8},{8,9},{11,10... | collective-permute-start | bytes 393224 | tf_op jit(solution)/shard_map/ppermute | solution.py:449
  53.2 7.8 %collective-permute-start.20 = (bf16[264,128]{1,0:T(8,128)(2,1)S(1)}, bf16[264,128]{1,0:T(8,128)(2,1)S(1)}, u32[]{:S(2)}, u32[]{:S(2)}) collective-permute-start(bf16[264,128]{1,0:T(8,128)(2,1)S(1)} %series.1.refs_0_), channel_id=1, source_target_pairs={{0,16},{2,18},{4,20},{6,22},{8,24},{10,26},{12,28},{14,30},{16,0},... | collective-permute-start | bytes 202760 | tf_op jit(solution)/shard_map/ppermute | solution.py:446
  56.9 6.5 %collective-permute-start.19 = (bf16[264,128]{1,0:T(8,128)(2,1)S(1)}, bf16[264,128]{1,0:T(8,128)(2,1)S(1)}, u32[]{:S(2)}, u32[]{:S(2)}) collective-permute-start(bf16[264,128]{1,0:T(8,128)(2,1)S(1)} %series.1.refs_0_), channel_id=1, source_target_pairs={{0,24},{2,26},{4,28},{6,30},{8,16},{10,18},{12,20},{14,22},{16,8},... | collective-permute-start | bytes 202760 | tf_op jit(solution)/shard_map/ppermute | solution.py:446
  57.4 6.2 %collective-permute-start.18 = (bf16[264,128]{1,0:T(8,128)(2,1)S(1)}, bf16[264,128]{1,0:T(8,128)(2,1)S(1)}, u32[]{:S(2)}, u32[]{:S(2)}) collective-permute-start(bf16[264,128]{1,0:T(8,128)(2,1)S(1)} %series.1.refs_0_), channel_id=1, source_target_pairs={{0,8},{2,10},{4,12},{6,14},{8,0},{10,2},{12,4},{14,6},{16,24},{18,... | collective-permute-start | bytes 202760 | tf_op jit(solution)/shard_map/ppermute | solution.py:446
  57.5 6.1 %collective-permute-start.17 = (bf16[264,128]{1,0:T(8,128)(2,1)S(1)}, bf16[264,128]{1,0:T(8,128)(2,1)S(1)}, u32[]{:S(2)}, u32[]{:S(2)}) collective-permute-start(bf16[264,128]{1,0:T(8,128)(2,1)S(1)} %series.1.refs_0_), channel_id=1, source_target_pairs={{0,6},{2,4},{4,2},{6,0},{8,14},{10,12},{12,10},{14,8},{16,22},{18,... | collective-permute-start | bytes 202760 | tf_op jit(solution)/shard_map/ppermute | solution.py:443
  58.8 4.8 %collective-permute-start.16 = (bf16[264,128]{1,0:T(8,128)(2,1)S(1)}, bf16[264,128]{1,0:T(8,128)(2,1)S(1)}, u32[]{:S(2)}, u32[]{:S(2)}) collective-permute-start(bf16[264,128]{1,0:T(8,128)(2,1)S(1)} %series.1.refs_0_), channel_id=1, source_target_pairs={{0,4},{2,6},{4,0},{6,2},{8,12},{10,14},{12,8},{14,10},{16,20},{18,... | collective-permute-start | bytes 202760 | tf_op jit(solution)/shard_map/ppermute | solution.py:443
  63.6 12.8 %collective-permute-start.23 = (bf16[3,264,128]{2,1,0:T(8,128)(2,1)S(1)}, bf16[3,264,128]{2,1,0:T(8,128)(2,1)S(1)}, u32[]{:S(2)}, u32[]{:S(2)}) collective-permute-start(bf16[3,264,128]{2,1,0:T(8,128)(2,1)S(1)} %get-tuple-element.63.refs_4_), channel_id=1, source_target_pairs={{0,6},{2,4},{4,2},{6,0},{8,14},{10,12},{12,10},{14,8},{16,22},{18,... | collective-permute-start | bytes 608264 | tf_op jit(solution)/shard_map/ppermute | solution.py:443
  65.0 11.4 %collective-permute-start.22 = (bf16[3,264,128]{2,1,0:T(8,128)(2,1)S(1)}, bf16[3,264,128]{2,1,0:T(8,128)(2,1)S(1)}, u32[]{:S(2)}, u32[]{:S(2)}) collective-permute-start(bf16[3,264,128]{2,1,0:T(8,128)(2,1)S(1)} %get-tuple-element.63.refs_4_), channel_id=1, source_target_pairs={{0,4},{2,6},{4,0},{6,2},{8,12},{10,14},{12,8},{14,10},{16,20},{18,... | collective-permute-start | bytes 608264 | tf_op jit(solution)/shard_map/ppermute | solution.py:443
  66.7 9.7 %collective-permute-start.21 = (bf16[3,264,128]{2,1,0:T(8,128)(2,1)S(1)}, bf16[3,264,128]{2,1,0:T(8,128)(2,1)S(1)}, u32[]{:S(2)}, u32[]{:S(2)}) collective-permute-start(bf16[3,264,128]{2,1,0:T(8,128)(2,1)S(1)} %get-tuple-element.63.refs_4_), channel_id=1, source_target_pairs={{0,2},{2,0},{4,6},{6,4},{8,10},{10,8},{12,14},{14,12},{16,18},{18,... | collective-permute-start | bytes 608264 | tf_op jit(solution)/shard_map/ppermute | solution.py:443
  67.2 9.2 %collective-permute-start.15 = (bf16[264,128]{1,0:T(8,128)(2,1)S(1)}, bf16[264,128]{1,0:T(8,128)(2,1)S(1)}, u32[]{:S(2)}, u32[]{:S(2)}) collective-permute-start(bf16[264,128]{1,0:T(8,128)(2,1)S(1)} %series.1.refs_0_), channel_id=1, source_target_pairs={{0,2},{2,0},{4,6},{6,4},{8,10},{10,8},{12,14},{14,12},{16,18},{18,... | collective-permute-start | bytes 202760 | tf_op jit(solution)/shard_map/ppermute | solution.py:443

commit v12 on v10

--- a/solution.py
+++ b/solution.py
@@ -12,6 +12,7 @@
 ROWBLK = 4
 LANES = 2 * BLOCK
 CHUNK = 16
+EXTRA = 8
 MIB = 1024 * 1024
 
 
@@ -86,7 +87,7 @@
     bias_ref[...] = jnp.zeros_like(bias_ref)
     first = lax.broadcasted_iota(jnp.int32, (CHUNK * CHUNK, LANES), 1) < BLOCK
 
-    def step(t, carry):
+    def step(t, side):
         for copy in copies(t):
             copy.wait()
         local = lax.div(t, steps)
@@ -108,18 +109,20 @@
             for k, piece in enumerate(pieces):
                 piece = piece.astype(jnp.bfloat16)
                 for i in range(CHUNK):
-                    gs[k * walk + w:k * walk + w + CHUNK, i * LANES:(i + 1) * LANES] = piece[i * CHUNK:(i + 1) * CHUNK]
+                    gs[side, k * walk + w:k * walk + w + CHUNK, i * LANES:(i + 1) * LANES] = (
+                        piece[i * CHUNK:(i + 1) * CHUNK]
+                    )
         for g in range(0, vectors, 2 * CHUNK):
-            both = [vals[t, g + side * CHUNK:g + (side + 1) * CHUNK].reshape(CHUNK * CHUNK, LANES) for side in range(2)]
+            both = [vals[t, g + k * CHUNK:g + (k + 1) * CHUNK].reshape(CHUNK * CHUNK, LANES) for k in range(2)]
             both = jnp.dot(swap[...], jnp.concatenate(both, axis=1), preferred_element_type=jnp.float32)
             both = both.astype(jnp.bfloat16)
             for i in range(CHUNK):
-                for side in range(2):
-                    turned_ref[t, g + side * CHUNK:g + (side + 1) * CHUNK, i * LANES:(i + 1) * LANES] = (
-                        both[i * CHUNK:(i + 1) * CHUNK, side * LANES:(side + 1) * LANES]
+                for k in range(2):
+                    turned_ref[t, g + k * CHUNK:g + (k + 1) * CHUNK, i * LANES:(i + 1) * LANES] = (
+                        both[i * CHUNK:(i + 1) * CHUNK, k * LANES:(k + 1) * LANES]
                     )
         part = lax.dot_general(
-            turned_ref[t], gs[...], (((1,), (1,)), ((), ())), preferred_element_type=jnp.float32
+            turned_ref[t], gs[side], (((1,), (1,)), ((), ())), preferred_element_type=jnp.float32
         )
         begins = lax.rem(t, steps) == 0
         acc[...] = jnp.where(begins, 0.0, acc[...]) + part
@@ -133,11 +136,14 @@
                 total = total + jnp.where(mask, flat[(k + 1) * walk:(k + 2) * walk], 0.0)
             bias_ref[...] += total
 
+    def pair(t, carry):
+        step(2 * t, 0)
+        step(2 * t + 1, 1)
         return carry
 
     acc[...] = jnp.zeros_like(acc)
     take_cols.wait()
-    lax.fori_loop(0, total_steps, step, 0)
+    lax.fori_loop(0, total_steps // 2, pair, 0)
     take.wait()
 
 
@@ -162,7 +168,7 @@
             pltpu.VMEM((steps, vectors, CHUNK, LANES), jnp.bfloat16),
             pltpu.VMEM((steps, walk, CHUNK, norb), jnp.bfloat16),
             pltpu.VMEM((CHUNK * CHUNK, CHUNK * CHUNK), jnp.bfloat16),
-            pltpu.VMEM((4 * walk, wide), jnp.bfloat16),
+            pltpu.VMEM((2, 4 * walk, wide), jnp.bfloat16),
             pltpu.VMEM((vectors, 4 * walk), jnp.float32),
             pltpu.SemaphoreType.DMA((steps,)),
             pltpu.SemaphoreType.DMA((steps,)),
@@ -175,7 +181,7 @@
     )(*in_hbm(vals, greens, walkers, cols))
 
 
-def potential_kernel(start, steps, layout, by_plane, fields_ref, own_ref, *refs):
+def potential_kernel(begin, end, layout, by_plane, fields_ref, own_ref, *refs):
     nz, plane, own = layout
     others = refs[:lax.axis_size("orb") - 1]
     cols_ref, turned_ref = refs[len(others):len(others) + 2]
@@ -209,18 +215,17 @@
     swap[...] = swap_matrix()
     first = lax.broadcasted_iota(jnp.int32, (walk, LANES), 1) < BLOCK
 
-    def step(t, carry):
-        left = s_ref[lax.div(start + t, BLOCK // CHUNK)]
+    def step(t, halves=(0, 1)):
+        left = s_ref[lax.div(t, BLOCK // CHUNK)]
         tiles = []
         for i in range(0, CHUNK, 2):
-            both = jnp.dot(
-                left, turned_ref[start + t, :, i * LANES:(i + 2) * LANES], preferred_element_type=jnp.float32
-            )
+            both = jnp.dot(left, turned_ref[t, :, i * LANES:(i + 2) * LANES], preferred_element_type=jnp.float32)
             for side in range(2):
                 out = both[:, side * LANES:(side + 1) * LANES]
                 near = jnp.where(first, out[0:walk], out[walk:2 * walk])
                 far = jnp.where(first, pltpu.roll(out[2 * walk:3 * walk], BLOCK, 1), out[3 * walk:])
-                tiles.append(jnp.concatenate([near, far], axis=1).astype(jnp.bfloat16))
+                wanted = [(near, far)[half] for half in halves]
+                tiles.append(jnp.concatenate(wanted, axis=1).astype(jnp.bfloat16))
         for w0 in range(0, walk, CHUNK):
             mixed = jnp.concatenate([tile[w0:w0 + CHUNK] for tile in tiles], axis=0)
             mixed = jnp.dot(swap[...], mixed, preferred_element_type=jnp.float32).astype(jnp.bfloat16)
@@ -233,25 +238,35 @@
                     out, inner = outs[dp], (dz - 1,)
                 else:
                     out, inner = outs[plane + dp], ()
-                for half in range(2):
-                    rows = pl.ds(pl.multiple_of((2 * t + half) * CHUNK, CHUNK), CHUNK)
-                    out[(*inner, j, rows)] = mixed[w * CHUNK:(w + 1) * CHUNK, half * LANES:(half + 1) * LANES]
+                for k, half in enumerate(halves):
+                    at = (2 * t + half - begin) * CHUNK
+                    rows = pl.ds(at if isinstance(t, int) else pl.multiple_of(at, CHUNK), CHUNK)
+                    out[(*inner, j, rows)] = mixed[w * CHUNK:(w + 1) * CHUNK, k * LANES:(k + 1) * LANES]
+
+    def pair(t, carry):
+        step(from_step + 2 * t)
+        step(from_step + 2 * t + 1)
         return carry
 
-    lax.fori_loop(0, steps // 2, lambda t, carry: step(2 * t + 1, step(2 * t, carry)), 0)
-    if steps % 2:
-        step(steps - 1, 0)
-
-
-def potential_call(start, steps, layout, by_plane, fields, bias, others, cols, turned):
+    from_step, to_step = (begin + 1) // 2, end // 2
+    if begin % 2:
+        step(begin // 2, (1,))
+    lax.fori_loop(0, (to_step - from_step) // 2, pair, 0)
+    if (to_step - from_step) % 2:
+        step(to_step - 1)
+    if end % 2:
+        step(end // 2, (0,))
+
+
+def potential_call(begin, end, layout, by_plane, fields, bias, others, cols, turned):
     nz, plane, own = layout
     walk, vectors = fields.shape
     leading = [(nz - 1,)] * plane + [()] * plane if by_plane else [(plane,)] * nz
-    rows = 2 * CHUNK
+    rows = (end - begin) * CHUNK
     *parts, energy = pl.pallas_call(
-        functools.partial(potential_kernel, start, steps, layout, by_plane),
+        functools.partial(potential_kernel, begin, end, layout, by_plane),
         out_shape=[
-            *[pltpu.VMEM((*inner, own, steps * rows, LANES), jnp.bfloat16) for inner in leading],
+            *[pltpu.VMEM((*inner, own, rows, LANES), jnp.bfloat16) for inner in leading],
             pltpu.VMEM((CHUNK, LANES), jnp.float32),
         ],
         scratch_shapes=[
@@ -357,8 +372,8 @@
             moved = begin[r].astype(jnp.float32) + sums[r]
             total[r // rowblocks, j, (r % rowblocks) * BLOCK:(r % rowblocks + 1) * BLOCK] = moved.astype(jnp.bfloat16)
     mine = total[pl.ds(me, 1)][0]
-    at = lax.broadcasted_iota(jnp.int32, (CHUNK, LANES), 0)
-    high, middle, low = (part.astype(jnp.float32) for part in split(energy_ref[...]))
+    at = lax.broadcasted_iota(jnp.int32, (EXTRA, LANES), 0)
+    high, middle, low = (part.astype(jnp.float32) for part in split(energy_ref[:EXTRA]))
     tile = jnp.where(at == 0, high, jnp.where(at == 1, middle, jnp.where(at == 2, low, 0.0)))
     moved_ref[:own * half_rows] = mine.reshape(own * half_rows, mine.shape[2])
     moved_ref[own * half_rows:] = tile.astype(jnp.bfloat16)
@@ -369,7 +384,7 @@
     own, half_rows, nocc = start[0].shape
     return pl.pallas_call(
         functools.partial(series_kernel, n_orb),
-        out_shape=pltpu.VMEM((own * half_rows + CHUNK, nocc), jnp.bfloat16),
+        out_shape=pltpu.VMEM((own * half_rows + EXTRA, nocc), jnp.bfloat16),
         scratch_shapes=[
             pltpu.VMEM((ROWBLK, own, BLOCK, 2 * LANES), jnp.bfloat16),
             pltpu.VMEM((n_orb, own, half_rows, nocc), jnp.bfloat16),
@@ -387,7 +402,7 @@
     out, energy_ref = refs[2 * plane:]
     me = lax.axis_index("chol")
     rows = out.shape[1]
-    energy = jnp.zeros((CHUNK, LANES), jnp.float32)
+    energy = jnp.zeros((EXTRA, LANES), jnp.float32)
     for dp in range(plane):
         for dz in range(nz):
             z = hop(lax.div(me, plane), -dz if nz & (nz - 1) else dz, nz)
@@ -402,7 +417,7 @@
 def place_call(layout, near, far):
     nz, plane, own = layout
     walk = nz * plane * own
-    rows = (near[0].shape[0] - CHUNK) // own
+    rows = (near[0].shape[0] - EXTRA) // own
     return pl.pallas_call(
         functools.partial(place_kernel, layout),
         out_shape=[
@@ -441,9 +456,8 @@
     bias, *others = around_orb(partial_bias)
     start, others = lax.optimization_barrier((start, others))
 
-    total_steps = rowblocks * BLOCK // CHUNK
-    early_steps = total_steps // 8
-    late_steps = total_steps - early_steps
+    units = 2 * rowblocks * BLOCK // CHUNK
+    early_units = units * 3 // 16
     fields_t = fields.T
     def all_plane(arrays):
         return [to_plane(arrays[dp - 1], dp) for dp in reversed(range(1, plane))]
@@ -453,9 +467,9 @@
     def all_z(arrays):
         return [to_z(arrays[dz - 1], dz) for dz in z_order]
 
-    late, energy = potential_call(early_steps, late_steps, layout, True, fields_t, bias, others, cols, turned)
+    late, energy = potential_call(early_units, units, layout, True, fields_t, bias, others, cols, turned)
     far, near = late[:plane], late[plane:]
-    early, _ = potential_call(0, early_steps, layout, False, fields_t, bias, others, cols, turned)
+    early, _ = potential_call(0, early_units, layout, False, fields_t, bias, others, cols, turned)
     early_came = all_z(early[1:])
     merged = merge_call([early[0], *early_came], near)
     far_came = all_z(sum_call([far[0], *all_plane(far[1:])], merged[:1]))
@@ -464,7 +478,7 @@
     piece = series_call(around_orb(found), start, energy)
     near = [piece, *(to_plane(piece, dp) for dp in range(1, plane))]
     came = all_z([piece] * (nz - 1))
-    pieces, *near[1:] = stack_call(near[1:], came[::-1], [dz - 1 for dz in z_order[::-1]])
+    pieces, *near[2:] = stack_call(near[2:], came[::-1], [dz - 1 for dz in z_order[::-1]])
     far = {dp: to_plane(pieces, dp) for dp in reversed(range(1, plane))}
     moved, energy = place_call(layout, near, [pieces, *(far[dp] for dp in range(1, plane))])
     return moved, energy.reshape(walk)

time: 74.5 us -> 74.8 us (level)
  waiting for transfers between devices: 23.3 us -> 31.6 us
  starting transfers between devices: 34.2 us -> 26 us
    ppermute x9, waiting for transfers between devices: 11.2 us -> 20.9 us  [to_z(): lax.ppermute(a, 'chol', [(c, hop(c // plane, dz, nz) * plane + c % plane)...]
    ppermute x9, starting transfers between devices: 16.6 us -> 11.1 us  [to_z(): lax.ppermute(a, 'chol', [(c, hop(c // plane, dz, nz) * plane + c % plane)...]
    ppermute x12, starting transfers between devices: 16.9 us -> 14.3 us  [to_plane(): lax.ppermute(a, 'chol', [(c, c // plane * plane + hop(c % plane, dp, plan...]
    ppermute x12, waiting for transfers between devices: 9.57 us -> 8.29 us  [to_plane(): lax.ppermute(a, 'chol', [(c, c // plane * plane + hop(c % plane, dp, plan...]
  transfers between devices with their start and end apart: 24 -> 24, of which waited for: 14 -> 10; matrix products, arithmetic and copies ran while one was open for 0% -> 0% of each run, Pallas kernels for 2% -> 2%
where the time goes in v12:
time: 74.8 us; the launch traced here: 74.7 us
  waiting for transfers between devices  31.6 us (42%)
  starting transfers between devices  26 us (35%)
  Pallas kernels  16.3 us (22%)
    ppermute x9, waiting for transfers between devices, to_z(): lax.ppermute(a, 'chol', [(c, hop(c // plane, dz, nz) * plane + c % plane)...  20.9 us
    ppermute x12, starting transfers between devices, to_plane(): lax.ppermute(a, 'chol', [(c, c // plane * plane + hop(c % plane, dp, plan...  14.3 us
    ppermute x9, starting transfers between devices, to_z(): lax.ppermute(a, 'chol', [(c, hop(c // plane, dz, nz) * plane + c % plane)...  11.1 us
    pallas_call x1, Pallas kernels, bias_call(): pl.pallas_call(bias_kernel, in_specs=[*[pl.BlockSpec(memory_space=pl.ANY)...  8.42 us
    ppermute x12, waiting for transfers between devices, to_plane(): lax.ppermute(a, 'chol', [(c, c // plane * plane + hop(c % plane, dp, plan...  8.29 us
    pallas_call x2, Pallas kernels, potential_call(): pl.pallas_call(functools.partial(potential_kernel, begin, end, layout, by...  5.24 us
    ppermute x3, waiting for transfers between devices, around_orb(): lax.ppermute(a, 'orb', [((c + d) % n_orb, c) for c in range(n_orb)])  2.47 us
  transfers between devices with their start and end apart: 24, of which 10 were waited for; matrix products, arithmetic and copies ran while one was open for 0% of the time, Pallas kernels for 2%

profile of v12, /device:TPU:0, one launch (start us, length us, event | category | flops | bytes accessed | tf_op | source)
XLA Modules:
  0.0 74.7 jit_solution(17877651482952522513)
XLA Ops:
  0.6 0.0 copy-start
  0.6 8.4 %force_bias.1 = (bf16[8,256,2048]{2,1,0:T(8,128)(2,1)S(1)}, f32[32,256]{1,0:T(8,128)S(1)}, bf16[2,128,128]{2,1,0:T(8,128)(2,1)S(1)}, s32[2,2,256]{2,1,0:T(2,128)S(1)}) custom-call(bf16[256,2,64,128]{3,2,1,0:T(8,128)(2,1)} %vals_hbm.1, bf16[32,128,256]{2,1,0:T(8,128)(2,1)} %greens_hbm.1, bf16[32,128,128]{2,1,0:T(8,128)(2,1)} %walkers_hbm.1, s32[2,2,256]{2,1,0:T(2,128)} %bitcast.5), custom_call_target="tpu_custom_call" | custom-call | tf_op jit(solution)/shard_map/force_bias/pallas_call | solution.py:155
  9.1 0.5 collective-permute-start
  9.6 0.1 collective-permute-start.1
  9.7 1.1 %collective-permute-done.1.refs_0_ = f32[32,256]{1,0:T(8,128)S(1)} collective-permute-done((f32[32,256]{1,0:T(8,128)S(1)}, f32[32,256]{1,0:T(8,128)S(1)}, u32[]{:S(2)}, u32[]{:S(2)}) %collective-permute-start.1) | collective-permute-done | bytes 32800 | tf_op jit(solution)/shard_map/ppermute | solution.py:451
  10.8 0.0 collective-permute-done.refs_3_
  10.8 0.0 copy-done
  10.8 3.7 %potential.2 = (bf16[3,2,208,128]{3,2,1,0:T(8,128)(2,1)S(1)}, bf16[3,2,208,128]{3,2,1,0:T(8,128)(2,1)S(1)}, bf16[3,2,208,128]{3,2,1,0:T(8,128)(2,1)S(1)}, bf16[3...) custom-call(f32[32,256]{1,0:T(8,128)S(1)} %bitcast.3, ...), custom_call_target="tpu_custom_call" | custom-call | tf_op jit(solution)/shard_map/potential/pallas_call | solution.py:266
  14.5 3.7 %collective-permute-start.2 = (bf16[3,2,208,128]{3,2,1,0:T(8,128)(2,1)S(1)}, bf16[3,2,208,128]{3,2,1,0:T(8,128)(2,1)S(1)}, u32[]{:S(2)}, u32[]{:S(2)}) collective-permute-start(bf16[3,2,208,128]{3,2,1,0:T(8,128)(2,1)S(1)} %get-tuple-element.40), channel_id=1, source_target_pairs={{0,6},{2,4},{4,2},{6,0},{8,14},{10,12},{12,10},{14,8},{16,22},{18,... | collective-permute-start | bytes 958472 | tf_op jit(solution)/shard_map/ppermute | solution.py:445
  18.2 1.5 %potential.3 = (bf16[4,2,48,128]{3,2,1,0:T(8,128)(2,1)S(1)}, bf16[4,2,48,128]{3,2,1,0:T(8,128)(2,1)S(1)}, bf16[4,2,48,128]{3,2,1,0:T(8,128)(2,1)S(1)}, bf16[4,2,48,128]{3,2,1,0:T(8,128)(2,1)S(1)}, f32[16,128]{1,0:T(8,128)}) custom-call(f32[32,256]{1,0:T(8,128)S(1)} %bitcast.4, f32[32,256]{1,0:T(8,128)S(1)} %get-tuple-element.34.own_ref, ...), custom_call_target="tpu_custom_call" | custom-call | tf_op jit(solution)/shard_map/potential/pallas_call | solution.py:266
  19.7 2.6 %collective-permute-start.5 = (bf16[4,2,48,128]{3,2,1,0:T(8,128)(2,1)S(1)}, bf16[4,2,48,128]{3,2,1,0:T(8,128)(2,1)S(1)}, u32[]{:S(2)}, u32[]{:S(2)}) collective-permute-start(bf16[4,2,48,128]{3,2,1,0:T(8,128)(2,1)S(1)} %get-tuple-element.44), channel_id=1, source_target_pairs={{0,16},{2,18},{4,20},{6,22},{8,24},{10,26},{12,28},{14,30},{16,0},... | collective-permute-start | bytes 294920 | tf_op jit(solution)/shard_map/ppermute | solution.py:448
  22.3 0.5 collective-permute-start.3
  22.8 0.5 collective-permute-start.4
  23.4 1.3 %collective-permute-start.6 = (bf16[4,2,48,128]{3,2,1,0:T(8,128)(2,1)S(1)}, bf16[4,2,48,128]{3,2,1,0:T(8,128)(2,1)S(1)}, u32[]{:S(2)}, u32[]{:S(2)}) collective-permute-start(bf16[4,2,48,128]{3,2,1,0:T(8,128)(2,1)S(1)} %get-tuple-element.45), channel_id=1, source_target_pairs={{0,24},{2,26},{4,28},{6,30},{8,16},{10,18},{12,20},{14,22},{16,8},... | collective-permute-start | bytes 294920 | tf_op jit(solution)/shard_map/ppermute | solution.py:448
  24.7 5.8 %collective-permute-done.5.refs_1_ = bf16[4,2,48,128]{3,2,1,0:T(8,128)(2,1)S(1)} collective-permute-done((bf16[4,2,48,128]{3,2,1,0:T(8,128)(2,1)S(1)}, bf16[4,2,48,128]{3,2,1,0:T(8,128)(2,1)S(1)}, u32[]{:S(2)}, u32[]{:S(2)}) %collective-permute-start.5) | collective-permute-done | bytes 98336 | tf_op jit(solution)/shard_map/ppermute | solution.py:448
  30.5 0.0 collective-permute-start.7
  30.5 0.0 collective-permute-done.6.refs_2_
  30.5 4.6 %collective-permute-done.7.refs_3_ = bf16[4,2,48,128]{3,2,1,0:T(8,128)(2,1)S(1)} collective-permute-done((bf16[4,2,48,128]{3,2,1,0:T(8,128)(2,1)S(1)}, bf16[4,2,48,128]{3,2,1,0:T(8,128)(2,1)S(1)}, u32[]{:S(2)}, u32[]{:S(2)}) %collective-permute-start.7) | collective-permute-done | bytes 98336 | tf_op jit(solution)/shard_map/ppermute | solution.py:448
  35.1 0.1 merge_parts.1
  35.2 0.1 collective-permute-start.11
  35.2 0.2 collective-permute-start.12
  35.4 0.0 collective-permute-done.2.refs_1_
  35.4 3.3 %collective-permute-start.13 = (bf16[2,256,128]{2,1,0:T(8,128)(2,1)S(1)}, bf16[2,256,128]{2,1,0:T(8,128)(2,1)S(1)}, u32[]{:S(2)}, u32[]{:S(2)}) collective-permute-start(bf16[2,256,128]{2,1,0:T(8,128)(2,1)S(1)} %get-tuple-element.57), channel_id=1, source_target_pairs={{0,2},{2,0},{4,6},{6,4},{8,10},{10,8},{12,14},{14,12},{16,18},{18,... | collective-permute-start | bytes 393224 | tf_op jit(solution)/shard_map/ppermute | solution.py:445
  38.7 0.0 collective-permute-done.3.refs_2_
  38.7 0.0 collective-permute-done.4.refs_3_
  38.7 0.2 sum_parts.1
  38.9 1.6 %collective-permute-start.8 = (bf16[2,208,128]{2,1,0:T(8,128)(2,1)S(1)}, bf16[2,208,128]{2,1,0:T(8,128)(2,1)S(1)}, u32[]{:S(2)}, u32[]{:S(2)}) collective-permute-start(bf16[2,208,128]{2,1,0:T(8,128)(2,1)S(1)} %get-tuple-element.52), channel_id=1, source_target_pairs={{0,16},{2,18},{4,20},{6,22},{8,24},{10,26},{12,28},{14,30},{16,0},... | collective-permute-start | bytes 319496 | tf_op jit(solution)/shard_map/ppermute | solution.py:448
  40.5 1.3 %collective-permute-start.9 = (bf16[2,208,128]{2,1,0:T(8,128)(2,1)S(1)}, bf16[2,208,128]{2,1,0:T(8,128)(2,1)S(1)}, u32[]{:S(2)}, u32[]{:S(2)}) collective-permute-start(bf16[2,208,128]{2,1,0:T(8,128)(2,1)S(1)} %get-tuple-element.53), channel_id=1, source_target_pairs={{0,24},{2,26},{4,28},{6,30},{8,16},{10,18},{12,20},{14,22},{16,8},... | collective-permute-start | bytes 319496 | tf_op jit(solution)/shard_map/ppermute | solution.py:448
  41.8 0.0 collective-permute-done.11.refs_4_
  41.8 0.7 collective-permute-start.10
  42.4 0.0 collective-permute-done.12.refs_5_
  42.5 0.0 collective-permute-done.13.refs_6_
  42.5 5.6 %collective-permute-done.8.refs_0_ = bf16[2,208,128]{2,1,0:T(8,128)(2,1)S(1)} collective-permute-done((bf16[2,208,128]{2,1,0:T(8,128)(2,1)S(1)}, bf16[2,208,128]{2,1,0:T(8,128)(2,1)S(1)}, u32[]{:S(2)}, u32[]{:S(2)}) %collective-permute-start.8) | collective-permute-done | bytes 106528 | tf_op jit(solution)/shard_map/ppermute | solution.py:448
  48.0 0.0 collective-permute-done.9.refs_1_
  48.0 0.8 %collective-permute-done.10.refs_2_ = bf16[2,208,128]{2,1,0:T(8,128)(2,1)S(1)} collective-permute-done((bf16[2,208,128]{2,1,0:T(8,128)(2,1)S(1)}, bf16[2,208,128]{2,1,0:T(8,128)(2,1)S(1)}, u32[]{:S(2)}, u32[]{:S(2)}) %collective-permute-start.10) | collective-permute-done | bytes 106528 | tf_op jit(solution)/shard_map/ppermute | solution.py:448
  48.9 0.1 finish.1.refs_0_
  49.0 0.1 collective-permute-start.14
  49.1 1.3 %collective-permute-done.14.refs_1_ = bf16[2,256,128]{2,1,0:T(8,128)(2,1)S(1)} collective-permute-done((bf16[2,256,128]{2,1,0:T(8,128)(2,1)S(1)}, bf16[2,256,128]{2,1,0:T(8,128)(2,1)S(1)}, u32[]{:S(2)}, u32[]{:S(2)}) %collective-permute-start.14) | collective-permute-done | bytes 131104 | tf_op jit(solution)/shard_map/ppermute | solution.py:451
  50.4 1.3 %series.1.refs_0_ = bf16[264,128]{1,0:T(8,128)(2,1)S(1)} custom-call(bf16[2,256,128]{2,1,0:T(8,128)(2,1)S(1)} %finish.1.refs_0_, bf16[2,256,128]{2,1,0:T(8,128)(2,1)S(1)} %collective-permute-done.14.refs_1_, bf16[2,128,128]{2,1,0:T(8,128)(2,1)S(1)} %get-tuple-element.58.refs_2_, bf16[2,128,128]{2,1,0:T(8,128)(2,1)S(1)} %collective-permute-done.refs_3_, ...), custom_call_target="tpu_custom_call" | custom-call | tf_op jit(solution)/shard_map/series/pallas_call | solution.py:385
  51.7 2.9 %collective-permute-start.20 = (bf16[264,128]{1,0:T(8,128)(2,1)S(1)}, bf16[264,128]{1,0:T(8,128)(2,1)S(1)}, u32[]{:S(2)}, u32[]{:S(2)}) collective-permute-start(bf16[264,128]{1,0:T(8,128)(2,1)S(1)} %series.1.refs_0_), channel_id=1, source_target_pairs={{0,16},{2,18},{4,20},{6,22},{8,24},{10,26},{12,28},{14,30},{16,0},... | collective-permute-start | bytes 202760 | tf_op jit(solution)/shard_map/ppermute | solution.py:448
  54.5 0.4 collective-permute-start.19
  55.0 0.2 collective-permute-start.18
  55.2 0.3 collective-permute-start.17
  55.5 1.6 %collective-permute-start.16 = (bf16[264,128]{1,0:T(8,128)(2,1)S(1)}, bf16[264,128]{1,0:T(8,128)(2,1)S(1)}, u32[]{:S(2)}, u32[]{:S(2)}) collective-permute-start(bf16[264,128]{1,0:T(8,128)(2,1)S(1)} %series.1.refs_0_), channel_id=1, source_target_pairs={{0,4},{2,6},{4,0},{6,2},{8,12},{10,14},{12,8},{14,10},{16,20},{18,... | collective-permute-start | bytes 202760 | tf_op jit(solution)/shard_map/ppermute | solution.py:445
  57.2 1.5 %collective-permute-done.20.refs_4_ = bf16[264,128]{1,0:T(8,128)(2,1)S(1)} collective-permute-done((bf16[264,128]{1,0:T(8,128)(2,1)S(1)}, bf16[264,128]{1,0:T(8,128)(2,1)S(1)}, u32[]{:S(2)}, u32[]{:S(2)}) %collective-permute-start.20) | collective-permute-done | bytes 67616 | tf_op jit(solution)/shard_map/ppermute | solution.py:448
  58.7 2.3 %collective-permute-done.19.refs_3_ = bf16[264,128]{1,0:T(8,128)(2,1)S(1)} collective-permute-done((bf16[264,128]{1,0:T(8,128)(2,1)S(1)}, bf16[264,128]{1,0:T(8,128)(2,1)S(1)}, u32[]{:S(2)}, u32[]{:S(2)}) %collective-permute-start.19) | collective-permute-done | bytes 67616 | tf_op jit(solution)/shard_map/ppermute | solution.py:448
  61.0 0.2 collective-permute-done.18.refs_2_
  61.3 0.0 collective-permute-done.17.refs_1_
  61.3 0.0 collective-permute-done.16.refs_0_
  61.3 1.2 %collective-permute-start.23 = (bf16[3,264,128]{2,1,0:T(8,128)(2,1)S(1)}, bf16[3,264,128]{2,1,0:T(8,128)(2,1)S(1)}, u32[]{:S(2)}, u32[]{:S(2)}) collective-permute-start(bf16[3,264,128]{2,1,0:T(8,128)(2,1)S(1)} %get-tuple-element.63.refs_4_), channel_id=1, source_target_pairs={{0,6},{2,4},{4,2},{6,0},{8,14},{10,12},{12,10},{14,8},{16,22},{18,... | collective-permute-start | bytes 608264 | tf_op jit(solution)/shard_map/ppermute | solution.py:445
  62.5 0.8 %collective-permute-start.22 = (bf16[3,264,128]{2,1,0:T(8,128)(2,1)S(1)}, bf16[3,264,128]{2,1,0:T(8,128)(2,1)S(1)}, u32[]{:S(2)}, u32[]{:S(2)}) collective-permute-start(bf16[3,264,128]{2,1,0:T(8,128)(2,1)S(1)} %get-tuple-element.63.refs_4_), channel_id=1, source_target_pairs={{0,4},{2,6},{4,0},{6,2},{8,12},{10,14},{12,8},{14,10},{16,20},{18,... | collective-permute-start | bytes 608264 | tf_op jit(solution)/shard_map/ppermute | solution.py:445
  63.3 1.5 %collective-permute-start.21 = (bf16[3,264,128]{2,1,0:T(8,128)(2,1)S(1)}, bf16[3,264,128]{2,1,0:T(8,128)(2,1)S(1)}, u32[]{:S(2)}, u32[]{:S(2)}) collective-permute-start(bf16[3,264,128]{2,1,0:T(8,128)(2,1)S(1)} %get-tuple-element.63.refs_4_), channel_id=1, source_target_pairs={{0,2},{2,0},{4,6},{6,4},{8,10},{10,8},{12,14},{14,12},{16,18},{18,... | collective-permute-start | bytes 608264 | tf_op jit(solution)/shard_map/ppermute | solution.py:445
  64.8 0.5 collective-permute-start.15
  65.4 8.3 %collective-permute-done.15.refs_1_ = bf16[264,128]{1,0:T(8,128)(2,1)S(1)} collective-permute-done((bf16[264,128]{1,0:T(8,128)(2,1)S(1)}, bf16[264,128]{1,0:T(8,128)(2,1)S(1)}, u32[]{:S(2)}, u32[]{:S(2)}) %collective-permute-start.15) | collective-permute-done | bytes 67616 | tf_op jit(solution)/shard_map/ppermute | solution.py:445
  73.6 0.0 collective-permute-done.23.refs_7_
  73.6 0.0 collective-permute-done.22.refs_6_
  73.6 0.0 collective-permute-done.21.refs_5_
  73.6 1.1 %place_walkers.1 = (bf16[32,128,128]{2,1,0:T(8,128)(2,1)}, f32[1,32]{1,0:T(1,128)}) custom-call(bf16[264,128]{1,0:T(8,128)(2,1)S(1)} %series.1.refs_0_, bf16[264,128]{1,0:T(8,128)(2,1)S(1)} %collective-permute-done.15.refs_1_, bf16[264,128]{1,0:T(8,128)(2,1)S(1)} %get-tuple-element.61.refs_2_, bf16[264,128]{1,0:T(8,128)(2,1)S(1)} %get-tuple-element.62.refs_3_, ...), custom_call_target="tpu_custom_call" | custom-call | tf_op jit(solution)/shard_map/place_walkers/pallas_call | solution.py:421
  (1 shorter events, 0.0 us)
Async XLA Ops:
  0.6 10.2 %copy-start = (f32[256,32]{0,1:T(8,128)S(1)}, f32[256,32]{0,1:T(8,128)}, u32[]{:S(2)}) copy-start(f32[256,32]{0,1:T(8,128)} %param.9) | copy-start | bytes 98308
  9.1 1.7 %collective-permute-start = (bf16[2,128,128]{2,1,0:T(8,128)(2,1)S(1)}, bf16[2,128,128]{2,1,0:T(8,128)(2,1)S(1)}, u32[]{:S(2)}, u32[]{:S(2)}) collective-permute-start(bf16[2,128,128]{2,1,0:T(8,128)(2,1)S(1)} %get-tuple-element.58.refs_2_), channel_id=1, source_target_pairs={{1,0},{0,1},{3,2},{2,3},{5,4},{4,5},{7,6},{6,7},{9,8},{8,9},{11,10... | collective-permute-start | bytes 196616 | tf_op jit(solution)/shard_map/ppermute | solution.py:451
  9.6 1.2 %collective-permute-start.1 = (f32[32,256]{1,0:T(8,128)S(1)}, f32[32,256]{1,0:T(8,128)S(1)}, u32[]{:S(2)}, u32[]{:S(2)}) collective-permute-start(f32[32,256]{1,0:T(8,128)S(1)} %get-tuple-element.34.own_ref), channel_id=1, source_target_pairs={{1,0},{0,1},{3,2},{2,3},{5,4},{4,5},{7,6},{6,7},{9,8},{8,9},{11,10... | collective-permute-start | bytes 98312 | tf_op jit(solution)/shard_map/ppermute | solution.py:451
  14.5 20.9 %collective-permute-start.2 = (bf16[3,2,208,128]{3,2,1,0:T(8,128)(2,1)S(1)}, bf16[3,2,208,128]{3,2,1,0:T(8,128)(2,1)S(1)}, u32[]{:S(2)}, u32[]{:S(2)}) collective-permute-start(bf16[3,2,208,128]{3,2,1,0:T(8,128)(2,1)S(1)} %get-tuple-element.40), channel_id=1, source_target_pairs={{0,6},{2,4},{4,2},{6,0},{8,14},{10,12},{12,10},{14,8},{16,22},{18,... | collective-permute-start | bytes 958472 | tf_op jit(solution)/shard_map/ppermute | solution.py:445
  19.7 10.8 %collective-permute-start.5 = (bf16[4,2,48,128]{3,2,1,0:T(8,128)(2,1)S(1)}, bf16[4,2,48,128]{3,2,1,0:T(8,128)(2,1)S(1)}, u32[]{:S(2)}, u32[]{:S(2)}) collective-permute-start(bf16[4,2,48,128]{3,2,1,0:T(8,128)(2,1)S(1)} %get-tuple-element.44), channel_id=1, source_target_pairs={{0,16},{2,18},{4,20},{6,22},{8,24},{10,26},{12,28},{14,30},{16,0},... | collective-permute-start | bytes 294920 | tf_op jit(solution)/shard_map/ppermute | solution.py:448
  22.3 16.4 %collective-permute-start.3 = (bf16[3,2,208,128]{3,2,1,0:T(8,128)(2,1)S(1)}, bf16[3,2,208,128]{3,2,1,0:T(8,128)(2,1)S(1)}, u32[]{:S(2)}, u32[]{:S(2)}) collective-permute-start(bf16[3,2,208,128]{3,2,1,0:T(8,128)(2,1)S(1)} %get-tuple-element.41), channel_id=1, source_target_pairs={{0,4},{2,6},{4,0},{6,2},{8,12},{10,14},{12,8},{14,10},{16,20},{18,... | collective-permute-start | bytes 958472 | tf_op jit(solution)/shard_map/ppermute | solution.py:445
  22.8 15.9 %collective-permute-start.4 = (bf16[3,2,208,128]{3,2,1,0:T(8,128)(2,1)S(1)}, bf16[3,2,208,128]{3,2,1,0:T(8,128)(2,1)S(1)}, u32[]{:S(2)}, u32[]{:S(2)}) collective-permute-start(bf16[3,2,208,128]{3,2,1,0:T(8,128)(2,1)S(1)} %get-tuple-element.42), channel_id=1, source_target_pairs={{0,2},{2,0},{4,6},{6,4},{8,10},{10,8},{12,14},{14,12},{16,18},{18,... | collective-permute-start | bytes 958472 | tf_op jit(solution)/shard_map/ppermute | solution.py:445
  23.4 7.1 %collective-permute-start.6 = (bf16[4,2,48,128]{3,2,1,0:T(8,128)(2,1)S(1)}, bf16[4,2,48,128]{3,2,1,0:T(8,128)(2,1)S(1)}, u32[]{:S(2)}, u32[]{:S(2)}) collective-permute-start(bf16[4,2,48,128]{3,2,1,0:T(8,128)(2,1)S(1)} %get-tuple-element.45), channel_id=1, source_target_pairs={{0,24},{2,26},{4,28},{6,30},{8,16},{10,18},{12,20},{14,22},{16,8},... | collective-permute-start | bytes 294920 | tf_op jit(solution)/shard_map/ppermute | solution.py:448
  30.5 4.6 %collective-permute-start.7 = (bf16[4,2,48,128]{3,2,1,0:T(8,128)(2,1)S(1)}, bf16[4,2,48,128]{3,2,1,0:T(8,128)(2,1)S(1)}, u32[]{:S(2)}, u32[]{:S(2)}) collective-permute-start(bf16[4,2,48,128]{3,2,1,0:T(8,128)(2,1)S(1)} %get-tuple-element.46), channel_id=1, source_target_pairs={{0,8},{2,10},{4,12},{6,14},{8,0},{10,2},{12,4},{14,6},{16,24},{18,... | collective-permute-start | bytes 294920 | tf_op jit(solution)/shard_map/ppermute | solution.py:448
  35.2 6.6 %collective-permute-start.11 = (bf16[2,256,128]{2,1,0:T(8,128)(2,1)S(1)}, bf16[2,256,128]{2,1,0:T(8,128)(2,1)S(1)}, u32[]{:S(2)}, u32[]{:S(2)}) collective-permute-start(bf16[2,256,128]{2,1,0:T(8,128)(2,1)S(1)} %get-tuple-element.55), channel_id=1, source_target_pairs={{0,6},{2,4},{4,2},{6,0},{8,14},{10,12},{12,10},{14,8},{16,22},{18,... | collective-permute-start | bytes 393224 | tf_op jit(solution)/shard_map/ppermute | solution.py:445
  35.2 7.2 %collective-permute-start.12 = (bf16[2,256,128]{2,1,0:T(8,128)(2,1)S(1)}, bf16[2,256,128]{2,1,0:T(8,128)(2,1)S(1)}, u32[]{:S(2)}, u32[]{:S(2)}) collective-permute-start(bf16[2,256,128]{2,1,0:T(8,128)(2,1)S(1)} %get-tuple-element.56), channel_id=1, source_target_pairs={{0,4},{2,6},{4,0},{6,2},{8,12},{10,14},{12,8},{14,10},{16,20},{18,... | collective-permute-start | bytes 393224 | tf_op jit(solution)/shard_map/ppermute | solution.py:445
  35.4 7.1 %collective-permute-start.13 = (bf16[2,256,128]{2,1,0:T(8,128)(2,1)S(1)}, bf16[2,256,128]{2,1,0:T(8,128)(2,1)S(1)}, u32[]{:S(2)}, u32[]{:S(2)}) collective-permute-start(bf16[2,256,128]{2,1,0:T(8,128)(2,1)S(1)} %get-tuple-element.57), channel_id=1, source_target_pairs={{0,2},{2,0},{4,6},{6,4},{8,10},{10,8},{12,14},{14,12},{16,18},{18,... | collective-permute-start | bytes 393224 | tf_op jit(solution)/shard_map/ppermute | solution.py:445
  38.9 9.1 %collective-permute-start.8 = (bf16[2,208,128]{2,1,0:T(8,128)(2,1)S(1)}, bf16[2,208,128]{2,1,0:T(8,128)(2,1)S(1)}, u32[]{:S(2)}, u32[]{:S(2)}) collective-permute-start(bf16[2,208,128]{2,1,0:T(8,128)(2,1)S(1)} %get-tuple-element.52), channel_id=1, source_target_pairs={{0,16},{2,18},{4,20},{6,22},{8,24},{10,26},{12,28},{14,30},{16,0},... | collective-permute-start | bytes 319496 | tf_op jit(solution)/shard_map/ppermute | solution.py:448
  40.5 7.5 %collective-permute-start.9 = (bf16[2,208,128]{2,1,0:T(8,128)(2,1)S(1)}, bf16[2,208,128]{2,1,0:T(8,128)(2,1)S(1)}, u32[]{:S(2)}, u32[]{:S(2)}) collective-permute-start(bf16[2,208,128]{2,1,0:T(8,128)(2,1)S(1)} %get-tuple-element.53), channel_id=1, source_target_pairs={{0,24},{2,26},{4,28},{6,30},{8,16},{10,18},{12,20},{14,22},{16,8},... | collective-permute-start | bytes 319496 | tf_op jit(solution)/shard_map/ppermute | solution.py:448
  41.8 7.1 %collective-permute-start.10 = (bf16[2,208,128]{2,1,0:T(8,128)(2,1)S(1)}, bf16[2,208,128]{2,1,0:T(8,128)(2,1)S(1)}, u32[]{:S(2)}, u32[]{:S(2)}) collective-permute-start(bf16[2,208,128]{2,1,0:T(8,128)(2,1)S(1)} %get-tuple-element.54), channel_id=1, source_target_pairs={{0,8},{2,10},{4,12},{6,14},{8,0},{10,2},{12,4},{14,6},{16,24},{18,... | collective-permute-start | bytes 319496 | tf_op jit(solution)/shard_map/ppermute | solution.py:448
  49.0 1.4 %collective-permute-start.14 = (bf16[2,256,128]{2,1,0:T(8,128)(2,1)S(1)}, bf16[2,256,128]{2,1,0:T(8,128)(2,1)S(1)}, u32[]{:S(2)}, u32[]{:S(2)}) collective-permute-start(bf16[2,256,128]{2,1,0:T(8,128)(2,1)S(1)} %finish.1.refs_0_), channel_id=1, source_target_pairs={{1,0},{0,1},{3,2},{2,3},{5,4},{4,5},{7,6},{6,7},{9,8},{8,9},{11,10... | collective-permute-start | bytes 393224 | tf_op jit(solution)/shard_map/ppermute | solution.py:451
  51.7 7.0 %collective-permute-start.20 = (bf16[264,128]{1,0:T(8,128)(2,1)S(1)}, bf16[264,128]{1,0:T(8,128)(2,1)S(1)}, u32[]{:S(2)}, u32[]{:S(2)}) collective-permute-start(bf16[264,128]{1,0:T(8,128)(2,1)S(1)} %series.1.refs_0_), channel_id=1, source_target_pairs={{0,16},{2,18},{4,20},{6,22},{8,24},{10,26},{12,28},{14,30},{16,0},... | collective-permute-start | bytes 202760 | tf_op jit(solution)/shard_map/ppermute | solution.py:448
  54.5 6.5 %collective-permute-start.19 = (bf16[264,128]{1,0:T(8,128)(2,1)S(1)}, bf16[264,128]{1,0:T(8,128)(2,1)S(1)}, u32[]{:S(2)}, u32[]{:S(2)}) collective-permute-start(bf16[264,128]{1,0:T(8,128)(2,1)S(1)} %series.1.refs_0_), channel_id=1, source_target_pairs={{0,24},{2,26},{4,28},{6,30},{8,16},{10,18},{12,20},{14,22},{16,8},... | collective-permute-start | bytes 202760 | tf_op jit(solution)/shard_map/ppermute | solution.py:448
  55.0 6.3 %collective-permute-start.18 = (bf16[264,128]{1,0:T(8,128)(2,1)S(1)}, bf16[264,128]{1,0:T(8,128)(2,1)S(1)}, u32[]{:S(2)}, u32[]{:S(2)}) collective-permute-start(bf16[264,128]{1,0:T(8,128)(2,1)S(1)} %series.1.refs_0_), channel_id=1, source_target_pairs={{0,8},{2,10},{4,12},{6,14},{8,0},{10,2},{12,4},{14,6},{16,24},{18,... | collective-permute-start | bytes 202760 | tf_op jit(solution)/shard_map/ppermute | solution.py:448
  55.2 6.0 %collective-permute-start.17 = (bf16[264,128]{1,0:T(8,128)(2,1)S(1)}, bf16[264,128]{1,0:T(8,128)(2,1)S(1)}, u32[]{:S(2)}, u32[]{:S(2)}) collective-permute-start(bf16[264,128]{1,0:T(8,128)(2,1)S(1)} %series.1.refs_0_), channel_id=1, source_target_pairs={{0,6},{2,4},{4,2},{6,0},{8,14},{10,12},{12,10},{14,8},{16,22},{18,... | collective-permute-start | bytes 202760 | tf_op jit(solution)/shard_map/ppermute | solution.py:445
  55.5 5.7 %collective-permute-start.16 = (bf16[264,128]{1,0:T(8,128)(2,1)S(1)}, bf16[264,128]{1,0:T(8,128)(2,1)S(1)}, u32[]{:S(2)}, u32[]{:S(2)}) collective-permute-start(bf16[264,128]{1,0:T(8,128)(2,1)S(1)} %series.1.refs_0_), channel_id=1, source_target_pairs={{0,4},{2,6},{4,0},{6,2},{8,12},{10,14},{12,8},{14,10},{16,20},{18,... | collective-permute-start | bytes 202760 | tf_op jit(solution)/shard_map/ppermute | solution.py:445
  61.3 12.3 %collective-permute-start.23 = (bf16[3,264,128]{2,1,0:T(8,128)(2,1)S(1)}, bf16[3,264,128]{2,1,0:T(8,128)(2,1)S(1)}, u32[]{:S(2)}, u32[]{:S(2)}) collective-permute-start(bf16[3,264,128]{2,1,0:T(8,128)(2,1)S(1)} %get-tuple-element.63.refs_4_), channel_id=1, source_target_pairs={{0,6},{2,4},{4,2},{6,0},{8,14},{10,12},{12,10},{14,8},{16,22},{18,... | collective-permute-start | bytes 608264 | tf_op jit(solution)/shard_map/ppermute | solution.py:445
  62.5 11.1 %collective-permute-start.22 = (bf16[3,264,128]{2,1,0:T(8,128)(2,1)S(1)}, bf16[3,264,128]{2,1,0:T(8,128)(2,1)S(1)}, u32[]{:S(2)}, u32[]{:S(2)}) collective-permute-start(bf16[3,264,128]{2,1,0:T(8,128)(2,1)S(1)} %get-tuple-element.63.refs_4_), channel_id=1, source_target_pairs={{0,4},{2,6},{4,0},{6,2},{8,12},{10,14},{12,8},{14,10},{16,20},{18,... | collective-permute-start | bytes 608264 | tf_op jit(solution)/shard_map/ppermute | solution.py:445
  63.3 10.3 %collective-permute-start.21 = (bf16[3,264,128]{2,1,0:T(8,128)(2,1)S(1)}, bf16[3,264,128]{2,1,0:T(8,128)(2,1)S(1)}, u32[]{:S(2)}, u32[]{:S(2)}) collective-permute-start(bf16[3,264,128]{2,1,0:T(8,128)(2,1)S(1)} %get-tuple-element.63.refs_4_), channel_id=1, source_target_pairs={{0,2},{2,0},{4,6},{6,4},{8,10},{10,8},{12,14},{14,12},{16,18},{18,... | collective-permute-start | bytes 608264 | tf_op jit(solution)/shard_map/ppermute | solution.py:445
  64.8 8.8 %collective-permute-start.15 = (bf16[264,128]{1,0:T(8,128)(2,1)S(1)}, bf16[264,128]{1,0:T(8,128)(2,1)S(1)}, u32[]{:S(2)}, u32[]{:S(2)}) collective-permute-start(bf16[264,128]{1,0:T(8,128)(2,1)S(1)} %series.1.refs_0_), channel_id=1, source_target_pairs={{0,2},{2,0},{4,6},{6,4},{8,10},{10,8},{12,14},{14,12},{16,18},{18,... | collective-permute-start | bytes 202760 | tf_op jit(solution)/shard_map/ppermute | solution.py:445

commit v13 on v12

--- a/solution.py
+++ b/solution.py
@@ -9,7 +9,6 @@
 
 BLOCK = 64
 TAYLOR = 4
-ROWBLK = 4
 LANES = 2 * BLOCK
 CHUNK = 16
 EXTRA = 8
@@ -316,14 +315,21 @@
 
 
 def finish_call(factor, far, merged):
-    rows = merged[0].shape[1] - far[0].shape[1]
+    early = merged[0].shape[1] - far[0].shape[1]
 
     def kernel(*refs):
         far_refs, merged_refs, out = refs[:len(far)], refs[len(far):-1], refs[-1]
-        total = add(merged_refs, slice(None), slice(0, rows))
-        out[:, :rows] = (factor * total).astype(out.dtype)
-        total = add(merged_refs, slice(None), slice(rows, None)) + add(far_refs, Ellipsis)
-        out[:, rows:] = (factor * total).astype(out.dtype)
+        rowblocks = out.shape[1] // (2 * BLOCK)
+        for unit in range(out.shape[1] // CHUNK):
+            at = unit * CHUNK
+            for j in range(out.shape[0]):
+                total = add(merged_refs, j, slice(at, at + CHUNK))
+                if at >= early:
+                    total = total + add(far_refs, j, slice(at - early, at - early + CHUNK))
+                if unit % 2 == 0:
+                    row = lax.axis_index("orb") * rowblocks + at // (2 * BLOCK)
+                    total = jnp.where(row % 2 == 1, pltpu.roll(total, BLOCK, 1), total)
+                out[j, at:at + CHUNK] = (factor * total).astype(out.dtype)
 
     return vmem_call(kernel, "finish", pltpu.VMEM(merged[0].shape, jnp.bfloat16), *far, *merged)
 
@@ -343,35 +349,31 @@
 
 def series_kernel(n_orb, *refs):
     found, start = refs[:n_orb], refs[n_orb:2 * n_orb]
-    energy_ref, moved_ref, pot, term, total = refs[2 * n_orb:]
+    energy_ref, moved_ref, pot, begin, total = refs[2 * n_orb:]
     me = lax.axis_index("orb")
     own, half_rows = start[0].shape[:2]
-    rowblocks = half_rows // BLOCK
     per = BLOCK // CHUNK
     for d in range(n_orb):
         at = lax.rem(me + d, n_orb)
-        term[pl.ds(at, 1)] = start[d][...][None]
-        for t in range(rowblocks * per):
+        begin[:, pl.ds(pl.multiple_of(at * half_rows, half_rows), half_rows)] = start[d][...]
+        for t in range(half_rows // CHUNK):
+            row = at * (half_rows // BLOCK) + t // per
+            rows = pl.ds(pl.multiple_of(row * BLOCK + t % per * CHUNK, CHUNK), CHUNK)
             for half in range(2):
-                rows = slice((2 * t + half) * CHUNK, (2 * t + half + 1) * CHUNK)
-                pot[pl.ds(at * rowblocks + t // per, 1), :, (t % per) * CHUNK:(t % per + 1) * CHUNK,
-                    half * LANES:(half + 1) * LANES] = found[d][:, rows, :][None]
+                side = lax.rem(lax.div(row, 2) + half, 2)
+                lanes = pl.ds(pl.multiple_of(side * LANES, LANES), LANES)
+                pot[:, rows, lanes] = found[d][:, (2 * t + half) * CHUNK:(2 * t + half + 1) * CHUNK]
+    terms = [begin[j] for j in range(own)]
+    sums = [term.astype(jnp.float32) for term in terms]
+    added = [jnp.zeros(terms[0].shape, jnp.float32)] * own
+    for degree in range(1, TAYLOR + 1):
+        for j in range(own):
+            product = jnp.dot(pot[j], terms[j], preferred_element_type=jnp.float32)
+            terms[j] = (product / degree).astype(jnp.bfloat16)
+            added[j] = added[j] + terms[j].astype(jnp.float32)
     for j in range(own):
-        blocks = [term[r // rowblocks, j, (r % rowblocks) * BLOCK:(r % rowblocks + 1) * BLOCK] for r in range(ROWBLK)]
-        sums = [jnp.zeros(blocks[0].shape, jnp.float32)] * ROWBLK
-        begin = blocks
-        for degree in range(1, TAYLOR + 1):
-            after = []
-            for r in range(ROWBLK):
-                right = jnp.concatenate([blocks[c] for c in column_order(r)], axis=0)
-                product = jnp.dot(pot[r, j], right, preferred_element_type=jnp.float32)
-                after.append((product / degree).astype(jnp.bfloat16))
-            blocks = after
-            sums = [s + b.astype(jnp.float32) for s, b in zip(sums, blocks)]
-        for r in range(ROWBLK):
-            moved = begin[r].astype(jnp.float32) + sums[r]
-            total[r // rowblocks, j, (r % rowblocks) * BLOCK:(r % rowblocks + 1) * BLOCK] = moved.astype(jnp.bfloat16)
-    mine = total[pl.ds(me, 1)][0]
+        total[j] = (sums[j] + added[j]).astype(jnp.bfloat16)
+    mine = total[:, pl.ds(pl.multiple_of(me * half_rows, half_rows), half_rows)]
     at = lax.broadcasted_iota(jnp.int32, (EXTRA, LANES), 0)
     high, middle, low = (part.astype(jnp.float32) for part in split(energy_ref[:EXTRA]))
     tile = jnp.where(at == 0, high, jnp.where(at == 1, middle, jnp.where(at == 2, low, 0.0)))
@@ -386,9 +388,9 @@
         functools.partial(series_kernel, n_orb),
         out_shape=pltpu.VMEM((own * half_rows + EXTRA, nocc), jnp.bfloat16),
         scratch_shapes=[
-            pltpu.VMEM((ROWBLK, own, BLOCK, 2 * LANES), jnp.bfloat16),
-            pltpu.VMEM((n_orb, own, half_rows, nocc), jnp.bfloat16),
-            pltpu.VMEM((n_orb, own, half_rows, nocc), jnp.bfloat16),
+            pltpu.VMEM((own, n_orb * half_rows, 2 * LANES), jnp.bfloat16),
+            pltpu.VMEM((own, n_orb * half_rows, nocc), jnp.bfloat16),
+            pltpu.VMEM((own, n_orb * half_rows, nocc), jnp.bfloat16),
         ],
         cost_estimate=FREE,
         compiler_params=params(16),
@@ -457,7 +459,7 @@
     start, others = lax.optimization_barrier((start, others))
 
     units = 2 * rowblocks * BLOCK // CHUNK
-    early_units = units * 3 // 16
+    early_units = units // 8
     fields_t = fields.T
     def all_plane(arrays):
         return [to_plane(arrays[dp - 1], dp) for dp in reversed(range(1, plane))]

time: 74.8 us -> 73.9 us (0.988)
  waiting for transfers between devices: 31.6 us -> 24.1 us
  starting transfers between devices: 26 us -> 33.2 us
    ppermute x9, waiting for transfers between devices: 20.9 us -> 13.5 us  [to_z(): lax.ppermute(a, 'chol', [(c, hop(c // plane, dz, nz) * plane + c % plane)...]
    ppermute x9, starting transfers between devices: 11.1 us -> 16.6 us  [to_z(): lax.ppermute(a, 'chol', [(c, hop(c // plane, dz, nz) * plane + c % plane)...]
    ppermute x12, starting transfers between devices: 14.3 us -> 15.9 us  [to_plane(): lax.ppermute(a, 'chol', [(c, c // plane * plane + hop(c % plane, dp, plan...]
  transfers between devices with their start and end apart: 24 -> 24, of which waited for: 10 -> 12; matrix products, arithmetic and copies ran while one was open for 0% -> 0% of each run, Pallas kernels for 2% -> 2%
where the time goes in v13:
time: 73.9 us; the launch traced here: 73.7 us
  starting transfers between devices  33.2 us (45%)
  waiting for transfers between devices  24.1 us (33%)
  Pallas kernels  15.7 us (21%)
    ppermute x9, starting transfers between devices, to_z(): lax.ppermute(a, 'chol', [(c, hop(c // plane, dz, nz) * plane + c % plane)...  16.6 us
    ppermute x12, starting transfers between devices, to_plane(): lax.ppermute(a, 'chol', [(c, c // plane * plane + hop(c % plane, dp, plan...  15.9 us
    ppermute x9, waiting for transfers between devices, to_z(): lax.ppermute(a, 'chol', [(c, hop(c // plane, dz, nz) * plane + c % plane)...  13.5 us
    pallas_call x1, Pallas kernels, bias_call(): pl.pallas_call(bias_kernel, in_specs=[*[pl.BlockSpec(memory_space=pl.ANY)...  8.42 us
    ppermute x12, waiting for transfers between devices, to_plane(): lax.ppermute(a, 'chol', [(c, c // plane * plane + hop(c % plane, dp, plan...  8.12 us
    pallas_call x2, Pallas kernels, potential_call(): pl.pallas_call(functools.partial(potential_kernel, begin, end, layout, by...  4.96 us
    ppermute x3, waiting for transfers between devices, around_orb(): lax.ppermute(a, 'orb', [((c + d) % n_orb, c) for c in range(n_orb)])  2.47 us
  transfers between devices with their start and end apart: 24, of which 12 were waited for; matrix products, arithmetic and copies ran while one was open for 0% of the time, Pallas kernels for 2%

profile of v13, /device:TPU:0, one launch (start us, length us, event | category | flops | bytes accessed | tf_op | source)
XLA Modules:
  0.0 73.7 jit_solution(296964734672947894)
XLA Ops:
  0.6 0.0 copy-start
  0.6 8.4 %force_bias.1 = (bf16[8,256,2048]{2,1,0:T(8,128)(2,1)S(1)}, f32[32,256]{1,0:T(8,128)S(1)}, bf16[2,128,128]{2,1,0:T(8,128)(2,1)S(1)}, s32[2,2,256]{2,1,0:T(2,128)S(1)}) custom-call(bf16[256,2,64,128]{3,2,1,0:T(8,128)(2,1)} %vals_hbm.1, bf16[32,128,256]{2,1,0:T(8,128)(2,1)} %greens_hbm.1, bf16[32,128,128]{2,1,0:T(8,128)(2,1)} %walkers_hbm.1, s32[2,2,256]{2,1,0:T(2,128)} %bitcast.5), custom_call_target="tpu_custom_call" | custom-call | tf_op jit(solution)/shard_map/force_bias/pallas_call | solution.py:154
  9.1 0.5 collective-permute-start
  9.6 0.1 collective-permute-start.1
  9.7 1.1 %collective-permute-done.1.refs_0_ = f32[32,256]{1,0:T(8,128)S(1)} collective-permute-done((f32[32,256]{1,0:T(8,128)S(1)}, f32[32,256]{1,0:T(8,128)S(1)}, u32[]{:S(2)}, u32[]{:S(2)}) %collective-permute-start.1) | collective-permute-done | bytes 32800 | tf_op jit(solution)/shard_map/ppermute | solution.py:453
  10.8 0.0 collective-permute-done.refs_3_
  10.8 0.0 copy-done
  10.8 3.7 %potential.2 = (bf16[3,2,224,128]{3,2,1,0:T(8,128)(2,1)S(1)}, bf16[3,2,224,128]{3,2,1,0:T(8,128)(2,1)S(1)}, bf16[3,2,224,128]{3,2,1,0:T(8,128)(2,1)S(1)}, bf16[3...) custom-call(f32[32,256]{1,0:T(8,128)S(1)} %bitcast.3, ...), custom_call_target="tpu_custom_call" | custom-call | tf_op jit(solution)/shard_map/potential/pallas_call | solution.py:265
  14.5 3.7 %collective-permute-start.2 = (bf16[3,2,224,128]{3,2,1,0:T(8,128)(2,1)S(1)}, bf16[3,2,224,128]{3,2,1,0:T(8,128)(2,1)S(1)}, u32[]{:S(2)}, u32[]{:S(2)}) collective-permute-start(bf16[3,2,224,128]{3,2,1,0:T(8,128)(2,1)S(1)} %get-tuple-element.40), channel_id=1, source_target_pairs={{0,6},{2,4},{4,2},{6,0},{8,14},{10,12},{12,10},{14,8},{16,22},{18,... | collective-permute-start | bytes 1032200 | tf_op jit(solution)/shard_map/ppermute | solution.py:447
  18.2 0.5 collective-permute-start.3
  18.7 0.1 collective-permute-start.4
  18.9 1.2 %potential.3 = (bf16[4,2,32,128]{3,2,1,0:T(8,128)(2,1)S(1)}, bf16[4,2,32,128]{3,2,1,0:T(8,128)(2,1)S(1)}, bf16[4,2,32,128]{3,2,1,0:T(8,128)(2,1)S(1)}, bf16[4,2,32,128]{3,2,1,0:T(8,128)(2,1)S(1)}, f32[16,128]{1,0:T(8,128)}) custom-call(f32[32,256]{1,0:T(8,128)S(1)} %bitcast.4, f32[32,256]{1,0:T(8,128)S(1)} %get-tuple-element.34.own_ref, ...), custom_call_target="tpu_custom_call" | custom-call | tf_op jit(solution)/shard_map/potential/pallas_call | solution.py:265
  20.1 3.0 %collective-permute-start.5 = (bf16[4,2,32,128]{3,2,1,0:T(8,128)(2,1)S(1)}, bf16[4,2,32,128]{3,2,1,0:T(8,128)(2,1)S(1)}, u32[]{:S(2)}, u32[]{:S(2)}) collective-permute-start(bf16[4,2,32,128]{3,2,1,0:T(8,128)(2,1)S(1)} %get-tuple-element.44), channel_id=1, source_target_pairs={{0,16},{2,18},{4,20},{6,22},{8,24},{10,26},{12,28},{14,30},{16,0},... | collective-permute-start | bytes 196616 | tf_op jit(solution)/shard_map/ppermute | solution.py:450
  23.1 1.3 %collective-permute-start.6 = (bf16[4,2,32,128]{3,2,1,0:T(8,128)(2,1)S(1)}, bf16[4,2,32,128]{3,2,1,0:T(8,128)(2,1)S(1)}, u32[]{:S(2)}, u32[]{:S(2)}) collective-permute-start(bf16[4,2,32,128]{3,2,1,0:T(8,128)(2,1)S(1)} %get-tuple-element.45), channel_id=1, source_target_pairs={{0,24},{2,26},{4,28},{6,30},{8,16},{10,18},{12,20},{14,22},{16,8},... | collective-permute-start | bytes 196616 | tf_op jit(solution)/shard_map/ppermute | solution.py:450
  24.4 1.5 %collective-permute-done.5.refs_1_ = bf16[4,2,32,128]{3,2,1,0:T(8,128)(2,1)S(1)} collective-permute-done((bf16[4,2,32,128]{3,2,1,0:T(8,128)(2,1)S(1)}, bf16[4,2,32,128]{3,2,1,0:T(8,128)(2,1)S(1)}, u32[]{:S(2)}, u32[]{:S(2)}) %collective-permute-start.5) | collective-permute-done | bytes 65568 | tf_op jit(solution)/shard_map/ppermute | solution.py:450
  25.9 2.9 %collective-permute-start.7 = (bf16[4,2,32,128]{3,2,1,0:T(8,128)(2,1)S(1)}, bf16[4,2,32,128]{3,2,1,0:T(8,128)(2,1)S(1)}, u32[]{:S(2)}, u32[]{:S(2)}) collective-permute-start(bf16[4,2,32,128]{3,2,1,0:T(8,128)(2,1)S(1)} %get-tuple-element.46), channel_id=1, source_target_pairs={{0,8},{2,10},{4,12},{6,14},{8,0},{10,2},{12,4},{14,6},{16,24},{18,... | collective-permute-start | bytes 196616 | tf_op jit(solution)/shard_map/ppermute | solution.py:450
  28.8 0.5 collective-permute-done.6.refs_2_
  29.3 1.7 %collective-permute-done.7.refs_3_ = bf16[4,2,32,128]{3,2,1,0:T(8,128)(2,1)S(1)} collective-permute-done((bf16[4,2,32,128]{3,2,1,0:T(8,128)(2,1)S(1)}, bf16[4,2,32,128]{3,2,1,0:T(8,128)(2,1)S(1)}, u32[]{:S(2)}, u32[]{:S(2)}) %collective-permute-start.7) | collective-permute-done | bytes 65568 | tf_op jit(solution)/shard_map/ppermute | solution.py:450
  31.1 2.5 %collective-permute-start.11 = (bf16[2,256,128]{2,1,0:T(8,128)(2,1)S(1)}, bf16[2,256,128]{2,1,0:T(8,128)(2,1)S(1)}, u32[]{:S(2)}, u32[]{:S(2)}) collective-permute-start(bf16[2,256,128]{2,1,0:T(8,128)(2,1)S(1)} %get-tuple-element.55), channel_id=1, source_target_pairs={{0,6},{2,4},{4,2},{6,0},{8,14},{10,12},{12,10},{14,8},{16,22},{18,... | collective-permute-start | bytes 393224 | tf_op jit(solution)/shard_map/ppermute | solution.py:447
  33.6 0.5 collective-permute-start.12
  34.1 0.0 collective-permute-done.2.refs_1_
  34.1 0.5 collective-permute-start.13
  34.6 0.0 collective-permute-done.3.refs_2_
  34.6 0.4 collective-permute-done.4.refs_3_
  35.0 0.2 sum_parts.1
  35.2 3.1 %collective-permute-start.8 = (bf16[2,224,128]{2,1,0:T(8,128)(2,1)S(1)}, bf16[2,224,128]{2,1,0:T(8,128)(2,1)S(1)}, u32[]{:S(2)}, u32[]{:S(2)}) collective-permute-start(bf16[2,224,128]{2,1,0:T(8,128)(2,1)S(1)} %get-tuple-element.52), channel_id=1, source_target_pairs={{0,16},{2,18},{4,20},{6,22},{8,24},{10,26},{12,28},{14,30},{16,0},... | collective-permute-start | bytes 344072 | tf_op jit(solution)/shard_map/ppermute | solution.py:450
  38.3 1.5 %collective-permute-start.9 = (bf16[2,224,128]{2,1,0:T(8,128)(2,1)S(1)}, bf16[2,224,128]{2,1,0:T(8,128)(2,1)S(1)}, u32[]{:S(2)}, u32[]{:S(2)}) collective-permute-start(bf16[2,224,128]{2,1,0:T(8,128)(2,1)S(1)} %get-tuple-element.53), channel_id=1, source_target_pairs={{0,24},{2,26},{4,28},{6,30},{8,16},{10,18},{12,20},{14,22},{16,8},... | collective-permute-start | bytes 344072 | tf_op jit(solution)/shard_map/ppermute | solution.py:450
  39.8 0.0 collective-permute-done.11.refs_4_
  39.8 0.5 collective-permute-start.10
  40.3 0.0 collective-permute-done.12.refs_5_
  40.3 0.0 collective-permute-done.13.refs_6_
  40.3 6.6 %collective-permute-done.8.refs_0_ = bf16[2,224,128]{2,1,0:T(8,128)(2,1)S(1)} collective-permute-done((bf16[2,224,128]{2,1,0:T(8,128)(2,1)S(1)}, bf16[2,224,128]{2,1,0:T(8,128)(2,1)S(1)}, u32[]{:S(2)}, u32[]{:S(2)}) %collective-permute-start.8) | collective-permute-done | bytes 114720 | tf_op jit(solution)/shard_map/ppermute | solution.py:450
  46.9 0.0 collective-permute-done.9.refs_1_
  46.9 0.2 collective-permute-done.10.refs_2_
  47.0 0.2 finish.1.refs_0_
  47.2 0.1 collective-permute-start.14
  47.3 1.3 %collective-permute-done.14.refs_1_ = bf16[2,256,128]{2,1,0:T(8,128)(2,1)S(1)} collective-permute-done((bf16[2,256,128]{2,1,0:T(8,128)(2,1)S(1)}, bf16[2,256,128]{2,1,0:T(8,128)(2,1)S(1)}, u32[]{:S(2)}, u32[]{:S(2)}) %collective-permute-start.14) | collective-permute-done | bytes 131104 | tf_op jit(solution)/shard_map/ppermute | solution.py:453
  48.6 0.9 %series.1.refs_0_ = bf16[264,128]{1,0:T(8,128)(2,1)S(1)} custom-call(bf16[2,256,128]{2,1,0:T(8,128)(2,1)S(1)} %finish.1.refs_0_, bf16[2,256,128]{2,1,0:T(8,128)(2,1)S(1)} %collective-permute-done.14.refs_1_, bf16[2,128,128]{2,1,0:T(8,128)(2,1)S(1)} %get-tuple-element.58.refs_2_, bf16[2,128,128]{2,1,0:T(8,128)(2,1)S(1)} %collective-permute-done.refs_3_, ...), custom_call_target="tpu_custom_call" | custom-call | tf_op jit(solution)/shard_map/series/pallas_call | solution.py:387
  49.5 3.6 %collective-permute-start.20 = (bf16[264,128]{1,0:T(8,128)(2,1)S(1)}, bf16[264,128]{1,0:T(8,128)(2,1)S(1)}, u32[]{:S(2)}, u32[]{:S(2)}) collective-permute-start(bf16[264,128]{1,0:T(8,128)(2,1)S(1)} %series.1.refs_0_), channel_id=1, source_target_pairs={{0,16},{2,18},{4,20},{6,22},{8,24},{10,26},{12,28},{14,30},{16,0},... | collective-permute-start | bytes 202760 | tf_op jit(solution)/shard_map/ppermute | solution.py:450
  53.2 0.5 collective-permute-start.19
  53.7 0.1 collective-permute-start.18
  53.8 1.3 %collective-permute-start.17 = (bf16[264,128]{1,0:T(8,128)(2,1)S(1)}, bf16[264,128]{1,0:T(8,128)(2,1)S(1)}, u32[]{:S(2)}, u32[]{:S(2)}) collective-permute-start(bf16[264,128]{1,0:T(8,128)(2,1)S(1)} %series.1.refs_0_), channel_id=1, source_target_pairs={{0,6},{2,4},{4,2},{6,0},{8,14},{10,12},{12,10},{14,8},{16,22},{18,... | collective-permute-start | bytes 202760 | tf_op jit(solution)/shard_map/ppermute | solution.py:447
  55.1 1.7 %collective-permute-start.16 = (bf16[264,128]{1,0:T(8,128)(2,1)S(1)}, bf16[264,128]{1,0:T(8,128)(2,1)S(1)}, u32[]{:S(2)}, u32[]{:S(2)}) collective-permute-start(bf16[264,128]{1,0:T(8,128)(2,1)S(1)} %series.1.refs_0_), channel_id=1, source_target_pairs={{0,4},{2,6},{4,0},{6,2},{8,12},{10,14},{12,8},{14,10},{16,20},{18,... | collective-permute-start | bytes 202760 | tf_op jit(solution)/shard_map/ppermute | solution.py:447
  56.8 0.6 collective-permute-done.20.refs_4_
  57.4 2.3 %collective-permute-done.19.refs_3_ = bf16[264,128]{1,0:T(8,128)(2,1)S(1)} collective-permute-done((bf16[264,128]{1,0:T(8,128)(2,1)S(1)}, bf16[264,128]{1,0:T(8,128)(2,1)S(1)}, u32[]{:S(2)}, u32[]{:S(2)}) %collective-permute-start.19) | collective-permute-done | bytes 67616 | tf_op jit(solution)/shard_map/ppermute | solution.py:450
  59.6 0.2 collective-permute-done.18.refs_2_
  59.9 0.0 collective-permute-done.17.refs_1_
  59.9 0.0 collective-permute-done.16.refs_0_
  59.9 1.3 %collective-permute-start.23 = (bf16[3,264,128]{2,1,0:T(8,128)(2,1)S(1)}, bf16[3,264,128]{2,1,0:T(8,128)(2,1)S(1)}, u32[]{:S(2)}, u32[]{:S(2)}) collective-permute-start(bf16[3,264,128]{2,1,0:T(8,128)(2,1)S(1)} %get-tuple-element.63.refs_4_), channel_id=1, source_target_pairs={{0,6},{2,4},{4,2},{6,0},{8,14},{10,12},{12,10},{14,8},{16,22},{18,... | collective-permute-start | bytes 608264 | tf_op jit(solution)/shard_map/ppermute | solution.py:447
  61.3 1.7 %collective-permute-start.22 = (bf16[3,264,128]{2,1,0:T(8,128)(2,1)S(1)}, bf16[3,264,128]{2,1,0:T(8,128)(2,1)S(1)}, u32[]{:S(2)}, u32[]{:S(2)}) collective-permute-start(bf16[3,264,128]{2,1,0:T(8,128)(2,1)S(1)} %get-tuple-element.63.refs_4_), channel_id=1, source_target_pairs={{0,4},{2,6},{4,0},{6,2},{8,12},{10,14},{12,8},{14,10},{16,20},{18,... | collective-permute-start | bytes 608264 | tf_op jit(solution)/shard_map/ppermute | solution.py:447
  62.9 0.5 collective-permute-start.21
  63.5 1.5 %collective-permute-start.15 = (bf16[264,128]{1,0:T(8,128)(2,1)S(1)}, bf16[264,128]{1,0:T(8,128)(2,1)S(1)}, u32[]{:S(2)}, u32[]{:S(2)}) collective-permute-start(bf16[264,128]{1,0:T(8,128)(2,1)S(1)} %series.1.refs_0_), channel_id=1, source_target_pairs={{0,2},{2,0},{4,6},{6,4},{8,10},{10,8},{12,14},{14,12},{16,18},{18,... | collective-permute-start | bytes 202760 | tf_op jit(solution)/shard_map/ppermute | solution.py:447
  65.0 7.7 %collective-permute-done.15.refs_1_ = bf16[264,128]{1,0:T(8,128)(2,1)S(1)} collective-permute-done((bf16[264,128]{1,0:T(8,128)(2,1)S(1)}, bf16[264,128]{1,0:T(8,128)(2,1)S(1)}, u32[]{:S(2)}, u32[]{:S(2)}) %collective-permute-start.15) | collective-permute-done | bytes 67616 | tf_op jit(solution)/shard_map/ppermute | solution.py:447
  72.7 0.0 collective-permute-done.23.refs_7_
  72.7 0.0 collective-permute-done.22.refs_6_
  72.7 0.0 collective-permute-done.21.refs_5_
  72.7 1.1 %place_walkers.1 = (bf16[32,128,128]{2,1,0:T(8,128)(2,1)}, f32[1,32]{1,0:T(1,128)}) custom-call(bf16[264,128]{1,0:T(8,128)(2,1)S(1)} %series.1.refs_0_, bf16[264,128]{1,0:T(8,128)(2,1)S(1)} %collective-permute-done.15.refs_1_, bf16[264,128]{1,0:T(8,128)(2,1)S(1)} %get-tuple-element.61.refs_2_, bf16[264,128]{1,0:T(8,128)(2,1)S(1)} %get-tuple-element.62.refs_3_, ...), custom_call_target="tpu_custom_call" | custom-call | tf_op jit(solution)/shard_map/place_walkers/pallas_call | solution.py:423
  (2 shorter events, 0.1 us)
Async XLA Ops:
  0.6 10.2 %copy-start = (f32[256,32]{0,1:T(8,128)S(1)}, f32[256,32]{0,1:T(8,128)}, u32[]{:S(2)}) copy-start(f32[256,32]{0,1:T(8,128)} %param.9) | copy-start | bytes 98308
  9.1 1.7 %collective-permute-start = (bf16[2,128,128]{2,1,0:T(8,128)(2,1)S(1)}, bf16[2,128,128]{2,1,0:T(8,128)(2,1)S(1)}, u32[]{:S(2)}, u32[]{:S(2)}) collective-permute-start(bf16[2,128,128]{2,1,0:T(8,128)(2,1)S(1)} %get-tuple-element.58.refs_2_), channel_id=1, source_target_pairs={{1,0},{0,1},{3,2},{2,3},{5,4},{4,5},{7,6},{6,7},{9,8},{8,9},{11,10... | collective-permute-start | bytes 196616 | tf_op jit(solution)/shard_map/ppermute | solution.py:453
  9.6 1.2 %collective-permute-start.1 = (f32[32,256]{1,0:T(8,128)S(1)}, f32[32,256]{1,0:T(8,128)S(1)}, u32[]{:S(2)}, u32[]{:S(2)}) collective-permute-start(f32[32,256]{1,0:T(8,128)S(1)} %get-tuple-element.34.own_ref), channel_id=1, source_target_pairs={{1,0},{0,1},{3,2},{2,3},{5,4},{4,5},{7,6},{6,7},{9,8},{8,9},{11,10... | collective-permute-start | bytes 98312 | tf_op jit(solution)/shard_map/ppermute | solution.py:453
  14.5 19.6 %collective-permute-start.2 = (bf16[3,2,224,128]{3,2,1,0:T(8,128)(2,1)S(1)}, bf16[3,2,224,128]{3,2,1,0:T(8,128)(2,1)S(1)}, u32[]{:S(2)}, u32[]{:S(2)}) collective-permute-start(bf16[3,2,224,128]{3,2,1,0:T(8,128)(2,1)S(1)} %get-tuple-element.40), channel_id=1, source_target_pairs={{0,6},{2,4},{4,2},{6,0},{8,14},{10,12},{12,10},{14,8},{16,22},{18,... | collective-permute-start | bytes 1032200 | tf_op jit(solution)/shard_map/ppermute | solution.py:447
  18.2 16.4 %collective-permute-start.3 = (bf16[3,2,224,128]{3,2,1,0:T(8,128)(2,1)S(1)}, bf16[3,2,224,128]{3,2,1,0:T(8,128)(2,1)S(1)}, u32[]{:S(2)}, u32[]{:S(2)}) collective-permute-start(bf16[3,2,224,128]{3,2,1,0:T(8,128)(2,1)S(1)} %get-tuple-element.41), channel_id=1, source_target_pairs={{0,4},{2,6},{4,0},{6,2},{8,12},{10,14},{12,8},{14,10},{16,20},{18,... | collective-permute-start | bytes 1032200 | tf_op jit(solution)/shard_map/ppermute | solution.py:447
  18.7 16.3 %collective-permute-start.4 = (bf16[3,2,224,128]{3,2,1,0:T(8,128)(2,1)S(1)}, bf16[3,2,224,128]{3,2,1,0:T(8,128)(2,1)S(1)}, u32[]{:S(2)}, u32[]{:S(2)}) collective-permute-start(bf16[3,2,224,128]{3,2,1,0:T(8,128)(2,1)S(1)} %get-tuple-element.42), channel_id=1, source_target_pairs={{0,2},{2,0},{4,6},{6,4},{8,10},{10,8},{12,14},{14,12},{16,18},{18,... | collective-permute-start | bytes 1032200 | tf_op jit(solution)/shard_map/ppermute | solution.py:447
  20.1 5.8 %collective-permute-start.5 = (bf16[4,2,32,128]{3,2,1,0:T(8,128)(2,1)S(1)}, bf16[4,2,32,128]{3,2,1,0:T(8,128)(2,1)S(1)}, u32[]{:S(2)}, u32[]{:S(2)}) collective-permute-start(bf16[4,2,32,128]{3,2,1,0:T(8,128)(2,1)S(1)} %get-tuple-element.44), channel_id=1, source_target_pairs={{0,16},{2,18},{4,20},{6,22},{8,24},{10,26},{12,28},{14,30},{16,0},... | collective-permute-start | bytes 196616 | tf_op jit(solution)/shard_map/ppermute | solution.py:450
  23.1 6.2 %collective-permute-start.6 = (bf16[4,2,32,128]{3,2,1,0:T(8,128)(2,1)S(1)}, bf16[4,2,32,128]{3,2,1,0:T(8,128)(2,1)S(1)}, u32[]{:S(2)}, u32[]{:S(2)}) collective-permute-start(bf16[4,2,32,128]{3,2,1,0:T(8,128)(2,1)S(1)} %get-tuple-element.45), channel_id=1, source_target_pairs={{0,24},{2,26},{4,28},{6,30},{8,16},{10,18},{12,20},{14,22},{16,8},... | collective-permute-start | bytes 196616 | tf_op jit(solution)/shard_map/ppermute | solution.py:450
  25.9 5.1 %collective-permute-start.7 = (bf16[4,2,32,128]{3,2,1,0:T(8,128)(2,1)S(1)}, bf16[4,2,32,128]{3,2,1,0:T(8,128)(2,1)S(1)}, u32[]{:S(2)}, u32[]{:S(2)}) collective-permute-start(bf16[4,2,32,128]{3,2,1,0:T(8,128)(2,1)S(1)} %get-tuple-element.46), channel_id=1, source_target_pairs={{0,8},{2,10},{4,12},{6,14},{8,0},{10,2},{12,4},{14,6},{16,24},{18,... | collective-permute-start | bytes 196616 | tf_op jit(solution)/shard_map/ppermute | solution.py:450
  31.1 8.7 %collective-permute-start.11 = (bf16[2,256,128]{2,1,0:T(8,128)(2,1)S(1)}, bf16[2,256,128]{2,1,0:T(8,128)(2,1)S(1)}, u32[]{:S(2)}, u32[]{:S(2)}) collective-permute-start(bf16[2,256,128]{2,1,0:T(8,128)(2,1)S(1)} %get-tuple-element.55), channel_id=1, source_target_pairs={{0,6},{2,4},{4,2},{6,0},{8,14},{10,12},{12,10},{14,8},{16,22},{18,... | collective-permute-start | bytes 393224 | tf_op jit(solution)/shard_map/ppermute | solution.py:447
  33.6 6.7 %collective-permute-start.12 = (bf16[2,256,128]{2,1,0:T(8,128)(2,1)S(1)}, bf16[2,256,128]{2,1,0:T(8,128)(2,1)S(1)}, u32[]{:S(2)}, u32[]{:S(2)}) collective-permute-start(bf16[2,256,128]{2,1,0:T(8,128)(2,1)S(1)} %get-tuple-element.56), channel_id=1, source_target_pairs={{0,4},{2,6},{4,0},{6,2},{8,12},{10,14},{12,8},{14,10},{16,20},{18,... | collective-permute-start | bytes 393224 | tf_op jit(solution)/shard_map/ppermute | solution.py:447
  34.1 6.2 %collective-permute-start.13 = (bf16[2,256,128]{2,1,0:T(8,128)(2,1)S(1)}, bf16[2,256,128]{2,1,0:T(8,128)(2,1)S(1)}, u32[]{:S(2)}, u32[]{:S(2)}) collective-permute-start(bf16[2,256,128]{2,1,0:T(8,128)(2,1)S(1)} %get-tuple-element.57), channel_id=1, source_target_pairs={{0,2},{2,0},{4,6},{6,4},{8,10},{10,8},{12,14},{14,12},{16,18},{18,... | collective-permute-start | bytes 393224 | tf_op jit(solution)/shard_map/ppermute | solution.py:447
  35.2 11.7 %collective-permute-start.8 = (bf16[2,224,128]{2,1,0:T(8,128)(2,1)S(1)}, bf16[2,224,128]{2,1,0:T(8,128)(2,1)S(1)}, u32[]{:S(2)}, u32[]{:S(2)}) collective-permute-start(bf16[2,224,128]{2,1,0:T(8,128)(2,1)S(1)} %get-tuple-element.52), channel_id=1, source_target_pairs={{0,16},{2,18},{4,20},{6,22},{8,24},{10,26},{12,28},{14,30},{16,0},... | collective-permute-start | bytes 344072 | tf_op jit(solution)/shard_map/ppermute | solution.py:450
  38.3 8.6 %collective-permute-start.9 = (bf16[2,224,128]{2,1,0:T(8,128)(2,1)S(1)}, bf16[2,224,128]{2,1,0:T(8,128)(2,1)S(1)}, u32[]{:S(2)}, u32[]{:S(2)}) collective-permute-start(bf16[2,224,128]{2,1,0:T(8,128)(2,1)S(1)} %get-tuple-element.53), channel_id=1, source_target_pairs={{0,24},{2,26},{4,28},{6,30},{8,16},{10,18},{12,20},{14,22},{16,8},... | collective-permute-start | bytes 344072 | tf_op jit(solution)/shard_map/ppermute | solution.py:450
  39.8 7.2 %collective-permute-start.10 = (bf16[2,224,128]{2,1,0:T(8,128)(2,1)S(1)}, bf16[2,224,128]{2,1,0:T(8,128)(2,1)S(1)}, u32[]{:S(2)}, u32[]{:S(2)}) collective-permute-start(bf16[2,224,128]{2,1,0:T(8,128)(2,1)S(1)} %get-tuple-element.54), channel_id=1, source_target_pairs={{0,8},{2,10},{4,12},{6,14},{8,0},{10,2},{12,4},{14,6},{16,24},{18,... | collective-permute-start | bytes 344072 | tf_op jit(solution)/shard_map/ppermute | solution.py:450
  47.2 1.4 %collective-permute-start.14 = (bf16[2,256,128]{2,1,0:T(8,128)(2,1)S(1)}, bf16[2,256,128]{2,1,0:T(8,128)(2,1)S(1)}, u32[]{:S(2)}, u32[]{:S(2)}) collective-permute-start(bf16[2,256,128]{2,1,0:T(8,128)(2,1)S(1)} %finish.1.refs_0_), channel_id=1, source_target_pairs={{1,0},{0,1},{3,2},{2,3},{5,4},{4,5},{7,6},{6,7},{9,8},{8,9},{11,10... | collective-permute-start | bytes 393224 | tf_op jit(solution)/shard_map/ppermute | solution.py:453
  49.5 7.9 %collective-permute-start.20 = (bf16[264,128]{1,0:T(8,128)(2,1)S(1)}, bf16[264,128]{1,0:T(8,128)(2,1)S(1)}, u32[]{:S(2)}, u32[]{:S(2)}) collective-permute-start(bf16[264,128]{1,0:T(8,128)(2,1)S(1)} %series.1.refs_0_), channel_id=1, source_target_pairs={{0,16},{2,18},{4,20},{6,22},{8,24},{10,26},{12,28},{14,30},{16,0},... | collective-permute-start | bytes 202760 | tf_op jit(solution)/shard_map/ppermute | solution.py:450
  53.2 6.5 %collective-permute-start.19 = (bf16[264,128]{1,0:T(8,128)(2,1)S(1)}, bf16[264,128]{1,0:T(8,128)(2,1)S(1)}, u32[]{:S(2)}, u32[]{:S(2)}) collective-permute-start(bf16[264,128]{1,0:T(8,128)(2,1)S(1)} %series.1.refs_0_), channel_id=1, source_target_pairs={{0,24},{2,26},{4,28},{6,30},{8,16},{10,18},{12,20},{14,22},{16,8},... | collective-permute-start | bytes 202760 | tf_op jit(solution)/shard_map/ppermute | solution.py:450
  53.7 6.2 %collective-permute-start.18 = (bf16[264,128]{1,0:T(8,128)(2,1)S(1)}, bf16[264,128]{1,0:T(8,128)(2,1)S(1)}, u32[]{:S(2)}, u32[]{:S(2)}) collective-permute-start(bf16[264,128]{1,0:T(8,128)(2,1)S(1)} %series.1.refs_0_), channel_id=1, source_target_pairs={{0,8},{2,10},{4,12},{6,14},{8,0},{10,2},{12,4},{14,6},{16,24},{18,... | collective-permute-start | bytes 202760 | tf_op jit(solution)/shard_map/ppermute | solution.py:450
  53.8 6.1 %collective-permute-start.17 = (bf16[264,128]{1,0:T(8,128)(2,1)S(1)}, bf16[264,128]{1,0:T(8,128)(2,1)S(1)}, u32[]{:S(2)}, u32[]{:S(2)}) collective-permute-start(bf16[264,128]{1,0:T(8,128)(2,1)S(1)} %series.1.refs_0_), channel_id=1, source_target_pairs={{0,6},{2,4},{4,2},{6,0},{8,14},{10,12},{12,10},{14,8},{16,22},{18,... | collective-permute-start | bytes 202760 | tf_op jit(solution)/shard_map/ppermute | solution.py:447
  55.1 4.8 %collective-permute-start.16 = (bf16[264,128]{1,0:T(8,128)(2,1)S(1)}, bf16[264,128]{1,0:T(8,128)(2,1)S(1)}, u32[]{:S(2)}, u32[]{:S(2)}) collective-permute-start(bf16[264,128]{1,0:T(8,128)(2,1)S(1)} %series.1.refs_0_), channel_id=1, source_target_pairs={{0,4},{2,6},{4,0},{6,2},{8,12},{10,14},{12,8},{14,10},{16,20},{18,... | collective-permute-start | bytes 202760 | tf_op jit(solution)/shard_map/ppermute | solution.py:447
  59.9 12.8 %collective-permute-start.23 = (bf16[3,264,128]{2,1,0:T(8,128)(2,1)S(1)}, bf16[3,264,128]{2,1,0:T(8,128)(2,1)S(1)}, u32[]{:S(2)}, u32[]{:S(2)}) collective-permute-start(bf16[3,264,128]{2,1,0:T(8,128)(2,1)S(1)} %get-tuple-element.63.refs_4_), channel_id=1, source_target_pairs={{0,6},{2,4},{4,2},{6,0},{8,14},{10,12},{12,10},{14,8},{16,22},{18,... | collective-permute-start | bytes 608264 | tf_op jit(solution)/shard_map/ppermute | solution.py:447
  61.3 11.4 %collective-permute-start.22 = (bf16[3,264,128]{2,1,0:T(8,128)(2,1)S(1)}, bf16[3,264,128]{2,1,0:T(8,128)(2,1)S(1)}, u32[]{:S(2)}, u32[]{:S(2)}) collective-permute-start(bf16[3,264,128]{2,1,0:T(8,128)(2,1)S(1)} %get-tuple-element.63.refs_4_), channel_id=1, source_target_pairs={{0,4},{2,6},{4,0},{6,2},{8,12},{10,14},{12,8},{14,10},{16,20},{18,... | collective-permute-start | bytes 608264 | tf_op jit(solution)/shard_map/ppermute | solution.py:447
  62.9 9.7 %collective-permute-start.21 = (bf16[3,264,128]{2,1,0:T(8,128)(2,1)S(1)}, bf16[3,264,128]{2,1,0:T(8,128)(2,1)S(1)}, u32[]{:S(2)}, u32[]{:S(2)}) collective-permute-start(bf16[3,264,128]{2,1,0:T(8,128)(2,1)S(1)} %get-tuple-element.63.refs_4_), channel_id=1, source_target_pairs={{0,2},{2,0},{4,6},{6,4},{8,10},{10,8},{12,14},{14,12},{16,18},{18,... | collective-permute-start | bytes 608264 | tf_op jit(solution)/shard_map/ppermute | solution.py:447
  63.5 9.2 %collective-permute-start.15 = (bf16[264,128]{1,0:T(8,128)(2,1)S(1)}, bf16[264,128]{1,0:T(8,128)(2,1)S(1)}, u32[]{:S(2)}, u32[]{:S(2)}) collective-permute-start(bf16[264,128]{1,0:T(8,128)(2,1)S(1)} %series.1.refs_0_), channel_id=1, source_target_pairs={{0,2},{2,0},{4,6},{6,4},{8,10},{10,8},{12,14},{14,12},{16,18},{18,... | collective-permute-start | bytes 202760 | tf_op jit(solution)/shard_map/ppermute | solution.py:447

commit v14 on v13

--- a/solution.py
+++ b/solution.py
@@ -111,7 +111,7 @@
                     gs[side, k * walk + w:k * walk + w + CHUNK, i * LANES:(i + 1) * LANES] = (
                         piece[i * CHUNK:(i + 1) * CHUNK]
                     )
-        for g in range(0, vectors, 2 * CHUNK):
+        for g in range(0, vectors, 4 * CHUNK):
             both = [vals[t, g + k * CHUNK:g + (k + 1) * CHUNK].reshape(CHUNK * CHUNK, LANES) for k in range(2)]
             both = jnp.dot(swap[...], jnp.concatenate(both, axis=1), preferred_element_type=jnp.float32)
             both = both.astype(jnp.bfloat16)
@@ -120,6 +120,11 @@
                     turned_ref[t, g + k * CHUNK:g + (k + 1) * CHUNK, i * LANES:(i + 1) * LANES] = (
                         both[i * CHUNK:(i + 1) * CHUNK, k * LANES:(k + 1) * LANES]
                     )
+            for k in range(2, 4):
+                other = vals[t, g + k * CHUNK:g + (k + 1) * CHUNK].astype(jnp.float32)
+                other = jnp.swapaxes(other, 0, 1).astype(jnp.bfloat16)
+                for i in range(CHUNK):
+                    turned_ref[t, g + k * CHUNK:g + (k + 1) * CHUNK, i * LANES:(i + 1) * LANES] = other[i]
         part = lax.dot_general(
             turned_ref[t], gs[side], (((1,), (1,)), ((), ())), preferred_element_type=jnp.float32
         )

time: 73.9 us -> 74.1 us (level)
  no operation moved by 1% of the time
where the time goes in v14:
time: 74.1 us; the launch traced here: 74 us
  starting transfers between devices  33.2 us (45%)
  waiting for transfers between devices  24.1 us (33%)
  Pallas kernels  16 us (22%)
    ppermute x9, starting transfers between devices, to_z(): lax.ppermute(a, 'chol', [(c, hop(c // plane, dz, nz) * plane + c % plane)...  16.6 us
    ppermute x12, starting transfers between devices, to_plane(): lax.ppermute(a, 'chol', [(c, c // plane * plane + hop(c % plane, dp, plan...  15.9 us
    ppermute x9, waiting for transfers between devices, to_z(): lax.ppermute(a, 'chol', [(c, hop(c // plane, dz, nz) * plane + c % plane)...  13.5 us
    pallas_call x1, Pallas kernels, bias_call(): pl.pallas_call(bias_kernel, in_specs=[*[pl.BlockSpec(memory_space=pl.ANY)...  8.65 us
    ppermute x12, waiting for transfers between devices, to_plane(): lax.ppermute(a, 'chol', [(c, c // plane * plane + hop(c % plane, dp, plan...  8.11 us
    pallas_call x2, Pallas kernels, potential_call(): pl.pallas_call(functools.partial(potential_kernel, begin, end, layout, by...  4.95 us
    ppermute x3, waiting for transfers between devices, around_orb(): lax.ppermute(a, 'orb', [((c + d) % n_orb, c) for c in range(n_orb)])  2.47 us
  transfers between devices with their start and end apart: 24, of which 12 were waited for; matrix products, arithmetic and copies ran while one was open for 0% of the time, Pallas kernels for 2%

profile of v14, /device:TPU:0, one launch (start us, length us, event | category | flops | bytes accessed | tf_op | source)
XLA Modules:
  0.0 74.0 jit_solution(3454951228112074277)
XLA Ops:
  0.6 0.0 copy-start
  0.6 8.7 %force_bias.1 = (bf16[8,256,2048]{2,1,0:T(8,128)(2,1)S(1)}, f32[32,256]{1,0:T(8,128)S(1)}, bf16[2,128,128]{2,1,0:T(8,128)(2,1)S(1)}, s32[2,2,256]{2,1,0:T(2,128)S(1)}) custom-call(bf16[256,2,64,128]{3,2,1,0:T(8,128)(2,1)} %vals_hbm.1, bf16[32,128,256]{2,1,0:T(8,128)(2,1)} %greens_hbm.1, bf16[32,128,128]{2,1,0:T(8,128)(2,1)} %walkers_hbm.1, s32[2,2,256]{2,1,0:T(2,128)} %bitcast.5), custom_call_target="tpu_custom_call" | custom-call | tf_op jit(solution)/shard_map/force_bias/pallas_call | solution.py:159
  9.3 0.5 collective-permute-start
  9.8 0.1 collective-permute-start.1
  9.9 1.1 %collective-permute-done.1.refs_0_ = f32[32,256]{1,0:T(8,128)S(1)} collective-permute-done((f32[32,256]{1,0:T(8,128)S(1)}, f32[32,256]{1,0:T(8,128)S(1)}, u32[]{:S(2)}, u32[]{:S(2)}) %collective-permute-start.1) | collective-permute-done | bytes 32800 | tf_op jit(solution)/shard_map/ppermute | solution.py:458
  11.0 0.0 collective-permute-done.refs_3_
  11.0 0.0 copy-done
  11.0 3.7 %potential.2 = (bf16[3,2,224,128]{3,2,1,0:T(8,128)(2,1)S(1)}, bf16[3,2,224,128]{3,2,1,0:T(8,128)(2,1)S(1)}, bf16[3,2,224,128]{3,2,1,0:T(8,128)(2,1)S(1)}, bf16[3...) custom-call(f32[32,256]{1,0:T(8,128)S(1)} %bitcast.3, ...), custom_call_target="tpu_custom_call" | custom-call | tf_op jit(solution)/shard_map/potential/pallas_call | solution.py:270
  14.8 3.7 %collective-permute-start.2 = (bf16[3,2,224,128]{3,2,1,0:T(8,128)(2,1)S(1)}, bf16[3,2,224,128]{3,2,1,0:T(8,128)(2,1)S(1)}, u32[]{:S(2)}, u32[]{:S(2)}) collective-permute-start(bf16[3,2,224,128]{3,2,1,0:T(8,128)(2,1)S(1)} %get-tuple-element.40), channel_id=1, source_target_pairs={{0,6},{2,4},{4,2},{6,0},{8,14},{10,12},{12,10},{14,8},{16,22},{18,... | collective-permute-start | bytes 1032200 | tf_op jit(solution)/shard_map/ppermute | solution.py:452
  18.4 0.5 collective-permute-start.3
  18.9 0.1 collective-permute-start.4
  19.1 1.2 %potential.3 = (bf16[4,2,32,128]{3,2,1,0:T(8,128)(2,1)S(1)}, bf16[4,2,32,128]{3,2,1,0:T(8,128)(2,1)S(1)}, bf16[4,2,32,128]{3,2,1,0:T(8,128)(2,1)S(1)}, bf16[4,2,32,128]{3,2,1,0:T(8,128)(2,1)S(1)}, f32[16,128]{1,0:T(8,128)}) custom-call(f32[32,256]{1,0:T(8,128)S(1)} %bitcast.4, f32[32,256]{1,0:T(8,128)S(1)} %get-tuple-element.34.own_ref, ...), custom_call_target="tpu_custom_call" | custom-call | tf_op jit(solution)/shard_map/potential/pallas_call | solution.py:270
  20.3 3.0 %collective-permute-start.5 = (bf16[4,2,32,128]{3,2,1,0:T(8,128)(2,1)S(1)}, bf16[4,2,32,128]{3,2,1,0:T(8,128)(2,1)S(1)}, u32[]{:S(2)}, u32[]{:S(2)}) collective-permute-start(bf16[4,2,32,128]{3,2,1,0:T(8,128)(2,1)S(1)} %get-tuple-element.44), channel_id=1, source_target_pairs={{0,16},{2,18},{4,20},{6,22},{8,24},{10,26},{12,28},{14,30},{16,0},... | collective-permute-start | bytes 196616 | tf_op jit(solution)/shard_map/ppermute | solution.py:455
  23.3 1.3 %collective-permute-start.6 = (bf16[4,2,32,128]{3,2,1,0:T(8,128)(2,1)S(1)}, bf16[4,2,32,128]{3,2,1,0:T(8,128)(2,1)S(1)}, u32[]{:S(2)}, u32[]{:S(2)}) collective-permute-start(bf16[4,2,32,128]{3,2,1,0:T(8,128)(2,1)S(1)} %get-tuple-element.45), channel_id=1, source_target_pairs={{0,24},{2,26},{4,28},{6,30},{8,16},{10,18},{12,20},{14,22},{16,8},... | collective-permute-start | bytes 196616 | tf_op jit(solution)/shard_map/ppermute | solution.py:455
  24.6 1.5 %collective-permute-done.5.refs_1_ = bf16[4,2,32,128]{3,2,1,0:T(8,128)(2,1)S(1)} collective-permute-done((bf16[4,2,32,128]{3,2,1,0:T(8,128)(2,1)S(1)}, bf16[4,2,32,128]{3,2,1,0:T(8,128)(2,1)S(1)}, u32[]{:S(2)}, u32[]{:S(2)}) %collective-permute-start.5) | collective-permute-done | bytes 65568 | tf_op jit(solution)/shard_map/ppermute | solution.py:455
  26.1 2.9 %collective-permute-start.7 = (bf16[4,2,32,128]{3,2,1,0:T(8,128)(2,1)S(1)}, bf16[4,2,32,128]{3,2,1,0:T(8,128)(2,1)S(1)}, u32[]{:S(2)}, u32[]{:S(2)}) collective-permute-start(bf16[4,2,32,128]{3,2,1,0:T(8,128)(2,1)S(1)} %get-tuple-element.46), channel_id=1, source_target_pairs={{0,8},{2,10},{4,12},{6,14},{8,0},{10,2},{12,4},{14,6},{16,24},{18,... | collective-permute-start | bytes 196616 | tf_op jit(solution)/shard_map/ppermute | solution.py:455
  29.0 0.5 collective-permute-done.6.refs_2_
  29.5 1.7 %collective-permute-done.7.refs_3_ = bf16[4,2,32,128]{3,2,1,0:T(8,128)(2,1)S(1)} collective-permute-done((bf16[4,2,32,128]{3,2,1,0:T(8,128)(2,1)S(1)}, bf16[4,2,32,128]{3,2,1,0:T(8,128)(2,1)S(1)}, u32[]{:S(2)}, u32[]{:S(2)}) %collective-permute-start.7) | collective-permute-done | bytes 65568 | tf_op jit(solution)/shard_map/ppermute | solution.py:455
  31.3 2.5 %collective-permute-start.11 = (bf16[2,256,128]{2,1,0:T(8,128)(2,1)S(1)}, bf16[2,256,128]{2,1,0:T(8,128)(2,1)S(1)}, u32[]{:S(2)}, u32[]{:S(2)}) collective-permute-start(bf16[2,256,128]{2,1,0:T(8,128)(2,1)S(1)} %get-tuple-element.55), channel_id=1, source_target_pairs={{0,6},{2,4},{4,2},{6,0},{8,14},{10,12},{12,10},{14,8},{16,22},{18,... | collective-permute-start | bytes 393224 | tf_op jit(solution)/shard_map/ppermute | solution.py:452
  33.8 0.5 collective-permute-start.12
  34.3 0.0 collective-permute-done.2.refs_1_
  34.3 0.5 collective-permute-start.13
  34.9 0.0 collective-permute-done.3.refs_2_
  34.9 0.4 collective-permute-done.4.refs_3_
  35.2 0.2 sum_parts.1
  35.4 3.1 %collective-permute-start.8 = (bf16[2,224,128]{2,1,0:T(8,128)(2,1)S(1)}, bf16[2,224,128]{2,1,0:T(8,128)(2,1)S(1)}, u32[]{:S(2)}, u32[]{:S(2)}) collective-permute-start(bf16[2,224,128]{2,1,0:T(8,128)(2,1)S(1)} %get-tuple-element.52), channel_id=1, source_target_pairs={{0,16},{2,18},{4,20},{6,22},{8,24},{10,26},{12,28},{14,30},{16,0},... | collective-permute-start | bytes 344072 | tf_op jit(solution)/shard_map/ppermute | solution.py:455
  38.5 1.5 %collective-permute-start.9 = (bf16[2,224,128]{2,1,0:T(8,128)(2,1)S(1)}, bf16[2,224,128]{2,1,0:T(8,128)(2,1)S(1)}, u32[]{:S(2)}, u32[]{:S(2)}) collective-permute-start(bf16[2,224,128]{2,1,0:T(8,128)(2,1)S(1)} %get-tuple-element.53), channel_id=1, source_target_pairs={{0,24},{2,26},{4,28},{6,30},{8,16},{10,18},{12,20},{14,22},{16,8},... | collective-permute-start | bytes 344072 | tf_op jit(solution)/shard_map/ppermute | solution.py:455
  40.0 0.0 collective-permute-done.11.refs_4_
  40.0 0.5 collective-permute-start.10
  40.5 0.0 collective-permute-done.12.refs_5_
  40.5 0.0 collective-permute-done.13.refs_6_
  40.5 6.6 %collective-permute-done.8.refs_0_ = bf16[2,224,128]{2,1,0:T(8,128)(2,1)S(1)} collective-permute-done((bf16[2,224,128]{2,1,0:T(8,128)(2,1)S(1)}, bf16[2,224,128]{2,1,0:T(8,128)(2,1)S(1)}, u32[]{:S(2)}, u32[]{:S(2)}) %collective-permute-start.8) | collective-permute-done | bytes 114720 | tf_op jit(solution)/shard_map/ppermute | solution.py:455
  47.1 0.0 collective-permute-done.9.refs_1_
  47.1 0.2 collective-permute-done.10.refs_2_
  47.3 0.2 finish.1.refs_0_
  47.5 0.1 collective-permute-start.14
  47.5 1.3 %collective-permute-done.14.refs_1_ = bf16[2,256,128]{2,1,0:T(8,128)(2,1)S(1)} collective-permute-done((bf16[2,256,128]{2,1,0:T(8,128)(2,1)S(1)}, bf16[2,256,128]{2,1,0:T(8,128)(2,1)S(1)}, u32[]{:S(2)}, u32[]{:S(2)}) %collective-permute-start.14) | collective-permute-done | bytes 131104 | tf_op jit(solution)/shard_map/ppermute | solution.py:458
  48.9 0.9 %series.1.refs_0_ = bf16[264,128]{1,0:T(8,128)(2,1)S(1)} custom-call(bf16[2,256,128]{2,1,0:T(8,128)(2,1)S(1)} %finish.1.refs_0_, bf16[2,256,128]{2,1,0:T(8,128)(2,1)S(1)} %collective-permute-done.14.refs_1_, bf16[2,128,128]{2,1,0:T(8,128)(2,1)S(1)} %get-tuple-element.58.refs_2_, bf16[2,128,128]{2,1,0:T(8,128)(2,1)S(1)} %collective-permute-done.refs_3_, ...), custom_call_target="tpu_custom_call" | custom-call | tf_op jit(solution)/shard_map/series/pallas_call | solution.py:392
  49.8 3.6 %collective-permute-start.20 = (bf16[264,128]{1,0:T(8,128)(2,1)S(1)}, bf16[264,128]{1,0:T(8,128)(2,1)S(1)}, u32[]{:S(2)}, u32[]{:S(2)}) collective-permute-start(bf16[264,128]{1,0:T(8,128)(2,1)S(1)} %series.1.refs_0_), channel_id=1, source_target_pairs={{0,16},{2,18},{4,20},{6,22},{8,24},{10,26},{12,28},{14,30},{16,0},... | collective-permute-start | bytes 202760 | tf_op jit(solution)/shard_map/ppermute | solution.py:455
  53.4 0.5 collective-permute-start.19
  53.9 0.2 collective-permute-start.18
  54.0 1.3 %collective-permute-start.17 = (bf16[264,128]{1,0:T(8,128)(2,1)S(1)}, bf16[264,128]{1,0:T(8,128)(2,1)S(1)}, u32[]{:S(2)}, u32[]{:S(2)}) collective-permute-start(bf16[264,128]{1,0:T(8,128)(2,1)S(1)} %series.1.refs_0_), channel_id=1, source_target_pairs={{0,6},{2,4},{4,2},{6,0},{8,14},{10,12},{12,10},{14,8},{16,22},{18,... | collective-permute-start | bytes 202760 | tf_op jit(solution)/shard_map/ppermute | solution.py:452
  55.3 1.7 %collective-permute-start.16 = (bf16[264,128]{1,0:T(8,128)(2,1)S(1)}, bf16[264,128]{1,0:T(8,128)(2,1)S(1)}, u32[]{:S(2)}, u32[]{:S(2)}) collective-permute-start(bf16[264,128]{1,0:T(8,128)(2,1)S(1)} %series.1.refs_0_), channel_id=1, source_target_pairs={{0,4},{2,6},{4,0},{6,2},{8,12},{10,14},{12,8},{14,10},{16,20},{18,... | collective-permute-start | bytes 202760 | tf_op jit(solution)/shard_map/ppermute | solution.py:452
  57.0 0.6 collective-permute-done.20.refs_4_
  57.6 2.3 %collective-permute-done.19.refs_3_ = bf16[264,128]{1,0:T(8,128)(2,1)S(1)} collective-permute-done((bf16[264,128]{1,0:T(8,128)(2,1)S(1)}, bf16[264,128]{1,0:T(8,128)(2,1)S(1)}, u32[]{:S(2)}, u32[]{:S(2)}) %collective-permute-start.19) | collective-permute-done | bytes 67616 | tf_op jit(solution)/shard_map/ppermute | solution.py:455
  59.9 0.2 collective-permute-done.18.refs_2_
  60.1 0.0 collective-permute-done.17.refs_1_
  60.1 0.0 collective-permute-done.16.refs_0_
  60.2 1.3 %collective-permute-start.23 = (bf16[3,264,128]{2,1,0:T(8,128)(2,1)S(1)}, bf16[3,264,128]{2,1,0:T(8,128)(2,1)S(1)}, u32[]{:S(2)}, u32[]{:S(2)}) collective-permute-start(bf16[3,264,128]{2,1,0:T(8,128)(2,1)S(1)} %get-tuple-element.63.refs_4_), channel_id=1, source_target_pairs={{0,6},{2,4},{4,2},{6,0},{8,14},{10,12},{12,10},{14,8},{16,22},{18,... | collective-permute-start | bytes 608264 | tf_op jit(solution)/shard_map/ppermute | solution.py:452
  61.5 1.7 %collective-permute-start.22 = (bf16[3,264,128]{2,1,0:T(8,128)(2,1)S(1)}, bf16[3,264,128]{2,1,0:T(8,128)(2,1)S(1)}, u32[]{:S(2)}, u32[]{:S(2)}) collective-permute-start(bf16[3,264,128]{2,1,0:T(8,128)(2,1)S(1)} %get-tuple-element.63.refs_4_), channel_id=1, source_target_pairs={{0,4},{2,6},{4,0},{6,2},{8,12},{10,14},{12,8},{14,10},{16,20},{18,... | collective-permute-start | bytes 608264 | tf_op jit(solution)/shard_map/ppermute | solution.py:452
  63.2 0.5 collective-permute-start.21
  63.7 1.5 %collective-permute-start.15 = (bf16[264,128]{1,0:T(8,128)(2,1)S(1)}, bf16[264,128]{1,0:T(8,128)(2,1)S(1)}, u32[]{:S(2)}, u32[]{:S(2)}) collective-permute-start(bf16[264,128]{1,0:T(8,128)(2,1)S(1)} %series.1.refs_0_), channel_id=1, source_target_pairs={{0,2},{2,0},{4,6},{6,4},{8,10},{10,8},{12,14},{14,12},{16,18},{18,... | collective-permute-start | bytes 202760 | tf_op jit(solution)/shard_map/ppermute | solution.py:452
  65.2 7.7 %collective-permute-done.15.refs_1_ = bf16[264,128]{1,0:T(8,128)(2,1)S(1)} collective-permute-done((bf16[264,128]{1,0:T(8,128)(2,1)S(1)}, bf16[264,128]{1,0:T(8,128)(2,1)S(1)}, u32[]{:S(2)}, u32[]{:S(2)}) %collective-permute-start.15) | collective-permute-done | bytes 67616 | tf_op jit(solution)/shard_map/ppermute | solution.py:452
  72.9 0.0 collective-permute-done.23.refs_7_
  72.9 0.0 collective-permute-done.22.refs_6_
  72.9 0.0 collective-permute-done.21.refs_5_
  72.9 1.1 %place_walkers.1 = (bf16[32,128,128]{2,1,0:T(8,128)(2,1)}, f32[1,32]{1,0:T(1,128)}) custom-call(bf16[264,128]{1,0:T(8,128)(2,1)S(1)} %series.1.refs_0_, bf16[264,128]{1,0:T(8,128)(2,1)S(1)} %collective-permute-done.15.refs_1_, bf16[264,128]{1,0:T(8,128)(2,1)S(1)} %get-tuple-element.61.refs_2_, bf16[264,128]{1,0:T(8,128)(2,1)S(1)} %get-tuple-element.62.refs_3_, ...), custom_call_target="tpu_custom_call" | custom-call | tf_op jit(solution)/shard_map/place_walkers/pallas_call | solution.py:428
  (2 shorter events, 0.1 us)
Async XLA Ops:
  0.6 10.4 %copy-start = (f32[256,32]{0,1:T(8,128)S(1)}, f32[256,32]{0,1:T(8,128)}, u32[]{:S(2)}) copy-start(f32[256,32]{0,1:T(8,128)} %param.9) | copy-start | bytes 98308
  9.3 1.7 %collective-permute-start = (bf16[2,128,128]{2,1,0:T(8,128)(2,1)S(1)}, bf16[2,128,128]{2,1,0:T(8,128)(2,1)S(1)}, u32[]{:S(2)}, u32[]{:S(2)}) collective-permute-start(bf16[2,128,128]{2,1,0:T(8,128)(2,1)S(1)} %get-tuple-element.58.refs_2_), channel_id=1, source_target_pairs={{1,0},{0,1},{3,2},{2,3},{5,4},{4,5},{7,6},{6,7},{9,8},{8,9},{11,10... | collective-permute-start | bytes 196616 | tf_op jit(solution)/shard_map/ppermute | solution.py:458
  9.8 1.2 %collective-permute-start.1 = (f32[32,256]{1,0:T(8,128)S(1)}, f32[32,256]{1,0:T(8,128)S(1)}, u32[]{:S(2)}, u32[]{:S(2)}) collective-permute-start(f32[32,256]{1,0:T(8,128)S(1)} %get-tuple-element.34.own_ref), channel_id=1, source_target_pairs={{1,0},{0,1},{3,2},{2,3},{5,4},{4,5},{7,6},{6,7},{9,8},{8,9},{11,10... | collective-permute-start | bytes 98312 | tf_op jit(solution)/shard_map/ppermute | solution.py:458
  14.8 19.6 %collective-permute-start.2 = (bf16[3,2,224,128]{3,2,1,0:T(8,128)(2,1)S(1)}, bf16[3,2,224,128]{3,2,1,0:T(8,128)(2,1)S(1)}, u32[]{:S(2)}, u32[]{:S(2)}) collective-permute-start(bf16[3,2,224,128]{3,2,1,0:T(8,128)(2,1)S(1)} %get-tuple-element.40), channel_id=1, source_target_pairs={{0,6},{2,4},{4,2},{6,0},{8,14},{10,12},{12,10},{14,8},{16,22},{18,... | collective-permute-start | bytes 1032200 | tf_op jit(solution)/shard_map/ppermute | solution.py:452
  18.4 16.4 %collective-permute-start.3 = (bf16[3,2,224,128]{3,2,1,0:T(8,128)(2,1)S(1)}, bf16[3,2,224,128]{3,2,1,0:T(8,128)(2,1)S(1)}, u32[]{:S(2)}, u32[]{:S(2)}) collective-permute-start(bf16[3,2,224,128]{3,2,1,0:T(8,128)(2,1)S(1)} %get-tuple-element.41), channel_id=1, source_target_pairs={{0,4},{2,6},{4,0},{6,2},{8,12},{10,14},{12,8},{14,10},{16,20},{18,... | collective-permute-start | bytes 1032200 | tf_op jit(solution)/shard_map/ppermute | solution.py:452
  18.9 16.3 %collective-permute-start.4 = (bf16[3,2,224,128]{3,2,1,0:T(8,128)(2,1)S(1)}, bf16[3,2,224,128]{3,2,1,0:T(8,128)(2,1)S(1)}, u32[]{:S(2)}, u32[]{:S(2)}) collective-permute-start(bf16[3,2,224,128]{3,2,1,0:T(8,128)(2,1)S(1)} %get-tuple-element.42), channel_id=1, source_target_pairs={{0,2},{2,0},{4,6},{6,4},{8,10},{10,8},{12,14},{14,12},{16,18},{18,... | collective-permute-start | bytes 1032200 | tf_op jit(solution)/shard_map/ppermute | solution.py:452
  20.3 5.8 %collective-permute-start.5 = (bf16[4,2,32,128]{3,2,1,0:T(8,128)(2,1)S(1)}, bf16[4,2,32,128]{3,2,1,0:T(8,128)(2,1)S(1)}, u32[]{:S(2)}, u32[]{:S(2)}) collective-permute-start(bf16[4,2,32,128]{3,2,1,0:T(8,128)(2,1)S(1)} %get-tuple-element.44), channel_id=1, source_target_pairs={{0,16},{2,18},{4,20},{6,22},{8,24},{10,26},{12,28},{14,30},{16,0},... | collective-permute-start | bytes 196616 | tf_op jit(solution)/shard_map/ppermute | solution.py:455
  23.3 6.2 %collective-permute-start.6 = (bf16[4,2,32,128]{3,2,1,0:T(8,128)(2,1)S(1)}, bf16[4,2,32,128]{3,2,1,0:T(8,128)(2,1)S(1)}, u32[]{:S(2)}, u32[]{:S(2)}) collective-permute-start(bf16[4,2,32,128]{3,2,1,0:T(8,128)(2,1)S(1)} %get-tuple-element.45), channel_id=1, source_target_pairs={{0,24},{2,26},{4,28},{6,30},{8,16},{10,18},{12,20},{14,22},{16,8},... | collective-permute-start | bytes 196616 | tf_op jit(solution)/shard_map/ppermute | solution.py:455
  26.1 5.1 %collective-permute-start.7 = (bf16[4,2,32,128]{3,2,1,0:T(8,128)(2,1)S(1)}, bf16[4,2,32,128]{3,2,1,0:T(8,128)(2,1)S(1)}, u32[]{:S(2)}, u32[]{:S(2)}) collective-permute-start(bf16[4,2,32,128]{3,2,1,0:T(8,128)(2,1)S(1)} %get-tuple-element.46), channel_id=1, source_target_pairs={{0,8},{2,10},{4,12},{6,14},{8,0},{10,2},{12,4},{14,6},{16,24},{18,... | collective-permute-start | bytes 196616 | tf_op jit(solution)/shard_map/ppermute | solution.py:455
  31.3 8.7 %collective-permute-start.11 = (bf16[2,256,128]{2,1,0:T(8,128)(2,1)S(1)}, bf16[2,256,128]{2,1,0:T(8,128)(2,1)S(1)}, u32[]{:S(2)}, u32[]{:S(2)}) collective-permute-start(bf16[2,256,128]{2,1,0:T(8,128)(2,1)S(1)} %get-tuple-element.55), channel_id=1, source_target_pairs={{0,6},{2,4},{4,2},{6,0},{8,14},{10,12},{12,10},{14,8},{16,22},{18,... | collective-permute-start | bytes 393224 | tf_op jit(solution)/shard_map/ppermute | solution.py:452
  33.8 6.7 %collective-permute-start.12 = (bf16[2,256,128]{2,1,0:T(8,128)(2,1)S(1)}, bf16[2,256,128]{2,1,0:T(8,128)(2,1)S(1)}, u32[]{:S(2)}, u32[]{:S(2)}) collective-permute-start(bf16[2,256,128]{2,1,0:T(8,128)(2,1)S(1)} %get-tuple-element.56), channel_id=1, source_target_pairs={{0,4},{2,6},{4,0},{6,2},{8,12},{10,14},{12,8},{14,10},{16,20},{18,... | collective-permute-start | bytes 393224 | tf_op jit(solution)/shard_map/ppermute | solution.py:452
  34.3 6.2 %collective-permute-start.13 = (bf16[2,256,128]{2,1,0:T(8,128)(2,1)S(1)}, bf16[2,256,128]{2,1,0:T(8,128)(2,1)S(1)}, u32[]{:S(2)}, u32[]{:S(2)}) collective-permute-start(bf16[2,256,128]{2,1,0:T(8,128)(2,1)S(1)} %get-tuple-element.57), channel_id=1, source_target_pairs={{0,2},{2,0},{4,6},{6,4},{8,10},{10,8},{12,14},{14,12},{16,18},{18,... | collective-permute-start | bytes 393224 | tf_op jit(solution)/shard_map/ppermute | solution.py:452
  35.4 11.7 %collective-permute-start.8 = (bf16[2,224,128]{2,1,0:T(8,128)(2,1)S(1)}, bf16[2,224,128]{2,1,0:T(8,128)(2,1)S(1)}, u32[]{:S(2)}, u32[]{:S(2)}) collective-permute-start(bf16[2,224,128]{2,1,0:T(8,128)(2,1)S(1)} %get-tuple-element.52), channel_id=1, source_target_pairs={{0,16},{2,18},{4,20},{6,22},{8,24},{10,26},{12,28},{14,30},{16,0},... | collective-permute-start | bytes 344072 | tf_op jit(solution)/shard_map/ppermute | solution.py:455
  38.5 8.6 %collective-permute-start.9 = (bf16[2,224,128]{2,1,0:T(8,128)(2,1)S(1)}, bf16[2,224,128]{2,1,0:T(8,128)(2,1)S(1)}, u32[]{:S(2)}, u32[]{:S(2)}) collective-permute-start(bf16[2,224,128]{2,1,0:T(8,128)(2,1)S(1)} %get-tuple-element.53), channel_id=1, source_target_pairs={{0,24},{2,26},{4,28},{6,30},{8,16},{10,18},{12,20},{14,22},{16,8},... | collective-permute-start | bytes 344072 | tf_op jit(solution)/shard_map/ppermute | solution.py:455
  40.0 7.2 %collective-permute-start.10 = (bf16[2,224,128]{2,1,0:T(8,128)(2,1)S(1)}, bf16[2,224,128]{2,1,0:T(8,128)(2,1)S(1)}, u32[]{:S(2)}, u32[]{:S(2)}) collective-permute-start(bf16[2,224,128]{2,1,0:T(8,128)(2,1)S(1)} %get-tuple-element.54), channel_id=1, source_target_pairs={{0,8},{2,10},{4,12},{6,14},{8,0},{10,2},{12,4},{14,6},{16,24},{18,... | collective-permute-start | bytes 344072 | tf_op jit(solution)/shard_map/ppermute | solution.py:455
  47.5 1.4 %collective-permute-start.14 = (bf16[2,256,128]{2,1,0:T(8,128)(2,1)S(1)}, bf16[2,256,128]{2,1,0:T(8,128)(2,1)S(1)}, u32[]{:S(2)}, u32[]{:S(2)}) collective-permute-start(bf16[2,256,128]{2,1,0:T(8,128)(2,1)S(1)} %finish.1.refs_0_), channel_id=1, source_target_pairs={{1,0},{0,1},{3,2},{2,3},{5,4},{4,5},{7,6},{6,7},{9,8},{8,9},{11,10... | collective-permute-start | bytes 393224 | tf_op jit(solution)/shard_map/ppermute | solution.py:458
  49.8 7.8 %collective-permute-start.20 = (bf16[264,128]{1,0:T(8,128)(2,1)S(1)}, bf16[264,128]{1,0:T(8,128)(2,1)S(1)}, u32[]{:S(2)}, u32[]{:S(2)}) collective-permute-start(bf16[264,128]{1,0:T(8,128)(2,1)S(1)} %series.1.refs_0_), channel_id=1, source_target_pairs={{0,16},{2,18},{4,20},{6,22},{8,24},{10,26},{12,28},{14,30},{16,0},... | collective-permute-start | bytes 202760 | tf_op jit(solution)/shard_map/ppermute | solution.py:455
  53.4 6.5 %collective-permute-start.19 = (bf16[264,128]{1,0:T(8,128)(2,1)S(1)}, bf16[264,128]{1,0:T(8,128)(2,1)S(1)}, u32[]{:S(2)}, u32[]{:S(2)}) collective-permute-start(bf16[264,128]{1,0:T(8,128)(2,1)S(1)} %series.1.refs_0_), channel_id=1, source_target_pairs={{0,24},{2,26},{4,28},{6,30},{8,16},{10,18},{12,20},{14,22},{16,8},... | collective-permute-start | bytes 202760 | tf_op jit(solution)/shard_map/ppermute | solution.py:455
  53.9 6.2 %collective-permute-start.18 = (bf16[264,128]{1,0:T(8,128)(2,1)S(1)}, bf16[264,128]{1,0:T(8,128)(2,1)S(1)}, u32[]{:S(2)}, u32[]{:S(2)}) collective-permute-start(bf16[264,128]{1,0:T(8,128)(2,1)S(1)} %series.1.refs_0_), channel_id=1, source_target_pairs={{0,8},{2,10},{4,12},{6,14},{8,0},{10,2},{12,4},{14,6},{16,24},{18,... | collective-permute-start | bytes 202760 | tf_op jit(solution)/shard_map/ppermute | solution.py:455
  54.0 6.1 %collective-permute-start.17 = (bf16[264,128]{1,0:T(8,128)(2,1)S(1)}, bf16[264,128]{1,0:T(8,128)(2,1)S(1)}, u32[]{:S(2)}, u32[]{:S(2)}) collective-permute-start(bf16[264,128]{1,0:T(8,128)(2,1)S(1)} %series.1.refs_0_), channel_id=1, source_target_pairs={{0,6},{2,4},{4,2},{6,0},{8,14},{10,12},{12,10},{14,8},{16,22},{18,... | collective-permute-start | bytes 202760 | tf_op jit(solution)/shard_map/ppermute | solution.py:452
  55.3 4.8 %collective-permute-start.16 = (bf16[264,128]{1,0:T(8,128)(2,1)S(1)}, bf16[264,128]{1,0:T(8,128)(2,1)S(1)}, u32[]{:S(2)}, u32[]{:S(2)}) collective-permute-start(bf16[264,128]{1,0:T(8,128)(2,1)S(1)} %series.1.refs_0_), channel_id=1, source_target_pairs={{0,4},{2,6},{4,0},{6,2},{8,12},{10,14},{12,8},{14,10},{16,20},{18,... | collective-permute-start | bytes 202760 | tf_op jit(solution)/shard_map/ppermute | solution.py:452
  60.2 12.8 %collective-permute-start.23 = (bf16[3,264,128]{2,1,0:T(8,128)(2,1)S(1)}, bf16[3,264,128]{2,1,0:T(8,128)(2,1)S(1)}, u32[]{:S(2)}, u32[]{:S(2)}) collective-permute-start(bf16[3,264,128]{2,1,0:T(8,128)(2,1)S(1)} %get-tuple-element.63.refs_4_), channel_id=1, source_target_pairs={{0,6},{2,4},{4,2},{6,0},{8,14},{10,12},{12,10},{14,8},{16,22},{18,... | collective-permute-start | bytes 608264 | tf_op jit(solution)/shard_map/ppermute | solution.py:452
  61.5 11.4 %collective-permute-start.22 = (bf16[3,264,128]{2,1,0:T(8,128)(2,1)S(1)}, bf16[3,264,128]{2,1,0:T(8,128)(2,1)S(1)}, u32[]{:S(2)}, u32[]{:S(2)}) collective-permute-start(bf16[3,264,128]{2,1,0:T(8,128)(2,1)S(1)} %get-tuple-element.63.refs_4_), channel_id=1, source_target_pairs={{0,4},{2,6},{4,0},{6,2},{8,12},{10,14},{12,8},{14,10},{16,20},{18,... | collective-permute-start | bytes 608264 | tf_op jit(solution)/shard_map/ppermute | solution.py:452
  63.2 9.8 %collective-permute-start.21 = (bf16[3,264,128]{2,1,0:T(8,128)(2,1)S(1)}, bf16[3,264,128]{2,1,0:T(8,128)(2,1)S(1)}, u32[]{:S(2)}, u32[]{:S(2)}) collective-permute-start(bf16[3,264,128]{2,1,0:T(8,128)(2,1)S(1)} %get-tuple-element.63.refs_4_), channel_id=1, source_target_pairs={{0,2},{2,0},{4,6},{6,4},{8,10},{10,8},{12,14},{14,12},{16,18},{18,... | collective-permute-start | bytes 608264 | tf_op jit(solution)/shard_map/ppermute | solution.py:452
  63.7 9.2 %collective-permute-start.15 = (bf16[264,128]{1,0:T(8,128)(2,1)S(1)}, bf16[264,128]{1,0:T(8,128)(2,1)S(1)}, u32[]{:S(2)}, u32[]{:S(2)}) collective-permute-start(bf16[264,128]{1,0:T(8,128)(2,1)S(1)} %series.1.refs_0_), channel_id=1, source_target_pairs={{0,2},{2,0},{4,6},{6,4},{8,10},{10,8},{12,14},{14,12},{16,18},{18,... | collective-permute-start | bytes 202760 | tf_op jit(solution)/shard_map/ppermute | solution.py:452

commit v15 on v13

--- a/solution.py
+++ b/solution.py
@@ -58,8 +58,8 @@
     return [cols == column for column in column_order(row)[1:]]
 
 
-def bias_kernel(vals_hbm, greens_hbm, walkers_hbm, cols_hbm, turned_ref, bias_ref, mine_ref, cols_ref, vals, greens, swap, gs,
-                acc, vsem, gsem, wsem, csem):
+def bias_kernel(vals_hbm, greens_hbm, walkers_hbm, cols_hbm, turned_ref, bias_ref, mine_ref, cols_ref, vals, greens, swap, packed,
+                gs, acc, vsem, gsem, wsem, csem):
     total_steps, vectors = turned_ref.shape[:2]
     walk = bias_ref.shape[0]
     steps = BLOCK // CHUNK
@@ -84,7 +84,9 @@
     lax.fori_loop(0, total_steps, begin, 0)
     swap[...] = swap_matrix()
     bias_ref[...] = jnp.zeros_like(bias_ref)
-    first = lax.broadcasted_iota(jnp.int32, (CHUNK * CHUNK, LANES), 1) < BLOCK
+    first = lax.broadcasted_iota(jnp.int32, (CHUNK, LANES), 1) < BLOCK
+    kept_shape = (LANES, 4 * walk)
+    kept = (lax.broadcasted_iota(jnp.int32, kept_shape, 0) < BLOCK) == (lax.broadcasted_iota(jnp.int32, kept_shape, 1) < walk)
 
     def step(t, side):
         for copy in copies(t):
@@ -99,18 +101,23 @@
             pair = jnp.where(upper, mixed[:, LANES:], mixed[:, :LANES])
             rest = jnp.where(upper, mixed[:, :LANES], mixed[:, LANES:])
             pair = jnp.where(odd, pltpu.roll(pair, BLOCK, 1), pair)
-            pieces = (
-                jnp.where(first, pair, 0.0),
-                jnp.where(first, 0.0, pair),
-                jnp.where(first, 0.0, pltpu.roll(rest, BLOCK, 1)),
-                jnp.where(first, 0.0, rest),
-            )
-            for k, piece in enumerate(pieces):
-                piece = piece.astype(jnp.bfloat16)
-                for i in range(CHUNK):
-                    gs[side, k * walk + w:k * walk + w + CHUNK, i * LANES:(i + 1) * LANES] = (
-                        piece[i * CHUNK:(i + 1) * CHUNK]
-                    )
+            pair_turned = pltpu.roll(pair, BLOCK, 1)
+            rest_turned = pltpu.roll(rest, BLOCK, 1)
+            for i in range(0, CHUNK, 2):
+                even, odd_row = slice(i * CHUNK, (i + 1) * CHUNK), slice((i + 1) * CHUNK, (i + 2) * CHUNK)
+                pieces = (
+                    jnp.where(first, pair[even], pair_turned[odd_row]),
+                    jnp.where(first, pair_turned[odd_row], pair[even]),
+                    jnp.where(first, rest[odd_row], rest_turned[even]),
+                    jnp.where(first, rest_turned[odd_row], rest[even]),
+                )
+                for k, piece in enumerate(pieces):
+                    packed[side, i // 2, k * walk + w:k * walk + w + CHUNK, :] = piece.astype(jnp.bfloat16)
+        for i in range(0, CHUNK, 2):
+            both = packed[side, i // 2].T.astype(jnp.float32)
+            swapped = jnp.concatenate([both[BLOCK:], both[:BLOCK]], axis=0)
+            gs[side, i * LANES:(i + 1) * LANES] = jnp.where(kept, both, 0.0).astype(jnp.bfloat16)
+            gs[side, (i + 1) * LANES:(i + 2) * LANES] = jnp.where(kept, swapped, 0.0).astype(jnp.bfloat16)
         for g in range(0, vectors, 2 * CHUNK):
             both = [vals[t, g + k * CHUNK:g + (k + 1) * CHUNK].reshape(CHUNK * CHUNK, LANES) for k in range(2)]
             both = jnp.dot(swap[...], jnp.concatenate(both, axis=1), preferred_element_type=jnp.float32)
@@ -121,7 +128,7 @@
                         both[i * CHUNK:(i + 1) * CHUNK, k * LANES:(k + 1) * LANES]
                     )
         part = lax.dot_general(
-            turned_ref[t], gs[side], (((1,), (1,)), ((), ())), preferred_element_type=jnp.float32
+            turned_ref[t], gs[side], (((1,), (0,)), ((), ())), preferred_element_type=jnp.float32
         )
         begins = lax.rem(t, steps) == 0
         acc[...] = jnp.where(begins, 0.0, acc[...]) + part
@@ -167,7 +174,8 @@
             pltpu.VMEM((steps, vectors, CHUNK, LANES), jnp.bfloat16),
             pltpu.VMEM((steps, walk, CHUNK, norb), jnp.bfloat16),
             pltpu.VMEM((CHUNK * CHUNK, CHUNK * CHUNK), jnp.bfloat16),
-            pltpu.VMEM((2, 4 * walk, wide), jnp.bfloat16),
+            pltpu.VMEM((2, CHUNK // 2, 4 * walk, LANES), jnp.bfloat16),
+            pltpu.VMEM((2, wide, 4 * walk), jnp.bfloat16),
             pltpu.VMEM((vectors, 4 * walk), jnp.float32),
             pltpu.SemaphoreType.DMA((steps,)),
             pltpu.SemaphoreType.DMA((steps,)),

time: 73.9 us -> 75.7 us (1.024)
  Pallas kernels: 15.7 us -> 17.5 us
    pallas_call x1, Pallas kernels: 8.42 us -> 10.2 us  [bias_call(): pl.pallas_call(bias_kernel, in_specs=[*[pl.BlockSpec(memory_space=pl.ANY)...]
where the time goes in v15:
time: 75.7 us; the launch traced here: 75.5 us
  starting transfers between devices  33.2 us (44%)
  waiting for transfers between devices  24.1 us (32%)
  Pallas kernels  17.5 us (23%)
    ppermute x9, starting transfers between devices, to_z(): lax.ppermute(a, 'chol', [(c, hop(c // plane, dz, nz) * plane + c % plane)...  16.6 us
    ppermute x12, starting transfers between devices, to_plane(): lax.ppermute(a, 'chol', [(c, c // plane * plane + hop(c % plane, dp, plan...  16 us
    ppermute x9, waiting for transfers between devices, to_z(): lax.ppermute(a, 'chol', [(c, hop(c // plane, dz, nz) * plane + c % plane)...  13.5 us
    pallas_call x1, Pallas kernels, bias_call(): pl.pallas_call(bias_kernel, in_specs=[*[pl.BlockSpec(memory_space=pl.ANY)...  10.2 us
    ppermute x12, waiting for transfers between devices, to_plane(): lax.ppermute(a, 'chol', [(c, c // plane * plane + hop(c % plane, dp, plan...  8.14 us
    pallas_call x2, Pallas kernels, potential_call(): pl.pallas_call(functools.partial(potential_kernel, begin, end, layout, by...  4.96 us
    ppermute x3, waiting for transfers between devices, around_orb(): lax.ppermute(a, 'orb', [((c + d) % n_orb, c) for c in range(n_orb)])  2.47 us
  transfers between devices with their start and end apart: 24, of which 12 were waited for; matrix products, arithmetic and copies ran while one was open for 0% of the time, Pallas kernels for 2%

profile of v15, /device:TPU:0, one launch (start us, length us, event | category | flops | bytes accessed | tf_op | source)
XLA Modules:
  0.0 75.5 jit_solution(141124568972827059)
XLA Ops:
  0.6 0.0 copy-start
  0.6 10.2 %force_bias.1 = (bf16[8,256,2048]{2,1,0:T(8,128)(2,1)S(1)}, f32[32,256]{1,0:T(8,128)S(1)}, bf16[2,128,128]{2,1,0:T(8,128)(2,1)S(1)}, s32[2,2,256]{2,1,0:T(2,128)S(1)}) custom-call(bf16[256,2,64,128]{3,2,1,0:T(8,128)(2,1)} %vals_hbm.1, bf16[32,128,256]{2,1,0:T(8,128)(2,1)} %greens_hbm.1, bf16[32,128,128]{2,1,0:T(8,128)(2,1)} %walkers_hbm.1, s32[2,2,256]{2,1,0:T(2,128)} %bitcast.5), custom_call_target="tpu_custom_call" | custom-call | tf_op jit(solution)/shard_map/force_bias/pallas_call | solution.py:161
  10.8 0.5 collective-permute-start
  11.3 0.1 collective-permute-start.1
  11.4 1.1 %collective-permute-done.1.refs_0_ = f32[32,256]{1,0:T(8,128)S(1)} collective-permute-done((f32[32,256]{1,0:T(8,128)S(1)}, f32[32,256]{1,0:T(8,128)S(1)}, u32[]{:S(2)}, u32[]{:S(2)}) %collective-permute-start.1) | collective-permute-done | bytes 32800 | tf_op jit(solution)/shard_map/ppermute | solution.py:461
  12.5 0.0 collective-permute-done.refs_3_
  12.5 0.0 copy-done
  12.6 3.7 %potential.2 = (bf16[3,2,224,128]{3,2,1,0:T(8,128)(2,1)S(1)}, bf16[3,2,224,128]{3,2,1,0:T(8,128)(2,1)S(1)}, bf16[3,2,224,128]{3,2,1,0:T(8,128)(2,1)S(1)}, bf16[3...) custom-call(f32[32,256]{1,0:T(8,128)S(1)} %bitcast.3, ...), custom_call_target="tpu_custom_call" | custom-call | tf_op jit(solution)/shard_map/potential/pallas_call | solution.py:273
  16.3 3.7 %collective-permute-start.2 = (bf16[3,2,224,128]{3,2,1,0:T(8,128)(2,1)S(1)}, bf16[3,2,224,128]{3,2,1,0:T(8,128)(2,1)S(1)}, u32[]{:S(2)}, u32[]{:S(2)}) collective-permute-start(bf16[3,2,224,128]{3,2,1,0:T(8,128)(2,1)S(1)} %get-tuple-element.40), channel_id=1, source_target_pairs={{0,6},{2,4},{4,2},{6,0},{8,14},{10,12},{12,10},{14,8},{16,22},{18,... | collective-permute-start | bytes 1032200 | tf_op jit(solution)/shard_map/ppermute | solution.py:455
  20.0 0.5 collective-permute-start.3
  20.5 0.2 collective-permute-start.4
  20.6 1.2 %potential.3 = (bf16[4,2,32,128]{3,2,1,0:T(8,128)(2,1)S(1)}, bf16[4,2,32,128]{3,2,1,0:T(8,128)(2,1)S(1)}, bf16[4,2,32,128]{3,2,1,0:T(8,128)(2,1)S(1)}, bf16[4,2,32,128]{3,2,1,0:T(8,128)(2,1)S(1)}, f32[16,128]{1,0:T(8,128)}) custom-call(f32[32,256]{1,0:T(8,128)S(1)} %bitcast.4, f32[32,256]{1,0:T(8,128)S(1)} %get-tuple-element.34.own_ref, ...), custom_call_target="tpu_custom_call" | custom-call | tf_op jit(solution)/shard_map/potential/pallas_call | solution.py:273
  21.8 3.0 %collective-permute-start.5 = (bf16[4,2,32,128]{3,2,1,0:T(8,128)(2,1)S(1)}, bf16[4,2,32,128]{3,2,1,0:T(8,128)(2,1)S(1)}, u32[]{:S(2)}, u32[]{:S(2)}) collective-permute-start(bf16[4,2,32,128]{3,2,1,0:T(8,128)(2,1)S(1)} %get-tuple-element.44), channel_id=1, source_target_pairs={{0,16},{2,18},{4,20},{6,22},{8,24},{10,26},{12,28},{14,30},{16,0},... | collective-permute-start | bytes 196616 | tf_op jit(solution)/shard_map/ppermute | solution.py:458
  24.8 1.3 %collective-permute-start.6 = (bf16[4,2,32,128]{3,2,1,0:T(8,128)(2,1)S(1)}, bf16[4,2,32,128]{3,2,1,0:T(8,128)(2,1)S(1)}, u32[]{:S(2)}, u32[]{:S(2)}) collective-permute-start(bf16[4,2,32,128]{3,2,1,0:T(8,128)(2,1)S(1)} %get-tuple-element.45), channel_id=1, source_target_pairs={{0,24},{2,26},{4,28},{6,30},{8,16},{10,18},{12,20},{14,22},{16,8},... | collective-permute-start | bytes 196616 | tf_op jit(solution)/shard_map/ppermute | solution.py:458
  26.1 1.5 %collective-permute-done.5.refs_1_ = bf16[4,2,32,128]{3,2,1,0:T(8,128)(2,1)S(1)} collective-permute-done((bf16[4,2,32,128]{3,2,1,0:T(8,128)(2,1)S(1)}, bf16[4,2,32,128]{3,2,1,0:T(8,128)(2,1)S(1)}, u32[]{:S(2)}, u32[]{:S(2)}) %collective-permute-start.5) | collective-permute-done | bytes 65568 | tf_op jit(solution)/shard_map/ppermute | solution.py:458
  27.6 2.9 %collective-permute-start.7 = (bf16[4,2,32,128]{3,2,1,0:T(8,128)(2,1)S(1)}, bf16[4,2,32,128]{3,2,1,0:T(8,128)(2,1)S(1)}, u32[]{:S(2)}, u32[]{:S(2)}) collective-permute-start(bf16[4,2,32,128]{3,2,1,0:T(8,128)(2,1)S(1)} %get-tuple-element.46), channel_id=1, source_target_pairs={{0,8},{2,10},{4,12},{6,14},{8,0},{10,2},{12,4},{14,6},{16,24},{18,... | collective-permute-start | bytes 196616 | tf_op jit(solution)/shard_map/ppermute | solution.py:458
  30.5 0.5 collective-permute-done.6.refs_2_
  31.0 1.7 %collective-permute-done.7.refs_3_ = bf16[4,2,32,128]{3,2,1,0:T(8,128)(2,1)S(1)} collective-permute-done((bf16[4,2,32,128]{3,2,1,0:T(8,128)(2,1)S(1)}, bf16[4,2,32,128]{3,2,1,0:T(8,128)(2,1)S(1)}, u32[]{:S(2)}, u32[]{:S(2)}) %collective-permute-start.7) | collective-permute-done | bytes 65568 | tf_op jit(solution)/shard_map/ppermute | solution.py:458
  32.8 2.5 %collective-permute-start.11 = (bf16[2,256,128]{2,1,0:T(8,128)(2,1)S(1)}, bf16[2,256,128]{2,1,0:T(8,128)(2,1)S(1)}, u32[]{:S(2)}, u32[]{:S(2)}) collective-permute-start(bf16[2,256,128]{2,1,0:T(8,128)(2,1)S(1)} %get-tuple-element.55), channel_id=1, source_target_pairs={{0,6},{2,4},{4,2},{6,0},{8,14},{10,12},{12,10},{14,8},{16,22},{18,... | collective-permute-start | bytes 393224 | tf_op jit(solution)/shard_map/ppermute | solution.py:455
  35.3 0.5 collective-permute-start.12
  35.8 0.0 collective-permute-done.2.refs_1_
  35.8 0.5 collective-permute-start.13
  36.4 0.0 collective-permute-done.3.refs_2_
  36.4 0.4 collective-permute-done.4.refs_3_
  36.8 0.2 sum_parts.1
  36.9 3.1 %collective-permute-start.8 = (bf16[2,224,128]{2,1,0:T(8,128)(2,1)S(1)}, bf16[2,224,128]{2,1,0:T(8,128)(2,1)S(1)}, u32[]{:S(2)}, u32[]{:S(2)}) collective-permute-start(bf16[2,224,128]{2,1,0:T(8,128)(2,1)S(1)} %get-tuple-element.52), channel_id=1, source_target_pairs={{0,16},{2,18},{4,20},{6,22},{8,24},{10,26},{12,28},{14,30},{16,0},... | collective-permute-start | bytes 344072 | tf_op jit(solution)/shard_map/ppermute | solution.py:458
  40.0 1.5 %collective-permute-start.9 = (bf16[2,224,128]{2,1,0:T(8,128)(2,1)S(1)}, bf16[2,224,128]{2,1,0:T(8,128)(2,1)S(1)}, u32[]{:S(2)}, u32[]{:S(2)}) collective-permute-start(bf16[2,224,128]{2,1,0:T(8,128)(2,1)S(1)} %get-tuple-element.53), channel_id=1, source_target_pairs={{0,24},{2,26},{4,28},{6,30},{8,16},{10,18},{12,20},{14,22},{16,8},... | collective-permute-start | bytes 344072 | tf_op jit(solution)/shard_map/ppermute | solution.py:458
  41.5 0.0 collective-permute-done.11.refs_4_
  41.5 0.5 collective-permute-start.10
  42.0 0.0 collective-permute-done.12.refs_5_
  42.0 0.0 collective-permute-done.13.refs_6_
  42.0 6.6 %collective-permute-done.8.refs_0_ = bf16[2,224,128]{2,1,0:T(8,128)(2,1)S(1)} collective-permute-done((bf16[2,224,128]{2,1,0:T(8,128)(2,1)S(1)}, bf16[2,224,128]{2,1,0:T(8,128)(2,1)S(1)}, u32[]{:S(2)}, u32[]{:S(2)}) %collective-permute-start.8) | collective-permute-done | bytes 114720 | tf_op jit(solution)/shard_map/ppermute | solution.py:458
  48.6 0.0 collective-permute-done.9.refs_1_
  48.6 0.2 collective-permute-done.10.refs_2_
  48.8 0.2 finish.1.refs_0_
  49.0 0.1 collective-permute-start.14
  49.0 1.3 %collective-permute-done.14.refs_1_ = bf16[2,256,128]{2,1,0:T(8,128)(2,1)S(1)} collective-permute-done((bf16[2,256,128]{2,1,0:T(8,128)(2,1)S(1)}, bf16[2,256,128]{2,1,0:T(8,128)(2,1)S(1)}, u32[]{:S(2)}, u32[]{:S(2)}) %collective-permute-start.14) | collective-permute-done | bytes 131104 | tf_op jit(solution)/shard_map/ppermute | solution.py:461
  50.4 0.9 %series.1.refs_0_ = bf16[264,128]{1,0:T(8,128)(2,1)S(1)} custom-call(bf16[2,256,128]{2,1,0:T(8,128)(2,1)S(1)} %finish.1.refs_0_, bf16[2,256,128]{2,1,0:T(8,128)(2,1)S(1)} %collective-permute-done.14.refs_1_, bf16[2,128,128]{2,1,0:T(8,128)(2,1)S(1)} %get-tuple-element.58.refs_2_, bf16[2,128,128]{2,1,0:T(8,128)(2,1)S(1)} %collective-permute-done.refs_3_, ...), custom_call_target="tpu_custom_call" | custom-call | tf_op jit(solution)/shard_map/series/pallas_call | solution.py:395
  51.3 3.6 %collective-permute-start.20 = (bf16[264,128]{1,0:T(8,128)(2,1)S(1)}, bf16[264,128]{1,0:T(8,128)(2,1)S(1)}, u32[]{:S(2)}, u32[]{:S(2)}) collective-permute-start(bf16[264,128]{1,0:T(8,128)(2,1)S(1)} %series.1.refs_0_), channel_id=1, source_target_pairs={{0,16},{2,18},{4,20},{6,22},{8,24},{10,26},{12,28},{14,30},{16,0},... | collective-permute-start | bytes 202760 | tf_op jit(solution)/shard_map/ppermute | solution.py:458
  54.9 0.5 collective-permute-start.19
  55.4 0.2 collective-permute-start.18
  55.6 1.3 %collective-permute-start.17 = (bf16[264,128]{1,0:T(8,128)(2,1)S(1)}, bf16[264,128]{1,0:T(8,128)(2,1)S(1)}, u32[]{:S(2)}, u32[]{:S(2)}) collective-permute-start(bf16[264,128]{1,0:T(8,128)(2,1)S(1)} %series.1.refs_0_), channel_id=1, source_target_pairs={{0,6},{2,4},{4,2},{6,0},{8,14},{10,12},{12,10},{14,8},{16,22},{18,... | collective-permute-start | bytes 202760 | tf_op jit(solution)/shard_map/ppermute | solution.py:455
  56.8 1.7 %collective-permute-start.16 = (bf16[264,128]{1,0:T(8,128)(2,1)S(1)}, bf16[264,128]{1,0:T(8,128)(2,1)S(1)}, u32[]{:S(2)}, u32[]{:S(2)}) collective-permute-start(bf16[264,128]{1,0:T(8,128)(2,1)S(1)} %series.1.refs_0_), channel_id=1, source_target_pairs={{0,4},{2,6},{4,0},{6,2},{8,12},{10,14},{12,8},{14,10},{16,20},{18,... | collective-permute-start | bytes 202760 | tf_op jit(solution)/shard_map/ppermute | solution.py:455
  58.6 0.5 collective-permute-done.20.refs_4_
  59.1 2.3 %collective-permute-done.19.refs_3_ = bf16[264,128]{1,0:T(8,128)(2,1)S(1)} collective-permute-done((bf16[264,128]{1,0:T(8,128)(2,1)S(1)}, bf16[264,128]{1,0:T(8,128)(2,1)S(1)}, u32[]{:S(2)}, u32[]{:S(2)}) %collective-permute-start.19) | collective-permute-done | bytes 67616 | tf_op jit(solution)/shard_map/ppermute | solution.py:458
  61.4 0.2 collective-permute-done.18.refs_2_
  61.6 0.0 collective-permute-done.17.refs_1_
  61.6 0.0 collective-permute-done.16.refs_0_
  61.7 1.3 %collective-permute-start.23 = (bf16[3,264,128]{2,1,0:T(8,128)(2,1)S(1)}, bf16[3,264,128]{2,1,0:T(8,128)(2,1)S(1)}, u32[]{:S(2)}, u32[]{:S(2)}) collective-permute-start(bf16[3,264,128]{2,1,0:T(8,128)(2,1)S(1)} %get-tuple-element.63.refs_4_), channel_id=1, source_target_pairs={{0,6},{2,4},{4,2},{6,0},{8,14},{10,12},{12,10},{14,8},{16,22},{18,... | collective-permute-start | bytes 608264 | tf_op jit(solution)/shard_map/ppermute | solution.py:455
  63.0 1.7 %collective-permute-start.22 = (bf16[3,264,128]{2,1,0:T(8,128)(2,1)S(1)}, bf16[3,264,128]{2,1,0:T(8,128)(2,1)S(1)}, u32[]{:S(2)}, u32[]{:S(2)}) collective-permute-start(bf16[3,264,128]{2,1,0:T(8,128)(2,1)S(1)} %get-tuple-element.63.refs_4_), channel_id=1, source_target_pairs={{0,4},{2,6},{4,0},{6,2},{8,12},{10,14},{12,8},{14,10},{16,20},{18,... | collective-permute-start | bytes 608264 | tf_op jit(solution)/shard_map/ppermute | solution.py:455
  64.7 0.5 collective-permute-start.21
  65.2 1.5 %collective-permute-start.15 = (bf16[264,128]{1,0:T(8,128)(2,1)S(1)}, bf16[264,128]{1,0:T(8,128)(2,1)S(1)}, u32[]{:S(2)}, u32[]{:S(2)}) collective-permute-start(bf16[264,128]{1,0:T(8,128)(2,1)S(1)} %series.1.refs_0_), channel_id=1, source_target_pairs={{0,2},{2,0},{4,6},{6,4},{8,10},{10,8},{12,14},{14,12},{16,18},{18,... | collective-permute-start | bytes 202760 | tf_op jit(solution)/shard_map/ppermute | solution.py:455
  66.7 7.7 %collective-permute-done.15.refs_1_ = bf16[264,128]{1,0:T(8,128)(2,1)S(1)} collective-permute-done((bf16[264,128]{1,0:T(8,128)(2,1)S(1)}, bf16[264,128]{1,0:T(8,128)(2,1)S(1)}, u32[]{:S(2)}, u32[]{:S(2)}) %collective-permute-start.15) | collective-permute-done | bytes 67616 | tf_op jit(solution)/shard_map/ppermute | solution.py:455
  74.4 0.0 collective-permute-done.23.refs_7_
  74.5 0.0 collective-permute-done.22.refs_6_
  74.5 0.0 collective-permute-done.21.refs_5_
  74.5 1.1 %place_walkers.1 = (bf16[32,128,128]{2,1,0:T(8,128)(2,1)}, f32[1,32]{1,0:T(1,128)}) custom-call(bf16[264,128]{1,0:T(8,128)(2,1)S(1)} %series.1.refs_0_, bf16[264,128]{1,0:T(8,128)(2,1)S(1)} %collective-permute-done.15.refs_1_, bf16[264,128]{1,0:T(8,128)(2,1)S(1)} %get-tuple-element.61.refs_2_, bf16[264,128]{1,0:T(8,128)(2,1)S(1)} %get-tuple-element.62.refs_3_, ...), custom_call_target="tpu_custom_call" | custom-call | tf_op jit(solution)/shard_map/place_walkers/pallas_call | solution.py:431
  (2 shorter events, 0.1 us)
Async XLA Ops:
  0.6 11.9 %copy-start = (f32[256,32]{0,1:T(8,128)S(1)}, f32[256,32]{0,1:T(8,128)}, u32[]{:S(2)}) copy-start(f32[256,32]{0,1:T(8,128)} %param.9) | copy-start | bytes 98308
  10.8 1.7 %collective-permute-start = (bf16[2,128,128]{2,1,0:T(8,128)(2,1)S(1)}, bf16[2,128,128]{2,1,0:T(8,128)(2,1)S(1)}, u32[]{:S(2)}, u32[]{:S(2)}) collective-permute-start(bf16[2,128,128]{2,1,0:T(8,128)(2,1)S(1)} %get-tuple-element.58.refs_2_), channel_id=1, source_target_pairs={{1,0},{0,1},{3,2},{2,3},{5,4},{4,5},{7,6},{6,7},{9,8},{8,9},{11,10... | collective-permute-start | bytes 196616 | tf_op jit(solution)/shard_map/ppermute | solution.py:461
  11.3 1.2 %collective-permute-start.1 = (f32[32,256]{1,0:T(8,128)S(1)}, f32[32,256]{1,0:T(8,128)S(1)}, u32[]{:S(2)}, u32[]{:S(2)}) collective-permute-start(f32[32,256]{1,0:T(8,128)S(1)} %get-tuple-element.34.own_ref), channel_id=1, source_target_pairs={{1,0},{0,1},{3,2},{2,3},{5,4},{4,5},{7,6},{6,7},{9,8},{8,9},{11,10... | collective-permute-start | bytes 98312 | tf_op jit(solution)/shard_map/ppermute | solution.py:461
  16.3 19.5 %collective-permute-start.2 = (bf16[3,2,224,128]{3,2,1,0:T(8,128)(2,1)S(1)}, bf16[3,2,224,128]{3,2,1,0:T(8,128)(2,1)S(1)}, u32[]{:S(2)}, u32[]{:S(2)}) collective-permute-start(bf16[3,2,224,128]{3,2,1,0:T(8,128)(2,1)S(1)} %get-tuple-element.40), channel_id=1, source_target_pairs={{0,6},{2,4},{4,2},{6,0},{8,14},{10,12},{12,10},{14,8},{16,22},{18,... | collective-permute-start | bytes 1032200 | tf_op jit(solution)/shard_map/ppermute | solution.py:455
  20.0 16.4 %collective-permute-start.3 = (bf16[3,2,224,128]{3,2,1,0:T(8,128)(2,1)S(1)}, bf16[3,2,224,128]{3,2,1,0:T(8,128)(2,1)S(1)}, u32[]{:S(2)}, u32[]{:S(2)}) collective-permute-start(bf16[3,2,224,128]{3,2,1,0:T(8,128)(2,1)S(1)} %get-tuple-element.41), channel_id=1, source_target_pairs={{0,4},{2,6},{4,0},{6,2},{8,12},{10,14},{12,8},{14,10},{16,20},{18,... | collective-permute-start | bytes 1032200 | tf_op jit(solution)/shard_map/ppermute | solution.py:455
  20.5 16.3 %collective-permute-start.4 = (bf16[3,2,224,128]{3,2,1,0:T(8,128)(2,1)S(1)}, bf16[3,2,224,128]{3,2,1,0:T(8,128)(2,1)S(1)}, u32[]{:S(2)}, u32[]{:S(2)}) collective-permute-start(bf16[3,2,224,128]{3,2,1,0:T(8,128)(2,1)S(1)} %get-tuple-element.42), channel_id=1, source_target_pairs={{0,2},{2,0},{4,6},{6,4},{8,10},{10,8},{12,14},{14,12},{16,18},{18,... | collective-permute-start | bytes 1032200 | tf_op jit(solution)/shard_map/ppermute | solution.py:455
  21.8 5.8 %collective-permute-start.5 = (bf16[4,2,32,128]{3,2,1,0:T(8,128)(2,1)S(1)}, bf16[4,2,32,128]{3,2,1,0:T(8,128)(2,1)S(1)}, u32[]{:S(2)}, u32[]{:S(2)}) collective-permute-start(bf16[4,2,32,128]{3,2,1,0:T(8,128)(2,1)S(1)} %get-tuple-element.44), channel_id=1, source_target_pairs={{0,16},{2,18},{4,20},{6,22},{8,24},{10,26},{12,28},{14,30},{16,0},... | collective-permute-start | bytes 196616 | tf_op jit(solution)/shard_map/ppermute | solution.py:458
  24.8 6.2 %collective-permute-start.6 = (bf16[4,2,32,128]{3,2,1,0:T(8,128)(2,1)S(1)}, bf16[4,2,32,128]{3,2,1,0:T(8,128)(2,1)S(1)}, u32[]{:S(2)}, u32[]{:S(2)}) collective-permute-start(bf16[4,2,32,128]{3,2,1,0:T(8,128)(2,1)S(1)} %get-tuple-element.45), channel_id=1, source_target_pairs={{0,24},{2,26},{4,28},{6,30},{8,16},{10,18},{12,20},{14,22},{16,8},... | collective-permute-start | bytes 196616 | tf_op jit(solution)/shard_map/ppermute | solution.py:458
  27.6 5.1 %collective-permute-start.7 = (bf16[4,2,32,128]{3,2,1,0:T(8,128)(2,1)S(1)}, bf16[4,2,32,128]{3,2,1,0:T(8,128)(2,1)S(1)}, u32[]{:S(2)}, u32[]{:S(2)}) collective-permute-start(bf16[4,2,32,128]{3,2,1,0:T(8,128)(2,1)S(1)} %get-tuple-element.46), channel_id=1, source_target_pairs={{0,8},{2,10},{4,12},{6,14},{8,0},{10,2},{12,4},{14,6},{16,24},{18,... | collective-permute-start | bytes 196616 | tf_op jit(solution)/shard_map/ppermute | solution.py:458
  32.8 8.7 %collective-permute-start.11 = (bf16[2,256,128]{2,1,0:T(8,128)(2,1)S(1)}, bf16[2,256,128]{2,1,0:T(8,128)(2,1)S(1)}, u32[]{:S(2)}, u32[]{:S(2)}) collective-permute-start(bf16[2,256,128]{2,1,0:T(8,128)(2,1)S(1)} %get-tuple-element.55), channel_id=1, source_target_pairs={{0,6},{2,4},{4,2},{6,0},{8,14},{10,12},{12,10},{14,8},{16,22},{18,... | collective-permute-start | bytes 393224 | tf_op jit(solution)/shard_map/ppermute | solution.py:455
  35.3 6.7 %collective-permute-start.12 = (bf16[2,256,128]{2,1,0:T(8,128)(2,1)S(1)}, bf16[2,256,128]{2,1,0:T(8,128)(2,1)S(1)}, u32[]{:S(2)}, u32[]{:S(2)}) collective-permute-start(bf16[2,256,128]{2,1,0:T(8,128)(2,1)S(1)} %get-tuple-element.56), channel_id=1, source_target_pairs={{0,4},{2,6},{4,0},{6,2},{8,12},{10,14},{12,8},{14,10},{16,20},{18,... | collective-permute-start | bytes 393224 | tf_op jit(solution)/shard_map/ppermute | solution.py:455
  35.8 6.2 %collective-permute-start.13 = (bf16[2,256,128]{2,1,0:T(8,128)(2,1)S(1)}, bf16[2,256,128]{2,1,0:T(8,128)(2,1)S(1)}, u32[]{:S(2)}, u32[]{:S(2)}) collective-permute-start(bf16[2,256,128]{2,1,0:T(8,128)(2,1)S(1)} %get-tuple-element.57), channel_id=1, source_target_pairs={{0,2},{2,0},{4,6},{6,4},{8,10},{10,8},{12,14},{14,12},{16,18},{18,... | collective-permute-start | bytes 393224 | tf_op jit(solution)/shard_map/ppermute | solution.py:455
  36.9 11.7 %collective-permute-start.8 = (bf16[2,224,128]{2,1,0:T(8,128)(2,1)S(1)}, bf16[2,224,128]{2,1,0:T(8,128)(2,1)S(1)}, u32[]{:S(2)}, u32[]{:S(2)}) collective-permute-start(bf16[2,224,128]{2,1,0:T(8,128)(2,1)S(1)} %get-tuple-element.52), channel_id=1, source_target_pairs={{0,16},{2,18},{4,20},{6,22},{8,24},{10,26},{12,28},{14,30},{16,0},... | collective-permute-start | bytes 344072 | tf_op jit(solution)/shard_map/ppermute | solution.py:458
  40.0 8.6 %collective-permute-start.9 = (bf16[2,224,128]{2,1,0:T(8,128)(2,1)S(1)}, bf16[2,224,128]{2,1,0:T(8,128)(2,1)S(1)}, u32[]{:S(2)}, u32[]{:S(2)}) collective-permute-start(bf16[2,224,128]{2,1,0:T(8,128)(2,1)S(1)} %get-tuple-element.53), channel_id=1, source_target_pairs={{0,24},{2,26},{4,28},{6,30},{8,16},{10,18},{12,20},{14,22},{16,8},... | collective-permute-start | bytes 344072 | tf_op jit(solution)/shard_map/ppermute | solution.py:458
  41.5 7.2 %collective-permute-start.10 = (bf16[2,224,128]{2,1,0:T(8,128)(2,1)S(1)}, bf16[2,224,128]{2,1,0:T(8,128)(2,1)S(1)}, u32[]{:S(2)}, u32[]{:S(2)}) collective-permute-start(bf16[2,224,128]{2,1,0:T(8,128)(2,1)S(1)} %get-tuple-element.54), channel_id=1, source_target_pairs={{0,8},{2,10},{4,12},{6,14},{8,0},{10,2},{12,4},{14,6},{16,24},{18,... | collective-permute-start | bytes 344072 | tf_op jit(solution)/shard_map/ppermute | solution.py:458
  49.0 1.4 %collective-permute-start.14 = (bf16[2,256,128]{2,1,0:T(8,128)(2,1)S(1)}, bf16[2,256,128]{2,1,0:T(8,128)(2,1)S(1)}, u32[]{:S(2)}, u32[]{:S(2)}) collective-permute-start(bf16[2,256,128]{2,1,0:T(8,128)(2,1)S(1)} %finish.1.refs_0_), channel_id=1, source_target_pairs={{1,0},{0,1},{3,2},{2,3},{5,4},{4,5},{7,6},{6,7},{9,8},{8,9},{11,10... | collective-permute-start | bytes 393224 | tf_op jit(solution)/shard_map/ppermute | solution.py:461
  51.3 7.8 %collective-permute-start.20 = (bf16[264,128]{1,0:T(8,128)(2,1)S(1)}, bf16[264,128]{1,0:T(8,128)(2,1)S(1)}, u32[]{:S(2)}, u32[]{:S(2)}) collective-permute-start(bf16[264,128]{1,0:T(8,128)(2,1)S(1)} %series.1.refs_0_), channel_id=1, source_target_pairs={{0,16},{2,18},{4,20},{6,22},{8,24},{10,26},{12,28},{14,30},{16,0},... | collective-permute-start | bytes 202760 | tf_op jit(solution)/shard_map/ppermute | solution.py:458
  54.9 6.5 %collective-permute-start.19 = (bf16[264,128]{1,0:T(8,128)(2,1)S(1)}, bf16[264,128]{1,0:T(8,128)(2,1)S(1)}, u32[]{:S(2)}, u32[]{:S(2)}) collective-permute-start(bf16[264,128]{1,0:T(8,128)(2,1)S(1)} %series.1.refs_0_), channel_id=1, source_target_pairs={{0,24},{2,26},{4,28},{6,30},{8,16},{10,18},{12,20},{14,22},{16,8},... | collective-permute-start | bytes 202760 | tf_op jit(solution)/shard_map/ppermute | solution.py:458
  55.4 6.2 %collective-permute-start.18 = (bf16[264,128]{1,0:T(8,128)(2,1)S(1)}, bf16[264,128]{1,0:T(8,128)(2,1)S(1)}, u32[]{:S(2)}, u32[]{:S(2)}) collective-permute-start(bf16[264,128]{1,0:T(8,128)(2,1)S(1)} %series.1.refs_0_), channel_id=1, source_target_pairs={{0,8},{2,10},{4,12},{6,14},{8,0},{10,2},{12,4},{14,6},{16,24},{18,... | collective-permute-start | bytes 202760 | tf_op jit(solution)/shard_map/ppermute | solution.py:458
  55.6 6.1 %collective-permute-start.17 = (bf16[264,128]{1,0:T(8,128)(2,1)S(1)}, bf16[264,128]{1,0:T(8,128)(2,1)S(1)}, u32[]{:S(2)}, u32[]{:S(2)}) collective-permute-start(bf16[264,128]{1,0:T(8,128)(2,1)S(1)} %series.1.refs_0_), channel_id=1, source_target_pairs={{0,6},{2,4},{4,2},{6,0},{8,14},{10,12},{12,10},{14,8},{16,22},{18,... | collective-permute-start | bytes 202760 | tf_op jit(solution)/shard_map/ppermute | solution.py:455
  56.8 4.8 %collective-permute-start.16 = (bf16[264,128]{1,0:T(8,128)(2,1)S(1)}, bf16[264,128]{1,0:T(8,128)(2,1)S(1)}, u32[]{:S(2)}, u32[]{:S(2)}) collective-permute-start(bf16[264,128]{1,0:T(8,128)(2,1)S(1)} %series.1.refs_0_), channel_id=1, source_target_pairs={{0,4},{2,6},{4,0},{6,2},{8,12},{10,14},{12,8},{14,10},{16,20},{18,... | collective-permute-start | bytes 202760 | tf_op jit(solution)/shard_map/ppermute | solution.py:455
  61.7 12.8 %collective-permute-start.23 = (bf16[3,264,128]{2,1,0:T(8,128)(2,1)S(1)}, bf16[3,264,128]{2,1,0:T(8,128)(2,1)S(1)}, u32[]{:S(2)}, u32[]{:S(2)}) collective-permute-start(bf16[3,264,128]{2,1,0:T(8,128)(2,1)S(1)} %get-tuple-element.63.refs_4_), channel_id=1, source_target_pairs={{0,6},{2,4},{4,2},{6,0},{8,14},{10,12},{12,10},{14,8},{16,22},{18,... | collective-permute-start | bytes 608264 | tf_op jit(solution)/shard_map/ppermute | solution.py:455
  63.0 11.4 %collective-permute-start.22 = (bf16[3,264,128]{2,1,0:T(8,128)(2,1)S(1)}, bf16[3,264,128]{2,1,0:T(8,128)(2,1)S(1)}, u32[]{:S(2)}, u32[]{:S(2)}) collective-permute-start(bf16[3,264,128]{2,1,0:T(8,128)(2,1)S(1)} %get-tuple-element.63.refs_4_), channel_id=1, source_target_pairs={{0,4},{2,6},{4,0},{6,2},{8,12},{10,14},{12,8},{14,10},{16,20},{18,... | collective-permute-start | bytes 608264 | tf_op jit(solution)/shard_map/ppermute | solution.py:455
  64.7 9.8 %collective-permute-start.21 = (bf16[3,264,128]{2,1,0:T(8,128)(2,1)S(1)}, bf16[3,264,128]{2,1,0:T(8,128)(2,1)S(1)}, u32[]{:S(2)}, u32[]{:S(2)}) collective-permute-start(bf16[3,264,128]{2,1,0:T(8,128)(2,1)S(1)} %get-tuple-element.63.refs_4_), channel_id=1, source_target_pairs={{0,2},{2,0},{4,6},{6,4},{8,10},{10,8},{12,14},{14,12},{16,18},{18,... | collective-permute-start | bytes 608264 | tf_op jit(solution)/shard_map/ppermute | solution.py:455
  65.2 9.2 %collective-permute-start.15 = (bf16[264,128]{1,0:T(8,128)(2,1)S(1)}, bf16[264,128]{1,0:T(8,128)(2,1)S(1)}, u32[]{:S(2)}, u32[]{:S(2)}) collective-permute-start(bf16[264,128]{1,0:T(8,128)(2,1)S(1)} %series.1.refs_0_), channel_id=1, source_target_pairs={{0,2},{2,0},{4,6},{6,4},{8,10},{10,8},{12,14},{14,12},{16,18},{18,... | collective-permute-start | bytes 202760 | tf_op jit(solution)/shard_map/ppermute | solution.py:455

commit v16 on v13

--- a/solution.py
+++ b/solution.py
@@ -194,9 +194,10 @@
     bias = own_ref[...]
     for other in others:
         bias = bias + other[...]
-    energy = 0.5 * jnp.sum(bias * bias, axis=1, keepdims=True)
     energy_ref[...] = jnp.zeros_like(energy_ref)
-    energy_ref[:, :walk] = jnp.broadcast_to(energy, (walk, LANES)).T[:CHUNK]
+    if not by_plane:
+        energy = 0.5 * jnp.sum(bias * bias, axis=1, keepdims=True)
+        energy_ref[:, :walk] = jnp.broadcast_to(energy, (walk, LANES)).T[:CHUNK]
     shifted = (fields_ref[...] - bias).astype(jnp.bfloat16)
     at = lax.broadcasted_iota(jnp.int32, (walk, walk), 0)
     source = lax.broadcasted_iota(jnp.int32, (walk, walk), 1)
@@ -456,7 +457,6 @@
     turned, partial_bias, mine, cols = bias_call(chol_vals, greens, walkers, cols, own)
     start = around_orb(mine)
     bias, *others = around_orb(partial_bias)
-    start, others = lax.optimization_barrier((start, others))
 
     units = 2 * rowblocks * BLOCK // CHUNK
     early_units = units // 8
@@ -469,9 +469,9 @@
     def all_z(arrays):
         return [to_z(arrays[dz - 1], dz) for dz in z_order]
 
-    late, energy = potential_call(early_units, units, layout, True, fields_t, bias, others, cols, turned)
+    late, _ = potential_call(early_units, units, layout, True, fields_t, bias, others, cols, turned)
     far, near = late[:plane], late[plane:]
-    early, _ = potential_call(0, early_units, layout, False, fields_t, bias, others, cols, turned)
+    early, energy = potential_call(0, early_units, layout, False, fields_t, bias, others, cols, turned)
     early_came = all_z(early[1:])
     merged = merge_call([early[0], *early_came], near)
     far_came = all_z(sum_call([far[0], *all_plane(far[1:])], merged[:1]))

time: 73.9 us -> 77.8 us (1.053)
  waiting for transfers between devices: 24.1 us -> 28.3 us
    ppermute x9, waiting for transfers between devices: 13.5 us -> 16.8 us  [to_z(): lax.ppermute(a, 'chol', [(c, hop(c // plane, dz, nz) * plane + c % plane)...]
    ppermute x12, waiting for transfers between devices: 8.12 us -> 9.7 us  [to_plane(): lax.ppermute(a, 'chol', [(c, c // plane * plane + hop(c % plane, dp, plan...]
  transfers between devices with their start and end apart: 24 -> 24, of which waited for: 12 -> 12; matrix products, arithmetic and copies ran while one was open for 0% -> 0% of each run, Pallas kernels for 2% -> 1%
where the time goes in v16:
time: 77.8 us; the launch traced here: 77.7 us
  starting transfers between devices  33.4 us (43%)
  waiting for transfers between devices  28.3 us (36%)
  Pallas kernels  15.2 us (20%)
    ppermute x9, starting transfers between devices, to_z(): lax.ppermute(a, 'chol', [(c, hop(c // plane, dz, nz) * plane + c % plane)...  17.2 us
    ppermute x9, waiting for transfers between devices, to_z(): lax.ppermute(a, 'chol', [(c, hop(c // plane, dz, nz) * plane + c % plane)...  16.8 us
    ppermute x12, starting transfers between devices, to_plane(): lax.ppermute(a, 'chol', [(c, c // plane * plane + hop(c % plane, dp, plan...  15.2 us
    ppermute x12, waiting for transfers between devices, to_plane(): lax.ppermute(a, 'chol', [(c, c // plane * plane + hop(c % plane, dp, plan...  9.7 us
    pallas_call x1, Pallas kernels, bias_call(): pl.pallas_call(bias_kernel, in_specs=[*[pl.BlockSpec(memory_space=pl.ANY)...  8.42 us
    pallas_call x2, Pallas kernels, potential_call(): pl.pallas_call(functools.partial(potential_kernel, begin, end, layout, by...  4.45 us
    ppermute x3, waiting for transfers between devices, around_orb(): lax.ppermute(a, 'orb', [((c + d) % n_orb, c) for c in range(n_orb)])  1.79 us
  transfers between devices with their start and end apart: 24, of which 12 were waited for; matrix products, arithmetic and copies ran while one was open for 0% of the time, Pallas kernels for 1%

profile of v16, /device:TPU:0, one launch (start us, length us, event | category | flops | bytes accessed | tf_op | source)
XLA Modules:
  0.0 77.7 jit_solution(11300407003564304090)
XLA Ops:
  0.6 0.0 copy-start
  0.6 8.4 %force_bias.1 = (bf16[8,256,2048]{2,1,0:T(8,128)(2,1)S(1)}, f32[32,256]{1,0:T(8,128)S(1)}, bf16[2,128,128]{2,1,0:T(8,128)(2,1)S(1)}, s32[2,2,256]{2,1,0:T(2,128)S(1)}) custom-call(bf16[256,2,64,128]{3,2,1,0:T(8,128)(2,1)} %vals_hbm.1, bf16[32,128,256]{2,1,0:T(8,128)(2,1)} %greens_hbm.1, bf16[32,128,128]{2,1,0:T(8,128)(2,1)} %walkers_hbm.1, s32[2,2,256]{2,1,0:T(2,128)} %bitcast.5), custom_call_target="tpu_custom_call" | custom-call | tf_op jit(solution)/shard_map/force_bias/pallas_call | solution.py:154
  9.1 0.5 collective-permute-start
  9.6 0.9 %collective-permute-done.refs_0_ = f32[32,256]{1,0:T(8,128)S(1)} collective-permute-done((f32[32,256]{1,0:T(8,128)S(1)}, f32[32,256]{1,0:T(8,128)S(1)}, u32[]{:S(2)}, u32[]{:S(2)}) %collective-permute-start) | collective-permute-done | bytes 32800 | tf_op jit(solution)/shard_map/ppermute | solution.py:454
  10.4 0.0 copy-done
  10.4 3.8 %potential.2 = (bf16[3,2,224,128]{3,2,1,0:T(8,128)(2,1)S(1)}, bf16[3,2,224,128]{3,2,1,0:T(8,128)(2,1)S(1)}, bf16[3,2,224,128]{3,2,1,0:T(8,128)(2,1)S(1)}, bf16[3...) custom-call(f32[32,256]{1,0:T(8,128)S(1)} %bitcast.3, ...), custom_call_target="tpu_custom_call" | custom-call | tf_op jit(solution)/shard_map/potential/pallas_call | solution.py:266
  14.2 3.8 %collective-permute-start.1 = (bf16[3,2,224,128]{3,2,1,0:T(8,128)(2,1)S(1)}, bf16[3,2,224,128]{3,2,1,0:T(8,128)(2,1)S(1)}, u32[]{:S(2)}, u32[]{:S(2)}) collective-permute-start(bf16[3,2,224,128]{3,2,1,0:T(8,128)(2,1)S(1)} %get-tuple-element.35), channel_id=1, source_target_pairs={{0,6},{2,4},{4,2},{6,0},{8,14},{10,12},{12,10},{14,8},{16,22},{18,... | collective-permute-start | bytes 1032200 | tf_op jit(solution)/shard_map/ppermute | solution.py:448
  18.0 0.5 collective-permute-start.2
  18.5 0.1 collective-permute-start.3
  18.7 0.7 potential.3
  19.4 3.1 %collective-permute-start.4 = (bf16[4,2,32,128]{3,2,1,0:T(8,128)(2,1)S(1)}, bf16[4,2,32,128]{3,2,1,0:T(8,128)(2,1)S(1)}, u32[]{:S(2)}, u32[]{:S(2)}) collective-permute-start(bf16[4,2,32,128]{3,2,1,0:T(8,128)(2,1)S(1)} %get-tuple-element.39), channel_id=1, source_target_pairs={{0,16},{2,18},{4,20},{6,22},{8,24},{10,26},{12,28},{14,30},{16,0},... | collective-permute-start | bytes 196616 | tf_op jit(solution)/shard_map/ppermute | solution.py:451
  22.4 1.3 %collective-permute-start.5 = (bf16[4,2,32,128]{3,2,1,0:T(8,128)(2,1)S(1)}, bf16[4,2,32,128]{3,2,1,0:T(8,128)(2,1)S(1)}, u32[]{:S(2)}, u32[]{:S(2)}) collective-permute-start(bf16[4,2,32,128]{3,2,1,0:T(8,128)(2,1)S(1)} %get-tuple-element.40), channel_id=1, source_target_pairs={{0,24},{2,26},{4,28},{6,30},{8,16},{10,18},{12,20},{14,22},{16,8},... | collective-permute-start | bytes 196616 | tf_op jit(solution)/shard_map/ppermute | solution.py:451
  23.8 1.3 %collective-permute-done.4.refs_1_ = bf16[4,2,32,128]{3,2,1,0:T(8,128)(2,1)S(1)} collective-permute-done((bf16[4,2,32,128]{3,2,1,0:T(8,128)(2,1)S(1)}, bf16[4,2,32,128]{3,2,1,0:T(8,128)(2,1)S(1)}, u32[]{:S(2)}, u32[]{:S(2)}) %collective-permute-start.4) | collective-permute-done | bytes 65568 | tf_op jit(solution)/shard_map/ppermute | solution.py:451
  25.1 2.9 %collective-permute-start.6 = (bf16[4,2,32,128]{3,2,1,0:T(8,128)(2,1)S(1)}, bf16[4,2,32,128]{3,2,1,0:T(8,128)(2,1)S(1)}, u32[]{:S(2)}, u32[]{:S(2)}) collective-permute-start(bf16[4,2,32,128]{3,2,1,0:T(8,128)(2,1)S(1)} %get-tuple-element.41), channel_id=1, source_target_pairs={{0,8},{2,10},{4,12},{6,14},{8,0},{10,2},{12,4},{14,6},{16,24},{18,... | collective-permute-start | bytes 196616 | tf_op jit(solution)/shard_map/ppermute | solution.py:451
  28.0 0.6 collective-permute-done.5.refs_2_
  28.6 1.6 %collective-permute-done.6.refs_3_ = bf16[4,2,32,128]{3,2,1,0:T(8,128)(2,1)S(1)} collective-permute-done((bf16[4,2,32,128]{3,2,1,0:T(8,128)(2,1)S(1)}, bf16[4,2,32,128]{3,2,1,0:T(8,128)(2,1)S(1)}, u32[]{:S(2)}, u32[]{:S(2)}) %collective-permute-start.6) | collective-permute-done | bytes 65568 | tf_op jit(solution)/shard_map/ppermute | solution.py:451
  30.3 2.5 %collective-permute-start.10 = (bf16[2,256,128]{2,1,0:T(8,128)(2,1)S(1)}, bf16[2,256,128]{2,1,0:T(8,128)(2,1)S(1)}, u32[]{:S(2)}, u32[]{:S(2)}) collective-permute-start(bf16[2,256,128]{2,1,0:T(8,128)(2,1)S(1)} %get-tuple-element.50), channel_id=1, source_target_pairs={{0,6},{2,4},{4,2},{6,0},{8,14},{10,12},{12,10},{14,8},{16,22},{18,... | collective-permute-start | bytes 393224 | tf_op jit(solution)/shard_map/ppermute | solution.py:448
  32.8 0.5 collective-permute-start.11
  33.3 0.0 collective-permute-done.1.refs_1_
  33.3 0.5 collective-permute-start.12
  33.8 0.5 collective-permute-done.2.refs_2_
  34.4 0.5 collective-permute-done.3.refs_3_
  34.9 0.2 sum_parts.1
  35.0 2.7 %collective-permute-start.7 = (bf16[2,224,128]{2,1,0:T(8,128)(2,1)S(1)}, bf16[2,224,128]{2,1,0:T(8,128)(2,1)S(1)}, u32[]{:S(2)}, u32[]{:S(2)}) collective-permute-start(bf16[2,224,128]{2,1,0:T(8,128)(2,1)S(1)} %get-tuple-element.47), channel_id=1, source_target_pairs={{0,16},{2,18},{4,20},{6,22},{8,24},{10,26},{12,28},{14,30},{16,0},... | collective-permute-start | bytes 344072 | tf_op jit(solution)/shard_map/ppermute | solution.py:451
  37.7 1.3 %collective-permute-start.8 = (bf16[2,224,128]{2,1,0:T(8,128)(2,1)S(1)}, bf16[2,224,128]{2,1,0:T(8,128)(2,1)S(1)}, u32[]{:S(2)}, u32[]{:S(2)}) collective-permute-start(bf16[2,224,128]{2,1,0:T(8,128)(2,1)S(1)} %get-tuple-element.48), channel_id=1, source_target_pairs={{0,24},{2,26},{4,28},{6,30},{8,16},{10,18},{12,20},{14,22},{16,8},... | collective-permute-start | bytes 344072 | tf_op jit(solution)/shard_map/ppermute | solution.py:451
  39.1 0.0 collective-permute-done.10.refs_4_
  39.1 0.6 collective-permute-start.9
  39.7 0.0 collective-permute-done.11.refs_5_
  39.7 0.1 collective-permute-done.12.refs_6_
  39.8 7.1 %collective-permute-done.7.refs_0_ = bf16[2,224,128]{2,1,0:T(8,128)(2,1)S(1)} collective-permute-done((bf16[2,224,128]{2,1,0:T(8,128)(2,1)S(1)}, bf16[2,224,128]{2,1,0:T(8,128)(2,1)S(1)}, u32[]{:S(2)}, u32[]{:S(2)}) %collective-permute-start.7) | collective-permute-done | bytes 114720 | tf_op jit(solution)/shard_map/ppermute | solution.py:451
  46.9 0.0 collective-permute-done.8.refs_1_
  46.9 0.2 collective-permute-done.9.refs_2_
  47.1 0.2 finish.1.refs_0_
  47.3 0.1 collective-permute-start.13
  47.4 0.5 collective-permute-start.14
  47.9 0.9 %collective-permute-done.14.refs_3_ = bf16[2,128,128]{2,1,0:T(8,128)(2,1)S(1)} collective-permute-done((bf16[2,128,128]{2,1,0:T(8,128)(2,1)S(1)}, bf16[2,128,128]{2,1,0:T(8,128)(2,1)S(1)}, u32[]{:S(2)}, u32[]{:S(2)}) %collective-permute-start.14) | collective-permute-done | bytes 65568 | tf_op jit(solution)/shard_map/ppermute | solution.py:454
  48.8 0.0 collective-permute-done.13.refs_1_
  48.8 0.9 %series.1.refs_0_ = bf16[264,128]{1,0:T(8,128)(2,1)S(1)} custom-call(bf16[2,256,128]{2,1,0:T(8,128)(2,1)S(1)} %finish.1.refs_0_, bf16[2,256,128]{2,1,0:T(8,128)(2,1)S(1)} %collective-permute-done.13.refs_1_, bf16[2,128,128]{2,1,0:T(8,128)(2,1)S(1)} %get-tuple-element.53.refs_2_, bf16[2,128,128]{2,1,0:T(8,128)(2,1)S(1)} %collective-permute-done.14.refs_3_, ...), custom_call_target="tpu_custom_call" | custom-call | tf_op jit(solution)/shard_map/series/pallas_call | solution.py:388
  49.7 1.6 %collective-permute-start.16 = (bf16[264,128]{1,0:T(8,128)(2,1)S(1)}, bf16[264,128]{1,0:T(8,128)(2,1)S(1)}, u32[]{:S(2)}, u32[]{:S(2)}) collective-permute-start(bf16[264,128]{1,0:T(8,128)(2,1)S(1)} %series.1.refs_0_), channel_id=1, source_target_pairs={{0,4},{2,6},{4,0},{6,2},{8,12},{10,14},{12,8},{14,10},{16,20},{18,... | collective-permute-start | bytes 202760 | tf_op jit(solution)/shard_map/ppermute | solution.py:448
  51.3 1.4 %collective-permute-start.17 = (bf16[264,128]{1,0:T(8,128)(2,1)S(1)}, bf16[264,128]{1,0:T(8,128)(2,1)S(1)}, u32[]{:S(2)}, u32[]{:S(2)}) collective-permute-start(bf16[264,128]{1,0:T(8,128)(2,1)S(1)} %series.1.refs_0_), channel_id=1, source_target_pairs={{0,6},{2,4},{4,2},{6,0},{8,14},{10,12},{12,10},{14,8},{16,22},{18,... | collective-permute-start | bytes 202760 | tf_op jit(solution)/shard_map/ppermute | solution.py:448
  52.8 1.8 %collective-permute-start.18 = (bf16[264,128]{1,0:T(8,128)(2,1)S(1)}, bf16[264,128]{1,0:T(8,128)(2,1)S(1)}, u32[]{:S(2)}, u32[]{:S(2)}) collective-permute-start(bf16[264,128]{1,0:T(8,128)(2,1)S(1)} %series.1.refs_0_), channel_id=1, source_target_pairs={{0,8},{2,10},{4,12},{6,14},{8,0},{10,2},{12,4},{14,6},{16,24},{18,... | collective-permute-start | bytes 202760 | tf_op jit(solution)/shard_map/ppermute | solution.py:451
  54.5 3.4 %collective-permute-start.19 = (bf16[264,128]{1,0:T(8,128)(2,1)S(1)}, bf16[264,128]{1,0:T(8,128)(2,1)S(1)}, u32[]{:S(2)}, u32[]{:S(2)}) collective-permute-start(bf16[264,128]{1,0:T(8,128)(2,1)S(1)} %series.1.refs_0_), channel_id=1, source_target_pairs={{0,24},{2,26},{4,28},{6,30},{8,16},{10,18},{12,20},{14,22},{16,8},... | collective-permute-start | bytes 202760 | tf_op jit(solution)/shard_map/ppermute | solution.py:451
  57.9 0.0 collective-permute-start.20
  57.9 0.0 collective-permute-done.16.refs_0_
  57.9 0.0 collective-permute-done.17.refs_1_
  57.9 0.0 collective-permute-done.18.refs_2_
  58.0 4.0 %collective-permute-done.19.refs_3_ = bf16[264,128]{1,0:T(8,128)(2,1)S(1)} collective-permute-done((bf16[264,128]{1,0:T(8,128)(2,1)S(1)}, bf16[264,128]{1,0:T(8,128)(2,1)S(1)}, u32[]{:S(2)}, u32[]{:S(2)}) %collective-permute-start.19) | collective-permute-done | bytes 67616 | tf_op jit(solution)/shard_map/ppermute | solution.py:451
  62.0 1.9 %collective-permute-done.20.refs_4_ = bf16[264,128]{1,0:T(8,128)(2,1)S(1)} collective-permute-done((bf16[264,128]{1,0:T(8,128)(2,1)S(1)}, bf16[264,128]{1,0:T(8,128)(2,1)S(1)}, u32[]{:S(2)}, u32[]{:S(2)}) %collective-permute-start.20) | collective-permute-done | bytes 67616 | tf_op jit(solution)/shard_map/ppermute | solution.py:451
  63.9 0.6 collective-permute-start.21
  64.5 1.5 %collective-permute-start.22 = (bf16[3,264,128]{2,1,0:T(8,128)(2,1)S(1)}, bf16[3,264,128]{2,1,0:T(8,128)(2,1)S(1)}, u32[]{:S(2)}, u32[]{:S(2)}) collective-permute-start(bf16[3,264,128]{2,1,0:T(8,128)(2,1)S(1)} %get-tuple-element.57.refs_4_), channel_id=1, source_target_pairs={{0,4},{2,6},{4,0},{6,2},{8,12},{10,14},{12,8},{14,10},{16,20},{18,... | collective-permute-start | bytes 608264 | tf_op jit(solution)/shard_map/ppermute | solution.py:448
  66.1 1.4 %collective-permute-start.23 = (bf16[3,264,128]{2,1,0:T(8,128)(2,1)S(1)}, bf16[3,264,128]{2,1,0:T(8,128)(2,1)S(1)}, u32[]{:S(2)}, u32[]{:S(2)}) collective-permute-start(bf16[3,264,128]{2,1,0:T(8,128)(2,1)S(1)} %get-tuple-element.57.refs_4_), channel_id=1, source_target_pairs={{0,6},{2,4},{4,2},{6,0},{8,14},{10,12},{12,10},{14,8},{16,22},{18,... | collective-permute-start | bytes 608264 | tf_op jit(solution)/shard_map/ppermute | solution.py:448
  67.5 0.5 collective-permute-start.15
  68.0 8.6 %collective-permute-done.15.refs_1_ = bf16[264,128]{1,0:T(8,128)(2,1)S(1)} collective-permute-done((bf16[264,128]{1,0:T(8,128)(2,1)S(1)}, bf16[264,128]{1,0:T(8,128)(2,1)S(1)}, u32[]{:S(2)}, u32[]{:S(2)}) %collective-permute-start.15) | collective-permute-done | bytes 67616 | tf_op jit(solution)/shard_map/ppermute | solution.py:448
  76.6 0.0 collective-permute-done.21.refs_5_
  76.6 0.0 collective-permute-done.22.refs_6_
  76.6 0.0 collective-permute-done.23.refs_7_
  76.6 1.1 %place_walkers.1 = (bf16[32,128,128]{2,1,0:T(8,128)(2,1)}, f32[1,32]{1,0:T(1,128)}) custom-call(bf16[264,128]{1,0:T(8,128)(2,1)S(1)} %series.1.refs_0_, bf16[264,128]{1,0:T(8,128)(2,1)S(1)} %collective-permute-done.15.refs_1_, bf16[264,128]{1,0:T(8,128)(2,1)S(1)} %get-tuple-element.55.refs_2_, bf16[264,128]{1,0:T(8,128)(2,1)S(1)} %get-tuple-element.56.refs_3_, ...), custom_call_target="tpu_custom_call" | custom-call | tf_op jit(solution)/shard_map/place_walkers/pallas_call | solution.py:424
  (2 shorter events, 0.1 us)
Async XLA Ops:
  0.6 9.8 %copy-start = (f32[256,32]{0,1:T(8,128)S(1)}, f32[256,32]{0,1:T(8,128)}, u32[]{:S(2)}) copy-start(f32[256,32]{0,1:T(8,128)} %param.9) | copy-start | bytes 98308
  9.1 1.4 %collective-permute-start = (f32[32,256]{1,0:T(8,128)S(1)}, f32[32,256]{1,0:T(8,128)S(1)}, u32[]{:S(2)}, u32[]{:S(2)}) collective-permute-start(f32[32,256]{1,0:T(8,128)S(1)} %get-tuple-element.31.own_ref), channel_id=1, source_target_pairs={{1,0},{0,1},{3,2},{2,3},{5,4},{4,5},{7,6},{6,7},{9,8},{8,9},{11,10... | collective-permute-start | bytes 98312 | tf_op jit(solution)/shard_map/ppermute | solution.py:454
  14.2 19.1 %collective-permute-start.1 = (bf16[3,2,224,128]{3,2,1,0:T(8,128)(2,1)S(1)}, bf16[3,2,224,128]{3,2,1,0:T(8,128)(2,1)S(1)}, u32[]{:S(2)}, u32[]{:S(2)}) collective-permute-start(bf16[3,2,224,128]{3,2,1,0:T(8,128)(2,1)S(1)} %get-tuple-element.35), channel_id=1, source_target_pairs={{0,6},{2,4},{4,2},{6,0},{8,14},{10,12},{12,10},{14,8},{16,22},{18,... | collective-permute-start | bytes 1032200 | tf_op jit(solution)/shard_map/ppermute | solution.py:448
  18.0 16.3 %collective-permute-start.2 = (bf16[3,2,224,128]{3,2,1,0:T(8,128)(2,1)S(1)}, bf16[3,2,224,128]{3,2,1,0:T(8,128)(2,1)S(1)}, u32[]{:S(2)}, u32[]{:S(2)}) collective-permute-start(bf16[3,2,224,128]{3,2,1,0:T(8,128)(2,1)S(1)} %get-tuple-element.36), channel_id=1, source_target_pairs={{0,4},{2,6},{4,0},{6,2},{8,12},{10,14},{12,8},{14,10},{16,20},{18,... | collective-permute-start | bytes 1032200 | tf_op jit(solution)/shard_map/ppermute | solution.py:448
  18.5 16.3 %collective-permute-start.3 = (bf16[3,2,224,128]{3,2,1,0:T(8,128)(2,1)S(1)}, bf16[3,2,224,128]{3,2,1,0:T(8,128)(2,1)S(1)}, u32[]{:S(2)}, u32[]{:S(2)}) collective-permute-start(bf16[3,2,224,128]{3,2,1,0:T(8,128)(2,1)S(1)} %get-tuple-element.37), channel_id=1, source_target_pairs={{0,2},{2,0},{4,6},{6,4},{8,10},{10,8},{12,14},{14,12},{16,18},{18,... | collective-permute-start | bytes 1032200 | tf_op jit(solution)/shard_map/ppermute | solution.py:448
  19.4 5.7 %collective-permute-start.4 = (bf16[4,2,32,128]{3,2,1,0:T(8,128)(2,1)S(1)}, bf16[4,2,32,128]{3,2,1,0:T(8,128)(2,1)S(1)}, u32[]{:S(2)}, u32[]{:S(2)}) collective-permute-start(bf16[4,2,32,128]{3,2,1,0:T(8,128)(2,1)S(1)} %get-tuple-element.39), channel_id=1, source_target_pairs={{0,16},{2,18},{4,20},{6,22},{8,24},{10,26},{12,28},{14,30},{16,0},... | collective-permute-start | bytes 196616 | tf_op jit(solution)/shard_map/ppermute | solution.py:451
  22.4 6.2 %collective-permute-start.5 = (bf16[4,2,32,128]{3,2,1,0:T(8,128)(2,1)S(1)}, bf16[4,2,32,128]{3,2,1,0:T(8,128)(2,1)S(1)}, u32[]{:S(2)}, u32[]{:S(2)}) collective-permute-start(bf16[4,2,32,128]{3,2,1,0:T(8,128)(2,1)S(1)} %get-tuple-element.40), channel_id=1, source_target_pairs={{0,24},{2,26},{4,28},{6,30},{8,16},{10,18},{12,20},{14,22},{16,8},... | collective-permute-start | bytes 196616 | tf_op jit(solution)/shard_map/ppermute | solution.py:451
  25.1 5.2 %collective-permute-start.6 = (bf16[4,2,32,128]{3,2,1,0:T(8,128)(2,1)S(1)}, bf16[4,2,32,128]{3,2,1,0:T(8,128)(2,1)S(1)}, u32[]{:S(2)}, u32[]{:S(2)}) collective-permute-start(bf16[4,2,32,128]{3,2,1,0:T(8,128)(2,1)S(1)} %get-tuple-element.41), channel_id=1, source_target_pairs={{0,8},{2,10},{4,12},{6,14},{8,0},{10,2},{12,4},{14,6},{16,24},{18,... | collective-permute-start | bytes 196616 | tf_op jit(solution)/shard_map/ppermute | solution.py:451
  30.3 8.8 %collective-permute-start.10 = (bf16[2,256,128]{2,1,0:T(8,128)(2,1)S(1)}, bf16[2,256,128]{2,1,0:T(8,128)(2,1)S(1)}, u32[]{:S(2)}, u32[]{:S(2)}) collective-permute-start(bf16[2,256,128]{2,1,0:T(8,128)(2,1)S(1)} %get-tuple-element.50), channel_id=1, source_target_pairs={{0,6},{2,4},{4,2},{6,0},{8,14},{10,12},{12,10},{14,8},{16,22},{18,... | collective-permute-start | bytes 393224 | tf_op jit(solution)/shard_map/ppermute | solution.py:448
  32.8 6.9 %collective-permute-start.11 = (bf16[2,256,128]{2,1,0:T(8,128)(2,1)S(1)}, bf16[2,256,128]{2,1,0:T(8,128)(2,1)S(1)}, u32[]{:S(2)}, u32[]{:S(2)}) collective-permute-start(bf16[2,256,128]{2,1,0:T(8,128)(2,1)S(1)} %get-tuple-element.51), channel_id=1, source_target_pairs={{0,4},{2,6},{4,0},{6,2},{8,12},{10,14},{12,8},{14,10},{16,20},{18,... | collective-permute-start | bytes 393224 | tf_op jit(solution)/shard_map/ppermute | solution.py:448
  33.3 6.4 %collective-permute-start.12 = (bf16[2,256,128]{2,1,0:T(8,128)(2,1)S(1)}, bf16[2,256,128]{2,1,0:T(8,128)(2,1)S(1)}, u32[]{:S(2)}, u32[]{:S(2)}) collective-permute-start(bf16[2,256,128]{2,1,0:T(8,128)(2,1)S(1)} %get-tuple-element.52), channel_id=1, source_target_pairs={{0,2},{2,0},{4,6},{6,4},{8,10},{10,8},{12,14},{14,12},{16,18},{18,... | collective-permute-start | bytes 393224 | tf_op jit(solution)/shard_map/ppermute | solution.py:448
  35.0 11.9 %collective-permute-start.7 = (bf16[2,224,128]{2,1,0:T(8,128)(2,1)S(1)}, bf16[2,224,128]{2,1,0:T(8,128)(2,1)S(1)}, u32[]{:S(2)}, u32[]{:S(2)}) collective-permute-start(bf16[2,224,128]{2,1,0:T(8,128)(2,1)S(1)} %get-tuple-element.47), channel_id=1, source_target_pairs={{0,16},{2,18},{4,20},{6,22},{8,24},{10,26},{12,28},{14,30},{16,0},... | collective-permute-start | bytes 344072 | tf_op jit(solution)/shard_map/ppermute | solution.py:451
  37.7 9.2 %collective-permute-start.8 = (bf16[2,224,128]{2,1,0:T(8,128)(2,1)S(1)}, bf16[2,224,128]{2,1,0:T(8,128)(2,1)S(1)}, u32[]{:S(2)}, u32[]{:S(2)}) collective-permute-start(bf16[2,224,128]{2,1,0:T(8,128)(2,1)S(1)} %get-tuple-element.48), channel_id=1, source_target_pairs={{0,24},{2,26},{4,28},{6,30},{8,16},{10,18},{12,20},{14,22},{16,8},... | collective-permute-start | bytes 344072 | tf_op jit(solution)/shard_map/ppermute | solution.py:451
  39.1 8.0 %collective-permute-start.9 = (bf16[2,224,128]{2,1,0:T(8,128)(2,1)S(1)}, bf16[2,224,128]{2,1,0:T(8,128)(2,1)S(1)}, u32[]{:S(2)}, u32[]{:S(2)}) collective-permute-start(bf16[2,224,128]{2,1,0:T(8,128)(2,1)S(1)} %get-tuple-element.49), channel_id=1, source_target_pairs={{0,8},{2,10},{4,12},{6,14},{8,0},{10,2},{12,4},{14,6},{16,24},{18,... | collective-permute-start | bytes 344072 | tf_op jit(solution)/shard_map/ppermute | solution.py:451
  47.3 1.5 %collective-permute-start.13 = (bf16[2,256,128]{2,1,0:T(8,128)(2,1)S(1)}, bf16[2,256,128]{2,1,0:T(8,128)(2,1)S(1)}, u32[]{:S(2)}, u32[]{:S(2)}) collective-permute-start(bf16[2,256,128]{2,1,0:T(8,128)(2,1)S(1)} %finish.1.refs_0_), channel_id=1, source_target_pairs={{1,0},{0,1},{3,2},{2,3},{5,4},{4,5},{7,6},{6,7},{9,8},{8,9},{11,10... | collective-permute-start | bytes 393224 | tf_op jit(solution)/shard_map/ppermute | solution.py:454
  47.4 1.4 %collective-permute-start.14 = (bf16[2,128,128]{2,1,0:T(8,128)(2,1)S(1)}, bf16[2,128,128]{2,1,0:T(8,128)(2,1)S(1)}, u32[]{:S(2)}, u32[]{:S(2)}) collective-permute-start(bf16[2,128,128]{2,1,0:T(8,128)(2,1)S(1)} %get-tuple-element.53.refs_2_), channel_id=1, source_target_pairs={{1,0},{0,1},{3,2},{2,3},{5,4},{4,5},{7,6},{6,7},{9,8},{8,9},{11,10... | collective-permute-start | bytes 196616 | tf_op jit(solution)/shard_map/ppermute | solution.py:454
  49.7 8.2 %collective-permute-start.16 = (bf16[264,128]{1,0:T(8,128)(2,1)S(1)}, bf16[264,128]{1,0:T(8,128)(2,1)S(1)}, u32[]{:S(2)}, u32[]{:S(2)}) collective-permute-start(bf16[264,128]{1,0:T(8,128)(2,1)S(1)} %series.1.refs_0_), channel_id=1, source_target_pairs={{0,4},{2,6},{4,0},{6,2},{8,12},{10,14},{12,8},{14,10},{16,20},{18,... | collective-permute-start | bytes 202760 | tf_op jit(solution)/shard_map/ppermute | solution.py:448
  51.3 6.6 %collective-permute-start.17 = (bf16[264,128]{1,0:T(8,128)(2,1)S(1)}, bf16[264,128]{1,0:T(8,128)(2,1)S(1)}, u32[]{:S(2)}, u32[]{:S(2)}) collective-permute-start(bf16[264,128]{1,0:T(8,128)(2,1)S(1)} %series.1.refs_0_), channel_id=1, source_target_pairs={{0,6},{2,4},{4,2},{6,0},{8,14},{10,12},{12,10},{14,8},{16,22},{18,... | collective-permute-start | bytes 202760 | tf_op jit(solution)/shard_map/ppermute | solution.py:448
  52.8 5.2 %collective-permute-start.18 = (bf16[264,128]{1,0:T(8,128)(2,1)S(1)}, bf16[264,128]{1,0:T(8,128)(2,1)S(1)}, u32[]{:S(2)}, u32[]{:S(2)}) collective-permute-start(bf16[264,128]{1,0:T(8,128)(2,1)S(1)} %series.1.refs_0_), channel_id=1, source_target_pairs={{0,8},{2,10},{4,12},{6,14},{8,0},{10,2},{12,4},{14,6},{16,24},{18,... | collective-permute-start | bytes 202760 | tf_op jit(solution)/shard_map/ppermute | solution.py:451
  54.5 7.5 %collective-permute-start.19 = (bf16[264,128]{1,0:T(8,128)(2,1)S(1)}, bf16[264,128]{1,0:T(8,128)(2,1)S(1)}, u32[]{:S(2)}, u32[]{:S(2)}) collective-permute-start(bf16[264,128]{1,0:T(8,128)(2,1)S(1)} %series.1.refs_0_), channel_id=1, source_target_pairs={{0,24},{2,26},{4,28},{6,30},{8,16},{10,18},{12,20},{14,22},{16,8},... | collective-permute-start | bytes 202760 | tf_op jit(solution)/shard_map/ppermute | solution.py:451
  57.9 6.0 %collective-permute-start.20 = (bf16[264,128]{1,0:T(8,128)(2,1)S(1)}, bf16[264,128]{1,0:T(8,128)(2,1)S(1)}, u32[]{:S(2)}, u32[]{:S(2)}) collective-permute-start(bf16[264,128]{1,0:T(8,128)(2,1)S(1)} %series.1.refs_0_), channel_id=1, source_target_pairs={{0,16},{2,18},{4,20},{6,22},{8,24},{10,26},{12,28},{14,30},{16,0},... | collective-permute-start | bytes 202760 | tf_op jit(solution)/shard_map/ppermute | solution.py:451
  63.9 12.7 %collective-permute-start.21 = (bf16[3,264,128]{2,1,0:T(8,128)(2,1)S(1)}, bf16[3,264,128]{2,1,0:T(8,128)(2,1)S(1)}, u32[]{:S(2)}, u32[]{:S(2)}) collective-permute-start(bf16[3,264,128]{2,1,0:T(8,128)(2,1)S(1)} %get-tuple-element.57.refs_4_), channel_id=1, source_target_pairs={{0,2},{2,0},{4,6},{6,4},{8,10},{10,8},{12,14},{14,12},{16,18},{18,... | collective-permute-start | bytes 608264 | tf_op jit(solution)/shard_map/ppermute | solution.py:448
  64.5 12.1 %collective-permute-start.22 = (bf16[3,264,128]{2,1,0:T(8,128)(2,1)S(1)}, bf16[3,264,128]{2,1,0:T(8,128)(2,1)S(1)}, u32[]{:S(2)}, u32[]{:S(2)}) collective-permute-start(bf16[3,264,128]{2,1,0:T(8,128)(2,1)S(1)} %get-tuple-element.57.refs_4_), channel_id=1, source_target_pairs={{0,4},{2,6},{4,0},{6,2},{8,12},{10,14},{12,8},{14,10},{16,20},{18,... | collective-permute-start | bytes 608264 | tf_op jit(solution)/shard_map/ppermute | solution.py:448
  66.1 10.6 %collective-permute-start.23 = (bf16[3,264,128]{2,1,0:T(8,128)(2,1)S(1)}, bf16[3,264,128]{2,1,0:T(8,128)(2,1)S(1)}, u32[]{:S(2)}, u32[]{:S(2)}) collective-permute-start(bf16[3,264,128]{2,1,0:T(8,128)(2,1)S(1)} %get-tuple-element.57.refs_4_), channel_id=1, source_target_pairs={{0,6},{2,4},{4,2},{6,0},{8,14},{10,12},{12,10},{14,8},{16,22},{18,... | collective-permute-start | bytes 608264 | tf_op jit(solution)/shard_map/ppermute | solution.py:448
  67.5 9.1 %collective-permute-start.15 = (bf16[264,128]{1,0:T(8,128)(2,1)S(1)}, bf16[264,128]{1,0:T(8,128)(2,1)S(1)}, u32[]{:S(2)}, u32[]{:S(2)}) collective-permute-start(bf16[264,128]{1,0:T(8,128)(2,1)S(1)} %series.1.refs_0_), channel_id=1, source_target_pairs={{0,2},{2,0},{4,6},{6,4},{8,10},{10,8},{12,14},{14,12},{16,18},{18,... | collective-permute-start | bytes 202760 | tf_op jit(solution)/shard_map/ppermute | solution.py:448
